TPU v7x, 32 devices: a whole 2x2x4 slice. The times are simulated.
32 devices in a mesh: ctx: 4 (over z), head: 4 (over y, x), rep: 2 (over core).
Axes of the slice: x: 2, y: 2, z: 4, core: 2. Of those that a mesh axis runs over, the one named last changes fastest.
Arguments:
- prefill_query: bfloat16 [2, 1024, 8192], P('rep', 'ctx', 'head'), may hold values from -6 to 6
- prefill_key: bfloat16 [2, 1024, 8192], P('rep', 'ctx', 'head'), may hold values from -0.5390625 to 0.5390625
- prefill_value: bfloat16 [2, 1024, 8192], P('rep', 'ctx', 'head'), as said below
- prefill_rate: float32 [2, 64, 1024], P('rep', 'head', 'ctx'), as said below
- out_weight: bfloat16 [8192, 6144], P('head'), may hold values from -0.0625 to 0.0625
- decode_query: bfloat16 [32, 2, 8192], P(('ctx', 'rep'), None, 'head'), may hold values from -6 to 6
- decode_key: bfloat16 [32, 2, 8192], P(('ctx', 'rep'), None, 'head'), may hold values from -0.5390625 to 0.5390625
- decode_value: bfloat16 [32, 2, 8192], P(('ctx', 'rep'), None, 'head'), may hold values from -6 to 6
- decode_rate: float32 [32, 64, 2], P(('ctx', 'rep'), 'head'), may hold values from 0.01 to 0.5
- prompt_of_row: int32 [32], P(('ctx', 'rep')), may hold values from 0 to 1
Outputs:
- prefill_out: bfloat16 [2, 1024, 6144], P('rep', 'ctx', 'head')
- decode_out: bfloat16 [32, 2, 6144], P(('ctx', 'rep'), None, 'head')
Inputs may be any that keep to these rules, and one draw needn't show every extreme that they name: `prefill_value`: values with row and column scales. `prefill_rate`: positive decay rates.
All inputs are finite; a program needn't handle non-finite values.
Results may differ from a plain program's by a relative error of at most 0.0055.
Values may be sent and summed in bfloat16 or wider, within the bound.
No kernel may reach another device: no remote copies, remote signals or barrier semaphores. Data moves between devices by JAX's collectives and lax.ppermute only.
A program may use at most 128 MiB of HBM per device.

v0:
```python
import jax
import jax.numpy as jnp
from jax import lax
from jax.sharding import PartitionSpec as P

HEAD_DIM = 128
BLOCK = 256


EPSILON = 1e-06
NEGATIVE = -1e30
HIGH = lax.Precision.HIGHEST


def normalize(array):
    return array * lax.rsqrt(jnp.mean(array * array, axis=-1, keepdims=True) + EPSILON)


def block_pass(queries, keys_local, values_local, rate_local):
    length_here = queries.shape[0]
    heads_here = queries.shape[1]
    count = length_here // BLOCK
    q_blocks = queries.reshape(count, BLOCK, heads_here, HEAD_DIM)
    k_blocks = keys_local.reshape(count, BLOCK, heads_here, HEAD_DIM)
    v_blocks = values_local.reshape(count, BLOCK, heads_here, HEAD_DIM)
    g_blocks = (-rate_local).reshape(heads_here, count, BLOCK).transpose(1, 0, 2)
    row_ids = jnp.arange(BLOCK)[:, None]
    col_ids = jnp.arange(BLOCK)[None, :]
    upper_ones = (row_ids <= col_ids).astype(jnp.float32)
    lower_mask = row_ids >= col_ids

    def advance(carry, inputs):
        state, offset = carry
        q_blk, k_blk, v_blk, g_blk = inputs
        cumul = jnp.dot(g_blk, upper_ones, precision=HIGH)
        total = cumul[:, -1]
        decay = jnp.exp(jnp.where(lower_mask, cumul[:, :, None] - cumul[:, None, :], NEGATIVE))
        scores = jnp.einsum("thd,shd->hts", q_blk, k_blk, preferred_element_type=jnp.float32)
        weights = (scores * decay).astype(jnp.bfloat16)
        intra = jnp.einsum("hts,she->the", weights, v_blk, preferred_element_type=jnp.float32)
        inter = (
            jnp.einsum("thd,hde->the", q_blk.astype(jnp.float32), state, precision=HIGH)
            * jnp.exp(cumul).T[:, :, None]
        )
        k_weighted = k_blk.astype(jnp.float32) * jnp.exp(total[:, None] - cumul).T[:, :, None]
        new_state = jnp.exp(total)[:, None, None] * state + jnp.einsum(
            "shd,she->hde", k_weighted, v_blk.astype(jnp.float32), precision=HIGH
        )
        return ((new_state, offset + total), (intra + inter, offset[:, None] + cumul))

    start = (
        jnp.zeros((heads_here, HEAD_DIM, HEAD_DIM), jnp.float32),
        jnp.zeros((heads_here,), jnp.float32),
    )
    (own_state, own_log), (outputs, dev_cumul) = lax.scan(
        advance, start, (q_blocks, k_blocks, v_blocks, g_blocks)
    )
    local_out = outputs.reshape(length_here, heads_here, HEAD_DIM)
    dev_cumul = dev_cumul.transpose(1, 0, 2).reshape(heads_here, length_here)
    return (local_out, dev_cumul, own_state, own_log)


def decode_pass(decode_query, decode_key, decode_value, decode_rate, prompt_of_row, finals):
    group_rows = decode_query.shape[0]
    heads_here = decode_rate.shape[1]
    steps_here = decode_query.shape[1]

    def split_heads(array):
        return array.reshape(group_rows, steps_here, heads_here, HEAD_DIM).astype(jnp.float32)

    d_query = split_heads(decode_query)
    d_key = split_heads(decode_key)
    d_value = split_heads(decode_value)
    cumul = jnp.cumsum(-decode_rate, axis=-1)
    onehot = (
        prompt_of_row[:, None] == jnp.arange(finals.shape[0], dtype=jnp.int32)[None, :]
    ).astype(jnp.float32)
    start_terms = jnp.einsum("rthd,phde->prthe", d_query, finals, precision=HIGH)
    baseline_level = (
        jnp.einsum("rp,prthe->rthe", onehot, start_terms, precision=HIGH)
        * jnp.exp(cumul).transpose(0, 2, 1)[..., None]
    )
    step_mask = jnp.arange(steps_here)[:, None] >= jnp.arange(steps_here)[None, :]
    decay = jnp.exp(jnp.where(step_mask, cumul[..., :, None] - cumul[..., None, :], NEGATIVE))
    scores = jnp.einsum("rthd,rshd->rhts", d_query, d_key, precision=HIGH)
    intra = jnp.einsum("rhts,rshe->rthe", scores * decay, d_value, precision=HIGH)
    return (
        normalize(baseline_level + intra)
        .astype(jnp.bfloat16)
        .reshape(group_rows * steps_here, heads_here * HEAD_DIM)
    )


def body(
    prefill_query,
    prefill_key,
    prefill_value,
    prefill_rate,
    out_weight,
    decode_query,
    decode_key,
    decode_value,
    decode_rate,
    prompt_of_row,
):
    heads_here = prefill_rate.shape[1]
    length_here = prefill_query.shape[1]
    queries = prefill_query[0].reshape(length_here, heads_here, HEAD_DIM)
    keys_local = prefill_key[0].reshape(length_here, heads_here, HEAD_DIM)
    values_local = prefill_value[0].reshape(length_here, heads_here, HEAD_DIM)
    local_out, dev_cumul, own_state, own_log = block_pass(
        queries, keys_local, values_local, prefill_rate[0]
    )
    group_logs = lax.all_gather(own_log[None, :], "ctx", axis=0, tiled=True)
    groups = group_logs.shape[0]
    my_group = lax.axis_index("ctx")
    inclusive = jnp.cumsum(group_logs, axis=0)
    exclusive = inclusive - group_logs
    mine = lax.dynamic_slice_in_dim(exclusive, my_group, 1, 0)
    group_ids = jnp.arange(groups, dtype=jnp.int32)[:, None]
    weight_in = jnp.where(group_ids < my_group, jnp.exp(jnp.minimum(mine - inclusive, 0.0)), 0.0)
    weight_end = jnp.exp(inclusive[-1:] - inclusive)
    piece = lax.all_gather(own_state[None], "ctx", axis=0, tiled=True)
    entering = jnp.einsum("ch,chde->hde", weight_in, piece, precision=HIGH)
    finals_here = jnp.einsum("ch,chde->hde", weight_end, piece, precision=HIGH)
    finals = lax.all_gather(finals_here[None], "rep", axis=0, tiled=True)
    carried = jnp.einsum("thd,hde->the", queries.astype(jnp.float32), entering, precision=HIGH)
    attended = local_out + jnp.exp(dev_cumul).T[:, :, None] * carried
    hidden = normalize(attended).astype(jnp.bfloat16).reshape(length_here, heads_here * HEAD_DIM)
    decode_hidden = decode_pass(
        decode_query, decode_key, decode_value, decode_rate, prompt_of_row, finals
    )
    group_rows = decode_query.shape[0]
    steps_here = decode_query.shape[1]
    token_terms = jnp.dot(hidden, out_weight, preferred_element_type=jnp.float32)
    prefill_part = lax.psum_scatter(token_terms, "head", scatter_dimension=1, tiled=True)
    decode_terms = jnp.dot(decode_hidden, out_weight, preferred_element_type=jnp.float32)
    decode_part = lax.psum_scatter(decode_terms, "head", scatter_dimension=1, tiled=True)
    prefill_out = prefill_part.astype(jnp.bfloat16)[None]
    decode_out = decode_part.astype(jnp.bfloat16).reshape(group_rows, steps_here, -1)
    return (prefill_out, decode_out)


def solution(mesh):
    return jax.shard_map(
        body,
        mesh=mesh,
        in_specs=(
            P("rep", "ctx", "head"),
            P("rep", "ctx", "head"),
            P("rep", "ctx", "head"),
            P("rep", "head", "ctx"),
            P("head", None),
            P(("ctx", "rep"), None, "head"),
            P(("ctx", "rep"), None, "head"),
            P(("ctx", "rep"), None, "head"),
            P(("ctx", "rep"), "head", None),
            P(("ctx", "rep")),
        ),
        out_specs=(P("rep", "ctx", "head"), P(("ctx", "rep"), None, "head")),
        check_vma=False,
    )
```

profile of v0, /device:TPU:0, one launch (start us, length us, event | category | flops | bytes accessed | tf_op | source)
XLA Modules:
  0.0 241.3 jit_solution(5645347157631992815)
XLA Ops:
  7.2 0.0 copy-start
  7.2 0.0 copy-start.4
  7.2 0.0 all-gather.6.cloned.1.call-start
  7.2 0.9 fusion.26
  8.2 0.2 slice_reduce_fusion
  8.4 0.1 fusion.42
  8.5 1.5 copy.83
  10.0 0.0 copy-start.1
  10.0 0.0 copy-done.4
  10.0 0.2 copy.85
  10.2 0.0 copy-start.2
  10.3 1.1 copy-done.2
  11.4 0.0 copy-start.7
  11.4 0.0 copy-start.10
  11.4 0.0 copy-start.6
  11.4 0.0 copy-start.5
  11.4 2.3 fusion.10
  13.7 0.0 copy-done.1
  13.7 0.0 copy-start.9
  13.7 0.0 all-gather.6.cloned.1.call-update
  13.8 0.0 all-gather.8.cloned.1.call-start
  13.8 0.0 copy-done.7
  13.8 0.0 copy-done.10
  13.8 0.6 dynamic-slice.1
  15.1 0.2 dynamic-update-slice
  15.4 13.5 %all-reduce = f32[64]{0:T(128)S(1)} all-reduce(f32[64]{0:T(128)S(1)} %dynamic-update-slice), channel_id=2, replica_groups=mesh['ctx'=4,'head'=4,'rep'=2] {'ctx'}, use_global_device_ids=true, to_apply=%add | all-reduce | flops 64 | bytes 512
  28.9 0.1 reshape.73
  29.0 0.1 exponential_bitcast_fusion.1
  29.1 0.1 copy.70
  29.2 0.1 copy.58
  29.3 0.1 copy.55
  29.4 0.0 copy-done.6
  29.4 0.0 copy-done.5
  29.4 0.2 copy.84
  29.7 0.0 copy-done.9
  29.7 0.1 fusion.39
  29.8 0.0 copy-done.8
  29.8 0.2 convolution_multiply_fusion
  30.0 67.4 %all-gather.6.cloned.1.call-done = f32[64,128,128]{2,1,0:T(8,128)} async-done(((f32[16,128,128]{2,1,0:T(8,128)}), f32[64,128,128]{2,1,0:T(8,128)}) %all-gather.6.cloned.1.call-update) | async-done | bytes 4194320 | tf_op jit(solution)/shard_map/all_gather | solution.py:123
  97.4 13.3 %fusion = f32[16,1,128,128]{3,1,2,0:T(1,128)} fusion(f32[4,16,1,1]{0,2,3,1:T(1,128)S(1)} %copy.70, f32[4,16,128,128]{3,2,1,0:T(8,128)} %bitcast.81), kind=kOutput, calls=%fused_computation | convolution fusion | flops 12582912 | bytes 5243136 | tf_op jit(solution)/shard_map/ch,chde->hde/dot_general | solution.py:125
  110.7 0.0 all-gather.8.cloned.1.call-update
  110.7 0.2 reduce-scatter.5.cloned.1.call-start
  111.0 1.0 fusion.21
  112.0 4.8 %fusion.9 = f32[16,256,128]{1,2,0:T(8,128)} fusion(bf16[256,16,128]{0,2,1:T(8,128)(2,1)} %bitcast.89, f32[16,256]{1,0:T(8,128)S(1)} %bitcast.98, pred[256,256]{1,0:T(8,128)(4,1)S(1)} %iota_compare_fusion.1, bf16[256,16,128]{2,1,0:T(8,128)(2,1)} %bitcast.91, bf16[256,16,128]{2,1,0:T(8,128)(2,1)S(1)} %bitcast.84), kind=kOutput, calls=%fused_computation.15 | convolution fusion | flops 541065216 | bytes 5324800 | tf_op jit(solution)/shard_map/while/body/eval_jaxpr/hts,she->the/dot_general | solution.py:40
  116.8 3.2 %multiply_reduce_fusion = f32[16,128,128]{2,1,0:T(8,128)S(1)} fusion(f32[16,4,128,128]{3,2,0,1:T(8,128)} %bitcast.82, f32[16,4]{0,1:T(4,128)S(1)} %get-tuple-element.27), kind=kLoop, calls=%fused_computation.2 | loop fusion | flops 1835008 | bytes 5243136 | tf_op jit(solution)/shard_map/ch,chde->hde/dot_general | solution.py:124
  120.0 0.1 copy-done.3
  120.1 1.6 multiply_reduce_fusion.1
  121.7 0.2 multiply_convert_fusion.1
  121.9 0.0 all-gather.8.cloned.1.call-done
  122.0 2.4 fusion.13
  124.3 0.4 fusion.27
  124.7 0.0 copy-done
  124.7 0.4 multiply_reduce_fusion.2
  125.2 0.1 multiply_convert_fusion.2
  125.4 10.6 %fusion.29 = f32[8,6144]{1,0:T(8,128)} fusion(bf16[2048,6144]{1,0:T(8,128)(2,1)} %param.14, bf16[1,8,16,128]{3,2,1,0:T(8,128)(2,1)S(1)} %bitcast.95), kind=kOutput, calls=%fused_computation.38 | convolution fusion | flops 201326592 | bytes 25395200 | tf_op jit(solution)/shard_map/dot_general | solution.py:137
  135.9 0.0 reduce-scatter.5.cloned.1.call-update
  136.0 0.3 reduce-scatter.3.cloned.1.call-start
  136.2 14.4 %fusion.43 = f32[256,6144]{1,0:T(8,128)} fusion(bf16[256,2048]{0,1:T(8,128)(2,1)S(1)} %bitcast.86, bf16[2048,6144]{1,0:T(8,128)(2,1)} %param.14), kind=kOutput, calls=%fused_computation.65 | convolution fusion | flops 6442450944 | bytes 32505856 | tf_op jit(solution)/shard_map/dot_general | solution.py:135
  150.6 0.0 reduce-scatter.3.cloned.1.call-update
  150.6 8.7 %reduce-scatter.5.cloned.1.call-done = f32[8,1536]{1,0:T(8,128)} async-done(((f32[8,6144]{1,0:T(8,128)}), f32[8,1536]{1,0:T(8,128)}) %reduce-scatter.5.cloned.1.call-update) | async-done | bytes 49168 | tf_op jit(solution)/shard_map/reduce_scatter | solution.py:138
  159.3 0.8 convert_element_type.35
  160.1 0.6 reshape.72
  160.7 71.7 %reduce-scatter.3.cloned.1.call-done = f32[256,1536]{1,0:T(8,128)} async-done(((f32[256,6144]{1,0:T(8,128)}), f32[256,1536]{1,0:T(8,128)}) %reduce-scatter.3.cloned.1.call-update) | async-done | bytes 1572880 | tf_op jit(solution)/shard_map/reduce_scatter | solution.py:136
  232.4 2.4 convert_bitcast_fusion
  (17 shorter events, 0.2 us)
Async XLA Ops:
  7.2 117.6 %copy-start = (bf16[4,2,2048]{2,1,0:T(2,128)(2,1)S(1)}, bf16[4,2,2048]{2,1,0:T(2,128)(2,1)}, u32[]{:S(2)}) copy-start(bf16[4,2,2048]{2,1,0:T(2,128)(2,1)} %param.17) | copy-start | bytes 98308
  7.2 2.8 %copy-start.4 = (bf16[1,256,2048]{2,1,0:T(8,128)(2,1)S(1)}, bf16[1,256,2048]{2,1,0:T(8,128)(2,1)}, u32[]{:S(2)}) copy-start(bf16[1,256,2048]{2,1,0:T(8,128)(2,1)} %param.12) | copy-start | bytes 3145732
  7.2 90.2 %all-gather.6.cloned.1.call-start = ((), (), s32[]{:S(2)}) async-start(), calls=%async_computation.4 | async-start | bytes 5242880 | tf_op jit(solution)/shard_map/all_gather | solution.py:123
  10.0 3.7 %copy-start.1 = (bf16[1,256,2048]{1,2,0:T(8,128)(2,1)}, bf16[1,256,2048]{1,2,0:T(8,128)(2,1)S(1)}, u32[]{:S(2)}) copy-start(bf16[1,256,2048]{1,2,0:T(8,128)(2,1)S(1)} %copy.83) | copy-start | bytes 3145732
  10.2 1.1 copy-start.2
  11.4 2.4 %copy-start.7 = (f32[4,16,2]{1,2,0:T(2,128)S(1)}, f32[4,16,2]{1,2,0:T(2,128)}, u32[]{:S(2)}) copy-start(f32[4,16,2]{1,2,0:T(2,128)} %param.18) | copy-start | bytes 1540
  11.4 2.5 %copy-start.10 = (u32[32]{0:T(128)S(1)}, u32[32]{0:T(128)}, u32[]{:S(2)}) copy-start(u32[32]{0:T(128)} %constant.59) | copy-start | bytes 388
  11.4 18.0 %copy-start.6 = (bf16[4,2,2048]{2,1,0:T(2,128)(2,1)S(1)}, bf16[4,2,2048]{2,1,0:T(2,128)(2,1)}, u32[]{:S(2)}) copy-start(bf16[4,2,2048]{2,1,0:T(2,128)(2,1)} %param.15) | copy-start | bytes 98308
  11.4 18.1 %copy-start.5 = (bf16[1,256,2048]{2,1,0:T(8,128)(2,1)S(1)}, bf16[1,256,2048]{2,1,0:T(8,128)(2,1)}, u32[]{:S(2)}) copy-start(bf16[1,256,2048]{2,1,0:T(8,128)(2,1)} %param.10) | copy-start | bytes 3145732
  13.7 16.0 %copy-start.9 = (s32[4]{0:T(128)S(1)}, s32[4]{0:T(128)}, u32[]{:S(2)}) copy-start(s32[4]{0:T(128)} %param.19) | copy-start | bytes 52
  13.7 16.1 %copy-start.8 = (bf16[4,2,2048]{2,1,0:T(2,128)(2,1)S(1)}, bf16[4,2,2048]{2,1,0:T(2,128)(2,1)}, u32[]{:S(2)}) copy-start(bf16[4,2,2048]{2,1,0:T(2,128)(2,1)} %param.16) | copy-start | bytes 98308
  13.8 108.2 %all-gather.8.cloned.1.call-start = ((), (), s32[]{:S(2)}) async-start(), calls=%async_computation.5 | async-start | bytes 3145728 | tf_op jit(solution)/shard_map/all_gather | solution.py:126
  110.7 48.6 %reduce-scatter.5.cloned.1.call-start = ((), (), s32[]{:S(2)}) async-start(), calls=%async_computation.3 | async-start | bytes 245760 | tf_op jit(solution)/shard_map/reduce_scatter | solution.py:138
  116.8 3.3 %copy-start.3 = (f32[16,256,128]{1,2,0:T(8,128)S(1)}, f32[16,256,128]{1,2,0:T(8,128)}, u32[]{:S(2)}) copy-start(f32[16,256,128]{1,2,0:T(8,128)} %fusion.9) | copy-start | bytes 6291460
  136.0 96.4 %reduce-scatter.3.cloned.1.call-start = ((), (), s32[]{:S(2)}) async-start(), calls=%async_computation.2 | async-start | bytes 7864320 | tf_op jit(solution)/shard_map/reduce_scatter | solution.py:136
Sparse Core Ops, SparseCore 0:
  13.9 83.4 all-gather.5
  110.8 9.0 all-gather.7
  136.1 23.1 reduce-scatter.4
  162.2 70.2 reduce-scatter.2
where the time goes:
time: 242 us; the launch traced here: 241 us
  waiting for transfers between devices  148 us (61%)
  matrix products  52.4 us (22%)
  between operations  14.7 us (6%)
  blocking collectives  13.5 us (6%)
  other arithmetic  7.12 us (3%)
  local copies, waits for them, and re-layouts  5.24 us (2%)
    reduce_scatter x1, waiting for transfers between devices, body(): lax.psum_scatter(token_terms, 'head', scatter_dimension=1, tiled=True)  71.7 us
    all_gather x1, waiting for transfers between devices, body(): piece = lax.all_gather(own_state[None], 'ctx', axis=0, tiled=True)  67.4 us
    dot_general x1, matrix products, body(): jnp.dot(hidden, out_weight, preferred_element_type=jnp.float32)  14.4 us
    unnamed x1, blocking collectives  13.5 us
    dot_general x1, matrix products, body(): finals_here = jnp.einsum('ch,chde->hde', weight_end, piece, precision=HIGH)  13.3 us
    dot_general x1, matrix products, body(): jnp.dot(decode_hidden, out_weight, preferred_element_type=jnp.float32)  10.6 us
    reduce_scatter x1, waiting for transfers between devices, body(): lax.psum_scatter(decode_terms, 'head', scatter_dimension=1, tiled=True)  8.67 us
  transfers between devices with their start and end apart: 4, of which 3 were waited for; matrix products, arithmetic and copies ran while one was open for 12% of the time, Pallas kernels for 0%

commit v1 on v0

v1 whole, which is shorter than its diff:
```python
import functools

import jax
import jax.numpy as jnp
from jax import lax
from jax.experimental import pallas as pl
from jax.experimental.pallas import tpu as pltpu
from jax.sharding import PartitionSpec as P

HEAD_DIM = 128
EPSILON = 1e-06
NEGATIVE = -1e30
HIGH = lax.Precision.HIGHEST
CHUNKS = 2
VMEM_BYTES = 40 * 2**20
F32 = jnp.float32
BF16 = jnp.bfloat16
NT = (((1,), (1,)), ((), ()))
TN = (((0,), (0,)), ((), ()))


def params():
    return pltpu.CompilerParams(vmem_limit_bytes=VMEM_BYTES)


def cost(flops, moved, exps=0):
    return pl.CostEstimate(flops=int(flops), bytes_accessed=int(moved), transcendentals=int(exps))


def normalize(array):
    return array * lax.rsqrt(jnp.mean(array * array, axis=-1, keepdims=True) + EPSILON)


def lower_ones(length):
    rows = lax.broadcasted_iota(jnp.int32, (length, length), 0)
    cols = lax.broadcasted_iota(jnp.int32, (length, length), 1)
    return rows >= cols


def decay_columns(rate, lower):
    return -lax.dot_general(lower.astype(F32), rate, NT, precision=HIGH, preferred_element_type=F32)


def decay_rows(rate, lower):
    return -lax.dot_general(rate, lower.astype(F32), NT, precision=HIGH, preferred_element_type=F32)


def head_slice(index):
    return slice(index * HEAD_DIM, (index + 1) * HEAD_DIM)


def halves(array):
    top = array.astype(BF16)
    return top, (array - top.astype(F32)).astype(BF16)


def state_kernel(k_ref, v_ref, rate_ref, own_ref):
    length = k_ref.shape[0]
    columns = decay_columns(rate_ref[...], lower_ones(length))
    factor = jnp.exp(columns[length - 1 :, :] - columns)
    for i in range(own_ref.shape[0]):
        values = v_ref[:, head_slice(i)]
        weighted = k_ref[:, head_slice(i)].astype(F32) * factor[:, i : i + 1]
        top, rest = halves(weighted)
        own_ref[i] = lax.dot_general(top, values, TN, preferred_element_type=F32) + lax.dot_general(
            rest, values, TN, preferred_element_type=F32
        )


def local_kernel(q_ref, k_ref, v_ref, rate_ref, local_ref):
    lower = lower_ones(q_ref.shape[0])
    rate = rate_ref[...]
    columns = decay_columns(rate, lower)
    rows = decay_rows(rate, lower)
    for i in range(rate.shape[0]):
        at = head_slice(i)
        scores = lax.dot_general(q_ref[:, at], k_ref[:, at], NT, preferred_element_type=F32)
        decay = jnp.exp(jnp.where(lower, columns[:, i : i + 1] - rows[i : i + 1, :], NEGATIVE))
        weights = (scores * decay).astype(BF16)
        local_ref[:, at] = jnp.dot(weights, v_ref[:, at], preferred_element_type=F32)


def hidden_kernel(q_ref, local_ref, state_ref, rate_ref, decode_ref, hidden_ref):
    length = q_ref.shape[0]
    factor = jnp.exp(decay_columns(rate_ref[...], lower_ones(length)))
    for i in range(state_ref.shape[0]):
        at = head_slice(i)
        inter = jnp.dot(q_ref[:, at], state_ref[i], preferred_element_type=F32)
        attended = local_ref[:, at] + inter * factor[:, i : i + 1]
        hidden_ref[:length, at] = normalize(attended).astype(BF16)
    hidden_ref[length:, :] = decode_ref[...]


def start_kernel(q_ref, own_ref, scale_ref, out_ref):
    for i in range(own_ref.shape[0]):
        at = head_slice(i)
        top, rest = halves(own_ref[i])
        queries = q_ref[:, at]
        terms = jnp.dot(queries, top, preferred_element_type=F32) + jnp.dot(
            queries, rest, preferred_element_type=F32
        )
        out_ref[:, at] = (terms * scale_ref[i : i + 1, :]).astype(BF16)


def project_kernel(place_ref, hidden_ref, weight_ref, out_ref):
    out_ref[...] = jnp.dot(
        hidden_ref[...], weight_ref[...], preferred_element_type=F32
    ).astype(out_ref.dtype)


def finish_kernel(own_p, ax_p, ay_p, bx_p, by_p, own_d, ax_d, ay_d, bx_d, by_d, prefill_ref, decode_ref):
    width = own_p.shape[2]
    rows = decode_ref.shape[0]

    def total(own, x_ref, y_ref, half):
        return own[half] + x_ref[0].astype(F32) + y_ref[0].astype(F32)

    prefill_ref[:, :width] = total(own_p, ax_p, ay_p, 0).astype(BF16)
    prefill_ref[:, width:] = total(own_p, bx_p, by_p, 1).astype(BF16)
    decode_ref[:, :width] = total(own_d, ax_d, ay_d, 0)[:rows].astype(BF16)
    decode_ref[:, width:] = total(own_d, bx_d, by_d, 1)[:rows].astype(BF16)


def swap(array, axis, size, bit):
    return lax.ppermute(array, axis, [(i, i ^ bit) for i in range(size)])


def body(
    prefill_query,
    prefill_key,
    prefill_value,
    prefill_rate,
    out_weight,
    decode_query,
    decode_key,
    decode_value,
    decode_rate,
    prompt_of_row,
    *,
    groups,
    reps,
    parts,
):
    length = prefill_query.shape[1]
    features = prefill_query.shape[2]
    heads = prefill_rate.shape[1]
    rows_here, steps = decode_query.shape[0], decode_query.shape[1]
    d_rows = rows_here * steps
    d_pad = -(-d_rows // 16) * 16
    total_rows = length + d_pad
    group = lax.axis_index("ctx")
    rep = lax.axis_index("rep")

    block_heads = 4 if heads % 4 == 0 else heads
    blocks = heads // block_heads
    wide = block_heads * HEAD_DIM
    rate = prefill_rate.reshape(blocks, block_heads, length)
    spec_tokens = pl.BlockSpec((None, length, wide), lambda i: (0, 0, i))
    spec_rate = pl.BlockSpec((None, block_heads, length), lambda i: (i, 0, 0))
    spec_state = pl.BlockSpec((block_heads, HEAD_DIM, HEAD_DIM), lambda i: (i, 0, 0))
    spec_local = pl.BlockSpec((length, wide), lambda i: (0, i))
    token_bytes = length * features * 2
    state_bytes = heads * HEAD_DIM * HEAD_DIM * 4

    own = pl.pallas_call(
        state_kernel,
        grid=(blocks,),
        in_specs=[spec_tokens, spec_tokens, spec_rate],
        out_specs=spec_state,
        out_shape=jax.ShapeDtypeStruct((heads, HEAD_DIM, HEAD_DIM), F32),
        compiler_params=params(),
        cost_estimate=cost(4 * length * features * HEAD_DIM, 2 * token_bytes + state_bytes),
        name="own_state",
    )(prefill_key, prefill_value, rate)
    log_total = -jnp.sum(prefill_rate[0], axis=-1)
    keep = jnp.exp(log_total)

    queries = decode_query.reshape(d_rows, features)
    log_top = log_total.astype(BF16)
    log_left = log_total - log_top.astype(F32)
    log_mid = log_left.astype(BF16)
    log_low = (log_left - log_mid.astype(F32)).astype(BF16)
    row_prompt = jnp.repeat(prompt_of_row, steps).astype(BF16)
    facts = jnp.concatenate([log_top, log_mid, log_low, row_prompt])
    facts = jnp.pad(facts, (0, features - facts.shape[0]))[None]
    message = jnp.concatenate([queries, facts], axis=0)
    message = jnp.pad(message, ((0, (-message.shape[0]) % 16), (0, 0)))
    slots = message[None]
    bit = 1
    while bit < groups:
        slots = jnp.concatenate([slots, swap(slots, "ctx", groups, bit)], axis=0)
        bit *= 2
    slot_facts = slots[:, d_rows, :].astype(F32)
    slot_logs = (
        slot_facts[:, :heads] + slot_facts[:, heads : 2 * heads] + slot_facts[:, 2 * heads : 3 * heads]
    )
    slot_prompts = slot_facts[:, 3 * heads : 3 * heads + d_rows]
    slot_groups = jnp.arange(groups, dtype=jnp.int32) ^ group
    later = jnp.sum(jnp.where((slot_groups > group)[:, None], slot_logs, 0.0), axis=0)
    scale = jnp.broadcast_to(jnp.exp(later)[:, None], (heads, HEAD_DIM))
    slot_queries = slots[:, :d_rows, :]
    both = jnp.concatenate([slot_queries[None], swap(slot_queries, "rep", reps, 1)[None]], axis=0)
    all_rows = reps * groups * d_rows
    part = pl.pallas_call(
        start_kernel,
        grid=(blocks,),
        in_specs=[
            pl.BlockSpec((all_rows, wide), lambda i: (0, i)),
            spec_state,
            pl.BlockSpec((None, block_heads, HEAD_DIM), lambda i: (i, 0, 0)),
        ],
        out_specs=pl.BlockSpec((all_rows, wide), lambda i: (0, i)),
        out_shape=jax.ShapeDtypeStruct((all_rows, features), BF16),
        compiler_params=params(),
        cost_estimate=cost(4 * all_rows * features * HEAD_DIM, state_bytes + all_rows * features * 4),
        name="decode_start",
    )(both.reshape(all_rows, features), own, scale.reshape(blocks, block_heads, HEAD_DIM))
    part = part.reshape(reps, groups, d_rows, features)
    other = swap(part[1], "rep", reps, 1)
    mine = (slot_prompts == rep.astype(F32))[:, :, None]
    base = jnp.where(mine, part[0], other)
    bit = groups // 2
    while bit >= 1:
        got = swap(base[bit:], "ctx", groups, bit)
        base = (base[:bit].astype(F32) + got.astype(F32)).astype(BF16 if bit > 1 else F32)
        bit //= 2

    def split_heads(array):
        return array.reshape(rows_here, steps, heads, HEAD_DIM).astype(F32)

    d_query, d_key, d_value = split_heads(decode_query), split_heads(decode_key), split_heads(decode_value)
    d_cumul = jnp.cumsum(-decode_rate, axis=-1)
    step_mask = jnp.arange(steps)[:, None] >= jnp.arange(steps)[None, :]
    d_decay = jnp.exp(
        jnp.where(step_mask, d_cumul[..., :, None] - d_cumul[..., None, :], NEGATIVE)
    )
    d_scores = jnp.einsum("rthd,rshd->rhts", d_query, d_key, precision=HIGH)
    d_intra = jnp.einsum("rhts,rshe->rthe", d_scores * d_decay, d_value, precision=HIGH)
    d_base = split_heads(base[0]) * jnp.exp(d_cumul).transpose(0, 2, 1)[..., None]
    decode_hidden = normalize(d_base + d_intra).astype(BF16).reshape(d_rows, features)
    decode_hidden = jnp.pad(decode_hidden, ((0, d_pad - d_rows), (0, 0)))

    chunks = CHUNKS if heads % CHUNKS == 0 else 1
    span = heads // chunks

    def pick(array, chunk):
        if isinstance(chunk, int):
            return array[:span]
        return lax.dynamic_slice_in_dim(array, jnp.clip(chunk, 0, chunks - 1) * span, span, 0)

    received = []
    for step in range(chunks + groups - 2):
        chunk = 0 if step == 0 else step - group
        value = pick(own, chunk)
        if received:
            value = value + pick(keep, chunk)[:, None, None] * received[-1].astype(F32)
        received.append(
            lax.ppermute(value.astype(BF16), "ctx", [(i, i + 1) for i in range(groups - 1)])
        )
    entering = []
    for chunk in range(chunks):
        state = received[chunk]
        for g in range(2, groups):
            state = jnp.where(group == g, received[chunk + g - 1], state)
        entering.append(state)
    entering = jnp.concatenate(entering, axis=0)

    local = pl.pallas_call(
        local_kernel,
        grid=(blocks,),
        in_specs=[spec_tokens, spec_tokens, spec_tokens, spec_rate],
        out_specs=spec_local,
        out_shape=jax.ShapeDtypeStruct((length, features), F32),
        compiler_params=params(),
        cost_estimate=cost(
            4 * length * length * features, 5 * token_bytes, heads * length * length
        ),
        name="local_attention",
    )(prefill_query, prefill_key, prefill_value, rate)

    hidden = pl.pallas_call(
        hidden_kernel,
        grid=(blocks,),
        in_specs=[
            spec_tokens,
            spec_local,
            spec_state,
            spec_rate,
            pl.BlockSpec((d_pad, wide), lambda i: (0, i)),
        ],
        out_specs=pl.BlockSpec((total_rows, wide), lambda i: (0, i)),
        out_shape=jax.ShapeDtypeStruct((total_rows, features), BF16),
        compiler_params=params(),
        cost_estimate=cost(2 * length * features * HEAD_DIM, 4 * token_bytes + state_bytes // 2),
        name="hidden",
    )(prefill_query, local, entering, rate, decode_hidden)

    out_columns = out_weight.shape[1]
    if parts != 4 or (out_columns // parts) % 512 != 0:
        terms = jnp.dot(hidden, out_weight, preferred_element_type=F32)
        summed = lax.psum_scatter(terms, "head", scatter_dimension=1, tiled=True)
        prefill_out = summed[:length].astype(BF16)[None]
        decode_out = summed[length : length + d_rows].astype(BF16)
        return prefill_out, decode_out.reshape(rows_here, steps, -1)

    half = out_columns // parts // 2
    tiles = 2
    tile = half // tiles
    me = lax.axis_index("head")
    x_side, y_side, far = me ^ 1, me ^ 2, me ^ 3

    def project(places, dtype):
        count = len(places)
        return pl.pallas_call(
            project_kernel,
            grid_spec=pltpu.PrefetchScalarGridSpec(
                num_scalar_prefetch=1,
                grid=(count, tiles),
                in_specs=[
                    pl.BlockSpec((total_rows, features), lambda i, j, place: (0, 0)),
                    pl.BlockSpec((features, tile), lambda i, j, place: (0, place[i] * tiles + j)),
                ],
                out_specs=pl.BlockSpec((None, total_rows, tile), lambda i, j, place: (i, 0, j)),
            ),
            out_shape=jax.ShapeDtypeStruct((count, total_rows, half), dtype),
            compiler_params=params(),
            cost_estimate=cost(
                2 * total_rows * features * half * count,
                count * half * (features * 2 + total_rows * 4) + total_rows * features * 2,
            ),
            name="project",
        )(jnp.stack(places).astype(jnp.int32), hidden, out_weight)

    far_a = swap(project([far * 2], BF16), "head", parts, 1)
    far_b = swap(project([far * 2 + 1], BF16), "head", parts, 2)
    x_a = swap(project([x_side * 2], BF16), "head", parts, 1)
    y_b = swap(project([y_side * 2 + 1], BF16), "head", parts, 2)
    relay = project([y_side * 2, x_side * 2 + 1], F32)
    mine_f = project([me * 2, me * 2 + 1], F32)
    y_a = swap((relay[:1] + far_a.astype(F32)).astype(BF16), "head", parts, 2)
    x_b = swap((relay[1:] + far_b.astype(F32)).astype(BF16), "head", parts, 1)

    row_tile = 64 if length % 64 == 0 else length
    def at_rows(count):
        return pl.BlockSpec((count, row_tile, half), lambda i: (0, i, 0))

    def at_tail(count):
        return pl.BlockSpec((count, 16, half), lambda i: (0, length // 16, 0))

    if d_pad != 16 or length % 16 != 0:
        both_halves = [
            mine_f[0] + x_a[0].astype(F32) + y_a[0].astype(F32),
            mine_f[1] + x_b[0].astype(F32) + y_b[0].astype(F32),
        ]
        summed = jnp.concatenate(both_halves, axis=1).astype(BF16)
        return summed[:length][None], summed[length : length + d_rows].reshape(rows_here, steps, -1)
    pieces = (mine_f, x_a, y_a, x_b, y_b)
    prefill_out, decode_out = pl.pallas_call(
        finish_kernel,
        grid=(length // row_tile,),
        in_specs=[at_rows(p.shape[0]) for p in pieces] + [at_tail(p.shape[0]) for p in pieces],
        out_specs=[
            pl.BlockSpec((None, row_tile, 2 * half), lambda i: (0, i, 0)),
            pl.BlockSpec((d_rows, 2 * half), lambda i: (0, 0)),
        ],
        out_shape=[
            jax.ShapeDtypeStruct((1, length, 2 * half), BF16),
            jax.ShapeDtypeStruct((d_rows, 2 * half), BF16),
        ],
        compiler_params=params(),
        cost_estimate=cost(6 * total_rows * half, 20 * total_rows * half),
        name="finish",
    )(*pieces, *pieces)
    return prefill_out, decode_out.reshape(rows_here, steps, -1)


def solution(mesh):
    return jax.shard_map(
        functools.partial(
            body, groups=mesh.shape["ctx"], reps=mesh.shape["rep"], parts=mesh.shape["head"]
        ),
        mesh=mesh,
        in_specs=(
            P("rep", "ctx", "head"),
            P("rep", "ctx", "head"),
            P("rep", "ctx", "head"),
            P("rep", "head", "ctx"),
            P("head", None),
            P(("ctx", "rep"), None, "head"),
            P(("ctx", "rep"), None, "head"),
            P(("ctx", "rep"), None, "head"),
            P(("ctx", "rep"), "head", None),
            P(("ctx", "rep")),
        ),
        out_specs=(P("rep", "ctx", "head"), P(("ctx", "rep"), None, "head")),
        check_vma=False,
    )
```

time: 242 us -> 110 us (0.45)
  waiting for transfers between devices: 148 us -> 16.1 us
  matrix products: 52.4 us -> 0.56 us
  Pallas kernels: 0 us -> 38.8 us
  starting transfers between devices: 0.56 us -> 30.4 us
  between operations: 14.7 us -> 1.05 us
  blocking collectives: 13.5 us -> 0 us
  local copies, waits for them, and re-layouts: 5.24 us -> 13.2 us
    reduce_scatter x2 -> x0, waiting for transfers between devices: 80.3 us -> none  [the longest x1 71.7 us: body(): lax.psum_scatter(token_terms, 'head', scatter_dimension=1, tiled=True)]
    all_gather x2 -> x0, waiting for transfers between devices: 67.4 us -> none  [the longest x1 67.4 us: body(): piece = lax.all_gather(own_state[None], 'ctx', axis=0, tiled=True)]
    dot_general x12 -> x2, matrix products: 52.4 us -> 0.56 us  [the longest x1 0.35 us: body(): jnp.einsum('rhts,rshe->rthe', d_scores * d_decay, d_value, precision=HIGH)]
    pallas_call x0 -> x11, Pallas kernels: none -> 38.8 us  [the longest x6 24.1 us: project(): pl.pallas_call(project_kernel, grid_spec=pltpu.PrefetchScalarGridSpec(num...]
    ppermute x0 -> x16, starting transfers between devices: none -> 30.4 us  [the longest x4 16.4 us: body(): lax.ppermute(value.astype(BF16), 'ctx', [(i, i + 1) for i in range(groups...]
    ppermute x0 -> x16, waiting for transfers between devices: none -> 16.1 us  [the longest x4 14 us: body(): lax.ppermute(value.astype(BF16), 'ctx', [(i, i + 1) for i in range(groups...]
    unnamed x1 -> x0, blocking collectives: 13.5 us -> none
    unnamed x27 -> x31, local copies, waits for them, and re-layouts: 2.49 us -> 6.21 us
  transfers between devices with their start and end apart: 4 -> 16, of which waited for: 3 -> 6; matrix products, arithmetic and copies ran while one was open for 12% -> 12% of each run, Pallas kernels for 0% -> 28%
where the time goes in v1:
time: 110 us; the launch traced here: 109 us
  Pallas kernels  38.8 us (35%)
  starting transfers between devices  30.4 us (28%)
  waiting for transfers between devices  16.1 us (15%)
  local copies, waits for them, and re-layouts  13.2 us (12%)
  other arithmetic  9.32 us (8%)
    pallas_call x6, Pallas kernels, project(): pl.pallas_call(project_kernel, grid_spec=pltpu.PrefetchScalarGridSpec(num...  24.1 us
    ppermute x4, starting transfers between devices, body(): lax.ppermute(value.astype(BF16), 'ctx', [(i, i + 1) for i in range(groups...  16.4 us
    ppermute x12, starting transfers between devices, swap(): return lax.ppermute(array, axis, [(i, i ^ bit) for i in range(size)])  14 us
    ppermute x4, waiting for transfers between devices, body(): lax.ppermute(value.astype(BF16), 'ctx', [(i, i + 1) for i in range(groups...  14 us
    unnamed x31, local copies, waits for them, and re-layouts  6.21 us
    pallas_call x1, Pallas kernels, body(): pl.pallas_call(state_kernel, grid=(blocks,), in_specs=[spec_tokens, spec_...  4.4 us
    pallas_call x1, Pallas kernels, body(): pl.pallas_call(local_kernel, grid=(blocks,), in_specs=[spec_tokens, spec_...  4.07 us
    pallas_call x1, Pallas kernels, body(): pl.pallas_call(hidden_kernel, grid=(blocks,), in_specs=[spec_tokens, spec...  3.47 us
  transfers between devices with their start and end apart: 16, of which 6 were waited for; matrix products, arithmetic and copies ran while one was open for 12% of the time, Pallas kernels for 28%

profile of v1, /device:TPU:0, one launch (start us, length us, event | category | flops | bytes accessed | tf_op | source)
XLA Modules:
  0.0 109.5 jit_solution(16060954481774706298)
XLA Ops:
  0.6 0.8 reduce_sum.27
  1.5 0.7 convert_element_type.100
  2.2 0.1 convert_element_type.101
  2.4 0.8 reshape.69
  3.2 3.1 %collective-permute-start.4 = (bf16[1,16,2048]{2,1,0:T(8,128)(2,1)S(1)}, bf16[1,16,2048]{2,1,0:T(8,128)(2,1)S(1)}, u32[]{:S(2)}, u32[]{:S(2)}) collective-permute-start(bf16[1,16,2048]{2,1,0:T(8,128)(2,1)S(1)} %fusion.6), channel_id=1, source_target_pairs={{0,8},{8,0},{16,24},{24,16},{1,9},{9,1},{17,25},{25,17},{2,10},{10... | collective-permute-start | bytes 196616 | tf_op jit(solution)/shard_map/ppermute | solution.py:125
  6.3 0.7 reshape.68.rate_ref
  7.0 1.2 %copy-done.1 = bf16[1,256,2048]{2,1,0:T(8,128)(2,1)S(1)} copy-done((bf16[1,256,2048]{2,1,0:T(8,128)(2,1)S(1)}, bf16[1,256,2048]{2,1,0:T(8,128)(2,1)}, u32[]{:S(2)}) %copy-start.1) | copy-done | bytes 1048600
  8.3 1.2 %copy-done.3 = bf16[1,256,2048]{2,1,0:T(8,128)(2,1)S(1)} copy-done((bf16[1,256,2048]{2,1,0:T(8,128)(2,1)S(1)}, bf16[1,256,2048]{2,1,0:T(8,128)(2,1)}, u32[]{:S(2)}) %copy-start.3) | copy-done | bytes 1048600
  9.5 4.4 %own_state.1.own_ref = f32[16,128,128]{2,1,0:T(8,128)S(1)} custom-call(bf16[1,256,2048]{2,1,0:T(8,128)(2,1)S(1)} %copy-done.1, bf16[1,256,2048]{2,1,0:T(8,128)(2,1)S(1)} %copy-done.3, f32[4,4,256]{2,1,0:T(4,128)S(1)} %reshape.68.rate_ref), custom_call_target="tpu_custom_call" | custom-call | flops 268435456 | bytes 3145728 | tf_op jit(solution)/shard_map/own_state/pallas_call | solution.py:165
  13.9 0.7 slice.99
  14.6 2.6 %collective-permute-start = (bf16[8,128,128]{2,1,0:T(8,128)(2,1)}, bf16[8,128,128]{2,1,0:T(8,128)(2,1)}, u32[]{:S(2)}, u32[]{:S(2)}) collective-permute-start(bf16[8,128,128]{2,1,0:T(8,128)(2,1)} %slice.99), channel_id=1, source_target_pairs={{0,8},{8,16},{16,24},{1,9},{9,17},{17,25},{2,10},{10,18},{18,26},{... | collective-permute-start | bytes 786440 | tf_op jit(solution)/shard_map/ppermute | solution.py:258
  17.3 0.1 copy.25
  17.4 0.6 exponential_bitcast_fusion
  18.0 0.2 convolution_multiply_fusion
  18.2 0.3 fusion.7
  18.6 0.5 xor_compare_fusion
  19.2 0.7 pad_maximum_fusion.4
  19.8 2.4 %collective-permute-start.5 = (bf16[2,16,2048]{2,1,0:T(8,128)(2,1)}, bf16[2,16,2048]{2,1,0:T(8,128)(2,1)S(1)}, u32[]{:S(2)}, u32[]{:S(2)}) collective-permute-start(bf16[2,16,2048]{2,1,0:T(8,128)(2,1)} %pad_maximum_fusion.4), channel_id=1, source_target_pairs={{0,16},{8,24},{16,0},{24,8},{1,17},{9,25},{17,1},{25,9},{2,18},{10... | collective-permute-start | bytes 393224 | tf_op jit(solution)/shard_map/ppermute | solution.py:125
  22.2 1.2 %copy-done.2 = bf16[1,256,2048]{2,1,0:T(8,128)(2,1)S(1)} copy-done((bf16[1,256,2048]{2,1,0:T(8,128)(2,1)S(1)}, bf16[1,256,2048]{2,1,0:T(8,128)(2,1)}, u32[]{:S(2)}) %copy-start.2) | copy-done | bytes 1048600
  23.4 1.2 %copy-done.4 = bf16[1,256,2048]{2,1,0:T(8,128)(2,1)S(1)} copy-done((bf16[1,256,2048]{2,1,0:T(8,128)(2,1)S(1)}, bf16[1,256,2048]{2,1,0:T(8,128)(2,1)}, u32[]{:S(2)}) %copy-start.4) | copy-done | bytes 1048600
  24.6 1.2 %copy-done.5 = bf16[1,256,2048]{2,1,0:T(8,128)(2,1)S(1)} copy-done((bf16[1,256,2048]{2,1,0:T(8,128)(2,1)S(1)}, bf16[1,256,2048]{2,1,0:T(8,128)(2,1)}, u32[]{:S(2)}) %copy-start.5) | copy-done | bytes 1048600
  25.8 4.1 %local_attention.1.local_ref = f32[256,2048]{1,0:T(8,128)S(1)} custom-call(bf16[1,256,2048]{2,1,0:T(8,128)(2,1)S(1)} %copy-done.5, bf16[1,256,2048]{2,1,0:T(8,128)(2,1)S(1)} %copy-done.2, bf16[1,256,2048]{2,1,0:T(8,128)(2,1)S(1)} %copy-done.4, f32[4,4,256]{2,1,0:T(4,128)S(1)} %reshape.68.rate_ref), custom_call_target="tpu_custom_call" | custom-call | flops 536870912 | bytes 5242880 | tf_op jit(solution)/shard_map/local_attention/pallas_call | solution.py:268
  29.9 0.7 fusion.21
  30.6 0.6 pad_maximum_fusion.2
  31.3 0.7 fusion.19
  32.0 0.5 exp.24
  32.6 1.3 %exp.25 = f32[4,4]{1,0:T(4,128)} reshape(f32[16]{0:T(128)} %exp.24) | data formatting | bytes 128 | tf_op jit(solution)/shard_map/exp | solution.py:200
  33.9 0.9 pad_maximum_fusion.1
  34.8 0.7 broadcast_in_dim.68.scale_ref
  35.6 1.0 decode_start.1
  36.6 0.6 collective-permute-start.7
  37.3 0.9 collective-permute-done.7
  38.2 0.1 fusion.2
  38.3 0.7 collective-permute-start.8
  38.9 1.1 add_convert_fusion.2
  40.0 4.9 %collective-permute-start.1 = (bf16[8,128,128]{2,1,0:T(8,128)(2,1)S(1)}, bf16[8,128,128]{2,1,0:T(8,128)(2,1)S(1)}, u32[]{:S(2)}, u32[]{:S(2)}) collective-permute-start(bf16[8,128,128]{2,1,0:T(8,128)(2,1)S(1)} %add_convert_fusion.2), channel_id=1, source_target_pairs={{0,8},{8,16},{16,24},{1,9},{9,17},{17,25},{2,10},{10,18},{18,26},{... | collective-permute-start | bytes 786440 | tf_op jit(solution)/shard_map/ppermute | solution.py:258
  44.9 0.1 collective-permute-done.8
  45.1 5.9 %collective-permute-done.1 = bf16[8,128,128]{2,1,0:T(8,128)(2,1)S(1)} collective-permute-done((bf16[8,128,128]{2,1,0:T(8,128)(2,1)S(1)}, bf16[8,128,128]{2,1,0:T(8,128)(2,1)S(1)}, u32[]{:S(2)}, u32[]{:S(2)}) %collective-permute-start.1) | collective-permute-done | bytes 262176 | tf_op jit(solution)/shard_map/ppermute | solution.py:258
  51.0 0.1 add_convert_fusion.1
  51.2 4.4 %collective-permute-start.2 = (bf16[8,128,128]{2,1,0:T(8,128)(2,1)S(1)}, bf16[8,128,128]{2,1,0:T(8,128)(2,1)S(1)}, u32[]{:S(2)}, u32[]{:S(2)}) collective-permute-start(bf16[8,128,128]{2,1,0:T(8,128)(2,1)S(1)} %add_convert_fusion.1), channel_id=1, source_target_pairs={{0,8},{8,16},{16,24},{1,9},{9,17},{17,25},{2,10},{10,18},{18,26},{... | collective-permute-start | bytes 786440 | tf_op jit(solution)/shard_map/ppermute | solution.py:258
  55.6 0.2 multiply_reduce_fusion
  55.8 4.3 %collective-permute-done.2 = bf16[8,128,128]{2,1,0:T(8,128)(2,1)S(1)} collective-permute-done((bf16[8,128,128]{2,1,0:T(8,128)(2,1)S(1)}, bf16[8,128,128]{2,1,0:T(8,128)(2,1)S(1)}, u32[]{:S(2)}, u32[]{:S(2)}) %collective-permute-start.2) | collective-permute-done | bytes 262176 | tf_op jit(solution)/shard_map/ppermute | solution.py:258
  60.2 0.1 add_convert_fusion
  60.3 4.5 %collective-permute-start.3 = (bf16[8,128,128]{2,1,0:T(8,128)(2,1)S(1)}, bf16[8,128,128]{2,1,0:T(8,128)(2,1)S(1)}, u32[]{:S(2)}, u32[]{:S(2)}) collective-permute-start(bf16[8,128,128]{2,1,0:T(8,128)(2,1)S(1)} %add_convert_fusion), channel_id=1, source_target_pairs={{0,8},{8,16},{16,24},{1,9},{9,17},{17,25},{2,10},{10,18},{18,26},{... | collective-permute-start | bytes 786440 | tf_op jit(solution)/shard_map/ppermute | solution.py:258
  64.9 0.1 multiply_convert_fusion
  65.0 3.7 %collective-permute-done.3 = bf16[8,128,128]{2,1,0:T(8,128)(2,1)S(1)} collective-permute-done((bf16[8,128,128]{2,1,0:T(8,128)(2,1)S(1)}, bf16[8,128,128]{2,1,0:T(8,128)(2,1)S(1)}, u32[]{:S(2)}, u32[]{:S(2)}) %collective-permute-start.3) | collective-permute-done | bytes 262176 | tf_op jit(solution)/shard_map/ppermute | solution.py:258
  68.7 1.0 select_select_fusion.1
  69.8 3.5 %hidden.1.hidden_ref = bf16[272,2048]{1,0:T(8,128)(2,1)S(1)} custom-call(bf16[1,256,2048]{2,1,0:T(8,128)(2,1)S(1)} %copy-done.6, f32[256,2048]{1,0:T(8,128)S(1)} %local_attention.1.local_ref, bf16[16,128,128]{2,1,0:T(8,128)(2,1)S(1)} %pad_maximum_fusion.state_ref, f32[4,4,256]{2,1,0:T(4,128)S(1)} %reshape.68.rate_ref, bf16[16,2048]{1,0:T(8,128)(2,1)S(1)} %pad.14.decode_ref), custom_call_target="tpu_custom_call" | custom-call | flops 134217728 | bytes 4718592 | tf_op jit(solution)/shard_map/hidden/pallas_call | solution.py:281
  73.3 3.0 %project.10 = bf16[1,272,768]{2,1,0:T(8,128)(2,1)S(1)} custom-call(s32[1]{0:T(128)} %bitcast.17.place_ref, bf16[272,2048]{1,0:T(8,128)(2,1)S(1)} %hidden.1.hidden_ref, bf16[2048,6144]{1,0:T(8,128)(2,1)} %weight_ref.11), custom_call_target="tpu_custom_call" | custom-call | flops 855638016 | bytes 5095424 | tf_op jit(solution)/shard_map/project/pallas_call | solution.py:314
  76.2 1.6 %collective-permute-start.13 = (bf16[1,272,768]{2,1,0:T(8,128)(2,1)S(1)}, bf16[1,272,768]{2,1,0:T(8,128)(2,1)S(1)}, u32[]{:S(2)}, u32[]{:S(2)}) collective-permute-start(bf16[1,272,768]{2,1,0:T(8,128)(2,1)S(1)} %project.10), channel_id=1, source_target_pairs={{0,4},{2,6},{4,0},{6,2},{1,5},{3,7},{5,1},{7,3},{8,12},{10,14},{12... | collective-permute-start | bytes 1253384 | tf_op jit(solution)/shard_map/ppermute | solution.py:125
  77.8 3.0 %project.9 = bf16[1,272,768]{2,1,0:T(8,128)(2,1)S(1)} custom-call(s32[1]{0:T(128)} %bitcast.16.place_ref, bf16[272,2048]{1,0:T(8,128)(2,1)S(1)} %hidden.1.hidden_ref, bf16[2048,6144]{1,0:T(8,128)(2,1)} %weight_ref.11), custom_call_target="tpu_custom_call" | custom-call | flops 855638016 | bytes 5095424 | tf_op jit(solution)/shard_map/project/pallas_call | solution.py:314
  80.8 1.5 %collective-permute-start.11 = (bf16[1,272,768]{2,1,0:T(8,128)(2,1)S(1)}, bf16[1,272,768]{2,1,0:T(8,128)(2,1)S(1)}, u32[]{:S(2)}, u32[]{:S(2)}) collective-permute-start(bf16[1,272,768]{2,1,0:T(8,128)(2,1)S(1)} %project.9), channel_id=1, source_target_pairs={{0,2},{2,0},{4,6},{6,4},{1,3},{3,1},{5,7},{7,5},{8,10},{10,8},{12,... | collective-permute-start | bytes 1253384 | tf_op jit(solution)/shard_map/ppermute | solution.py:125
  82.4 3.0 %project.11 = bf16[1,272,768]{2,1,0:T(8,128)(2,1)S(1)} custom-call(s32[1]{0:T(128)} %bitcast.18.place_ref, bf16[272,2048]{1,0:T(8,128)(2,1)S(1)} %hidden.1.hidden_ref, bf16[2048,6144]{1,0:T(8,128)(2,1)} %weight_ref.11), custom_call_target="tpu_custom_call" | custom-call | flops 855638016 | bytes 5095424 | tf_op jit(solution)/shard_map/project/pallas_call | solution.py:314
  85.4 0.6 collective-permute-start.15
  85.9 3.6 %project.7 = bf16[1,272,768]{2,1,0:T(8,128)(2,1)} custom-call(s32[1]{0:T(128)} %bitcast.13.place_ref, bf16[272,2048]{1,0:T(8,128)(2,1)S(1)} %hidden.1.hidden_ref, bf16[2048,6144]{1,0:T(8,128)(2,1)} %weight_ref.11), custom_call_target="tpu_custom_call" | custom-call | flops 855638016 | bytes 5095424 | tf_op jit(solution)/shard_map/project/pallas_call | solution.py:314
  89.5 0.5 collective-permute-start.10
  90.1 5.8 %project.8 = f32[2,272,768]{2,1,0:T(8,128)S(1)} custom-call(s32[2]{0:T(128)S(1)} %pad_add_fusion.1.place_ref, bf16[272,2048]{1,0:T(8,128)(2,1)S(1)} %hidden.1.hidden_ref, bf16[2048,6144]{1,0:T(8,128)(2,1)} %weight_ref.11), custom_call_target="tpu_custom_call" | custom-call | flops 1711276032 | bytes 9076736 | tf_op jit(solution)/shard_map/project/pallas_call | solution.py:314
  95.9 1.1 %fusion = (bf16[1,272,768]{2,1,0:T(8,128)(2,1)}, bf16[1,272,768]{2,1,0:T(8,128)(2,1)}) fusion(f32[2,272,768]{2,1,0:T(8,128)S(1)} %project.8, bf16[1,272,768]{2,1,0:T(8,128)(2,1)S(1)} %collective-permute-done.13, bf16[1,272,768]{2,1,0:T(8,128)(2,1)S(1)} %collective-permute-done.11), kind=kLoop, calls=%fused_computation.2 | loop fusion | flops 1253376 | bytes 3342336 | tf_op jit(solution)/shard_map/convert_element_type | solution.py:341
  97.1 1.5 %collective-permute-start.12 = (bf16[1,272,768]{2,1,0:T(8,128)(2,1)}, bf16[1,272,768]{2,1,0:T(8,128)(2,1)S(1)}, u32[]{:S(2)}, u32[]{:S(2)}) collective-permute-start(bf16[1,272,768]{2,1,0:T(8,128)(2,1)} %get-tuple-element.7), channel_id=1, source_target_pairs={{0,4},{2,6},{4,0},{6,2},{1,5},{3,7},{5,1},{7,3},{8,12},{10,14},{12... | collective-permute-start | bytes 1253384 | tf_op jit(solution)/shard_map/ppermute | solution.py:125
  98.6 1.5 %collective-permute-start.14 = (bf16[1,272,768]{2,1,0:T(8,128)(2,1)}, bf16[1,272,768]{2,1,0:T(8,128)(2,1)S(1)}, u32[]{:S(2)}, u32[]{:S(2)}) collective-permute-start(bf16[1,272,768]{2,1,0:T(8,128)(2,1)} %get-tuple-element.6), channel_id=1, source_target_pairs={{0,2},{2,0},{4,6},{6,4},{1,3},{3,1},{5,7},{7,5},{8,10},{10,8},{12,... | collective-permute-start | bytes 1253384 | tf_op jit(solution)/shard_map/ppermute | solution.py:125
  100.1 5.8 %project.6.own_p.own_d = f32[2,272,768]{2,1,0:T(8,128)S(1)} custom-call(s32[2]{0:T(128)S(1)} %pad_add_fusion.place_ref, bf16[272,2048]{1,0:T(8,128)(2,1)S(1)} %hidden.1.hidden_ref, bf16[2048,6144]{1,0:T(8,128)(2,1)} %weight_ref.11), custom_call_target="tpu_custom_call" | custom-call | flops 1711276032 | bytes 9076736 | tf_op jit(solution)/shard_map/project/pallas_call | solution.py:314
  106.0 1.1 %collective-permute-done.14.bx_p.bx_d = bf16[1,272,768]{2,1,0:T(8,128)(2,1)S(1)} collective-permute-done((bf16[1,272,768]{2,1,0:T(8,128)(2,1)}, bf16[1,272,768]{2,1,0:T(8,128)(2,1)S(1)}, u32[]{:S(2)}, u32[]{:S(2)}) %collective-permute-start.14) | collective-permute-done | bytes 417824 | tf_op jit(solution)/shard_map/ppermute | solution.py:125
  107.1 1.8 %finish.1 = (bf16[1,256,1536]{2,1,0:T(8,128)(2,1)}, bf16[8,1536]{1,0:T(8,128)(2,1)S(1)}) custom-call(f32[2,272,768]{2,1,0:T(8,128)S(1)} %project.6.own_p.own_d, bf16[1,272,768]{2,1,0:T(8,128)(2,1)S(1)} %collective-permute-done.10.ax_p.ax_d, bf16[1,272,768]{2,1,0:T(8,128)(2,1)S(1)} %collective-permute-done.12.ay_p.ay_d, ...), custom_call_target="tpu_custom_call" | custom-call | flops 1253376 | bytes 4177920 | tf_op jit(solution)/shard_map/finish/pallas_call | solution.py:358
  108.9 0.6 reshape.75
  (59 shorter events, 0.8 us)
Async XLA Ops:
  0.6 17.6 %copy-start = (bf16[4,2,2048]{2,1,0:T(2,128)(2,1)S(1)}, bf16[4,2,2048]{2,1,0:T(2,128)(2,1)}, u32[]{:S(2)}) copy-start(bf16[4,2,2048]{2,1,0:T(2,128)(2,1)} %param.17) | copy-start | bytes 98308
  3.2 15.9 %collective-permute-start.4 = (bf16[1,16,2048]{2,1,0:T(8,128)(2,1)S(1)}, bf16[1,16,2048]{2,1,0:T(8,128)(2,1)S(1)}, u32[]{:S(2)}, u32[]{:S(2)}) collective-permute-start(bf16[1,16,2048]{2,1,0:T(8,128)(2,1)S(1)} %fusion.6), channel_id=1, source_target_pairs={{0,8},{8,0},{16,24},{24,16},{1,9},{9,1},{17,25},{25,17},{2,10},{10... | collective-permute-start | bytes 196616 | tf_op jit(solution)/shard_map/ppermute | solution.py:125
  7.0 1.2 %copy-start.1 = (bf16[1,256,2048]{2,1,0:T(8,128)(2,1)S(1)}, bf16[1,256,2048]{2,1,0:T(8,128)(2,1)}, u32[]{:S(2)}) copy-start(bf16[1,256,2048]{2,1,0:T(8,128)(2,1)} %k_ref.3) | copy-start | bytes 3145732
  8.3 1.2 %copy-start.3 = (bf16[1,256,2048]{2,1,0:T(8,128)(2,1)S(1)}, bf16[1,256,2048]{2,1,0:T(8,128)(2,1)}, u32[]{:S(2)}) copy-start(bf16[1,256,2048]{2,1,0:T(8,128)(2,1)} %v_ref.3) | copy-start | bytes 3145732
  9.5 7.8 %copy-start.9 = (f32[4,16,2]{1,2,0:T(2,128)S(1)}, f32[4,16,2]{1,2,0:T(2,128)}, u32[]{:S(2)}) copy-start(f32[4,16,2]{1,2,0:T(2,128)} %param.18) | copy-start | bytes 1540
  9.5 8.5 %copy-start.8 = (bf16[4,2,2048]{2,1,0:T(2,128)(2,1)S(1)}, bf16[4,2,2048]{2,1,0:T(2,128)(2,1)}, u32[]{:S(2)}) copy-start(bf16[4,2,2048]{2,1,0:T(2,128)(2,1)} %param.15) | copy-start | bytes 98308
  9.5 8.5 %copy-start.13 = (bf16[4,2,2048]{2,1,0:T(2,128)(2,1)S(1)}, bf16[4,2,2048]{2,1,0:T(2,128)(2,1)}, u32[]{:S(2)}) copy-start(bf16[4,2,2048]{2,1,0:T(2,128)(2,1)} %param.16) | copy-start | bytes 98308
  14.6 24.3 %collective-permute-start = (bf16[8,128,128]{2,1,0:T(8,128)(2,1)}, bf16[8,128,128]{2,1,0:T(8,128)(2,1)}, u32[]{:S(2)}, u32[]{:S(2)}) collective-permute-start(bf16[8,128,128]{2,1,0:T(8,128)(2,1)} %slice.99), channel_id=1, source_target_pairs={{0,8},{8,16},{16,24},{1,9},{9,17},{17,25},{2,10},{10,18},{18,26},{... | collective-permute-start | bytes 786440 | tf_op jit(solution)/shard_map/ppermute | solution.py:258
  19.8 10.8 %collective-permute-start.5 = (bf16[2,16,2048]{2,1,0:T(8,128)(2,1)}, bf16[2,16,2048]{2,1,0:T(8,128)(2,1)S(1)}, u32[]{:S(2)}, u32[]{:S(2)}) collective-permute-start(bf16[2,16,2048]{2,1,0:T(8,128)(2,1)} %pad_maximum_fusion.4), channel_id=1, source_target_pairs={{0,16},{8,24},{16,0},{24,8},{1,17},{9,25},{17,1},{25,9},{2,18},{10... | collective-permute-start | bytes 393224 | tf_op jit(solution)/shard_map/ppermute | solution.py:125
  22.2 1.2 %copy-start.2 = (bf16[1,256,2048]{2,1,0:T(8,128)(2,1)S(1)}, bf16[1,256,2048]{2,1,0:T(8,128)(2,1)}, u32[]{:S(2)}) copy-start(bf16[1,256,2048]{2,1,0:T(8,128)(2,1)} %k_ref.3) | copy-start | bytes 3145732
  23.4 1.2 %copy-start.4 = (bf16[1,256,2048]{2,1,0:T(8,128)(2,1)S(1)}, bf16[1,256,2048]{2,1,0:T(8,128)(2,1)}, u32[]{:S(2)}) copy-start(bf16[1,256,2048]{2,1,0:T(8,128)(2,1)} %v_ref.3) | copy-start | bytes 3145732
  24.6 1.2 %copy-start.5 = (bf16[1,256,2048]{2,1,0:T(8,128)(2,1)S(1)}, bf16[1,256,2048]{2,1,0:T(8,128)(2,1)}, u32[]{:S(2)}) copy-start(bf16[1,256,2048]{2,1,0:T(8,128)(2,1)} %q_ref.3) | copy-start | bytes 3145732
  31.3 2.6 %collective-permute-start.6 = (bf16[4,8,2048]{2,1,0:T(8,128)(2,1)}, bf16[4,8,2048]{2,1,0:T(8,128)(2,1)}, u32[]{:S(2)}, u32[]{:S(2)}) collective-permute-start(bf16[4,8,2048]{2,1,0:T(8,128)(2,1)} %pad_maximum_fusion.2), channel_id=1, source_target_pairs={{0,1},{1,0},{2,3},{3,2},{4,5},{5,4},{6,7},{7,6},{8,9},{9,8},{10,11... | collective-permute-start | bytes 393224 | tf_op jit(solution)/shard_map/ppermute | solution.py:125
  33.9 5.0 %copy-start.12 = (f32[8]{0:T(128)S(1)}, f32[8]{0:T(128)}, u32[]{:S(2)}) copy-start(f32[8]{0:T(128)} %get-tuple-element.15) | copy-start | bytes 100
  35.6 15.4 %copy-start.11 = (f32[8]{0:T(128)S(1)}, f32[8]{0:T(128)}, u32[]{:S(2)}) copy-start(f32[8]{0:T(128)} %get-tuple-element.16) | copy-start | bytes 100
  36.6 19.1 %copy-start.7 = (f32[4,2,16]{2,1,0:T(2,128)S(1)}, f32[4,2,16]{2,1,0:T(2,128)}, u32[]{:S(2)}) copy-start(f32[4,2,16]{2,1,0:T(2,128)} %exponential_bitcast_fusion) | copy-start | bytes 1540
  36.6 23.6 %copy-start.10 = (f32[8]{0:T(128)S(1)}, f32[8]{0:T(128)}, u32[]{:S(2)}) copy-start(f32[8]{0:T(128)} %get-tuple-element.14) | copy-start | bytes 100
  36.6 1.6 %collective-permute-start.7 = (bf16[4,8,2048]{2,1,0:T(8,128)(2,1)S(1)}, bf16[4,8,2048]{2,1,0:T(8,128)(2,1)S(1)}, u32[]{:S(2)}, u32[]{:S(2)}) collective-permute-start(bf16[4,8,2048]{2,1,0:T(8,128)(2,1)S(1)} %slice_bitcast_fusion), channel_id=1, source_target_pairs={{0,1},{1,0},{2,3},{3,2},{4,5},{5,4},{6,7},{7,6},{8,9},{9,8},{10,11... | collective-permute-start | bytes 393224 | tf_op jit(solution)/shard_map/ppermute | solution.py:125
  38.3 6.7 %collective-permute-start.8 = (bf16[2,8,2048]{2,1,0:T(8,128)(2,1)S(1)}, bf16[2,8,2048]{2,1,0:T(8,128)(2,1)S(1)}, u32[]{:S(2)}, u32[]{:S(2)}) collective-permute-start(bf16[2,8,2048]{2,1,0:T(8,128)(2,1)S(1)} %slice.71), channel_id=1, source_target_pairs={{0,16},{8,24},{16,0},{24,8},{1,17},{9,25},{17,1},{25,9},{2,18},{10... | collective-permute-start | bytes 196616 | tf_op jit(solution)/shard_map/ppermute | solution.py:125
  40.0 11.0 %collective-permute-start.1 = (bf16[8,128,128]{2,1,0:T(8,128)(2,1)S(1)}, bf16[8,128,128]{2,1,0:T(8,128)(2,1)S(1)}, u32[]{:S(2)}, u32[]{:S(2)}) collective-permute-start(bf16[8,128,128]{2,1,0:T(8,128)(2,1)S(1)} %add_convert_fusion.2), channel_id=1, source_target_pairs={{0,8},{8,16},{16,24},{1,9},{9,17},{17,25},{2,10},{10,18},{18,26},{... | collective-permute-start | bytes 786440 | tf_op jit(solution)/shard_map/ppermute | solution.py:258
  45.0 10.6 %collective-permute-start.9 = (bf16[1,8,2048]{2,1,0:T(8,128)(2,1)S(1)}, bf16[1,8,2048]{2,1,0:T(8,128)(2,1)S(1)}, u32[]{:S(2)}, u32[]{:S(2)}) collective-permute-start(bf16[1,8,2048]{2,1,0:T(8,128)(2,1)S(1)} %slice.73), channel_id=1, source_target_pairs={{0,8},{8,0},{16,24},{24,16},{1,9},{9,1},{17,25},{25,17},{2,10},{10... | collective-permute-start | bytes 98312 | tf_op jit(solution)/shard_map/ppermute | solution.py:125
  51.2 9.0 %collective-permute-start.2 = (bf16[8,128,128]{2,1,0:T(8,128)(2,1)S(1)}, bf16[8,128,128]{2,1,0:T(8,128)(2,1)S(1)}, u32[]{:S(2)}, u32[]{:S(2)}) collective-permute-start(bf16[8,128,128]{2,1,0:T(8,128)(2,1)S(1)} %add_convert_fusion.1), channel_id=1, source_target_pairs={{0,8},{8,16},{16,24},{1,9},{9,17},{17,25},{2,10},{10,18},{18,26},{... | collective-permute-start | bytes 786440 | tf_op jit(solution)/shard_map/ppermute | solution.py:258
  60.3 9.5 %copy-start.6 = (bf16[1,256,2048]{2,1,0:T(8,128)(2,1)S(1)}, bf16[1,256,2048]{2,1,0:T(8,128)(2,1)}, u32[]{:S(2)}) copy-start(bf16[1,256,2048]{2,1,0:T(8,128)(2,1)} %q_ref.3) | copy-start | bytes 3145732
  60.3 8.4 %collective-permute-start.3 = (bf16[8,128,128]{2,1,0:T(8,128)(2,1)S(1)}, bf16[8,128,128]{2,1,0:T(8,128)(2,1)S(1)}, u32[]{:S(2)}, u32[]{:S(2)}) collective-permute-start(bf16[8,128,128]{2,1,0:T(8,128)(2,1)S(1)} %add_convert_fusion), channel_id=1, source_target_pairs={{0,8},{8,16},{16,24},{1,9},{9,17},{17,25},{2,10},{10,18},{18,26},{... | collective-permute-start | bytes 786440 | tf_op jit(solution)/shard_map/ppermute | solution.py:258
  76.2 19.7 %collective-permute-start.13 = (bf16[1,272,768]{2,1,0:T(8,128)(2,1)S(1)}, bf16[1,272,768]{2,1,0:T(8,128)(2,1)S(1)}, u32[]{:S(2)}, u32[]{:S(2)}) collective-permute-start(bf16[1,272,768]{2,1,0:T(8,128)(2,1)S(1)} %project.10), channel_id=1, source_target_pairs={{0,4},{2,6},{4,0},{6,2},{1,5},{3,7},{5,1},{7,3},{8,12},{10,14},{12... | collective-permute-start | bytes 1253384 | tf_op jit(solution)/shard_map/ppermute | solution.py:125
  80.8 15.2 %collective-permute-start.11 = (bf16[1,272,768]{2,1,0:T(8,128)(2,1)S(1)}, bf16[1,272,768]{2,1,0:T(8,128)(2,1)S(1)}, u32[]{:S(2)}, u32[]{:S(2)}) collective-permute-start(bf16[1,272,768]{2,1,0:T(8,128)(2,1)S(1)} %project.9), channel_id=1, source_target_pairs={{0,2},{2,0},{4,6},{6,4},{1,3},{3,1},{5,7},{7,5},{8,10},{10,8},{12,... | collective-permute-start | bytes 1253384 | tf_op jit(solution)/shard_map/ppermute | solution.py:125
  85.4 20.6 %collective-permute-start.15 = (bf16[1,272,768]{2,1,0:T(8,128)(2,1)S(1)}, bf16[1,272,768]{2,1,0:T(8,128)(2,1)S(1)}, u32[]{:S(2)}, u32[]{:S(2)}) collective-permute-start(bf16[1,272,768]{2,1,0:T(8,128)(2,1)S(1)} %project.11), channel_id=1, source_target_pairs={{0,4},{2,6},{4,0},{6,2},{1,5},{3,7},{5,1},{7,3},{8,12},{10,14},{12... | collective-permute-start | bytes 1253384 | tf_op jit(solution)/shard_map/ppermute | solution.py:125
  89.5 16.4 %collective-permute-start.10 = (bf16[1,272,768]{2,1,0:T(8,128)(2,1)}, bf16[1,272,768]{2,1,0:T(8,128)(2,1)S(1)}, u32[]{:S(2)}, u32[]{:S(2)}) collective-permute-start(bf16[1,272,768]{2,1,0:T(8,128)(2,1)} %project.7), channel_id=1, source_target_pairs={{0,2},{2,0},{4,6},{6,4},{1,3},{3,1},{5,7},{7,5},{8,10},{10,8},{12,... | collective-permute-start | bytes 1253384 | tf_op jit(solution)/shard_map/ppermute | solution.py:125
  97.1 8.9 %collective-permute-start.12 = (bf16[1,272,768]{2,1,0:T(8,128)(2,1)}, bf16[1,272,768]{2,1,0:T(8,128)(2,1)S(1)}, u32[]{:S(2)}, u32[]{:S(2)}) collective-permute-start(bf16[1,272,768]{2,1,0:T(8,128)(2,1)} %get-tuple-element.7), channel_id=1, source_target_pairs={{0,4},{2,6},{4,0},{6,2},{1,5},{3,7},{5,1},{7,3},{8,12},{10,14},{12... | collective-permute-start | bytes 1253384 | tf_op jit(solution)/shard_map/ppermute | solution.py:125
  98.6 8.5 %collective-permute-start.14 = (bf16[1,272,768]{2,1,0:T(8,128)(2,1)}, bf16[1,272,768]{2,1,0:T(8,128)(2,1)S(1)}, u32[]{:S(2)}, u32[]{:S(2)}) collective-permute-start(bf16[1,272,768]{2,1,0:T(8,128)(2,1)} %get-tuple-element.6), channel_id=1, source_target_pairs={{0,2},{2,0},{4,6},{6,4},{1,3},{3,1},{5,7},{7,5},{8,10},{10,8},{12,... | collective-permute-start | bytes 1253384 | tf_op jit(solution)/shard_map/ppermute | solution.py:125

commit v2 on v0

v2 whole, which is shorter than its diff:
```python
import functools

import jax
import jax.numpy as jnp
from jax import lax
from jax.experimental import pallas as pl
from jax.experimental.pallas import tpu as pltpu
from jax.sharding import PartitionSpec as P

HEAD_DIM = 128
EPSILON = 1e-06
NEGATIVE = -1e30
HIGH = lax.Precision.HIGHEST
CHUNKS = 4
LAG = 2
VMEM_BYTES = 16 * 2**20
F32 = jnp.float32
BF16 = jnp.bfloat16
NT = (((1,), (1,)), ((), ()))
TN = (((0,), (0,)), ((), ()))


def params():
    return pltpu.CompilerParams(vmem_limit_bytes=VMEM_BYTES)


def cost(flops, moved, exps=0):
    return pl.CostEstimate(flops=int(flops), bytes_accessed=int(moved), transcendentals=int(exps))


def normalize(array):
    return array * lax.rsqrt(jnp.mean(array * array, axis=-1, keepdims=True) + EPSILON)


def lower_ones(length):
    rows = lax.broadcasted_iota(jnp.int32, (length, length), 0)
    cols = lax.broadcasted_iota(jnp.int32, (length, length), 1)
    return rows >= cols


def decay_columns(rate, lower):
    return -lax.dot_general(lower.astype(F32), rate, NT, precision=HIGH, preferred_element_type=F32)


def decay_rows(rate, lower):
    return -lax.dot_general(rate, lower.astype(F32), NT, precision=HIGH, preferred_element_type=F32)


def identity(size):
    rows = lax.broadcasted_iota(jnp.int32, (size, size), 0)
    cols = lax.broadcasted_iota(jnp.int32, (size, size), 1)
    return rows, cols


def head_slice(index):
    return slice(index * HEAD_DIM, (index + 1) * HEAD_DIM)


def halves(array):
    top = array.astype(BF16)
    return top, (array - top.astype(F32)).astype(BF16)

VMEM = pl.BlockSpec(memory_space=pltpu.VMEM)
SMEM = pl.BlockSpec(memory_space=pltpu.SMEM)
ANY = pl.BlockSpec(memory_space=pl.ANY)
HBM = pl.BlockSpec(memory_space=pltpu.HBM)


def call(kernel, name, in_specs, out_shape, scratch=(), estimate=None, out_specs=None):
    if out_specs is None:
        out_specs = jax.tree.map(lambda _: VMEM, out_shape)
    return pl.pallas_call(
        kernel,
        in_specs=in_specs,
        out_specs=out_specs,
        out_shape=out_shape,
        scratch_shapes=list(scratch),
        compiler_params=params(),
        cost_estimate=estimate,
        name=name,
    )


def sds(shape, dtype):
    return jax.ShapeDtypeStruct(shape, dtype)


def state_kernel(span, k_hbm, v_hbm, rate_ref, own_ref, first_ref, second_ref, log_ref, col_ref, row_ref, k_ref, v_ref, sems):
    heads = own_ref.shape[0]
    wide = span * HEAD_DIM
    copies = []
    for c in range(heads // span):
        at = pl.ds(c * wide, wide)
        copies.append(pltpu.make_async_copy(k_hbm.at[0, :, at], k_ref.at[:, at], sems.at[0, c]))
        copies.append(pltpu.make_async_copy(v_hbm.at[0, :, at], v_ref.at[:, at], sems.at[1, c]))
    for copy in copies:
        copy.start()
    length = k_ref.shape[0]
    rate = rate_ref[0]
    lower = lower_ones(length)
    columns = decay_columns(rate, lower)
    col_ref[...] = columns
    row_ref[...] = decay_rows(rate, lower)
    total = columns[length - 1 :, :]
    factor = jnp.exp(total - columns)
    for i in range(heads):
        if i % span == 0:
            copies[2 * (i // span)].wait()
            copies[2 * (i // span) + 1].wait()
        at = head_slice(i)
        values = v_ref[:, at]
        weighted = k_ref[:, at].astype(F32) * factor[:, i : i + 1]
        top, rest = halves(weighted)
        both = lax.dot_general(
            jnp.concatenate([top, rest], axis=1), values, TN, preferred_element_type=F32
        )
        state = both[:HEAD_DIM] + both[HEAD_DIM:]
        own_ref[i] = state
        if i < span:
            first_ref[i] = state.astype(BF16)
        elif i < 2 * span:
            second_ref[i - span] = state.astype(BF16)
        log_ref[:, at] = jnp.broadcast_to(total[:, i : i + 1], (1, HEAD_DIM))


def chain_kernel(step, place_ref, own_ref, log_ref, got_ref, *rest):
    out_ref = rest[-1]
    span = out_ref.shape[0]
    chunks = own_ref.shape[0] // span
    chunk = jnp.clip(step - LAG * place_ref[0], 0, chunks - 1)
    wide = span * HEAD_DIM
    keep = jnp.exp(log_ref[:, pl.ds(pl.multiple_of(chunk * wide, HEAD_DIM), wide)])
    for i in range(span):
        out_ref[i] = (
            own_ref[chunk * span + i] + keep[:, head_slice(i)] * got_ref[i].astype(F32)
        ).astype(BF16)


def local_kernel(first, q_ref, k_ref, v_ref, col_ref, row_ref, *rest):
    local_ref = rest[-1]
    lower = lower_ones(q_ref.shape[1])
    for i in range(local_ref.shape[1] // HEAD_DIM):
        h = first + i
        at = head_slice(h)
        scores = lax.dot_general(q_ref[0, :, at], k_ref[:, at], NT, preferred_element_type=F32)
        decay = jnp.exp(
            jnp.where(lower, col_ref[:, h : h + 1] - row_ref[h : h + 1, :], NEGATIVE)
        )
        weights = (scores * decay).astype(BF16)
        local_ref[:, head_slice(i)] = jnp.dot(weights, v_ref[:, at], preferred_element_type=F32)


def hidden_kernel(chunks, groups, place_ref, q_ref, col_ref, decode_ref, *rest):
    locals_ref, got, hidden_ref = rest[:chunks], rest[chunks:-1], rest[-1]
    length = q_ref.shape[1]
    factor = jnp.exp(col_ref[...])
    span = got[0].shape[0]
    group = place_ref[0]
    for chunk in range(chunks):
        for i in range(span):
            state = got[chunk][i]
            for g in range(2, groups):
                state = jnp.where(group == g, got[chunk + LAG * (g - 1)][i], state)
            h = chunk * span + i
            at = head_slice(h)
            inter = jnp.dot(q_ref[0, :, at], state, preferred_element_type=F32)
            attended = locals_ref[chunk][:, head_slice(i)] + inter * factor[:, h : h + 1]
            hidden_ref[:length, at] = normalize(attended).astype(BF16)
    hidden_ref[length:, :] = decode_ref[...]


def flat_rows(ref, rows_ref):
    rows, steps = ref.shape[0], ref.shape[1]
    for r in range(rows):
        rows_ref[r * steps : (r + 1) * steps, :] = ref[r].astype(F32)


def message_kernel(q_ref, log_ref, prompt_ref, *rest):
    out_ref, rows_ref = rest[-2:]
    rows, steps = q_ref.shape[0], q_ref.shape[1]
    d_rows = rows * steps
    features = q_ref.shape[2]
    rows_ref[...] = jnp.zeros_like(rows_ref)
    flat_rows(q_ref, rows_ref)
    log = log_ref[...]
    top = log.astype(BF16).astype(F32)
    mid = (log - top).astype(BF16).astype(F32)
    rows_ref[d_rows : d_rows + 1, :] = top
    rows_ref[d_rows + 1 : d_rows + 2, :] = mid
    rows_ref[d_rows + 2 : d_rows + 3, :] = log - top - mid
    lane = lax.broadcasted_iota(jnp.int32, (1, features), 1)
    prompts = jnp.zeros((1, features), F32)
    for r in range(rows):
        here = (lane >= r * steps) & (lane < (r + 1) * steps)
        prompts = jnp.where(here, prompt_ref[r].astype(F32), prompts)
    rows_ref[d_rows + 3 : d_rows + 4, :] = prompts
    out_ref[...] = rows_ref[...].astype(BF16)


def start_kernel(groups, d_rows, place_ref, near_ref, far_ref, own_ref, *rest):
    near_out, far_out = rest[-2:]
    unit = near_ref.shape[0] // groups
    group = place_ref[0]
    later = jnp.zeros((1, near_ref.shape[1]), F32)
    for j in range(1, groups):
        facts = near_ref[j * unit : (j + 1) * unit, :].astype(F32)[d_rows : d_rows + 3]
        facts = jnp.sum(facts, axis=0, keepdims=True)
        later = later + jnp.where((group ^ j) > group, facts, 0.0)
    scale = jnp.exp(later)

    def strip(terms):
        return jnp.concatenate(
            [terms[j * unit : j * unit + d_rows] for j in range(groups)], axis=0
        )

    for i in range(own_ref.shape[0]):
        at = head_slice(i)
        top, low = halves(own_ref[i])
        both = jnp.concatenate([top, low], axis=1)
        for source, target in ((near_ref, near_out), (far_ref, far_out)):
            terms = jnp.dot(source[:, at], both, preferred_element_type=F32)
            terms = (terms[:, :HEAD_DIM] + terms[:, HEAD_DIM:]) * scale[:, at]
            target[:, at] = strip(terms).astype(target.dtype)


def select_kernel(groups, d_rows, place_ref, near_ref, mine_ref, other_ref, *rest):
    outs = rest[-groups:]
    unit = near_ref.shape[0] // groups
    rep = place_ref[1].astype(F32)
    wide = -(-d_rows // HEAD_DIM) * HEAD_DIM
    rows = lax.broadcasted_iota(jnp.int32, (d_rows, wide), 0)
    cols = lax.broadcasted_iota(jnp.int32, (d_rows, wide), 1)
    other = other_ref[...].astype(F32)
    for j in range(groups):
        facts = near_ref[j * unit : (j + 1) * unit, :wide].astype(F32)[d_rows + 3 : d_rows + 4]
        prompt = jnp.sum(jnp.where(rows == cols, facts, 0.0), axis=1, keepdims=True)
        at = slice(j * d_rows, (j + 1) * d_rows)
        picked = jnp.where(prompt == rep, mine_ref[at], other[at])
        outs[j][...] = picked.astype(outs[j].dtype)


def decode_kernel(groups, q_ref, k_ref, v_ref, rate_ref, base_ref, *rest):
    got = rest[: groups - 1]
    out_ref, q_rows, k_rows, v_rows, rate_rows = rest[-5:]
    steps = q_ref.shape[1]
    d_rows = q_rows.shape[0]
    flat_rows(q_ref, q_rows)
    flat_rows(k_ref, k_rows)
    flat_rows(v_ref, v_rows)
    flat_rows(rate_ref, rate_rows)
    rows, cols = identity(d_rows)
    seen = (rows // steps == cols // steps) & (rows >= cols)
    ones = seen.astype(F32)
    rates = rate_rows[...]
    down = -jnp.dot(ones, rates, precision=HIGH, preferred_element_type=F32)
    across = -lax.dot_general(
        rates, ones, (((0,), (1,)), ((), ())), precision=HIGH, preferred_element_type=F32
    )
    grow = jnp.exp(down)
    out_ref[...] = jnp.zeros_like(out_ref)
    for i in range(rates.shape[1]):
        at = head_slice(i)
        scores = lax.dot_general(
            q_rows[:, at], k_rows[:, at], NT, precision=HIGH, preferred_element_type=F32
        )
        decay = jnp.exp(jnp.where(seen, down[:, i : i + 1] - across[i : i + 1, :], NEGATIVE))
        intra = jnp.dot(scores * decay, v_rows[:, at], precision=HIGH, preferred_element_type=F32)
        base = base_ref[:, at]
        for ref in got:
            base = base + ref[:, at].astype(F32)
        q_rows[:, at] = normalize(base * grow[:, i : i + 1] + intra)
    pad = out_ref.shape[0] - d_rows
    value = q_rows[...]
    if pad:
        value = jnp.concatenate([value, jnp.zeros((pad, value.shape[1]), F32)], axis=0)
    out_ref[...] = value.astype(BF16)


def project_kernel(pieces, place_ref, hidden_ref, weight_ref, *outs):
    half = outs[0].shape[1]
    rows = hidden_ref[...]
    for (bits, part), out_ref in zip(pieces, outs):
        column = pl.multiple_of(((place_ref[2] ^ bits) * 2 + part) * half, HEAD_DIM)
        out_ref[...] = jnp.dot(
            rows, weight_ref[:, pl.ds(column, half)], preferred_element_type=F32
        ).astype(out_ref.dtype)


def relay_kernel(own_ref, got_ref, out_ref):
    out_ref[...] = (own_ref[...] + got_ref[...].astype(F32)).astype(BF16)


def finish_kernel(own_a, own_b, ax, ay, bx, by, prefill_hbm, decode_ref, out_ref, sems):
    width = own_a.shape[1]
    rows, steps = decode_ref.shape[0], decode_ref.shape[1]
    length = out_ref.shape[0]
    count = sems.shape[0]
    size = length // count
    copies = []
    for c in range(count):
        at = slice(c * size, (c + 1) * size)
        for at_cols, own, x_ref, y_ref in ((0, own_a, ax, ay), (width, own_b, bx, by)):
            total = own[at] + x_ref[at].astype(F32) + y_ref[at].astype(F32)
            out_ref[at, at_cols : at_cols + width] = total.astype(BF16)
        copy = pltpu.make_async_copy(
            out_ref.at[pl.ds(c * size, size)], prefill_hbm.at[0, pl.ds(c * size, size)], sems.at[c]
        )
        copy.start()
        copies.append(copy)
    for at_cols, own, x_ref, y_ref in ((0, own_a, ax, ay), (width, own_b, bx, by)):
        tail = own[length:] + x_ref[length:].astype(F32) + y_ref[length:].astype(F32)
        tail = tail.astype(BF16).astype(F32)
        for r in range(rows):
            decode_ref[r, :, at_cols : at_cols + width] = tail[r * steps : (r + 1) * steps].astype(BF16)
    for copy in copies:
        copy.wait()


def swap(array, axis, size, bit):
    return lax.ppermute(array, axis, [(i, i ^ bit) for i in range(size)])


def body(
    prefill_query,
    prefill_key,
    prefill_value,
    prefill_rate,
    out_weight,
    decode_query,
    decode_key,
    decode_value,
    decode_rate,
    prompt_of_row,
    *,
    groups,
    reps,
    parts,
):
    length = prefill_query.shape[1]
    features = prefill_query.shape[2]
    heads = prefill_rate.shape[1]
    rows_here, steps = decode_query.shape[0], decode_query.shape[1]
    d_rows = rows_here * steps
    d_pad = -(-d_rows // 16) * 16
    unit = -(-(d_rows + 4) // 16) * 16
    total_rows = length + d_pad
    place = jnp.stack([lax.axis_index("ctx"), lax.axis_index("rep"), lax.axis_index("head")])
    place = place.astype(jnp.int32)
    chunks = CHUNKS if heads % CHUNKS == 0 else heads
    span = heads // chunks
    wide = span * HEAD_DIM
    chunk_shape = (span, HEAD_DIM, HEAD_DIM)

    own, first, second, log_row, columns, rows, keys, values = call(
        functools.partial(state_kernel, span),
        "own_state",
        [HBM, HBM, VMEM],
        [
            sds((heads, HEAD_DIM, HEAD_DIM), F32),
            sds(chunk_shape, BF16),
            sds(chunk_shape, BF16),
            sds((1, features), F32),
            sds((length, heads), F32),
            sds((heads, length), F32),
            pltpu.VMEM((length, features), BF16),
            pltpu.VMEM((length, features), BF16),
        ],
        [pltpu.SemaphoreType.DMA((2, chunks))],
        cost(4 * length * features * HEAD_DIM, 4 * length * features),
    )(prefill_key, prefill_value, prefill_rate)

    def message(*after):
        return call(
            message_kernel,
            "decode_message",
            [VMEM, VMEM, SMEM] + [ANY] * len(after),
            sds((unit, features), BF16),
            [pltpu.VMEM((unit, features), F32)],
            cost(unit * features, unit * features * 8),
        )(decode_query, log_row, prompt_of_row, *after)

    def local(chunk, *after):
        return call(
            functools.partial(local_kernel, chunk * span),
            "local_attention",
            [VMEM] * 5 + [ANY] * len(after),
            sds((length, wide), F32),
            (),
            cost(4 * length * length * wide, 6 * length * wide, span * length * length),
        )(prefill_query, keys, values, columns, rows, *after)

    def start_terms(near, far, *after):
        return call(
            functools.partial(start_kernel, groups, d_rows),
            "decode_start",
            [SMEM, VMEM, VMEM, VMEM] + [ANY] * len(after),
            [sds((groups * d_rows, features), F32), sds((groups * d_rows, features), BF16)],
            (),
            cost(8 * groups * unit * features * HEAD_DIM, heads * HEAD_DIM * HEAD_DIM * 4),
        )(place, near, far, own, *after)

    def select_terms(near, mine, other, *after):
        return call(
            functools.partial(select_kernel, groups, d_rows),
            "decode_select",
            [SMEM, VMEM, VMEM, VMEM] + [ANY] * len(after),
            [sds((d_rows, features), F32)] + [sds((d_rows, features), BF16)] * (groups - 1),
            (),
            cost(groups * d_rows * features, groups * d_rows * features * 8),
        )(place, near, mine, other, *after)

    def decode_rows(base, got, *after):
        flat = pltpu.VMEM((d_rows, features), F32)
        return call(
            functools.partial(decode_kernel, groups),
            "decode_rows",
            [VMEM] * (5 + len(got)) + [ANY] * len(after),
            sds((d_pad, features), BF16),
            [flat, flat, flat, pltpu.VMEM((d_rows, heads), F32)],
            cost(4 * d_rows * features * d_rows, d_rows * features * 20),
        )(
            decode_query,
            decode_key,
            decode_value,
            jnp.transpose(decode_rate, (0, 2, 1)),
            base,
            *got,
            *after,
        )

    right = [(i, i + 1) for i in range(groups - 1)]
    steps_all = chunks + LAG * (groups - 2)
    received, locals_done, slot = [], [], {}

    def side_work(step, after):
        made = []
        if step == 0:
            slot["message"] = message(*after)
            slot["ctx"] = [swap(slot["message"], "ctx", groups, j) for j in range(1, groups)]
            made.append(slot["message"])
        if step == 2:
            slot["near"] = jnp.concatenate([slot["message"]] + slot["ctx"], axis=0)
            slot["far"] = swap(slot["near"], "rep", reps, 1)
        if step == 3:
            slot["mine"], away = start_terms(slot["near"], slot["far"], *after)
            slot["other"] = swap(away, "rep", reps, 1)
            made.append(slot["mine"])
        if step == 5:
            base, *terms = select_terms(slot["near"], slot["mine"], slot["other"], *after)
            slot["base"] = base
            slot["got"] = [
                swap(term, "ctx", groups, j) for j, term in zip(range(1, groups), terms)
            ]
            made.append(base)
        return made

    local_at = {1: 0, 2: 1, 4: 2, 6: 3}
    for step in range(steps_all):
        if step == 0:
            value = first
        elif step < LAG:
            value = second if chunks > 1 else first
        else:
            after = slot.pop("after", [])
            value = call(
                functools.partial(chain_kernel, step),
                "chain",
                [SMEM, VMEM, VMEM, VMEM] + [ANY] * len(after),
                sds(chunk_shape, BF16),
                (),
                cost(2 * span * HEAD_DIM * HEAD_DIM, 8 * span * HEAD_DIM * HEAD_DIM),
            )(place, own, log_row, received[step - LAG], *after)
        received.append(lax.ppermute(value, "ctx", right))
        ready = [received[step - LAG]] if step >= LAG else []
        made = side_work(step, ready)
        if step in local_at and local_at[step] < chunks:
            locals_done.append(local(len(locals_done), *ready))
            made.append(locals_done[-1])
        slot["after"] = made
    while len(locals_done) < chunks:
        locals_done.append(local(len(locals_done)))
    if "message" not in slot:
        side_work(0, [])
    for step, name in ((2, "near"), (3, "mine"), (5, "base")):
        if name not in slot:
            side_work(step, [])
    decode_hidden = decode_rows(slot["base"], slot["got"])

    hidden = call(
        functools.partial(hidden_kernel, chunks, groups),
        "hidden",
        [SMEM] + [VMEM] * (3 + chunks + len(received)),
        sds((total_rows, features), BF16),
        (),
        cost(2 * length * features * HEAD_DIM, 8 * length * features),
    )(place, prefill_query, columns, decode_hidden, *locals_done, *received)

    out_columns = out_weight.shape[1]
    if parts != 4 or (out_columns // parts) % 256 != 0 or length % 64 != 0:
        terms = jnp.dot(hidden, out_weight, preferred_element_type=F32)
        summed = lax.psum_scatter(terms, "head", scatter_dimension=1, tiled=True)
        prefill_out = summed[:length].astype(BF16)[None]
        decode_out = summed[length : length + d_rows].astype(BF16)
        return prefill_out, decode_out.reshape(rows_here, steps, -1)

    half = out_columns // parts // 2
    weight = pltpu.with_memory_space_constraint(out_weight, pltpu.VMEM)

    def project(pieces, dtype, *after):
        return call(
            functools.partial(project_kernel, pieces),
            "project",
            [SMEM, VMEM, VMEM],
            [sds((total_rows, half), dtype) for _ in pieces],
            (),
            cost(2 * total_rows * features * half * len(pieces), features * half * 2 * len(pieces)),
        )(place, hidden, weight)

    def relay(own_term, got):
        return call(
            relay_kernel,
            "relay",
            [VMEM, VMEM],
            sds((total_rows, half), BF16),
            (),
            cost(total_rows * half, total_rows * half * 8),
        )(own_term, got)

    far_a = swap(project([(3, 0)], BF16)[0], "head", parts, 1)
    far_b = swap(project([(3, 1)], BF16)[0], "head", parts, 2)
    x_a = swap(project([(1, 0)], BF16)[0], "head", parts, 1)
    y_b = swap(project([(2, 1)], BF16)[0], "head", parts, 2)
    pass_a, pass_b = project([(2, 0), (1, 1)], F32)
    own_a, own_b = project([(0, 0), (0, 1)], F32)
    y_a = swap(relay(pass_a, far_a), "head", parts, 2)
    x_b = swap(relay(pass_b, far_b), "head", parts, 1)

    prefill_out, decode_out = call(
        finish_kernel,
        "finish",
        [VMEM] * 6,
        [sds((1, length, 2 * half), BF16), sds((rows_here, steps, 2 * half), BF16)],
        [pltpu.VMEM((length, 2 * half), BF16), pltpu.SemaphoreType.DMA((4,))],
        cost(6 * total_rows * half, 20 * total_rows * half),
        out_specs=[HBM, VMEM],
    )(own_a, own_b, x_a, y_a, x_b, y_b)
    return prefill_out, decode_out


def solution(mesh):
    return jax.shard_map(
        functools.partial(
            body, groups=mesh.shape["ctx"], reps=mesh.shape["rep"], parts=mesh.shape["head"]
        ),
        mesh=mesh,
        in_specs=(
            P("rep", "ctx", "head"),
            P("rep", "ctx", "head"),
            P("rep", "ctx", "head"),
            P("rep", "head", "ctx"),
            P("head", None),
            P(("ctx", "rep"), None, "head"),
            P(("ctx", "rep"), None, "head"),
            P(("ctx", "rep"), None, "head"),
            P(("ctx", "rep"), "head", None),
            P(("ctx", "rep")),
        ),
        out_specs=(P("rep", "ctx", "head"), P(("ctx", "rep"), None, "head")),
        check_vma=False,
    )
```

time: 242 us -> 117 us (0.48)
  waiting for transfers between devices: 148 us -> 13.4 us
  matrix products: 52.4 us -> 0 us
  starting transfers between devices: 0.56 us -> 38.6 us
  Pallas kernels: 0 us -> 30.5 us
  local copies, waits for them, and re-layouts: 5.24 us -> 32 us
  blocking collectives: 13.5 us -> 0 us
  between operations: 14.7 us -> 1.24 us
  other arithmetic: 7.12 us -> 0.09 us
    reduce_scatter x2 -> x0, waiting for transfers between devices: 80.3 us -> none  [the longest x1 71.7 us: body(): lax.psum_scatter(token_terms, 'head', scatter_dimension=1, tiled=True)]
    all_gather x2 -> x0, waiting for transfers between devices: 67.4 us -> none  [the longest x1 67.4 us: body(): piece = lax.all_gather(own_state[None], 'ctx', axis=0, tiled=True)]
    dot_general x12 -> x0, matrix products: 52.4 us -> none  [the longest x1 14.4 us: body(): jnp.dot(hidden, out_weight, preferred_element_type=jnp.float32)]
    ppermute x0 -> x22, starting transfers between devices: none -> 38.6 us  [the longest x8 22.3 us: body(): received.append(lax.ppermute(value, 'ctx', right))]
    pallas_call x0 -> x25, Pallas kernels: none -> 30.5 us  [the longest x6 11.3 us: project(): call(functools.partial(project_kernel, pieces), 'project', [SMEM, VMEM, V...]
    unnamed x27 -> x46, local copies, waits for them, and re-layouts: 2.49 us -> 32 us
    unnamed x1 -> x0, blocking collectives: 13.5 us -> none
    ppermute x0 -> x22, waiting for transfers between devices: none -> 13.4 us  [the longest x14 13.4 us: swap(): return lax.ppermute(array, axis, [(i, i ^ bit) for i in range(size)])]
  transfers between devices with their start and end apart: 4 -> 22, of which waited for: 3 -> 7; matrix products, arithmetic and copies ran while one was open for 12% -> 0% of each run, Pallas kernels for 0% -> 17%
where the time goes in v2:
time: 117 us; the launch traced here: 116 us
  starting transfers between devices  38.6 us (33%)
  local copies, waits for them, and re-layouts  32 us (27%)
  Pallas kernels  30.5 us (26%)
  waiting for transfers between devices  13.4 us (11%)
  between operations  1.24 us (1%)
    unnamed x46, local copies, waits for them, and re-layouts  32 us
    ppermute x8, starting transfers between devices, body(): received.append(lax.ppermute(value, 'ctx', right))  22.3 us
    ppermute x14, starting transfers between devices, swap(): return lax.ppermute(array, axis, [(i, i ^ bit) for i in range(size)])  16.4 us
    ppermute x14, waiting for transfers between devices, swap(): return lax.ppermute(array, axis, [(i, i ^ bit) for i in range(size)])  13.4 us
    pallas_call x6, Pallas kernels, project(): call(functools.partial(project_kernel, pieces), 'project', [SMEM, VMEM, V...  11.3 us
    pallas_call x6, Pallas kernels, body(): call(functools.partial(chain_kernel, step), 'chain', [SMEM, VMEM, VMEM, V...  4.31 us
    pallas_call x1, Pallas kernels, body(): call(functools.partial(state_kernel, span), 'own_state', [HBM, HBM, VMEM]...  3.88 us
    pallas_call x1, Pallas kernels, body(): call(functools.partial(hidden_kernel, chunks, groups), 'hidden', [SMEM] +...  3.04 us
  transfers between devices with their start and end apart: 22, of which 7 were waited for; matrix products, arithmetic and copies ran while one was open for 0% of the time, Pallas kernels for 17%

profile of v2, /device:TPU:0, one launch (start us, length us, event | category | flops | bytes accessed | tf_op | source)
XLA Modules:
  0.0 115.8 jit_solution(14287975023740711174)
XLA Ops:
  0.7 1.3 %copy-done.12 = bf16[1,256,2048]{2,1,0:T(8,128)(2,1)S(1)} copy-done((bf16[1,256,2048]{2,1,0:T(8,128)(2,1)S(1)}, bf16[1,256,2048]{2,1,0:T(8,128)(2,1)}, u32[]{:S(2)}) %copy-start.12) | copy-done | bytes 1048600
  2.0 1.2 %copy-done.13 = bf16[1,256,2048]{2,1,0:T(8,128)(2,1)S(1)} copy-done((bf16[1,256,2048]{2,1,0:T(8,128)(2,1)S(1)}, bf16[1,256,2048]{2,1,0:T(8,128)(2,1)}, u32[]{:S(2)}) %copy-start.13) | copy-done | bytes 1048600
  3.2 0.7 copy-done.20
  3.9 3.9 %own_state.1 = (f32[16,128,128]{2,1,0:T(8,128)S(1)}, bf16[4,128,128]{2,1,0:T(8,128)(2,1)}, bf16[4,128,128]{2,1,0:T(8,128)(2,1)}, f32[1,2048]{1,0:T(1,128)S(1)}, ...) custom-call(bf16[1,256,2048]{2,1,0:T(8,128)(2,1)S(1)} %copy-done.12,, ...), custom_call_target="tpu_custom_call" | custom-call | flops 268435456 | bytes 2097152 | tf_op jit(solution)/shard_map/own_state/pallas_call | solution.py:354
  7.8 0.8 copy-done.16
  8.6 0.7 copy-done.22
  9.3 0.6 decode_message.1
  9.9 5.1 %collective-permute-start.2 = (bf16[16,2048]{1,0:T(8,128)(2,1)S(1)}, bf16[16,2048]{1,0:T(8,128)(2,1)S(1)}, u32[]{:S(2)}, u32[]{:S(2)}) collective-permute-start(bf16[16,2048]{1,0:T(8,128)(2,1)S(1)} %decode_message.1), channel_id=1, source_target_pairs={{0,24},{8,16},{16,8},{24,0},{1,25},{9,17},{17,9},{25,1},{2,26},{10... | collective-permute-start | bytes 196616 | tf_op jit(solution)/shard_map/ppermute | solution.py:320
  15.0 0.6 collective-permute-start
  15.6 1.9 %collective-permute-done.2 = bf16[16,2048]{1,0:T(8,128)(2,1)S(1)} collective-permute-done((bf16[16,2048]{1,0:T(8,128)(2,1)S(1)}, bf16[16,2048]{1,0:T(8,128)(2,1)S(1)}, u32[]{:S(2)}, u32[]{:S(2)}) %collective-permute-start.2) | collective-permute-done | bytes 65568 | tf_op jit(solution)/shard_map/ppermute | solution.py:320
  17.6 3.0 %collective-permute-done.1 = bf16[16,2048]{1,0:T(8,128)(2,1)S(1)} collective-permute-done((bf16[16,2048]{1,0:T(8,128)(2,1)S(1)}, bf16[16,2048]{1,0:T(8,128)(2,1)S(1)}, u32[]{:S(2)}, u32[]{:S(2)}) %collective-permute-start.1) | collective-permute-done | bytes 65568 | tf_op jit(solution)/shard_map/ppermute | solution.py:320
  20.7 3.7 %collective-permute-start.6 = (bf16[4,128,128]{2,1,0:T(8,128)(2,1)}, bf16[4,128,128]{2,1,0:T(8,128)(2,1)}, u32[]{:S(2)}, u32[]{:S(2)}) collective-permute-start(bf16[4,128,128]{2,1,0:T(8,128)(2,1)} %get-tuple-element.29), channel_id=1, source_target_pairs={{0,8},{8,16},{16,24},{1,9},{9,17},{17,25},{2,10},{10,18},{18,26},{... | collective-permute-start | bytes 393224 | tf_op jit(solution)/shard_map/ppermute | solution.py:473
  24.4 3.0 %collective-permute-start.4 = (bf16[4,128,128]{2,1,0:T(8,128)(2,1)}, bf16[4,128,128]{2,1,0:T(8,128)(2,1)}, u32[]{:S(2)}, u32[]{:S(2)}) collective-permute-start(bf16[4,128,128]{2,1,0:T(8,128)(2,1)} %get-tuple-element.23), channel_id=1, source_target_pairs={{0,8},{8,16},{16,24},{1,9},{9,17},{17,25},{2,10},{10,18},{18,26},{... | collective-permute-start | bytes 393224 | tf_op jit(solution)/shard_map/ppermute | solution.py:473
  27.3 1.2 %copy-done.2 = bf16[1,256,2048]{2,1,0:T(8,128)(2,1)S(1)} copy-done((bf16[1,256,2048]{2,1,0:T(8,128)(2,1)S(1)}, bf16[1,256,2048]{2,1,0:T(8,128)(2,1)}, u32[]{:S(2)}) %copy-start.2) | copy-done | bytes 1048600
  28.6 0.7 local_attention.5.rest_0_
  29.2 0.8 copy-done.9
  30.1 1.0 copy-done.10
  31.2 1.0 chain.7
  32.2 3.0 %collective-permute-start.11 = (bf16[4,128,128]{2,1,0:T(8,128)(2,1)S(1)}, bf16[4,128,128]{2,1,0:T(8,128)(2,1)S(1)}, u32[]{:S(2)}, u32[]{:S(2)}) collective-permute-start(bf16[4,128,128]{2,1,0:T(8,128)(2,1)S(1)} %chain.7), channel_id=1, source_target_pairs={{0,8},{8,16},{16,24},{1,9},{9,17},{17,25},{2,10},{10,18},{18,26},{... | collective-permute-start | bytes 393224 | tf_op jit(solution)/shard_map/ppermute | solution.py:473
  35.2 1.2 %copy-done.3 = bf16[1,256,2048]{2,1,0:T(8,128)(2,1)S(1)} copy-done((bf16[1,256,2048]{2,1,0:T(8,128)(2,1)S(1)}, bf16[1,256,2048]{2,1,0:T(8,128)(2,1)}, u32[]{:S(2)}) %copy-start.3) | copy-done | bytes 1048600
  36.4 1.2 %copy-done.6 = bf16[256,2048]{1,0:T(8,128)(2,1)S(1)} copy-done((bf16[256,2048]{1,0:T(8,128)(2,1)S(1)}, bf16[256,2048]{1,0:T(8,128)(2,1)}, u32[]{:S(2)}) %copy-start.6) | copy-done | bytes 1048600
  37.6 0.7 copy-done.15
  38.3 0.7 local_attention.4.rest_0_.rest_1_
  39.0 1.0 chain.6
  40.0 1.9 %collective-permute-start.7 = (bf16[4,128,128]{2,1,0:T(8,128)(2,1)S(1)}, bf16[4,128,128]{2,1,0:T(8,128)(2,1)S(1)}, u32[]{:S(2)}, u32[]{:S(2)}) collective-permute-start(bf16[4,128,128]{2,1,0:T(8,128)(2,1)S(1)} %chain.6), channel_id=1, source_target_pairs={{0,8},{8,16},{16,24},{1,9},{9,17},{17,25},{2,10},{10,18},{18,26},{... | collective-permute-start | bytes 393224 | tf_op jit(solution)/shard_map/ppermute | solution.py:473
  41.9 1.4 %decode_start.1 = (f32[32,2048]{1,0:T(8,128)S(1)}, bf16[32,2048]{1,0:T(8,128)(2,1)S(1)}) custom-call(s32[3]{0:T(128)S(1)} %pad_add_fusion.place_ref, bf16[64,2048]{1,0:T(8,128)(2,1)S(1)} %pad_maximum_fusion.near_ref, bf16[64,2048]{1,0:T(8,128)(2,1)} %collective-permute-done.3.far_ref, f32[16,128,128]{2,1,0:T(8,128)S(1)} %get-tuple-element.22.own_ref, ...), custom_call_target="tpu_custom_call" | custom-call | flops 134217728 | bytes 1048576 | tf_op jit(solution)/shard_map/decode_start/pallas_call | solution.py:393
  43.4 0.6 chain.8
  44.0 3.8 %collective-permute-start.12 = (bf16[4,128,128]{2,1,0:T(8,128)(2,1)S(1)}, bf16[4,128,128]{2,1,0:T(8,128)(2,1)S(1)}, u32[]{:S(2)}, u32[]{:S(2)}) collective-permute-start(bf16[4,128,128]{2,1,0:T(8,128)(2,1)S(1)} %chain.8), channel_id=1, source_target_pairs={{0,8},{8,16},{16,24},{1,9},{9,17},{17,25},{2,10},{10,18},{18,26},{... | collective-permute-start | bytes 393224 | tf_op jit(solution)/shard_map/ppermute | solution.py:473
  47.8 1.2 %copy-done.7 = bf16[256,2048]{1,0:T(8,128)(2,1)S(1)} copy-done((bf16[256,2048]{1,0:T(8,128)(2,1)S(1)}, bf16[256,2048]{1,0:T(8,128)(2,1)}, u32[]{:S(2)}) %copy-start.7) | copy-done | bytes 1048600
  49.0 0.7 local_attention.6.rest_0_.rest_2_
  49.7 0.6 chain.9
  50.3 1.9 %collective-permute-start.13 = (bf16[4,128,128]{2,1,0:T(8,128)(2,1)S(1)}, bf16[4,128,128]{2,1,0:T(8,128)(2,1)S(1)}, u32[]{:S(2)}, u32[]{:S(2)}) collective-permute-start(bf16[4,128,128]{2,1,0:T(8,128)(2,1)S(1)} %chain.9), channel_id=1, source_target_pairs={{0,8},{8,16},{16,24},{1,9},{9,17},{17,25},{2,10},{10,18},{18,26},{... | collective-permute-start | bytes 393224 | tf_op jit(solution)/shard_map/ppermute | solution.py:473
  52.2 0.6 decode_select.1
  52.9 0.6 chain.10
  53.5 2.7 %collective-permute-start.14 = (bf16[4,128,128]{2,1,0:T(8,128)(2,1)S(1)}, bf16[4,128,128]{2,1,0:T(8,128)(2,1)S(1)}, u32[]{:S(2)}, u32[]{:S(2)}) collective-permute-start(bf16[4,128,128]{2,1,0:T(8,128)(2,1)S(1)} %chain.10), channel_id=1, source_target_pairs={{0,8},{8,16},{16,24},{1,9},{9,17},{17,25},{2,10},{10,18},{18,26},{... | collective-permute-start | bytes 393224 | tf_op jit(solution)/shard_map/ppermute | solution.py:473
  56.2 1.2 %copy-done.8 = bf16[256,2048]{1,0:T(8,128)(2,1)S(1)} copy-done((bf16[256,2048]{1,0:T(8,128)(2,1)S(1)}, bf16[256,2048]{1,0:T(8,128)(2,1)}, u32[]{:S(2)}) %copy-start.8) | copy-done | bytes 1048600
  57.4 0.7 local_attention.7.rest_0_.rest_3_
  58.0 0.6 chain.11
  58.6 2.4 %collective-permute-start.15 = (bf16[4,128,128]{2,1,0:T(8,128)(2,1)S(1)}, bf16[4,128,128]{2,1,0:T(8,128)(2,1)S(1)}, u32[]{:S(2)}, u32[]{:S(2)}) collective-permute-start(bf16[4,128,128]{2,1,0:T(8,128)(2,1)S(1)} %chain.11), channel_id=1, source_target_pairs={{0,8},{8,16},{16,24},{1,9},{9,17},{17,25},{2,10},{10,18},{18,26},{... | collective-permute-start | bytes 393224 | tf_op jit(solution)/shard_map/ppermute | solution.py:473
  61.2 4.3 %collective-permute-start.10 = (bf16[8,2048]{1,0:T(8,128)(2,1)S(1)}, bf16[8,2048]{1,0:T(8,128)(2,1)S(1)}, u32[]{:S(2)}, u32[]{:S(2)}) collective-permute-start(bf16[8,2048]{1,0:T(8,128)(2,1)S(1)} %get-tuple-element.33), channel_id=1, source_target_pairs={{0,24},{8,16},{16,8},{24,0},{1,25},{9,17},{17,9},{25,1},{2,26},{10... | collective-permute-start | bytes 98312 | tf_op jit(solution)/shard_map/ppermute | solution.py:320
  65.5 0.7 collective-permute-done.9.rest_1_
  66.2 1.6 %collective-permute-done.10.rest_2_ = bf16[8,2048]{1,0:T(8,128)(2,1)S(1)} collective-permute-done((bf16[8,2048]{1,0:T(8,128)(2,1)S(1)}, bf16[8,2048]{1,0:T(8,128)(2,1)S(1)}, u32[]{:S(2)}, u32[]{:S(2)}) %collective-permute-start.10) | collective-permute-done | bytes 32800 | tf_op jit(solution)/shard_map/ppermute | solution.py:320
  67.7 0.8 copy-done.17
  68.5 0.8 copy-done.18
  69.2 0.8 copy-done.19
  70.0 0.8 decode_rows.1.decode_ref
  70.9 3.0 %hidden.1.hidden_ref = bf16[272,2048]{1,0:T(8,128)(2,1)S(1)} custom-call(s32[3]{0:T(128)S(1)} %pad_add_fusion.place_ref, bf16[1,256,2048]{2,1,0:T(8,128)(2,1)S(1)} %copy-done.4, f32[256,16]{1,0:T(8,128)S(1)} %get-tuple-element.20.col_ref, bf16[16,2048]{1,0:T(8,128)(2,1)S(1)} %decode_rows.1.decode_ref, f32[256,512]{1,0:T(8,128)S(1)} %copy-done.11, ...), custom_call_target="tpu_custom_call" | custom-call | flops 134217728 | bytes 4194304 | tf_op jit(solution)/shard_map/hidden/pallas_call | solution.py:489
  74.0 8.1 %copy-done = bf16[2048,6144]{1,0:T(8,128)(2,1)S(1)} copy-done((bf16[2048,6144]{1,0:T(8,128)(2,1)S(1)}, bf16[2048,6144]{1,0:T(8,128)(2,1)}, u32[]{:S(2)}) %copy-start) | copy-done | bytes 25165848
  82.1 1.6 %project.9 = bf16[272,768]{1,0:T(8,128)(2,1)S(1)} custom-call(s32[3]{0:T(128)S(1)} %pad_add_fusion.place_ref, bf16[272,2048]{1,0:T(8,128)(2,1)S(1)} %hidden.1.hidden_ref, bf16[2048,6144]{1,0:T(8,128)(2,1)S(1)} %copy-done), custom_call_target="tpu_custom_call" | custom-call | flops 855638016 | bytes 3145728 | tf_op jit(solution)/shard_map/project/pallas_call | solution.py:510
  83.7 1.5 %collective-permute-start.17 = (bf16[272,768]{1,0:T(8,128)(2,1)S(1)}, bf16[272,768]{1,0:T(8,128)(2,1)S(1)}, u32[]{:S(2)}, u32[]{:S(2)}) collective-permute-start(bf16[272,768]{1,0:T(8,128)(2,1)S(1)} %project.9), channel_id=1, source_target_pairs={{0,2},{2,0},{4,6},{6,4},{1,3},{3,1},{5,7},{7,5},{8,10},{10,8},{12,... | collective-permute-start | bytes 1253384 | tf_op jit(solution)/shard_map/ppermute | solution.py:320
  85.3 1.6 %project.10 = bf16[272,768]{1,0:T(8,128)(2,1)S(1)} custom-call(s32[3]{0:T(128)S(1)} %pad_add_fusion.place_ref, bf16[272,2048]{1,0:T(8,128)(2,1)S(1)} %hidden.1.hidden_ref, bf16[2048,6144]{1,0:T(8,128)(2,1)S(1)} %copy-done), custom_call_target="tpu_custom_call" | custom-call | flops 855638016 | bytes 3145728 | tf_op jit(solution)/shard_map/project/pallas_call | solution.py:510
  86.9 1.6 %collective-permute-start.19 = (bf16[272,768]{1,0:T(8,128)(2,1)S(1)}, bf16[272,768]{1,0:T(8,128)(2,1)S(1)}, u32[]{:S(2)}, u32[]{:S(2)}) collective-permute-start(bf16[272,768]{1,0:T(8,128)(2,1)S(1)} %project.10), channel_id=1, source_target_pairs={{0,4},{2,6},{4,0},{6,2},{1,5},{3,7},{5,1},{7,3},{8,12},{10,14},{12... | collective-permute-start | bytes 1253384 | tf_op jit(solution)/shard_map/ppermute | solution.py:320
  88.5 1.6 %project.7 = bf16[272,768]{1,0:T(8,128)(2,1)S(1)} custom-call(s32[3]{0:T(128)S(1)} %pad_add_fusion.place_ref, bf16[272,2048]{1,0:T(8,128)(2,1)S(1)} %hidden.1.hidden_ref, bf16[2048,6144]{1,0:T(8,128)(2,1)S(1)} %copy-done), custom_call_target="tpu_custom_call" | custom-call | flops 855638016 | bytes 3145728 | tf_op jit(solution)/shard_map/project/pallas_call | solution.py:510
  90.1 0.6 collective-permute-start.16
  90.7 1.6 %project.11 = bf16[272,768]{1,0:T(8,128)(2,1)S(1)} custom-call(s32[3]{0:T(128)S(1)} %pad_add_fusion.place_ref, bf16[272,2048]{1,0:T(8,128)(2,1)S(1)} %hidden.1.hidden_ref, bf16[2048,6144]{1,0:T(8,128)(2,1)S(1)} %copy-done), custom_call_target="tpu_custom_call" | custom-call | flops 855638016 | bytes 3145728 | tf_op jit(solution)/shard_map/project/pallas_call | solution.py:510
  92.3 0.6 collective-permute-start.21
  92.8 2.5 %project.8 = (f32[272,768]{1,0:T(8,128)S(1)}, f32[272,768]{1,0:T(8,128)S(1)}) custom-call(s32[3]{0:T(128)S(1)} %pad_add_fusion.place_ref, bf16[272,2048]{1,0:T(8,128)(2,1)S(1)} %hidden.1.hidden_ref, bf16[2048,6144]{1,0:T(8,128)(2,1)S(1)} %copy-done), custom_call_target="tpu_custom_call" | custom-call | flops 1711276032 | bytes 6291456 | tf_op jit(solution)/shard_map/project/pallas_call | solution.py:510
  95.3 1.1 collective-permute-done.17.got_ref
  96.5 1.6 %collective-permute-start.18 = (bf16[272,768]{1,0:T(8,128)(2,1)S(1)}, bf16[272,768]{1,0:T(8,128)(2,1)S(1)}, u32[]{:S(2)}, u32[]{:S(2)}) collective-permute-start(bf16[272,768]{1,0:T(8,128)(2,1)S(1)} %relay.2), channel_id=1, source_target_pairs={{0,4},{2,6},{4,0},{6,2},{1,5},{3,7},{5,1},{7,3},{8,12},{10,14},{12... | collective-permute-start | bytes 1253384 | tf_op jit(solution)/shard_map/ppermute | solution.py:320
  98.1 1.5 %collective-permute-done.19.got_ref = bf16[272,768]{1,0:T(8,128)(2,1)S(1)} collective-permute-done((bf16[272,768]{1,0:T(8,128)(2,1)S(1)}, bf16[272,768]{1,0:T(8,128)(2,1)S(1)}, u32[]{:S(2)}, u32[]{:S(2)}) %collective-permute-start.19) | collective-permute-done | bytes 417824 | tf_op jit(solution)/shard_map/ppermute | solution.py:320
  99.9 8.2 %copy-done.1 = bf16[2048,6144]{1,0:T(8,128)(2,1)S(1)} copy-done((bf16[2048,6144]{1,0:T(8,128)(2,1)S(1)}, bf16[2048,6144]{1,0:T(8,128)(2,1)}, u32[]{:S(2)}) %copy-start.1) | copy-done | bytes 25165848
  108.0 2.4 %project.6 = (f32[272,768]{1,0:T(8,128)S(1)}, f32[272,768]{1,0:T(8,128)S(1)}) custom-call(s32[3]{0:T(128)S(1)} %pad_add_fusion.place_ref, bf16[272,2048]{1,0:T(8,128)(2,1)S(1)} %hidden.1.hidden_ref, bf16[2048,6144]{1,0:T(8,128)(2,1)S(1)} %copy-done.1), custom_call_target="tpu_custom_call" | custom-call | flops 1711276032 | bytes 6291456 | tf_op jit(solution)/shard_map/project/pallas_call | solution.py:510
  110.5 3.6 %collective-permute-done.18.ay = bf16[272,768]{1,0:T(8,128)(2,1)S(1)} collective-permute-done((bf16[272,768]{1,0:T(8,128)(2,1)S(1)}, bf16[272,768]{1,0:T(8,128)(2,1)S(1)}, u32[]{:S(2)}, u32[]{:S(2)}) %collective-permute-start.18) | collective-permute-done | bytes 417824 | tf_op jit(solution)/shard_map/ppermute | solution.py:320
  114.1 1.6 %finish.1 = (bf16[1,256,1536]{2,1,0:T(8,128)(2,1)}, bf16[4,2,1536]{2,1,0:T(2,128)(2,1)}) custom-call(f32[272,768]{1,0:T(8,128)S(1)} %get-tuple-element.34.own_a, f32[272,768]{1,0:T(8,128)S(1)} %get-tuple-element.35.own_b, bf16[272,768]{1,0:T(8,128)(2,1)S(1)} %collective-permute-done.16.ax, bf16[272,768]{1,0:T(8,128)(2,1)S(1)} %collective-permute-done.18.ay, ...), custom_call_target="tpu_custom_call" | custom-call | flops 1253376 | bytes 4177920 | tf_op jit(solution)/shard_map/finish/pallas_call | solution.py:538
  (53 shorter events, 0.9 us)
Async XLA Ops:
  0.6 70.2 %copy-start.4 = (bf16[1,256,2048]{2,1,0:T(8,128)(2,1)S(1)}, bf16[1,256,2048]{2,1,0:T(8,128)(2,1)}, u32[]{:S(2)}) copy-start(bf16[1,256,2048]{2,1,0:T(8,128)(2,1)} %q_ref.13) | copy-start | bytes 3145732
  0.6 1.3 %copy-start.12 = (bf16[1,256,2048]{2,1,0:T(8,128)(2,1)S(1)}, bf16[1,256,2048]{2,1,0:T(8,128)(2,1)}, u32[]{:S(2)}) copy-start(bf16[1,256,2048]{2,1,0:T(8,128)(2,1)} %k_hbm.1) | copy-start | bytes 3145732
  2.0 1.2 %copy-start.13 = (bf16[1,256,2048]{2,1,0:T(8,128)(2,1)S(1)}, bf16[1,256,2048]{2,1,0:T(8,128)(2,1)}, u32[]{:S(2)}) copy-start(bf16[1,256,2048]{2,1,0:T(8,128)(2,1)} %v_hbm.1) | copy-start | bytes 3145732
  3.2 0.7 copy-start.20
  3.9 63.8 %copy-start.21 = (f32[4,16,2]{1,2,0:T(2,128)S(1)}, f32[4,16,2]{1,2,0:T(2,128)}, u32[]{:S(2)}) copy-start(f32[4,16,2]{1,2,0:T(2,128)} %param.18) | copy-start | bytes 1540
  7.8 21.4 %copy-start.5 = (bf16[256,2048]{1,0:T(8,128)(2,1)}, bf16[256,2048]{1,0:T(8,128)(2,1)S(1)}, u32[]{:S(2)}) copy-start(bf16[256,2048]{1,0:T(8,128)(2,1)S(1)} %get-tuple-element.27.v_ref) | copy-start | bytes 3145732
  7.8 21.4 %copy-start.14 = (f32[16,256]{1,0:T(8,128)}, f32[16,256]{1,0:T(8,128)S(1)}, u32[]{:S(2)}) copy-start(f32[16,256]{1,0:T(8,128)S(1)} %get-tuple-element.28.row_ref) | copy-start | bytes 49156
  7.8 0.8 copy-start.16
  8.6 0.7 copy-start.22
  9.9 7.7 %collective-permute-start.2 = (bf16[16,2048]{1,0:T(8,128)(2,1)S(1)}, bf16[16,2048]{1,0:T(8,128)(2,1)S(1)}, u32[]{:S(2)}, u32[]{:S(2)}) collective-permute-start(bf16[16,2048]{1,0:T(8,128)(2,1)S(1)} %decode_message.1), channel_id=1, source_target_pairs={{0,24},{8,16},{16,8},{24,0},{1,25},{9,17},{17,9},{25,1},{2,26},{10... | collective-permute-start | bytes 196616 | tf_op jit(solution)/shard_map/ppermute | solution.py:320
  15.0 5.6 %collective-permute-start.1 = (bf16[16,2048]{1,0:T(8,128)(2,1)S(1)}, bf16[16,2048]{1,0:T(8,128)(2,1)S(1)}, u32[]{:S(2)}, u32[]{:S(2)}) collective-permute-start(bf16[16,2048]{1,0:T(8,128)(2,1)S(1)} %decode_message.1), channel_id=1, source_target_pairs={{0,16},{8,24},{16,0},{24,8},{1,17},{9,25},{17,1},{25,9},{2,18},{10... | collective-permute-start | bytes 196616 | tf_op jit(solution)/shard_map/ppermute | solution.py:320
  15.0 5.6 %collective-permute-start = (bf16[16,2048]{1,0:T(8,128)(2,1)S(1)}, bf16[16,2048]{1,0:T(8,128)(2,1)S(1)}, u32[]{:S(2)}, u32[]{:S(2)}) collective-permute-start(bf16[16,2048]{1,0:T(8,128)(2,1)S(1)} %decode_message.1), channel_id=1, source_target_pairs={{0,8},{8,0},{16,24},{24,16},{1,9},{9,1},{17,25},{25,17},{2,10},{10... | collective-permute-start | bytes 196616 | tf_op jit(solution)/shard_map/ppermute | solution.py:320
  20.6 21.3 %collective-permute-start.3 = (bf16[64,2048]{1,0:T(8,128)(2,1)S(1)}, bf16[64,2048]{1,0:T(8,128)(2,1)}, u32[]{:S(2)}, u32[]{:S(2)}) collective-permute-start(bf16[64,2048]{1,0:T(8,128)(2,1)S(1)} %pad_maximum_fusion.near_ref), channel_id=1, source_target_pairs={{0,1},{1,0},{2,3},{3,2},{4,5},{5,4},{6,7},{7,6},{8,9},{9,8},{10,11... | collective-permute-start | bytes 786440 | tf_op jit(solution)/shard_map/ppermute | solution.py:320
  20.7 9.4 %collective-permute-start.6 = (bf16[4,128,128]{2,1,0:T(8,128)(2,1)}, bf16[4,128,128]{2,1,0:T(8,128)(2,1)}, u32[]{:S(2)}, u32[]{:S(2)}) collective-permute-start(bf16[4,128,128]{2,1,0:T(8,128)(2,1)} %get-tuple-element.29), channel_id=1, source_target_pairs={{0,8},{8,16},{16,24},{1,9},{9,17},{17,25},{2,10},{10,18},{18,26},{... | collective-permute-start | bytes 393224 | tf_op jit(solution)/shard_map/ppermute | solution.py:473
  24.4 14.6 %collective-permute-start.4 = (bf16[4,128,128]{2,1,0:T(8,128)(2,1)}, bf16[4,128,128]{2,1,0:T(8,128)(2,1)}, u32[]{:S(2)}, u32[]{:S(2)}) collective-permute-start(bf16[4,128,128]{2,1,0:T(8,128)(2,1)} %get-tuple-element.23), channel_id=1, source_target_pairs={{0,8},{8,16},{16,24},{1,9},{9,17},{17,25},{2,10},{10,18},{18,26},{... | collective-permute-start | bytes 393224 | tf_op jit(solution)/shard_map/ppermute | solution.py:473
  27.3 1.2 %copy-start.2 = (bf16[1,256,2048]{2,1,0:T(8,128)(2,1)S(1)}, bf16[1,256,2048]{2,1,0:T(8,128)(2,1)}, u32[]{:S(2)}) copy-start(bf16[1,256,2048]{2,1,0:T(8,128)(2,1)} %q_ref.13) | copy-start | bytes 3145732
  29.2 0.8 copy-start.9
  30.1 1.0 copy-start.10
  31.2 39.7 %copy-start.11 = (f32[256,512]{1,0:T(8,128)S(1)}, f32[256,512]{1,0:T(8,128)}, u32[]{:S(2)}) copy-start(f32[256,512]{1,0:T(8,128)} %copy-done.9) | copy-start | bytes 1572868
  32.2 11.2 %collective-permute-start.11 = (bf16[4,128,128]{2,1,0:T(8,128)(2,1)S(1)}, bf16[4,128,128]{2,1,0:T(8,128)(2,1)S(1)}, u32[]{:S(2)}, u32[]{:S(2)}) collective-permute-start(bf16[4,128,128]{2,1,0:T(8,128)(2,1)S(1)} %chain.7), channel_id=1, source_target_pairs={{0,8},{8,16},{16,24},{1,9},{9,17},{17,25},{2,10},{10,18},{18,26},{... | collective-permute-start | bytes 393224 | tf_op jit(solution)/shard_map/ppermute | solution.py:473
  35.2 1.2 %copy-start.3 = (bf16[1,256,2048]{2,1,0:T(8,128)(2,1)S(1)}, bf16[1,256,2048]{2,1,0:T(8,128)(2,1)}, u32[]{:S(2)}) copy-start(bf16[1,256,2048]{2,1,0:T(8,128)(2,1)} %q_ref.13) | copy-start | bytes 3145732
  36.4 1.2 %copy-start.6 = (bf16[256,2048]{1,0:T(8,128)(2,1)S(1)}, bf16[256,2048]{1,0:T(8,128)(2,1)}, u32[]{:S(2)}) copy-start(bf16[256,2048]{1,0:T(8,128)(2,1)} %copy-done.5) | copy-start | bytes 3145732
  37.6 0.7 copy-start.15
  40.0 9.7 %collective-permute-start.7 = (bf16[4,128,128]{2,1,0:T(8,128)(2,1)S(1)}, bf16[4,128,128]{2,1,0:T(8,128)(2,1)S(1)}, u32[]{:S(2)}, u32[]{:S(2)}) collective-permute-start(bf16[4,128,128]{2,1,0:T(8,128)(2,1)S(1)} %chain.6), channel_id=1, source_target_pairs={{0,8},{8,16},{16,24},{1,9},{9,17},{17,25},{2,10},{10,18},{18,26},{... | collective-permute-start | bytes 393224 | tf_op jit(solution)/shard_map/ppermute | solution.py:473
  43.3 8.9 %collective-permute-start.5 = (bf16[32,2048]{1,0:T(8,128)(2,1)S(1)}, bf16[32,2048]{1,0:T(8,128)(2,1)S(1)}, u32[]{:S(2)}, u32[]{:S(2)}) collective-permute-start(bf16[32,2048]{1,0:T(8,128)(2,1)S(1)} %get-tuple-element.25), channel_id=1, source_target_pairs={{0,1},{1,0},{2,3},{3,2},{4,5},{5,4},{6,7},{7,6},{8,9},{9,8},{10,11... | collective-permute-start | bytes 393224 | tf_op jit(solution)/shard_map/ppermute | solution.py:320
  44.0 8.9 %collective-permute-start.12 = (bf16[4,128,128]{2,1,0:T(8,128)(2,1)S(1)}, bf16[4,128,128]{2,1,0:T(8,128)(2,1)S(1)}, u32[]{:S(2)}, u32[]{:S(2)}) collective-permute-start(bf16[4,128,128]{2,1,0:T(8,128)(2,1)S(1)} %chain.8), channel_id=1, source_target_pairs={{0,8},{8,16},{16,24},{1,9},{9,17},{17,25},{2,10},{10,18},{18,26},{... | collective-permute-start | bytes 393224 | tf_op jit(solution)/shard_map/ppermute | solution.py:473
  47.8 1.2 %copy-start.7 = (bf16[256,2048]{1,0:T(8,128)(2,1)S(1)}, bf16[256,2048]{1,0:T(8,128)(2,1)}, u32[]{:S(2)}) copy-start(bf16[256,2048]{1,0:T(8,128)(2,1)} %copy-done.5) | copy-start | bytes 3145732
  50.3 7.8 %collective-permute-start.13 = (bf16[4,128,128]{2,1,0:T(8,128)(2,1)S(1)}, bf16[4,128,128]{2,1,0:T(8,128)(2,1)S(1)}, u32[]{:S(2)}, u32[]{:S(2)}) collective-permute-start(bf16[4,128,128]{2,1,0:T(8,128)(2,1)S(1)} %chain.9), channel_id=1, source_target_pairs={{0,8},{8,16},{16,24},{1,9},{9,17},{17,25},{2,10},{10,18},{18,26},{... | collective-permute-start | bytes 393224 | tf_op jit(solution)/shard_map/ppermute | solution.py:473
  53.5 17.4 %collective-permute-start.14 = (bf16[4,128,128]{2,1,0:T(8,128)(2,1)S(1)}, bf16[4,128,128]{2,1,0:T(8,128)(2,1)S(1)}, u32[]{:S(2)}, u32[]{:S(2)}) collective-permute-start(bf16[4,128,128]{2,1,0:T(8,128)(2,1)S(1)} %chain.10), channel_id=1, source_target_pairs={{0,8},{8,16},{16,24},{1,9},{9,17},{17,25},{2,10},{10,18},{18,26},{... | collective-permute-start | bytes 393224 | tf_op jit(solution)/shard_map/ppermute | solution.py:473
  56.1 1.2 %copy-start.8 = (bf16[256,2048]{1,0:T(8,128)(2,1)S(1)}, bf16[256,2048]{1,0:T(8,128)(2,1)}, u32[]{:S(2)}) copy-start(bf16[256,2048]{1,0:T(8,128)(2,1)} %copy-done.5) | copy-start | bytes 3145732
  58.6 12.2 %collective-permute-start.15 = (bf16[4,128,128]{2,1,0:T(8,128)(2,1)S(1)}, bf16[4,128,128]{2,1,0:T(8,128)(2,1)S(1)}, u32[]{:S(2)}, u32[]{:S(2)}) collective-permute-start(bf16[4,128,128]{2,1,0:T(8,128)(2,1)S(1)} %chain.11), channel_id=1, source_target_pairs={{0,8},{8,16},{16,24},{1,9},{9,17},{17,25},{2,10},{10,18},{18,26},{... | collective-permute-start | bytes 393224 | tf_op jit(solution)/shard_map/ppermute | solution.py:473
  61.0 4.5 %collective-permute-start.8 = (bf16[8,2048]{1,0:T(8,128)(2,1)S(1)}, bf16[8,2048]{1,0:T(8,128)(2,1)S(1)}, u32[]{:S(2)}, u32[]{:S(2)}) collective-permute-start(bf16[8,2048]{1,0:T(8,128)(2,1)S(1)} %get-tuple-element.31), channel_id=1, source_target_pairs={{0,8},{8,0},{16,24},{24,16},{1,9},{9,1},{17,25},{25,17},{2,10},{10... | collective-permute-start | bytes 98312 | tf_op jit(solution)/shard_map/ppermute | solution.py:320
  61.1 5.1 %collective-permute-start.9 = (bf16[8,2048]{1,0:T(8,128)(2,1)S(1)}, bf16[8,2048]{1,0:T(8,128)(2,1)S(1)}, u32[]{:S(2)}, u32[]{:S(2)}) collective-permute-start(bf16[8,2048]{1,0:T(8,128)(2,1)S(1)} %get-tuple-element.32), channel_id=1, source_target_pairs={{0,16},{8,24},{16,0},{24,8},{1,17},{9,25},{17,1},{25,9},{2,18},{10... | collective-permute-start | bytes 98312 | tf_op jit(solution)/shard_map/ppermute | solution.py:320
  61.2 6.5 %collective-permute-start.10 = (bf16[8,2048]{1,0:T(8,128)(2,1)S(1)}, bf16[8,2048]{1,0:T(8,128)(2,1)S(1)}, u32[]{:S(2)}, u32[]{:S(2)}) collective-permute-start(bf16[8,2048]{1,0:T(8,128)(2,1)S(1)} %get-tuple-element.33), channel_id=1, source_target_pairs={{0,24},{8,16},{16,8},{24,0},{1,25},{9,17},{17,9},{25,1},{2,26},{10... | collective-permute-start | bytes 98312 | tf_op jit(solution)/shard_map/ppermute | solution.py:320
  67.7 0.8 copy-start.17
  68.5 0.8 copy-start.18
  69.2 0.8 copy-start.19
  73.9 8.2 %copy-start = (bf16[2048,6144]{1,0:T(8,128)(2,1)S(1)}, bf16[2048,6144]{1,0:T(8,128)(2,1)}, u32[]{:S(2)}) copy-start(bf16[2048,6144]{1,0:T(8,128)(2,1)} %weight_ref.11) | copy-start | bytes 75497472
  83.7 12.6 %collective-permute-start.17 = (bf16[272,768]{1,0:T(8,128)(2,1)S(1)}, bf16[272,768]{1,0:T(8,128)(2,1)S(1)}, u32[]{:S(2)}, u32[]{:S(2)}) collective-permute-start(bf16[272,768]{1,0:T(8,128)(2,1)S(1)} %project.9), channel_id=1, source_target_pairs={{0,2},{2,0},{4,6},{6,4},{1,3},{3,1},{5,7},{7,5},{8,10},{10,8},{12,... | collective-permute-start | bytes 1253384 | tf_op jit(solution)/shard_map/ppermute | solution.py:320
  86.9 12.6 %collective-permute-start.19 = (bf16[272,768]{1,0:T(8,128)(2,1)S(1)}, bf16[272,768]{1,0:T(8,128)(2,1)S(1)}, u32[]{:S(2)}, u32[]{:S(2)}) collective-permute-start(bf16[272,768]{1,0:T(8,128)(2,1)S(1)} %project.10), channel_id=1, source_target_pairs={{0,4},{2,6},{4,0},{6,2},{1,5},{3,7},{5,1},{7,3},{8,12},{10,14},{12... | collective-permute-start | bytes 1253384 | tf_op jit(solution)/shard_map/ppermute | solution.py:320
  90.1 20.3 %collective-permute-start.16 = (bf16[272,768]{1,0:T(8,128)(2,1)S(1)}, bf16[272,768]{1,0:T(8,128)(2,1)S(1)}, u32[]{:S(2)}, u32[]{:S(2)}) collective-permute-start(bf16[272,768]{1,0:T(8,128)(2,1)S(1)} %project.7), channel_id=1, source_target_pairs={{0,2},{2,0},{4,6},{6,4},{1,3},{3,1},{5,7},{7,5},{8,10},{10,8},{12,... | collective-permute-start | bytes 1253384 | tf_op jit(solution)/shard_map/ppermute | solution.py:320
  92.3 18.2 %collective-permute-start.21 = (bf16[272,768]{1,0:T(8,128)(2,1)S(1)}, bf16[272,768]{1,0:T(8,128)(2,1)S(1)}, u32[]{:S(2)}, u32[]{:S(2)}) collective-permute-start(bf16[272,768]{1,0:T(8,128)(2,1)S(1)} %project.11), channel_id=1, source_target_pairs={{0,4},{2,6},{4,0},{6,2},{1,5},{3,7},{5,1},{7,3},{8,12},{10,14},{12... | collective-permute-start | bytes 1253384 | tf_op jit(solution)/shard_map/ppermute | solution.py:320
  96.5 17.6 %collective-permute-start.18 = (bf16[272,768]{1,0:T(8,128)(2,1)S(1)}, bf16[272,768]{1,0:T(8,128)(2,1)S(1)}, u32[]{:S(2)}, u32[]{:S(2)}) collective-permute-start(bf16[272,768]{1,0:T(8,128)(2,1)S(1)} %relay.2), channel_id=1, source_target_pairs={{0,4},{2,6},{4,0},{6,2},{1,5},{3,7},{5,1},{7,3},{8,12},{10,14},{12... | collective-permute-start | bytes 1253384 | tf_op jit(solution)/shard_map/ppermute | solution.py:320
  99.7 14.4 %collective-permute-start.20 = (bf16[272,768]{1,0:T(8,128)(2,1)S(1)}, bf16[272,768]{1,0:T(8,128)(2,1)S(1)}, u32[]{:S(2)}, u32[]{:S(2)}) collective-permute-start(bf16[272,768]{1,0:T(8,128)(2,1)S(1)} %relay.3), channel_id=1, source_target_pairs={{0,2},{2,0},{4,6},{6,4},{1,3},{3,1},{5,7},{7,5},{8,10},{10,8},{12,... | collective-permute-start | bytes 1253384 | tf_op jit(solution)/shard_map/ppermute | solution.py:320
  99.9 8.2 %copy-start.1 = (bf16[2048,6144]{1,0:T(8,128)(2,1)S(1)}, bf16[2048,6144]{1,0:T(8,128)(2,1)}, u32[]{:S(2)}) copy-start(bf16[2048,6144]{1,0:T(8,128)(2,1)} %weight_ref.11) | copy-start | bytes 75497472

commit v3 on v2

--- a/solution.py
+++ b/solution.py
@@ -13,7 +13,8 @@
 HIGH = lax.Precision.HIGHEST
 CHUNKS = 4
 LAG = 2
-VMEM_BYTES = 16 * 2**20
+VMEM_BYTES = 12 * 2**20
+PARTS_OF_COPY = 2
 F32 = jnp.float32
 BF16 = jnp.bfloat16
 NT = (((1,), (1,)), ((), ()))
@@ -85,19 +86,32 @@
     return jax.ShapeDtypeStruct(shape, dtype)
 
 
-def state_kernel(span, k_hbm, v_hbm, rate_ref, own_ref, first_ref, second_ref, log_ref, col_ref, row_ref, k_ref, v_ref, sems):
+def state_kernel(span, *refs):
+    k_hbm, v_hbm, rate_hbm, q_hbm, dq_hbm, dk_hbm, dv_hbm = refs[:7]
+    own_ref, first_ref, second_ref, log_ref, col_ref, row_ref = refs[7:13]
+    k_ref, v_ref, q_ref, dq_ref, dk_ref, dv_ref = refs[13:19]
+    rate_ref, sems, more = refs[19:]
     heads = own_ref.shape[0]
     wide = span * HEAD_DIM
+    rate_copy = pltpu.make_async_copy(rate_hbm, rate_ref, more.at[0])
+    rate_copy.start()
     copies = []
     for c in range(heads // span):
         at = pl.ds(c * wide, wide)
         copies.append(pltpu.make_async_copy(k_hbm.at[0, :, at], k_ref.at[:, at], sems.at[0, c]))
         copies.append(pltpu.make_async_copy(v_hbm.at[0, :, at], v_ref.at[:, at], sems.at[1, c]))
-    for copy in copies:
+    others = [
+        pltpu.make_async_copy(source, target, more.at[1 + i])
+        for i, (source, target) in enumerate(
+            ((dq_hbm, dq_ref), (dk_hbm, dk_ref), (dv_hbm, dv_ref), (q_hbm, q_ref))
+        )
+    ]
+    for copy in copies + others:
         copy.start()
     length = k_ref.shape[0]
+    lower = lower_ones(length)
+    rate_copy.wait()
     rate = rate_ref[0]
-    lower = lower_ones(length)
     columns = decay_columns(rate, lower)
     col_ref[...] = columns
     row_ref[...] = decay_rows(rate, lower)
@@ -121,6 +135,8 @@
         elif i < 2 * span:
             second_ref[i - span] = state.astype(BF16)
         log_ref[:, at] = jnp.broadcast_to(total[:, i : i + 1], (1, HEAD_DIM))
+    for copy in others:
+        copy.wait()
 
 
 def chain_kernel(step, place_ref, own_ref, log_ref, got_ref, *rest):
@@ -137,7 +153,8 @@
 
 
 def local_kernel(first, q_ref, k_ref, v_ref, col_ref, row_ref, *rest):
-    local_ref = rest[-1]
+    local_ref, token_ref = rest[-2:]
+    token_ref[...] = jnp.zeros_like(token_ref)
     lower = lower_ones(q_ref.shape[1])
     for i in range(local_ref.shape[1] // HEAD_DIM):
         h = first + i
@@ -150,23 +167,18 @@
         local_ref[:, head_slice(i)] = jnp.dot(weights, v_ref[:, at], preferred_element_type=F32)
 
 
-def hidden_kernel(chunks, groups, place_ref, q_ref, col_ref, decode_ref, *rest):
-    locals_ref, got, hidden_ref = rest[:chunks], rest[chunks:-1], rest[-1]
-    length = q_ref.shape[1]
-    factor = jnp.exp(col_ref[...])
-    span = got[0].shape[0]
+def hidden_kernel(first, place_ref, q_ref, col_ref, local_ref, *rest):
+    got, hidden_ref = rest[:-1], rest[-1]
     group = place_ref[0]
-    for chunk in range(chunks):
-        for i in range(span):
-            state = got[chunk][i]
-            for g in range(2, groups):
-                state = jnp.where(group == g, got[chunk + LAG * (g - 1)][i], state)
-            h = chunk * span + i
-            at = head_slice(h)
-            inter = jnp.dot(q_ref[0, :, at], state, preferred_element_type=F32)
-            attended = locals_ref[chunk][:, head_slice(i)] + inter * factor[:, h : h + 1]
-            hidden_ref[:length, at] = normalize(attended).astype(BF16)
-    hidden_ref[length:, :] = decode_ref[...]
+    for i in range(got[0].shape[0]):
+        state = got[0][i]
+        for g in range(1, len(got)):
+            state = jnp.where(group == g + 1, got[g][i], state)
+        h = first + i
+        at = head_slice(i)
+        inter = jnp.dot(q_ref[0, :, head_slice(h)], state, preferred_element_type=F32)
+        attended = local_ref[:, at] + inter * jnp.exp(col_ref[:, h : h + 1])
+        hidden_ref[:, at] = normalize(attended).astype(BF16)
 
 
 def flat_rows(ref, rows_ref):
@@ -276,14 +288,37 @@
     out_ref[...] = value.astype(BF16)
 
 
-def project_kernel(pieces, place_ref, hidden_ref, weight_ref, *outs):
+def project_kernel(pieces, chunks, place_ref, decode_ref, *rest):
+    hidden, weight_hbm = rest[:chunks], rest[chunks]
+    outs = rest[chunks + 1 : chunks + 1 + len(pieces)]
+    weight_ref, sems = rest[-2:]
     half = outs[0].shape[1]
-    rows = hidden_ref[...]
-    for (bits, part), out_ref in zip(pieces, outs):
-        column = pl.multiple_of(((place_ref[2] ^ bits) * 2 + part) * half, HEAD_DIM)
-        out_ref[...] = jnp.dot(
-            rows, weight_ref[:, pl.ds(column, half)], preferred_element_type=F32
-        ).astype(out_ref.dtype)
+    depth = hidden[0].shape[1]
+    part = depth // PARTS_OF_COPY
+    copies = []
+    for n, (bits, side) in enumerate(pieces):
+        column = pl.multiple_of(((place_ref[2] ^ bits) * 2 + side) * half, HEAD_DIM)
+        for k in range(chunks * PARTS_OF_COPY):
+            copy = pltpu.make_async_copy(
+                weight_hbm.at[pl.ds(k * part, part), pl.ds(column, half)],
+                weight_ref.at[n, pl.ds(k * part, part)],
+                sems.at[n, k],
+            )
+            copy.start()
+            copies.append(copy)
+    for n, out_ref in enumerate(outs):
+        total = None
+        for c in range(chunks):
+            rows = jnp.concatenate(
+                [hidden[c][...], decode_ref[:, c * depth : (c + 1) * depth]], axis=0
+            )
+            for k in range(c * PARTS_OF_COPY, (c + 1) * PARTS_OF_COPY):
+                copies[n * chunks * PARTS_OF_COPY + k].wait()
+            term = jnp.dot(
+                rows, weight_ref[n, c * depth : (c + 1) * depth], preferred_element_type=F32
+            )
+            total = term if total is None else total + term
+        out_ref[...] = total.astype(out_ref.dtype)
 
 
 def relay_kernel(own_ref, got_ref, out_ref):
@@ -351,23 +386,54 @@
     wide = span * HEAD_DIM
     chunk_shape = (span, HEAD_DIM, HEAD_DIM)
 
-    own, first, second, log_row, columns, rows, keys, values = call(
+    def in_hbm(array):
+        return pltpu.with_memory_space_constraint(array, pltpu.HBM)
+
+    def in_vmem(array):
+        return pltpu.with_memory_space_constraint(array, pltpu.VMEM)
+
+    decode_shape = (rows_here, steps, features)
+    own, first, second, log_row, columns, rows, keys, values, queries, d_query, d_key, d_value = call(
         functools.partial(state_kernel, span),
         "own_state",
-        [HBM, HBM, VMEM],
+        [HBM] * 7,
         [
-            sds((heads, HEAD_DIM, HEAD_DIM), F32),
+            pltpu.VMEM((heads, HEAD_DIM, HEAD_DIM), F32),
             sds(chunk_shape, BF16),
             sds(chunk_shape, BF16),
-            sds((1, features), F32),
-            sds((length, heads), F32),
-            sds((heads, length), F32),
+            pltpu.VMEM((1, features), F32),
+            pltpu.VMEM((length, heads), F32),
+            pltpu.VMEM((heads, length), F32),
             pltpu.VMEM((length, features), BF16),
             pltpu.VMEM((length, features), BF16),
+            pltpu.VMEM((1, length, features), BF16),
+            pltpu.VMEM(decode_shape, BF16),
+            pltpu.VMEM(decode_shape, BF16),
+            pltpu.VMEM(decode_shape, BF16),
         ],
-        [pltpu.SemaphoreType.DMA((2, chunks))],
+        [
+            pltpu.VMEM((1, heads, length), F32),
+            pltpu.SemaphoreType.DMA((2, chunks)),
+            pltpu.SemaphoreType.DMA((5,)),
+        ],
         cost(4 * length * features * HEAD_DIM, 4 * length * features),
-    )(prefill_key, prefill_value, prefill_rate)
+    )(
+        *[
+            in_hbm(array)
+            for array in (
+                prefill_key,
+                prefill_value,
+                prefill_rate,
+                prefill_query,
+                decode_query,
+                decode_key,
+                decode_value,
+            )
+        ]
+    )
+    own, log_row, columns, rows, keys, values, queries, d_query, d_key, d_value = map(
+        in_vmem, (own, log_row, columns, rows, keys, values, queries, d_query, d_key, d_value)
+    )
 
     def message(*after):
         return call(
@@ -377,17 +443,17 @@
             sds((unit, features), BF16),
             [pltpu.VMEM((unit, features), F32)],
             cost(unit * features, unit * features * 8),
-        )(decode_query, log_row, prompt_of_row, *after)
+        )(d_query, log_row, prompt_of_row, *after)
 
     def local(chunk, *after):
         return call(
             functools.partial(local_kernel, chunk * span),
             "local_attention",
             [VMEM] * 5 + [ANY] * len(after),
-            sds((length, wide), F32),
+            [pltpu.VMEM((length, wide), F32), sds((8, HEAD_DIM), F32)],
             (),
             cost(4 * length * length * wide, 6 * length * wide, span * length * length),
-        )(prefill_query, keys, values, columns, rows, *after)
+        )(queries, keys, values, columns, rows, *after)
 
     def start_terms(near, far, *after):
         return call(
@@ -419,9 +485,9 @@
             [flat, flat, flat, pltpu.VMEM((d_rows, heads), F32)],
             cost(4 * d_rows * features * d_rows, d_rows * features * 20),
         )(
-            decode_query,
-            decode_key,
-            decode_value,
+            d_query,
+            d_key,
+            d_value,
             jnp.transpose(decode_rate, (0, 2, 1)),
             base,
             *got,
@@ -430,38 +496,53 @@
 
     right = [(i, i + 1) for i in range(groups - 1)]
     steps_all = chunks + LAG * (groups - 2)
-    received, locals_done, slot = [], [], {}
-
-    def side_work(step, after):
-        made = []
-        if step == 0:
-            slot["message"] = message(*after)
-            slot["ctx"] = [swap(slot["message"], "ctx", groups, j) for j in range(1, groups)]
-            made.append(slot["message"])
-        if step == 2:
-            slot["near"] = jnp.concatenate([slot["message"]] + slot["ctx"], axis=0)
-            slot["far"] = swap(slot["near"], "rep", reps, 1)
-        if step == 3:
-            slot["mine"], away = start_terms(slot["near"], slot["far"], *after)
-            slot["other"] = swap(away, "rep", reps, 1)
-            made.append(slot["mine"])
-        if step == 5:
-            base, *terms = select_terms(slot["near"], slot["mine"], slot["other"], *after)
-            slot["base"] = base
-            slot["got"] = [
-                swap(term, "ctx", groups, j) for j, term in zip(range(1, groups), terms)
-            ]
-            made.append(base)
-        return made
-
-    local_at = {1: 0, 2: 1, 4: 2, 6: 3}
+    received, locals_done, waits = [], [], {}
+    decode = {}
+
+    def add_local(*after):
+        if len(locals_done) < chunks:
+            made, token = local(len(locals_done), *after)
+            locals_done.append(in_vmem(made))
+            return [token]
+        return []
+
+    def send_message(*after):
+        decode["message"] = message(*after)
+        decode["ctx"] = [swap(decode["message"], "ctx", groups, j) for j in range(1, groups)]
+        return [decode["message"]]
+
+    def share_message(*after):
+        decode["near"] = jnp.concatenate([decode["message"]] + decode["ctx"], axis=0)
+        decode["far"] = swap(decode["near"], "rep", reps, 1)
+        return [decode["near"]]
+
+    def start_rows(*after):
+        decode["mine"], away = start_terms(decode["near"], decode["far"], *after)
+        decode["other"] = swap(away, "rep", reps, 1)
+        return [decode["mine"]]
+
+    def select_rows(*after):
+        base, *terms = select_terms(decode["near"], decode["mine"], decode["other"], *after)
+        decode["got"] = [swap(term, "ctx", groups, j) for j, term in zip(range(1, groups), terms)]
+        decode["base"] = base
+        return [base]
+
+    plan = {
+        1: [add_local],
+        2: [send_message],
+        3: [add_local],
+        4: [share_message, add_local],
+        5: [start_rows],
+        6: [select_rows],
+        7: [add_local],
+    }
     for step in range(steps_all):
         if step == 0:
             value = first
         elif step < LAG:
             value = second if chunks > 1 else first
         else:
-            after = slot.pop("after", [])
+            after = waits.pop(step - 1, [])
             value = call(
                 functools.partial(chain_kernel, step),
                 "chain",
@@ -472,49 +553,56 @@
             )(place, own, log_row, received[step - LAG], *after)
         received.append(lax.ppermute(value, "ctx", right))
         ready = [received[step - LAG]] if step >= LAG else []
-        made = side_work(step, ready)
-        if step in local_at and local_at[step] < chunks:
-            locals_done.append(local(len(locals_done), *ready))
-            made.append(locals_done[-1])
-        slot["after"] = made
+        waits[step] = [token for work in plan.pop(step, []) for token in work(*ready)]
+    for step in sorted(plan):
+        for work in plan[step]:
+            work()
     while len(locals_done) < chunks:
-        locals_done.append(local(len(locals_done)))
-    if "message" not in slot:
-        side_work(0, [])
-    for step, name in ((2, "near"), (3, "mine"), (5, "base")):
-        if name not in slot:
-            side_work(step, [])
-    decode_hidden = decode_rows(slot["base"], slot["got"])
-
-    hidden = call(
-        functools.partial(hidden_kernel, chunks, groups),
-        "hidden",
-        [SMEM] + [VMEM] * (3 + chunks + len(received)),
-        sds((total_rows, features), BF16),
-        (),
-        cost(2 * length * features * HEAD_DIM, 8 * length * features),
-    )(place, prefill_query, columns, decode_hidden, *locals_done, *received)
+        add_local()
+    decode_hidden = decode_rows(decode["base"], decode["got"])
+
+    hidden = [
+        call(
+            functools.partial(hidden_kernel, chunk * span),
+            "hidden",
+            [SMEM] + [VMEM] * (3 + groups - 1),
+            sds((length, wide), BF16),
+            (),
+            cost(2 * length * wide * HEAD_DIM, 8 * length * wide),
+        )(
+            place,
+            queries,
+            columns,
+            locals_done[chunk],
+            *[received[chunk + LAG * g] for g in range(groups - 1)],
+        )
+        for chunk in range(chunks)
+    ]
 
     out_columns = out_weight.shape[1]
     if parts != 4 or (out_columns // parts) % 256 != 0 or length % 64 != 0:
-        terms = jnp.dot(hidden, out_weight, preferred_element_type=F32)
+        rows_all = jnp.concatenate([jnp.concatenate(hidden, axis=1), decode_hidden], axis=0)
+        terms = jnp.dot(rows_all, out_weight, preferred_element_type=F32)
         summed = lax.psum_scatter(terms, "head", scatter_dimension=1, tiled=True)
         prefill_out = summed[:length].astype(BF16)[None]
         decode_out = summed[length : length + d_rows].astype(BF16)
         return prefill_out, decode_out.reshape(rows_here, steps, -1)
 
     half = out_columns // parts // 2
-    weight = pltpu.with_memory_space_constraint(out_weight, pltpu.VMEM)
+    weight = in_hbm(out_weight)
 
     def project(pieces, dtype, *after):
         return call(
-            functools.partial(project_kernel, pieces),
+            functools.partial(project_kernel, pieces, chunks),
             "project",
-            [SMEM, VMEM, VMEM],
+            [SMEM, VMEM] + [VMEM] * chunks + [HBM],
             [sds((total_rows, half), dtype) for _ in pieces],
-            (),
+            [
+                pltpu.VMEM((len(pieces), features, half), BF16),
+                pltpu.SemaphoreType.DMA((len(pieces), chunks * PARTS_OF_COPY)),
+            ],
             cost(2 * total_rows * features * half * len(pieces), features * half * 2 * len(pieces)),
-        )(place, hidden, weight)
+        )(place, decode_hidden, *hidden, weight)
 
     def relay(own_term, got):
         return call(

time: 117 us -> 114 us (0.974)
  local copies, waits for them, and re-layouts: 32 us -> 13.2 us
  Pallas kernels: 30.5 us -> 48 us
  waiting for transfers between devices: 13.4 us -> 6.26 us
  starting transfers between devices: 38.6 us -> 44.3 us
    unnamed x46, local copies, waits for them, and re-layouts: 32 us -> 13.2 us
    pallas_call x8 -> x11, Pallas kernels: 18.3 us -> 35.8 us  [the longest x6 25.8 us: project(): call(functools.partial(project_kernel, pieces, chunks), 'project', [SMEM,...]
    ppermute x14, waiting for transfers between devices: 13.4 us -> 3.31 us  [swap(): return lax.ppermute(array, axis, [(i, i ^ bit) for i in range(size)])]
    ppermute x8, starting transfers between devices: 22.3 us -> 27.1 us  [body(): received.append(lax.ppermute(value, 'ctx', right))]
    ppermute x8, waiting for transfers between devices: 0.04 us -> 2.95 us  [body(): received.append(lax.ppermute(value, 'ctx', right))]
  transfers between devices with their start and end apart: 22 -> 22, of which waited for: 7 -> 4; matrix products, arithmetic and copies ran while one was open for 0% -> 0% of each run, Pallas kernels for 17% -> 32%
where the time goes in v3:
time: 114 us; the launch traced here: 113 us
  Pallas kernels  48 us (42%)
  starting transfers between devices  44.3 us (39%)
  local copies, waits for them, and re-layouts  13.2 us (12%)
  waiting for transfers between devices  6.26 us (5%)
  between operations  1.28 us (1%)
    ppermute x8, starting transfers between devices, body(): received.append(lax.ppermute(value, 'ctx', right))  27.1 us
    pallas_call x6, Pallas kernels, project(): call(functools.partial(project_kernel, pieces, chunks), 'project', [SMEM,...  25.8 us
    ppermute x14, starting transfers between devices, swap(): return lax.ppermute(array, axis, [(i, i ^ bit) for i in range(size)])  17.2 us
    unnamed x46, local copies, waits for them, and re-layouts  13.2 us
    pallas_call x1, Pallas kernels, body(): call(functools.partial(state_kernel, span), 'own_state', [HBM] * 7, [pltp...  5.11 us
    pallas_call x4, Pallas kernels, body(): call(functools.partial(hidden_kernel, chunk * span), 'hidden', [SMEM] + [...  4.86 us
    pallas_call x6, Pallas kernels, body(): call(functools.partial(chain_kernel, step), 'chain', [SMEM, VMEM, VMEM, V...  3.88 us
    ppermute x14, waiting for transfers between devices, swap(): return lax.ppermute(array, axis, [(i, i ^ bit) for i in range(size)])  3.31 us
  transfers between devices with their start and end apart: 22, of which 4 were waited for; matrix products, arithmetic and copies ran while one was open for 0% of the time, Pallas kernels for 32%

profile of v3, /device:TPU:0, one launch (start us, length us, event | category | flops | bytes accessed | tf_op | source)
XLA Modules:
  0.0 113.1 jit_solution(3200782243020723771)
XLA Ops:
  0.6 5.1 %own_state.1 = (f32[16,128,128]{2,1,0:T(8,128)S(1)}, bf16[4,128,128]{2,1,0:T(8,128)(2,1)S(1)}, bf16[4,128,128]{2,1,0:T(8,128)(2,1)}, f32[1,2048]{1,0:T(1,128)S(1...) custom-call(bf16[1,256,2048]{2,1,0:T(8,128)(2,1)} %refs_0_.1, ...), custom_call_target="tpu_custom_call" | custom-call | flops 268435456 | bytes 2097152 | tf_op jit(solution)/shard_map/own_state/pallas_call | solution.py:396
  5.8 0.6 copy-done.17
  6.4 4.9 %collective-permute-start = (bf16[4,128,128]{2,1,0:T(8,128)(2,1)S(1)}, bf16[4,128,128]{2,1,0:T(8,128)(2,1)S(1)}, u32[]{:S(2)}, u32[]{:S(2)}) collective-permute-start(bf16[4,128,128]{2,1,0:T(8,128)(2,1)S(1)} %get-tuple-element.35), channel_id=1, source_target_pairs={{0,8},{8,16},{16,24},{1,9},{9,17},{17,25},{2,10},{10,18},{18,26},{... | collective-permute-start | bytes 393224 | tf_op jit(solution)/shard_map/ppermute | solution.py:554
  11.3 2.7 %collective-permute-done.rest_0_.got_ref = bf16[4,128,128]{2,1,0:T(8,128)(2,1)S(1)} collective-permute-done((bf16[4,128,128]{2,1,0:T(8,128)(2,1)S(1)}, bf16[4,128,128]{2,1,0:T(8,128)(2,1)S(1)}, u32[]{:S(2)}, u32[]{:S(2)}) %collective-permute-start) | collective-permute-done | bytes 131104 | tf_op jit(solution)/shard_map/ppermute | solution.py:554
  14.0 0.7 copy-done.22
  14.7 0.6 decode_message.1.rest_0_
  15.3 4.6 %collective-permute-start.3 = (bf16[16,2048]{1,0:T(8,128)(2,1)S(1)}, bf16[16,2048]{1,0:T(8,128)(2,1)S(1)}, u32[]{:S(2)}, u32[]{:S(2)}) collective-permute-start(bf16[16,2048]{1,0:T(8,128)(2,1)S(1)} %decode_message.1.rest_0_), channel_id=1, source_target_pairs={{0,24},{8,16},{16,8},{24,0},{1,25},{9,17},{17,9},{25,1},{2,26},{10... | collective-permute-start | bytes 196616 | tf_op jit(solution)/shard_map/ppermute | solution.py:355
  19.9 0.6 collective-permute-start.1
  20.5 3.9 %collective-permute-start.5 = (bf16[4,128,128]{2,1,0:T(8,128)(2,1)}, bf16[4,128,128]{2,1,0:T(8,128)(2,1)}, u32[]{:S(2)}, u32[]{:S(2)}) collective-permute-start(bf16[4,128,128]{2,1,0:T(8,128)(2,1)} %get-tuple-element.37), channel_id=1, source_target_pairs={{0,8},{8,16},{16,24},{1,9},{9,17},{17,25},{2,10},{10,18},{18,26},{... | collective-permute-start | bytes 393224 | tf_op jit(solution)/shard_map/ppermute | solution.py:554
  24.4 0.8 collective-permute-done.2
  25.3 0.6 copy-done.7
  25.9 0.7 local_attention.4
  26.6 1.0 copy-done
  27.6 0.8 copy-done.9
  28.4 0.9 copy-done.5
  29.4 0.6 chain.7
  29.9 3.0 %collective-permute-start.8 = (bf16[4,128,128]{2,1,0:T(8,128)(2,1)S(1)}, bf16[4,128,128]{2,1,0:T(8,128)(2,1)S(1)}, u32[]{:S(2)}, u32[]{:S(2)}) collective-permute-start(bf16[4,128,128]{2,1,0:T(8,128)(2,1)S(1)} %chain.7), channel_id=1, source_target_pairs={{0,8},{8,16},{16,24},{1,9},{9,17},{17,25},{2,10},{10,18},{18,26},{... | collective-permute-start | bytes 393224 | tf_op jit(solution)/shard_map/ppermute | solution.py:554
  32.9 0.8 copy-done.8
  33.8 1.0 chain.6
  34.7 3.2 %collective-permute-start.6 = (bf16[4,128,128]{2,1,0:T(8,128)(2,1)S(1)}, bf16[4,128,128]{2,1,0:T(8,128)(2,1)S(1)}, u32[]{:S(2)}, u32[]{:S(2)}) collective-permute-start(bf16[4,128,128]{2,1,0:T(8,128)(2,1)S(1)} %chain.6), channel_id=1, source_target_pairs={{0,8},{8,16},{16,24},{1,9},{9,17},{17,25},{2,10},{10,18},{18,26},{... | collective-permute-start | bytes 393224 | tf_op jit(solution)/shard_map/ppermute | solution.py:554
  38.0 1.2 %copy-done.1 = bf16[256,2048]{1,0:T(8,128)(2,1)S(1)} copy-done((bf16[256,2048]{1,0:T(8,128)(2,1)S(1)}, bf16[256,2048]{1,0:T(8,128)(2,1)}, u32[]{:S(2)}) %copy-start.1) | copy-done | bytes 1048600
  39.2 0.7 copy-done.12
  39.9 0.7 local_attention.5
  40.6 0.6 chain.8
  41.2 3.4 %collective-permute-start.9 = (bf16[4,128,128]{2,1,0:T(8,128)(2,1)S(1)}, bf16[4,128,128]{2,1,0:T(8,128)(2,1)S(1)}, u32[]{:S(2)}, u32[]{:S(2)}) collective-permute-start(bf16[4,128,128]{2,1,0:T(8,128)(2,1)S(1)} %chain.8), channel_id=1, source_target_pairs={{0,8},{8,16},{16,24},{1,9},{9,17},{17,25},{2,10},{10,18},{18,26},{... | collective-permute-start | bytes 393224 | tf_op jit(solution)/shard_map/ppermute | solution.py:554
  44.6 1.2 %copy-done.2 = bf16[256,2048]{1,0:T(8,128)(2,1)S(1)} copy-done((bf16[256,2048]{1,0:T(8,128)(2,1)S(1)}, bf16[256,2048]{1,0:T(8,128)(2,1)}, u32[]{:S(2)}) %copy-start.2) | copy-done | bytes 1048600
  45.8 0.7 copy-done.13
  46.5 0.7 local_attention.6
  47.2 1.4 %decode_start.1 = (f32[32,2048]{1,0:T(8,128)S(1)}, bf16[32,2048]{1,0:T(8,128)(2,1)S(1)}) custom-call(s32[3]{0:T(128)S(1)} %pad_add_fusion.place_ref, bf16[64,2048]{1,0:T(8,128)(2,1)S(1)} %pad_maximum_fusion.near_ref.rest_0_, bf16[64,2048]{1,0:T(8,128)(2,1)} %collective-permute-done.4.far_ref, f32[16,128,128]{2,1,0:T(8,128)S(1)} %get-tuple-element.36.own_ref, ...), custom_call_target="tpu_custom_call" | custom-call | flops 134217728 | bytes 1048576 | tf_op jit(solution)/shard_map/decode_start/pallas_call | solution.py:459
  48.7 0.6 chain.9
  49.3 1.9 %collective-permute-start.13 = (bf16[4,128,128]{2,1,0:T(8,128)(2,1)S(1)}, bf16[4,128,128]{2,1,0:T(8,128)(2,1)S(1)}, u32[]{:S(2)}, u32[]{:S(2)}) collective-permute-start(bf16[4,128,128]{2,1,0:T(8,128)(2,1)S(1)} %chain.9), channel_id=1, source_target_pairs={{0,8},{8,16},{16,24},{1,9},{9,17},{17,25},{2,10},{10,18},{18,26},{... | collective-permute-start | bytes 393224 | tf_op jit(solution)/shard_map/ppermute | solution.py:554
  51.2 0.6 chain.10
  51.8 2.1 %collective-permute-start.14 = (bf16[4,128,128]{2,1,0:T(8,128)(2,1)S(1)}, bf16[4,128,128]{2,1,0:T(8,128)(2,1)S(1)}, u32[]{:S(2)}, u32[]{:S(2)}) collective-permute-start(bf16[4,128,128]{2,1,0:T(8,128)(2,1)S(1)} %chain.10), channel_id=1, source_target_pairs={{0,8},{8,16},{16,24},{1,9},{9,17},{17,25},{2,10},{10,18},{18,26},{... | collective-permute-start | bytes 393224 | tf_op jit(solution)/shard_map/ppermute | solution.py:554
  54.0 0.6 decode_select.1
  54.6 0.2 collective-permute-done.13.rest_2_.rest_0_.got_ref.rest_1_
  54.8 0.6 chain.11
  55.4 4.6 %collective-permute-start.15 = (bf16[4,128,128]{2,1,0:T(8,128)(2,1)S(1)}, bf16[4,128,128]{2,1,0:T(8,128)(2,1)S(1)}, u32[]{:S(2)}, u32[]{:S(2)}) collective-permute-start(bf16[4,128,128]{2,1,0:T(8,128)(2,1)S(1)} %chain.11), channel_id=1, source_target_pairs={{0,8},{8,16},{16,24},{1,9},{9,17},{17,25},{2,10},{10,18},{18,26},{... | collective-permute-start | bytes 393224 | tf_op jit(solution)/shard_map/ppermute | solution.py:554
  60.0 0.4 collective-permute-start.10
  60.4 4.1 %collective-permute-start.12 = (bf16[8,2048]{1,0:T(8,128)(2,1)S(1)}, bf16[8,2048]{1,0:T(8,128)(2,1)S(1)}, u32[]{:S(2)}, u32[]{:S(2)}) collective-permute-start(bf16[8,2048]{1,0:T(8,128)(2,1)S(1)} %get-tuple-element.50), channel_id=1, source_target_pairs={{0,24},{8,16},{16,8},{24,0},{1,25},{9,17},{17,9},{25,1},{2,26},{10... | collective-permute-start | bytes 98312 | tf_op jit(solution)/shard_map/ppermute | solution.py:355
  64.5 0.9 copy-done.6
  65.4 1.0 copy-done.10
  66.4 1.1 hidden.4.rest_0_
  67.5 1.5 %hidden.5.rest_1_ = bf16[256,512]{1,0:T(8,128)(2,1)S(1)} custom-call(s32[3]{0:T(128)S(1)} %pad_add_fusion.place_ref, bf16[1,256,2048]{2,1,0:T(8,128)(2,1)S(1)} %get-tuple-element.40.q_ref, f32[256,16]{1,0:T(8,128)S(1)} %get-tuple-element.43.col_ref, f32[256,512]{1,0:T(8,128)S(1)} %get-tuple-element.52.local_ref, ...), custom_call_target="tpu_custom_call" | custom-call | flops 33554432 | bytes 1048576 | tf_op jit(solution)/shard_map/hidden/pallas_call | solution.py:565
  69.0 1.2 %copy-done.3 = bf16[256,2048]{1,0:T(8,128)(2,1)S(1)} copy-done((bf16[256,2048]{1,0:T(8,128)(2,1)S(1)}, bf16[256,2048]{1,0:T(8,128)(2,1)}, u32[]{:S(2)}) %copy-start.3) | copy-done | bytes 1048600
  70.3 0.7 copy-done.14
  71.0 1.1 %local_attention.7 = (f32[256,512]{1,0:T(8,128)S(1)}, f32[8,128]{1,0:T(8,128)}) custom-call(bf16[1,256,2048]{2,1,0:T(8,128)(2,1)S(1)} %get-tuple-element.40.q_ref, bf16[256,2048]{1,0:T(8,128)(2,1)S(1)} %get-tuple-element.41.k_ref, bf16[256,2048]{1,0:T(8,128)(2,1)S(1)} %copy-done.3, f32[256,16]{1,0:T(8,128)S(1)} %get-tuple-element.43.col_ref, ...), custom_call_target="tpu_custom_call" | custom-call | flops 134217728 | bytes 786432 | tf_op jit(solution)/shard_map/local_attention/pallas_call | solution.py:449
  72.1 1.1 hidden.6.rest_2_
  73.3 0.8 decode_rows.1.decode_ref
  74.2 1.1 %hidden.7.rest_3_ = bf16[256,512]{1,0:T(8,128)(2,1)S(1)} custom-call(s32[3]{0:T(128)S(1)} %pad_add_fusion.place_ref, bf16[1,256,2048]{2,1,0:T(8,128)(2,1)S(1)} %get-tuple-element.40.q_ref, f32[256,16]{1,0:T(8,128)S(1)} %get-tuple-element.43.col_ref, f32[256,512]{1,0:T(8,128)S(1)} %get-tuple-element.55.local_ref, ...), custom_call_target="tpu_custom_call" | custom-call | flops 33554432 | bytes 1048576 | tf_op jit(solution)/shard_map/hidden/pallas_call | solution.py:565
  75.3 3.4 %project.9 = bf16[272,768]{1,0:T(8,128)(2,1)S(1)} custom-call(s32[3]{0:T(128)S(1)} %pad_add_fusion.place_ref, bf16[16,2048]{1,0:T(8,128)(2,1)S(1)} %decode_rows.1.decode_ref, bf16[256,512]{1,0:T(8,128)(2,1)S(1)} %hidden.4.rest_0_, bf16[256,512]{1,0:T(8,128)(2,1)S(1)} %hidden.5.rest_1_, bf16[256,512]{1,0:T(8,128)(2,1)S(1)} %hidden.6.rest_2_, ...), custom_call_target="tpu_custom_call" | custom-call | flops 855638016 | bytes 3145728 | tf_op jit(solution)/shard_map/project/pallas_call | solution.py:595
  78.7 1.6 %collective-permute-start.17 = (bf16[272,768]{1,0:T(8,128)(2,1)S(1)}, bf16[272,768]{1,0:T(8,128)(2,1)S(1)}, u32[]{:S(2)}, u32[]{:S(2)}) collective-permute-start(bf16[272,768]{1,0:T(8,128)(2,1)S(1)} %project.9), channel_id=1, source_target_pairs={{0,2},{2,0},{4,6},{6,4},{1,3},{3,1},{5,7},{7,5},{8,10},{10,8},{12,... | collective-permute-start | bytes 1253384 | tf_op jit(solution)/shard_map/ppermute | solution.py:355
  80.3 3.4 %project.10 = bf16[272,768]{1,0:T(8,128)(2,1)S(1)} custom-call(s32[3]{0:T(128)S(1)} %pad_add_fusion.place_ref, bf16[16,2048]{1,0:T(8,128)(2,1)S(1)} %decode_rows.1.decode_ref, bf16[256,512]{1,0:T(8,128)(2,1)S(1)} %hidden.4.rest_0_, bf16[256,512]{1,0:T(8,128)(2,1)S(1)} %hidden.5.rest_1_, bf16[256,512]{1,0:T(8,128)(2,1)S(1)} %hidden.6.rest_2_, ...), custom_call_target="tpu_custom_call" | custom-call | flops 855638016 | bytes 3145728 | tf_op jit(solution)/shard_map/project/pallas_call | solution.py:595
  83.7 1.6 %collective-permute-start.19 = (bf16[272,768]{1,0:T(8,128)(2,1)S(1)}, bf16[272,768]{1,0:T(8,128)(2,1)S(1)}, u32[]{:S(2)}, u32[]{:S(2)}) collective-permute-start(bf16[272,768]{1,0:T(8,128)(2,1)S(1)} %project.10), channel_id=1, source_target_pairs={{0,4},{2,6},{4,0},{6,2},{1,5},{3,7},{5,1},{7,3},{8,12},{10,14},{12... | collective-permute-start | bytes 1253384 | tf_op jit(solution)/shard_map/ppermute | solution.py:355
  85.3 3.4 %project.7 = bf16[272,768]{1,0:T(8,128)(2,1)S(1)} custom-call(s32[3]{0:T(128)S(1)} %pad_add_fusion.place_ref, bf16[16,2048]{1,0:T(8,128)(2,1)S(1)} %decode_rows.1.decode_ref, bf16[256,512]{1,0:T(8,128)(2,1)S(1)} %hidden.4.rest_0_, bf16[256,512]{1,0:T(8,128)(2,1)S(1)} %hidden.5.rest_1_, bf16[256,512]{1,0:T(8,128)(2,1)S(1)} %hidden.6.rest_2_, ...), custom_call_target="tpu_custom_call" | custom-call | flops 855638016 | bytes 3145728 | tf_op jit(solution)/shard_map/project/pallas_call | solution.py:595
  88.7 0.6 collective-permute-start.16
  89.3 3.4 %project.11 = bf16[272,768]{1,0:T(8,128)(2,1)S(1)} custom-call(s32[3]{0:T(128)S(1)} %pad_add_fusion.place_ref, bf16[16,2048]{1,0:T(8,128)(2,1)S(1)} %decode_rows.1.decode_ref, bf16[256,512]{1,0:T(8,128)(2,1)S(1)} %hidden.4.rest_0_, bf16[256,512]{1,0:T(8,128)(2,1)S(1)} %hidden.5.rest_1_, bf16[256,512]{1,0:T(8,128)(2,1)S(1)} %hidden.6.rest_2_, ...), custom_call_target="tpu_custom_call" | custom-call | flops 855638016 | bytes 3145728 | tf_op jit(solution)/shard_map/project/pallas_call | solution.py:595
  92.7 0.6 collective-permute-start.21
  93.3 6.1 %project.8 = (f32[272,768]{1,0:T(8,128)S(1)}, f32[272,768]{1,0:T(8,128)S(1)}) custom-call(s32[3]{0:T(128)S(1)} %pad_add_fusion.place_ref, bf16[16,2048]{1,0:T(8,128)(2,1)S(1)} %decode_rows.1.decode_ref, bf16[256,512]{1,0:T(8,128)(2,1)S(1)} %hidden.4.rest_0_, bf16[256,512]{1,0:T(8,128)(2,1)S(1)} %hidden.5.rest_1_, bf16[256,512]{1,0:T(8,128)(2,1)S(1)} %hidden.6.rest_2_, ...), custom_call_target="tpu_custom_call" | custom-call | flops 1711276032 | bytes 6291456 | tf_op jit(solution)/shard_map/project/pallas_call | solution.py:595
  99.4 0.1 relay.2
  99.5 1.6 %collective-permute-start.18 = (bf16[272,768]{1,0:T(8,128)(2,1)S(1)}, bf16[272,768]{1,0:T(8,128)(2,1)S(1)}, u32[]{:S(2)}, u32[]{:S(2)}) collective-permute-start(bf16[272,768]{1,0:T(8,128)(2,1)S(1)} %relay.2), channel_id=1, source_target_pairs={{0,4},{2,6},{4,0},{6,2},{1,5},{3,7},{5,1},{7,3},{8,12},{10,14},{12... | collective-permute-start | bytes 1253384 | tf_op jit(solution)/shard_map/ppermute | solution.py:355
  101.2 1.5 %collective-permute-start.20 = (bf16[272,768]{1,0:T(8,128)(2,1)S(1)}, bf16[272,768]{1,0:T(8,128)(2,1)S(1)}, u32[]{:S(2)}, u32[]{:S(2)}) collective-permute-start(bf16[272,768]{1,0:T(8,128)(2,1)S(1)} %relay.3), channel_id=1, source_target_pairs={{0,2},{2,0},{4,6},{6,4},{1,3},{3,1},{5,7},{7,5},{8,10},{10,8},{12,... | collective-permute-start | bytes 1253384 | tf_op jit(solution)/shard_map/ppermute | solution.py:355
  102.7 6.1 %project.6 = (f32[272,768]{1,0:T(8,128)S(1)}, f32[272,768]{1,0:T(8,128)S(1)}) custom-call(s32[3]{0:T(128)S(1)} %pad_add_fusion.place_ref, bf16[16,2048]{1,0:T(8,128)(2,1)S(1)} %decode_rows.1.decode_ref, bf16[256,512]{1,0:T(8,128)(2,1)S(1)} %hidden.4.rest_0_, bf16[256,512]{1,0:T(8,128)(2,1)S(1)} %hidden.5.rest_1_, bf16[256,512]{1,0:T(8,128)(2,1)S(1)} %hidden.6.rest_2_, ...), custom_call_target="tpu_custom_call" | custom-call | flops 1711276032 | bytes 6291456 | tf_op jit(solution)/shard_map/project/pallas_call | solution.py:595
  108.8 2.5 %collective-permute-done.18.ay = bf16[272,768]{1,0:T(8,128)(2,1)S(1)} collective-permute-done((bf16[272,768]{1,0:T(8,128)(2,1)S(1)}, bf16[272,768]{1,0:T(8,128)(2,1)S(1)}, u32[]{:S(2)}, u32[]{:S(2)}) %collective-permute-start.18) | collective-permute-done | bytes 417824 | tf_op jit(solution)/shard_map/ppermute | solution.py:355
  111.3 1.6 %finish.1 = (bf16[1,256,1536]{2,1,0:T(8,128)(2,1)}, bf16[4,2,1536]{2,1,0:T(2,128)(2,1)}) custom-call(f32[272,768]{1,0:T(8,128)S(1)} %get-tuple-element.56.own_a, f32[272,768]{1,0:T(8,128)S(1)} %get-tuple-element.57.own_b, bf16[272,768]{1,0:T(8,128)(2,1)S(1)} %collective-permute-done.16.ax, bf16[272,768]{1,0:T(8,128)(2,1)S(1)} %collective-permute-done.18.ay, ...), custom_call_target="tpu_custom_call" | custom-call | flops 1253376 | bytes 4177920 | tf_op jit(solution)/shard_map/finish/pallas_call | solution.py:626
  (56 shorter events, 0.3 us)
Async XLA Ops:
  0.6 72.6 %copy-start.21 = (f32[4,16,2]{1,2,0:T(2,128)S(1)}, f32[4,16,2]{1,2,0:T(2,128)}, u32[]{:S(2)}) copy-start(f32[4,16,2]{1,2,0:T(2,128)} %param.18) | copy-start | bytes 1540
  5.8 0.6 copy-start.17
  6.4 18.9 %copy-start.15 = (bf16[4,2,2048]{2,1,0:T(2,128)(2,1)}, bf16[4,2,2048]{2,1,0:T(2,128)(2,1)S(1)}, u32[]{:S(2)}) copy-start(bf16[4,2,2048]{2,1,0:T(2,128)(2,1)S(1)} %get-tuple-element.31.q_ref) | copy-start | bytes 98308
  6.4 18.9 %copy-start.19 = (bf16[4,2,2048]{2,1,0:T(2,128)(2,1)}, bf16[4,2,2048]{2,1,0:T(2,128)(2,1)S(1)}, u32[]{:S(2)}) copy-start(bf16[4,2,2048]{2,1,0:T(2,128)(2,1)S(1)} %get-tuple-element.33.v_ref) | copy-start | bytes 98308
  6.4 20.2 %copy-start.11 = (f32[16,256]{1,0:T(8,128)}, f32[16,256]{1,0:T(8,128)S(1)}, u32[]{:S(2)}) copy-start(f32[16,256]{1,0:T(8,128)S(1)} %get-tuple-element.44.row_ref) | copy-start | bytes 49156
  6.4 7.7 %collective-permute-start = (bf16[4,128,128]{2,1,0:T(8,128)(2,1)S(1)}, bf16[4,128,128]{2,1,0:T(8,128)(2,1)S(1)}, u32[]{:S(2)}, u32[]{:S(2)}) collective-permute-start(bf16[4,128,128]{2,1,0:T(8,128)(2,1)S(1)} %get-tuple-element.35), channel_id=1, source_target_pairs={{0,8},{8,16},{16,24},{1,9},{9,17},{17,25},{2,10},{10,18},{18,26},{... | collective-permute-start | bytes 393224 | tf_op jit(solution)/shard_map/ppermute | solution.py:554
  14.0 12.5 %copy-start.4 = (bf16[4,128,128]{2,1,0:T(8,128)(2,1)}, bf16[4,128,128]{2,1,0:T(8,128)(2,1)S(1)}, u32[]{:S(2)}) copy-start(bf16[4,128,128]{2,1,0:T(8,128)(2,1)S(1)} %collective-permute-done.rest_0_.got_ref) | copy-start | bytes 393220
  14.0 0.7 copy-start.22
  15.3 9.2 %collective-permute-start.3 = (bf16[16,2048]{1,0:T(8,128)(2,1)S(1)}, bf16[16,2048]{1,0:T(8,128)(2,1)S(1)}, u32[]{:S(2)}, u32[]{:S(2)}) collective-permute-start(bf16[16,2048]{1,0:T(8,128)(2,1)S(1)} %decode_message.1.rest_0_), channel_id=1, source_target_pairs={{0,24},{8,16},{16,8},{24,0},{1,25},{9,17},{17,9},{25,1},{2,26},{10... | collective-permute-start | bytes 196616 | tf_op jit(solution)/shard_map/ppermute | solution.py:355
  19.9 5.4 %collective-permute-start.2 = (bf16[16,2048]{1,0:T(8,128)(2,1)S(1)}, bf16[16,2048]{1,0:T(8,128)(2,1)S(1)}, u32[]{:S(2)}, u32[]{:S(2)}) collective-permute-start(bf16[16,2048]{1,0:T(8,128)(2,1)S(1)} %decode_message.1.rest_0_), channel_id=1, source_target_pairs={{0,16},{8,24},{16,0},{24,8},{1,17},{9,25},{17,1},{25,9},{2,18},{10... | collective-permute-start | bytes 196616 | tf_op jit(solution)/shard_map/ppermute | solution.py:355
  19.9 5.4 %collective-permute-start.1 = (bf16[16,2048]{1,0:T(8,128)(2,1)S(1)}, bf16[16,2048]{1,0:T(8,128)(2,1)S(1)}, u32[]{:S(2)}, u32[]{:S(2)}) collective-permute-start(bf16[16,2048]{1,0:T(8,128)(2,1)S(1)} %decode_message.1.rest_0_), channel_id=1, source_target_pairs={{0,8},{8,0},{16,24},{24,16},{1,9},{9,1},{17,25},{25,17},{2,10},{10... | collective-permute-start | bytes 196616 | tf_op jit(solution)/shard_map/ppermute | solution.py:355
  20.5 12.4 %collective-permute-start.5 = (bf16[4,128,128]{2,1,0:T(8,128)(2,1)}, bf16[4,128,128]{2,1,0:T(8,128)(2,1)}, u32[]{:S(2)}, u32[]{:S(2)}) collective-permute-start(bf16[4,128,128]{2,1,0:T(8,128)(2,1)} %get-tuple-element.37), channel_id=1, source_target_pairs={{0,8},{8,16},{16,24},{1,9},{9,17},{17,25},{2,10},{10,18},{18,26},{... | collective-permute-start | bytes 393224 | tf_op jit(solution)/shard_map/ppermute | solution.py:554
  25.3 0.6 copy-start.7
  25.9 21.3 %collective-permute-start.4 = (bf16[64,2048]{1,0:T(8,128)(2,1)S(1)}, bf16[64,2048]{1,0:T(8,128)(2,1)}, u32[]{:S(2)}, u32[]{:S(2)}) collective-permute-start(bf16[64,2048]{1,0:T(8,128)(2,1)S(1)} %pad_maximum_fusion.near_ref.rest_0_), channel_id=1, source_target_pairs={{0,1},{1,0},{2,3},{3,2},{4,5},{5,4},{6,7},{7,6},{8,9},{9,8},{10,11... | collective-permute-start | bytes 786440 | tf_op jit(solution)/shard_map/ppermute | solution.py:355
  26.6 1.0 copy-start
  27.6 0.8 copy-start.9
  28.4 0.9 copy-start.5
  29.4 43.9 %copy-start.16 = (bf16[4,2,2048]{2,1,0:T(2,128)(2,1)S(1)}, bf16[4,2,2048]{2,1,0:T(2,128)(2,1)}, u32[]{:S(2)}) copy-start(bf16[4,2,2048]{2,1,0:T(2,128)(2,1)} %copy-done.15) | copy-start | bytes 98308
  29.4 43.9 %copy-start.18 = (bf16[4,2,2048]{2,1,0:T(2,128)(2,1)S(1)}, bf16[4,2,2048]{2,1,0:T(2,128)(2,1)}, u32[]{:S(2)}) copy-start(bf16[4,2,2048]{2,1,0:T(2,128)(2,1)} %copy-done.17) | copy-start | bytes 98308
  29.4 44.0 %copy-start.20 = (bf16[4,2,2048]{2,1,0:T(2,128)(2,1)S(1)}, bf16[4,2,2048]{2,1,0:T(2,128)(2,1)}, u32[]{:S(2)}) copy-start(bf16[4,2,2048]{2,1,0:T(2,128)(2,1)} %copy-done.19) | copy-start | bytes 98308
  29.9 10.6 %collective-permute-start.8 = (bf16[4,128,128]{2,1,0:T(8,128)(2,1)S(1)}, bf16[4,128,128]{2,1,0:T(8,128)(2,1)S(1)}, u32[]{:S(2)}, u32[]{:S(2)}) collective-permute-start(bf16[4,128,128]{2,1,0:T(8,128)(2,1)S(1)} %chain.7), channel_id=1, source_target_pairs={{0,8},{8,16},{16,24},{1,9},{9,17},{17,25},{2,10},{10,18},{18,26},{... | collective-permute-start | bytes 393224 | tf_op jit(solution)/shard_map/ppermute | solution.py:554
  32.9 0.8 copy-start.8
  34.7 12.5 %collective-permute-start.6 = (bf16[4,128,128]{2,1,0:T(8,128)(2,1)S(1)}, bf16[4,128,128]{2,1,0:T(8,128)(2,1)S(1)}, u32[]{:S(2)}, u32[]{:S(2)}) collective-permute-start(bf16[4,128,128]{2,1,0:T(8,128)(2,1)S(1)} %chain.6), channel_id=1, source_target_pairs={{0,8},{8,16},{16,24},{1,9},{9,17},{17,25},{2,10},{10,18},{18,26},{... | collective-permute-start | bytes 393224 | tf_op jit(solution)/shard_map/ppermute | solution.py:554
  38.0 1.2 %copy-start.1 = (bf16[256,2048]{1,0:T(8,128)(2,1)S(1)}, bf16[256,2048]{1,0:T(8,128)(2,1)}, u32[]{:S(2)}) copy-start(bf16[256,2048]{1,0:T(8,128)(2,1)} %copy-done) | copy-start | bytes 3145732
  39.2 0.7 copy-start.12
  41.2 10.1 %collective-permute-start.9 = (bf16[4,128,128]{2,1,0:T(8,128)(2,1)S(1)}, bf16[4,128,128]{2,1,0:T(8,128)(2,1)S(1)}, u32[]{:S(2)}, u32[]{:S(2)}) collective-permute-start(bf16[4,128,128]{2,1,0:T(8,128)(2,1)S(1)} %chain.8), channel_id=1, source_target_pairs={{0,8},{8,16},{16,24},{1,9},{9,17},{17,25},{2,10},{10,18},{18,26},{... | collective-permute-start | bytes 393224 | tf_op jit(solution)/shard_map/ppermute | solution.py:554
  44.6 1.2 %copy-start.2 = (bf16[256,2048]{1,0:T(8,128)(2,1)S(1)}, bf16[256,2048]{1,0:T(8,128)(2,1)}, u32[]{:S(2)}) copy-start(bf16[256,2048]{1,0:T(8,128)(2,1)} %copy-done) | copy-start | bytes 3145732
  45.8 0.7 copy-start.13
  48.6 5.3 %collective-permute-start.7 = (bf16[32,2048]{1,0:T(8,128)(2,1)S(1)}, bf16[32,2048]{1,0:T(8,128)(2,1)S(1)}, u32[]{:S(2)}, u32[]{:S(2)}) collective-permute-start(bf16[32,2048]{1,0:T(8,128)(2,1)S(1)} %get-tuple-element.39), channel_id=1, source_target_pairs={{0,1},{1,0},{2,3},{3,2},{4,5},{5,4},{6,7},{7,6},{8,9},{9,8},{10,11... | collective-permute-start | bytes 393224 | tf_op jit(solution)/shard_map/ppermute | solution.py:355
  49.3 5.5 %collective-permute-start.13 = (bf16[4,128,128]{2,1,0:T(8,128)(2,1)S(1)}, bf16[4,128,128]{2,1,0:T(8,128)(2,1)S(1)}, u32[]{:S(2)}, u32[]{:S(2)}) collective-permute-start(bf16[4,128,128]{2,1,0:T(8,128)(2,1)S(1)} %chain.9), channel_id=1, source_target_pairs={{0,8},{8,16},{16,24},{1,9},{9,17},{17,25},{2,10},{10,18},{18,26},{... | collective-permute-start | bytes 393224 | tf_op jit(solution)/shard_map/ppermute | solution.py:554
  51.8 20.3 %collective-permute-start.14 = (bf16[4,128,128]{2,1,0:T(8,128)(2,1)S(1)}, bf16[4,128,128]{2,1,0:T(8,128)(2,1)S(1)}, u32[]{:S(2)}, u32[]{:S(2)}) collective-permute-start(bf16[4,128,128]{2,1,0:T(8,128)(2,1)S(1)} %chain.10), channel_id=1, source_target_pairs={{0,8},{8,16},{16,24},{1,9},{9,17},{17,25},{2,10},{10,18},{18,26},{... | collective-permute-start | bytes 393224 | tf_op jit(solution)/shard_map/ppermute | solution.py:554
  55.4 18.7 %collective-permute-start.15 = (bf16[4,128,128]{2,1,0:T(8,128)(2,1)S(1)}, bf16[4,128,128]{2,1,0:T(8,128)(2,1)S(1)}, u32[]{:S(2)}, u32[]{:S(2)}) collective-permute-start(bf16[4,128,128]{2,1,0:T(8,128)(2,1)S(1)} %chain.11), channel_id=1, source_target_pairs={{0,8},{8,16},{16,24},{1,9},{9,17},{17,25},{2,10},{10,18},{18,26},{... | collective-permute-start | bytes 393224 | tf_op jit(solution)/shard_map/ppermute | solution.py:554
  60.0 13.2 %collective-permute-start.10 = (bf16[8,2048]{1,0:T(8,128)(2,1)S(1)}, bf16[8,2048]{1,0:T(8,128)(2,1)S(1)}, u32[]{:S(2)}, u32[]{:S(2)}) collective-permute-start(bf16[8,2048]{1,0:T(8,128)(2,1)S(1)} %get-tuple-element.48), channel_id=1, source_target_pairs={{0,8},{8,0},{16,24},{24,16},{1,9},{9,1},{17,25},{25,17},{2,10},{10... | collective-permute-start | bytes 98312 | tf_op jit(solution)/shard_map/ppermute | solution.py:355
  60.4 12.9 %collective-permute-start.11 = (bf16[8,2048]{1,0:T(8,128)(2,1)S(1)}, bf16[8,2048]{1,0:T(8,128)(2,1)S(1)}, u32[]{:S(2)}, u32[]{:S(2)}) collective-permute-start(bf16[8,2048]{1,0:T(8,128)(2,1)S(1)} %get-tuple-element.49), channel_id=1, source_target_pairs={{0,16},{8,24},{16,0},{24,8},{1,17},{9,25},{17,1},{25,9},{2,18},{10... | collective-permute-start | bytes 98312 | tf_op jit(solution)/shard_map/ppermute | solution.py:355
  60.4 12.9 %collective-permute-start.12 = (bf16[8,2048]{1,0:T(8,128)(2,1)S(1)}, bf16[8,2048]{1,0:T(8,128)(2,1)S(1)}, u32[]{:S(2)}, u32[]{:S(2)}) collective-permute-start(bf16[8,2048]{1,0:T(8,128)(2,1)S(1)} %get-tuple-element.50), channel_id=1, source_target_pairs={{0,24},{8,16},{16,8},{24,0},{1,25},{9,17},{17,9},{25,1},{2,26},{10... | collective-permute-start | bytes 98312 | tf_op jit(solution)/shard_map/ppermute | solution.py:355
  64.5 0.9 copy-start.6
  65.4 1.0 copy-start.10
  69.0 1.2 %copy-start.3 = (bf16[256,2048]{1,0:T(8,128)(2,1)S(1)}, bf16[256,2048]{1,0:T(8,128)(2,1)}, u32[]{:S(2)}) copy-start(bf16[256,2048]{1,0:T(8,128)(2,1)} %copy-done) | copy-start | bytes 3145732
  70.3 0.7 copy-start.14
  78.7 20.7 %collective-permute-start.17 = (bf16[272,768]{1,0:T(8,128)(2,1)S(1)}, bf16[272,768]{1,0:T(8,128)(2,1)S(1)}, u32[]{:S(2)}, u32[]{:S(2)}) collective-permute-start(bf16[272,768]{1,0:T(8,128)(2,1)S(1)} %project.9), channel_id=1, source_target_pairs={{0,2},{2,0},{4,6},{6,4},{1,3},{3,1},{5,7},{7,5},{8,10},{10,8},{12,... | collective-permute-start | bytes 1253384 | tf_op jit(solution)/shard_map/ppermute | solution.py:355
  83.7 17.4 %collective-permute-start.19 = (bf16[272,768]{1,0:T(8,128)(2,1)S(1)}, bf16[272,768]{1,0:T(8,128)(2,1)S(1)}, u32[]{:S(2)}, u32[]{:S(2)}) collective-permute-start(bf16[272,768]{1,0:T(8,128)(2,1)S(1)} %project.10), channel_id=1, source_target_pairs={{0,4},{2,6},{4,0},{6,2},{1,5},{3,7},{5,1},{7,3},{8,12},{10,14},{12... | collective-permute-start | bytes 1253384 | tf_op jit(solution)/shard_map/ppermute | solution.py:355
  88.7 20.1 %collective-permute-start.16 = (bf16[272,768]{1,0:T(8,128)(2,1)S(1)}, bf16[272,768]{1,0:T(8,128)(2,1)S(1)}, u32[]{:S(2)}, u32[]{:S(2)}) collective-permute-start(bf16[272,768]{1,0:T(8,128)(2,1)S(1)} %project.7), channel_id=1, source_target_pairs={{0,2},{2,0},{4,6},{6,4},{1,3},{3,1},{5,7},{7,5},{8,10},{10,8},{12,... | collective-permute-start | bytes 1253384 | tf_op jit(solution)/shard_map/ppermute | solution.py:355
  92.7 16.1 %collective-permute-start.21 = (bf16[272,768]{1,0:T(8,128)(2,1)S(1)}, bf16[272,768]{1,0:T(8,128)(2,1)S(1)}, u32[]{:S(2)}, u32[]{:S(2)}) collective-permute-start(bf16[272,768]{1,0:T(8,128)(2,1)S(1)} %project.11), channel_id=1, source_target_pairs={{0,4},{2,6},{4,0},{6,2},{1,5},{3,7},{5,1},{7,3},{8,12},{10,14},{12... | collective-permute-start | bytes 1253384 | tf_op jit(solution)/shard_map/ppermute | solution.py:355
  99.5 11.8 %collective-permute-start.18 = (bf16[272,768]{1,0:T(8,128)(2,1)S(1)}, bf16[272,768]{1,0:T(8,128)(2,1)S(1)}, u32[]{:S(2)}, u32[]{:S(2)}) collective-permute-start(bf16[272,768]{1,0:T(8,128)(2,1)S(1)} %relay.2), channel_id=1, source_target_pairs={{0,4},{2,6},{4,0},{6,2},{1,5},{3,7},{5,1},{7,3},{8,12},{10,14},{12... | collective-permute-start | bytes 1253384 | tf_op jit(solution)/shard_map/ppermute | solution.py:355
  101.2 10.2 %collective-permute-start.20 = (bf16[272,768]{1,0:T(8,128)(2,1)S(1)}, bf16[272,768]{1,0:T(8,128)(2,1)S(1)}, u32[]{:S(2)}, u32[]{:S(2)}) collective-permute-start(bf16[272,768]{1,0:T(8,128)(2,1)S(1)} %relay.3), channel_id=1, source_target_pairs={{0,2},{2,0},{4,6},{6,4},{1,3},{3,1},{5,7},{7,5},{8,10},{10,8},{12,... | collective-permute-start | bytes 1253384 | tf_op jit(solution)/shard_map/ppermute | solution.py:355

commit v4 on v3

--- a/solution.py
+++ b/solution.py
@@ -13,8 +13,7 @@
 HIGH = lax.Precision.HIGHEST
 CHUNKS = 4
 LAG = 2
-VMEM_BYTES = 12 * 2**20
-PARTS_OF_COPY = 2
+VMEM_BYTES = 8 * 2**20
 F32 = jnp.float32
 BF16 = jnp.bfloat16
 NT = (((1,), (1,)), ((), ()))
@@ -86,20 +85,18 @@
     return jax.ShapeDtypeStruct(shape, dtype)
 
 
-def state_kernel(span, *refs):
+def state_kernel(span, place_ref, *refs):
     k_hbm, v_hbm, rate_hbm, q_hbm, dq_hbm, dk_hbm, dv_hbm = refs[:7]
     own_ref, first_ref, second_ref, log_ref, col_ref, row_ref = refs[7:13]
     k_ref, v_ref, q_ref, dq_ref, dk_ref, dv_ref = refs[13:19]
     rate_ref, sems, more = refs[19:]
     heads = own_ref.shape[0]
-    wide = span * HEAD_DIM
     rate_copy = pltpu.make_async_copy(rate_hbm, rate_ref, more.at[0])
     rate_copy.start()
-    copies = []
-    for c in range(heads // span):
-        at = pl.ds(c * wide, wide)
-        copies.append(pltpu.make_async_copy(k_hbm.at[0, :, at], k_ref.at[:, at], sems.at[0, c]))
-        copies.append(pltpu.make_async_copy(v_hbm.at[0, :, at], v_ref.at[:, at], sems.at[1, c]))
+    copies = [
+        pltpu.make_async_copy(k_hbm.at[0], k_ref, sems.at[0]),
+        pltpu.make_async_copy(v_hbm.at[0], v_ref, sems.at[1]),
+    ]
     others = [
         pltpu.make_async_copy(source, target, more.at[1 + i])
         for i, (source, target) in enumerate(
@@ -117,10 +114,9 @@
     row_ref[...] = decay_rows(rate, lower)
     total = columns[length - 1 :, :]
     factor = jnp.exp(total - columns)
+    for copy in copies:
+        copy.wait()
     for i in range(heads):
-        if i % span == 0:
-            copies[2 * (i // span)].wait()
-            copies[2 * (i // span) + 1].wait()
         at = head_slice(i)
         values = v_ref[:, at]
         weighted = k_ref[:, at].astype(F32) * factor[:, i : i + 1]
@@ -176,8 +172,9 @@
             state = jnp.where(group == g + 1, got[g][i], state)
         h = first + i
         at = head_slice(i)
-        inter = jnp.dot(q_ref[0, :, head_slice(h)], state, preferred_element_type=F32)
-        attended = local_ref[:, at] + inter * jnp.exp(col_ref[:, h : h + 1])
+        whole = head_slice(h)
+        inter = jnp.dot(q_ref[0, :, whole], state, preferred_element_type=F32)
+        attended = local_ref[:, whole] + inter * jnp.exp(col_ref[:, h : h + 1])
         hidden_ref[:, at] = normalize(attended).astype(BF16)
 
 
@@ -209,6 +206,13 @@
     out_ref[...] = rows_ref[...].astype(BF16)
 
 
+def join_kernel(first_ref, second_ref, *rest):
+    out_ref = rest[-1]
+    size = first_ref.shape[0]
+    out_ref[:size] = first_ref[...]
+    out_ref[size:] = second_ref[...]
+
+
 def start_kernel(groups, d_rows, place_ref, near_ref, far_ref, own_ref, *rest):
     near_out, far_out = rest[-2:]
     unit = near_ref.shape[0] // groups
@@ -236,23 +240,32 @@
 
 
 def select_kernel(groups, d_rows, place_ref, near_ref, mine_ref, other_ref, *rest):
-    outs = rest[-groups:]
+    keep_ref, send_ref = rest[-2:]
+    half = groups // 2
     unit = near_ref.shape[0] // groups
     rep = place_ref[1].astype(F32)
     wide = -(-d_rows // HEAD_DIM) * HEAD_DIM
     rows = lax.broadcasted_iota(jnp.int32, (d_rows, wide), 0)
     cols = lax.broadcasted_iota(jnp.int32, (d_rows, wide), 1)
     other = other_ref[...].astype(F32)
+    picked = []
     for j in range(groups):
         facts = near_ref[j * unit : (j + 1) * unit, :wide].astype(F32)[d_rows + 3 : d_rows + 4]
         prompt = jnp.sum(jnp.where(rows == cols, facts, 0.0), axis=1, keepdims=True)
         at = slice(j * d_rows, (j + 1) * d_rows)
-        picked = jnp.where(prompt == rep, mine_ref[at], other[at])
-        outs[j][...] = picked.astype(outs[j].dtype)
-
-
-def decode_kernel(groups, q_ref, k_ref, v_ref, rate_ref, base_ref, *rest):
-    got = rest[: groups - 1]
+        picked.append(jnp.where(prompt == rep, mine_ref[at], other[at]))
+    keep_ref[...] = jnp.concatenate(picked[:half], axis=0)
+    send_ref[...] = jnp.concatenate(picked[half:], axis=0).astype(BF16)
+
+
+def merge_kernel(kept_ref, got_ref, *rest):
+    keep_ref, send_ref = rest[-2:]
+    total = kept_ref[...] + got_ref[...].astype(F32)
+    keep_ref[...] = total[: keep_ref.shape[0]]
+    send_ref[...] = total[keep_ref.shape[0] :].astype(BF16)
+
+
+def decode_kernel(q_ref, k_ref, v_ref, rate_ref, base_ref, got_ref, *rest):
     out_ref, q_rows, k_rows, v_rows, rate_rows = rest[-5:]
     steps = q_ref.shape[1]
     d_rows = q_rows.shape[0]
@@ -277,9 +290,7 @@
         )
         decay = jnp.exp(jnp.where(seen, down[:, i : i + 1] - across[i : i + 1, :], NEGATIVE))
         intra = jnp.dot(scores * decay, v_rows[:, at], precision=HIGH, preferred_element_type=F32)
-        base = base_ref[:, at]
-        for ref in got:
-            base = base + ref[:, at].astype(F32)
+        base = base_ref[:, at] + got_ref[:, at].astype(F32)
         q_rows[:, at] = normalize(base * grow[:, i : i + 1] + intra)
     pad = out_ref.shape[0] - d_rows
     value = q_rows[...]
@@ -289,36 +300,21 @@
 
 
 def project_kernel(pieces, chunks, place_ref, decode_ref, *rest):
-    hidden, weight_hbm = rest[:chunks], rest[chunks]
-    outs = rest[chunks + 1 : chunks + 1 + len(pieces)]
-    weight_ref, sems = rest[-2:]
+    hidden, weight_ref, outs = rest[:chunks], rest[chunks], rest[chunks + 1 :]
     half = outs[0].shape[1]
     depth = hidden[0].shape[1]
-    part = depth // PARTS_OF_COPY
-    copies = []
-    for n, (bits, side) in enumerate(pieces):
+    rows = jnp.concatenate(
+        [
+            jnp.concatenate([ref[...], decode_ref[:, c * depth : (c + 1) * depth]], axis=0)
+            for c, ref in enumerate(hidden)
+        ],
+        axis=1,
+    )
+    for (bits, side), out_ref in zip(pieces, outs):
         column = pl.multiple_of(((place_ref[2] ^ bits) * 2 + side) * half, HEAD_DIM)
-        for k in range(chunks * PARTS_OF_COPY):
-            copy = pltpu.make_async_copy(
-                weight_hbm.at[pl.ds(k * part, part), pl.ds(column, half)],
-                weight_ref.at[n, pl.ds(k * part, part)],
-                sems.at[n, k],
-            )
-            copy.start()
-            copies.append(copy)
-    for n, out_ref in enumerate(outs):
-        total = None
-        for c in range(chunks):
-            rows = jnp.concatenate(
-                [hidden[c][...], decode_ref[:, c * depth : (c + 1) * depth]], axis=0
-            )
-            for k in range(c * PARTS_OF_COPY, (c + 1) * PARTS_OF_COPY):
-                copies[n * chunks * PARTS_OF_COPY + k].wait()
-            term = jnp.dot(
-                rows, weight_ref[n, c * depth : (c + 1) * depth], preferred_element_type=F32
-            )
-            total = term if total is None else total + term
-        out_ref[...] = total.astype(out_ref.dtype)
+        out_ref[...] = jnp.dot(
+            rows, weight_ref[:, pl.ds(column, half)], preferred_element_type=F32
+        ).astype(out_ref.dtype)
 
 
 def relay_kernel(own_ref, got_ref, out_ref):
@@ -396,7 +392,7 @@
     own, first, second, log_row, columns, rows, keys, values, queries, d_query, d_key, d_value = call(
         functools.partial(state_kernel, span),
         "own_state",
-        [HBM] * 7,
+        [SMEM] + [HBM] * 7,
         [
             pltpu.VMEM((heads, HEAD_DIM, HEAD_DIM), F32),
             sds(chunk_shape, BF16),
@@ -413,11 +409,12 @@
         ],
         [
             pltpu.VMEM((1, heads, length), F32),
-            pltpu.SemaphoreType.DMA((2, chunks)),
+            pltpu.SemaphoreType.DMA((2,)),
             pltpu.SemaphoreType.DMA((5,)),
         ],
         cost(4 * length * features * HEAD_DIM, 4 * length * features),
     )(
+        place,
         *[
             in_hbm(array)
             for array in (
@@ -445,15 +442,25 @@
             cost(unit * features, unit * features * 8),
         )(d_query, log_row, prompt_of_row, *after)
 
-    def local(chunk, *after):
-        return call(
-            functools.partial(local_kernel, chunk * span),
+    def local(*after):
+        return call(
+            functools.partial(local_kernel, 0),
             "local_attention",
             [VMEM] * 5 + [ANY] * len(after),
-            [pltpu.VMEM((length, wide), F32), sds((8, HEAD_DIM), F32)],
-            (),
-            cost(4 * length * length * wide, 6 * length * wide, span * length * length),
+            [pltpu.VMEM((length, features), F32), sds((8, HEAD_DIM), F32)],
+            (),
+            cost(4 * length * length * features, 6 * length * features, heads * length * length),
         )(queries, keys, values, columns, rows, *after)
+
+    def join(first, second, *after):
+        return call(
+            join_kernel,
+            "decode_join",
+            [VMEM, VMEM] + [ANY] * len(after),
+            sds((2 * first.shape[0], features), BF16),
+            (),
+            cost(first.size, first.size * 8),
+        )(first, second, *after)
 
     def start_terms(near, far, *after):
         return call(
@@ -470,17 +477,31 @@
             functools.partial(select_kernel, groups, d_rows),
             "decode_select",
             [SMEM, VMEM, VMEM, VMEM] + [ANY] * len(after),
-            [sds((d_rows, features), F32)] + [sds((d_rows, features), BF16)] * (groups - 1),
+            [
+                sds((groups // 2 * d_rows, features), F32),
+                sds((groups // 2 * d_rows, features), BF16),
+            ],
             (),
             cost(groups * d_rows * features, groups * d_rows * features * 8),
         )(place, near, mine, other, *after)
 
+    def merge_terms(kept, got, *after):
+        shape = (kept.shape[0] // 2, features)
+        return call(
+            merge_kernel,
+            "decode_merge",
+            [VMEM, VMEM] + [ANY] * len(after),
+            [sds(shape, F32), sds(shape, BF16)],
+            (),
+            cost(kept.size, kept.size * 10),
+        )(kept, got, *after)
+
     def decode_rows(base, got, *after):
         flat = pltpu.VMEM((d_rows, features), F32)
         return call(
-            functools.partial(decode_kernel, groups),
+            decode_kernel,
             "decode_rows",
-            [VMEM] * (5 + len(got)) + [ANY] * len(after),
+            [VMEM] * 6 + [ANY] * len(after),
             sds((d_pad, features), BF16),
             [flat, flat, flat, pltpu.VMEM((d_rows, heads), F32)],
             cost(4 * d_rows * features * d_rows, d_rows * features * 20),
@@ -490,30 +511,33 @@
             d_value,
             jnp.transpose(decode_rate, (0, 2, 1)),
             base,
-            *got,
+            got,
             *after,
         )
 
     right = [(i, i + 1) for i in range(groups - 1)]
     steps_all = chunks + LAG * (groups - 2)
-    received, locals_done, waits = [], [], {}
+    received, waits = [], {}
     decode = {}
+    attended_here, local_token = local()
+    attended_here = in_vmem(attended_here)
 
     def add_local(*after):
-        if len(locals_done) < chunks:
-            made, token = local(len(locals_done), *after)
-            locals_done.append(in_vmem(made))
-            return [token]
-        return []
+        return [local_token]
 
     def send_message(*after):
-        decode["message"] = message(*after)
-        decode["ctx"] = [swap(decode["message"], "ctx", groups, j) for j in range(1, groups)]
-        return [decode["message"]]
+        decode["near"] = message(*after)
+        decode["got"] = swap(decode["near"], "ctx", groups, 1)
+        decode["bit"] = 1
+        return [decode["near"]]
 
     def share_message(*after):
-        decode["near"] = jnp.concatenate([decode["message"]] + decode["ctx"], axis=0)
-        decode["far"] = swap(decode["near"], "rep", reps, 1)
+        decode["near"] = join(decode["near"], decode["got"], *after)
+        decode["bit"] *= 2
+        if decode["bit"] < groups:
+            decode["got"] = swap(decode["near"], "ctx", groups, decode["bit"])
+        else:
+            decode["far"] = swap(decode["near"], "rep", reps, 1)
         return [decode["near"]]
 
     def start_rows(*after):
@@ -522,20 +546,24 @@
         return [decode["mine"]]
 
     def select_rows(*after):
-        base, *terms = select_terms(decode["near"], decode["mine"], decode["other"], *after)
-        decode["got"] = [swap(term, "ctx", groups, j) for j, term in zip(range(1, groups), terms)]
-        decode["base"] = base
-        return [base]
-
-    plan = {
-        1: [add_local],
-        2: [send_message],
-        3: [add_local],
-        4: [share_message, add_local],
-        5: [start_rows],
-        6: [select_rows],
-        7: [add_local],
-    }
+        decode["base"], send = select_terms(
+            decode["near"], decode["mine"], decode["other"], *after
+        )
+        decode["bit"] = groups // 2
+        decode["got"] = swap(send, "ctx", groups, decode["bit"])
+        return [decode["base"]]
+
+    def merge_rows(*after):
+        decode["base"], send = merge_terms(decode["base"], decode["got"], *after)
+        decode["bit"] //= 2
+        decode["got"] = swap(send, "ctx", groups, decode["bit"])
+        return [decode["base"]]
+
+    levels = groups.bit_length() - 1
+    work = [send_message] + [share_message] * levels + [start_rows, select_rows]
+    work += [merge_rows] * (levels - 1)
+    plan = {step: [work[step - LAG]] for step in range(LAG, len(work) + LAG)}
+    plan[1] = [add_local]
     for step in range(steps_all):
         if step == 0:
             value = first
@@ -552,13 +580,11 @@
                 cost(2 * span * HEAD_DIM * HEAD_DIM, 8 * span * HEAD_DIM * HEAD_DIM),
             )(place, own, log_row, received[step - LAG], *after)
         received.append(lax.ppermute(value, "ctx", right))
-        ready = [received[step - LAG]] if step >= LAG else []
+        ready = [value, received[step - 1]] if step >= LAG else []
         waits[step] = [token for work in plan.pop(step, []) for token in work(*ready)]
     for step in sorted(plan):
         for work in plan[step]:
             work()
-    while len(locals_done) < chunks:
-        add_local()
     decode_hidden = decode_rows(decode["base"], decode["got"])
 
     hidden = [
@@ -573,7 +599,7 @@
             place,
             queries,
             columns,
-            locals_done[chunk],
+            attended_here,
             *[received[chunk + LAG * g] for g in range(groups - 1)],
         )
         for chunk in range(chunks)
@@ -589,18 +615,15 @@
         return prefill_out, decode_out.reshape(rows_here, steps, -1)
 
     half = out_columns // parts // 2
-    weight = in_hbm(out_weight)
+    weight = out_weight
 
     def project(pieces, dtype, *after):
         return call(
             functools.partial(project_kernel, pieces, chunks),
             "project",
-            [SMEM, VMEM] + [VMEM] * chunks + [HBM],
+            [SMEM, VMEM] + [VMEM] * chunks + [VMEM],
             [sds((total_rows, half), dtype) for _ in pieces],
-            [
-                pltpu.VMEM((len(pieces), features, half), BF16),
-                pltpu.SemaphoreType.DMA((len(pieces), chunks * PARTS_OF_COPY)),
-            ],
+            (),
             cost(2 * total_rows * features * half * len(pieces), features * half * 2 * len(pieces)),
         )(place, decode_hidden, *hidden, weight)
 

time: 114 us -> 98.8 us (0.87)
  Pallas kernels: 48 us -> 30.6 us
  waiting for transfers between devices: 6.26 us -> 22.9 us
  local copies, waits for them, and re-layouts: 13.2 us -> 0.66 us
  starting transfers between devices: 44.3 us -> 43.1 us
    ppermute x14 -> x12, waiting for transfers between devices: 3.31 us -> 22.7 us  [swap(): return lax.ppermute(array, axis, [(i, i ^ bit) for i in range(size)])]
    pallas_call x6, Pallas kernels: 25.8 us -> 11.4 us  [project(): call(functools.partial(project_kernel, pieces, chunks), 'project', [SMEM,...]
    unnamed x46 -> x6, local copies, waits for them, and re-layouts: 13.2 us -> 0.66 us
    ppermute x14 -> x12, starting transfers between devices: 17.2 us -> 14.1 us  [swap(): return lax.ppermute(array, axis, [(i, i ^ bit) for i in range(size)])]
    ppermute x8, waiting for transfers between devices: 2.95 us -> 0.21 us  [body(): received.append(lax.ppermute(value, 'ctx', right))]
    ppermute x8, starting transfers between devices: 27.1 us -> 29 us  [body(): received.append(lax.ppermute(value, 'ctx', right))]
    pallas_call x6, Pallas kernels: 9.08 us -> 7.14 us  [the longest x1 4.75 us: body(): call(functools.partial(state_kernel, span), 'own_state', [SMEM] + [HBM] *...]
  transfers between devices with their start and end apart: 22 -> 20, of which waited for: 4 -> 7; matrix products, arithmetic and copies ran while one was open for 0% -> 0% of each run, Pallas kernels for 32% -> 22%
where the time goes in v4:
time: 98.8 us; the launch traced here: 98.5 us
  starting transfers between devices  43.1 us (44%)
  Pallas kernels  30.6 us (31%)
  waiting for transfers between devices  22.9 us (23%)
  between operations  1.17 us (1%)
    ppermute x8, starting transfers between devices, body(): received.append(lax.ppermute(value, 'ctx', right))  29 us
    ppermute x12, waiting for transfers between devices, swap(): return lax.ppermute(array, axis, [(i, i ^ bit) for i in range(size)])  22.7 us
    ppermute x12, starting transfers between devices, swap(): return lax.ppermute(array, axis, [(i, i ^ bit) for i in range(size)])  14.1 us
    pallas_call x6, Pallas kernels, project(): call(functools.partial(project_kernel, pieces, chunks), 'project', [SMEM,...  11.4 us
    pallas_call x1, Pallas kernels, body(): call(functools.partial(state_kernel, span), 'own_state', [SMEM] + [HBM] *...  4.75 us
    pallas_call x4, Pallas kernels, body(): call(functools.partial(hidden_kernel, chunk * span), 'hidden', [SMEM] + [...  4.5 us
    pallas_call x6, Pallas kernels, body(): call(functools.partial(chain_kernel, step), 'chain', [SMEM, VMEM, VMEM, V...  3.51 us
  transfers between devices with their start and end apart: 20, of which 7 were waited for; matrix products, arithmetic and copies ran while one was open for 0% of the time, Pallas kernels for 22%

profile of v4, /device:TPU:0, one launch (start us, length us, event | category | flops | bytes accessed | tf_op | source)
XLA Modules:
  0.0 98.5 jit_solution(9178204121407040023)
XLA Ops:
  0.7 0.1 pad_add_fusion.place_ref
  0.7 4.8 %own_state.1 = (f32[16,128,128]{2,1,0:T(8,128)S(1)}, bf16[4,128,128]{2,1,0:T(8,128)(2,1)S(1)}, bf16[4,128,128]{2,1,0:T(8,128)(2,1)S(1)}, f32[1,2048]{1,0:T(1,128...) custom-call(s32[3]{0:T(128)S(1)} %pad_add_fusion.place_ref, ...), custom_call_target="tpu_custom_call" | custom-call | flops 268435456 | bytes 2097152 | tf_op jit(solution)/shard_map/own_state/pallas_call | solution.py:392
  5.5 5.2 %collective-permute-start = (bf16[4,128,128]{2,1,0:T(8,128)(2,1)S(1)}, bf16[4,128,128]{2,1,0:T(8,128)(2,1)S(1)}, u32[]{:S(2)}, u32[]{:S(2)}) collective-permute-start(bf16[4,128,128]{2,1,0:T(8,128)(2,1)S(1)} %get-tuple-element.31), channel_id=1, source_target_pairs={{0,8},{8,16},{16,24},{1,9},{9,17},{17,25},{2,10},{10,18},{18,26},{... | collective-permute-start | bytes 393224 | tf_op jit(solution)/shard_map/ppermute | solution.py:582
  10.7 3.6 %collective-permute-start.1 = (bf16[4,128,128]{2,1,0:T(8,128)(2,1)S(1)}, bf16[4,128,128]{2,1,0:T(8,128)(2,1)S(1)}, u32[]{:S(2)}, u32[]{:S(2)}) collective-permute-start(bf16[4,128,128]{2,1,0:T(8,128)(2,1)S(1)} %get-tuple-element.38), channel_id=1, source_target_pairs={{0,8},{8,16},{16,24},{1,9},{9,17},{17,25},{2,10},{10,18},{18,26},{... | collective-permute-start | bytes 393224 | tf_op jit(solution)/shard_map/ppermute | solution.py:582
  14.3 1.5 %local_attention.1 = (f32[256,2048]{1,0:T(8,128)S(1)}, f32[8,128]{1,0:T(8,128)S(1)}) custom-call(bf16[1,256,2048]{2,1,0:T(8,128)(2,1)S(1)} %get-tuple-element.32.q_ref, bf16[256,2048]{1,0:T(8,128)(2,1)S(1)} %get-tuple-element.33.k_ref, bf16[256,2048]{1,0:T(8,128)(2,1)S(1)} %get-tuple-element.34.v_ref, f32[256,16]{1,0:T(8,128)S(1)} %get-tuple-element.35.col_ref, ...), custom_call_target="tpu_custom_call" | custom-call | flops 536870912 | bytes 3145728 | tf_op jit(solution)/shard_map/local_attention/pallas_call | solution.py:446
  15.8 0.0 collective-permute-done.got_ref.rest_0_
  15.8 0.6 chain.6.rest_0_
  16.4 3.5 %collective-permute-start.3 = (bf16[4,128,128]{2,1,0:T(8,128)(2,1)S(1)}, bf16[4,128,128]{2,1,0:T(8,128)(2,1)S(1)}, u32[]{:S(2)}, u32[]{:S(2)}) collective-permute-start(bf16[4,128,128]{2,1,0:T(8,128)(2,1)S(1)} %chain.6.rest_0_), channel_id=1, source_target_pairs={{0,8},{8,16},{16,24},{1,9},{9,17},{17,25},{2,10},{10,18},{18,26},{... | collective-permute-start | bytes 393224 | tf_op jit(solution)/shard_map/ppermute | solution.py:582
  19.9 0.0 collective-permute-done.1.rest_1_.got_ref.rest_0_
  19.9 0.0 copy-start.2
  20.0 0.6 copy-done.2
  20.6 0.6 decode_message.1.rest_0_.first_ref
  21.2 0.3 collective-permute-start.2
  21.5 0.6 chain.7.rest_0_
  22.1 3.7 %collective-permute-start.5 = (bf16[4,128,128]{2,1,0:T(8,128)(2,1)S(1)}, bf16[4,128,128]{2,1,0:T(8,128)(2,1)S(1)}, u32[]{:S(2)}, u32[]{:S(2)}) collective-permute-start(bf16[4,128,128]{2,1,0:T(8,128)(2,1)S(1)} %chain.7.rest_0_), channel_id=1, source_target_pairs={{0,8},{8,16},{16,24},{1,9},{9,17},{17,25},{2,10},{10,18},{18,26},{... | collective-permute-start | bytes 393224 | tf_op jit(solution)/shard_map/ppermute | solution.py:582
  25.8 0.0 collective-permute-done.2.second_ref
  25.8 0.0 collective-permute-done.3.rest_1_.got_ref.rest_0_
  25.8 2.2 %collective-permute-start.4 = (bf16[32,2048]{1,0:T(8,128)(2,1)S(1)}, bf16[32,2048]{1,0:T(8,128)(2,1)S(1)}, u32[]{:S(2)}, u32[]{:S(2)}) collective-permute-start(bf16[32,2048]{1,0:T(8,128)(2,1)S(1)} %decode_join.2.rest_0_.first_ref), channel_id=1, source_target_pairs={{0,16},{8,24},{16,0},{24,8},{1,17},{9,25},{17,1},{25,9},{2,18},{10... | collective-permute-start | bytes 393224 | tf_op jit(solution)/shard_map/ppermute | solution.py:351
  28.0 0.6 chain.8.rest_0_
  28.6 0.2 collective-permute-done.5.rest_1_.got_ref.rest_0_
  28.8 4.4 %collective-permute-done.4.second_ref = bf16[32,2048]{1,0:T(8,128)(2,1)S(1)} collective-permute-done((bf16[32,2048]{1,0:T(8,128)(2,1)S(1)}, bf16[32,2048]{1,0:T(8,128)(2,1)S(1)}, u32[]{:S(2)}, u32[]{:S(2)}) %collective-permute-start.4) | collective-permute-done | bytes 131104 | tf_op jit(solution)/shard_map/ppermute | solution.py:351
  33.2 0.1 collective-permute-start.6
  33.3 2.1 %collective-permute-start.7 = (bf16[4,128,128]{2,1,0:T(8,128)(2,1)S(1)}, bf16[4,128,128]{2,1,0:T(8,128)(2,1)S(1)}, u32[]{:S(2)}, u32[]{:S(2)}) collective-permute-start(bf16[4,128,128]{2,1,0:T(8,128)(2,1)S(1)} %chain.8.rest_0_), channel_id=1, source_target_pairs={{0,8},{8,16},{16,24},{1,9},{9,17},{17,25},{2,10},{10,18},{18,26},{... | collective-permute-start | bytes 393224 | tf_op jit(solution)/shard_map/ppermute | solution.py:582
  35.3 0.6 chain.9.rest_0_
  35.9 3.1 %collective-permute-start.9 = (bf16[4,128,128]{2,1,0:T(8,128)(2,1)S(1)}, bf16[4,128,128]{2,1,0:T(8,128)(2,1)S(1)}, u32[]{:S(2)}, u32[]{:S(2)}) collective-permute-start(bf16[4,128,128]{2,1,0:T(8,128)(2,1)S(1)} %chain.9.rest_0_), channel_id=1, source_target_pairs={{0,8},{8,16},{16,24},{1,9},{9,17},{17,25},{2,10},{10,18},{18,26},{... | collective-permute-start | bytes 393224 | tf_op jit(solution)/shard_map/ppermute | solution.py:582
  39.1 0.0 collective-permute-done.7.rest_1_.got_ref.rest_2_
  39.1 0.0 collective-permute-done.6.far_ref
  39.1 1.0 decode_start.1
  40.1 0.1 collective-permute-start.8
  40.2 0.6 chain.10.rest_0_
  40.8 4.6 %collective-permute-start.11 = (bf16[4,128,128]{2,1,0:T(8,128)(2,1)S(1)}, bf16[4,128,128]{2,1,0:T(8,128)(2,1)S(1)}, u32[]{:S(2)}, u32[]{:S(2)}) collective-permute-start(bf16[4,128,128]{2,1,0:T(8,128)(2,1)S(1)} %chain.10.rest_0_), channel_id=1, source_target_pairs={{0,8},{8,16},{16,24},{1,9},{9,17},{17,25},{2,10},{10,18},{18,26},{... | collective-permute-start | bytes 393224 | tf_op jit(solution)/shard_map/ppermute | solution.py:582
  45.4 0.0 collective-permute-done.9.rest_1_.got_ref.rest_2_
  45.4 0.6 decode_select.1
  46.1 0.6 chain.11.rest_0_
  46.7 3.2 %collective-permute-start.13 = (bf16[4,128,128]{2,1,0:T(8,128)(2,1)S(1)}, bf16[4,128,128]{2,1,0:T(8,128)(2,1)S(1)}, u32[]{:S(2)}, u32[]{:S(2)}) collective-permute-start(bf16[4,128,128]{2,1,0:T(8,128)(2,1)S(1)} %chain.11.rest_0_), channel_id=1, source_target_pairs={{0,8},{8,16},{16,24},{1,9},{9,17},{17,25},{2,10},{10,18},{18,26},{... | collective-permute-start | bytes 393224 | tf_op jit(solution)/shard_map/ppermute | solution.py:582
  49.8 2.0 %collective-permute-start.10 = (bf16[16,2048]{1,0:T(8,128)(2,1)S(1)}, bf16[16,2048]{1,0:T(8,128)(2,1)S(1)}, u32[]{:S(2)}, u32[]{:S(2)}) collective-permute-start(bf16[16,2048]{1,0:T(8,128)(2,1)S(1)} %get-tuple-element.42), channel_id=1, source_target_pairs={{0,16},{8,24},{16,0},{24,8},{1,17},{9,25},{17,1},{25,9},{2,18},{10... | collective-permute-start | bytes 196616 | tf_op jit(solution)/shard_map/ppermute | solution.py:351
  51.8 0.0 collective-permute-done.11.rest_1_.rest_2_
  51.8 3.2 %collective-permute-done.10.got_ref = bf16[16,2048]{1,0:T(8,128)(2,1)S(1)} collective-permute-done((bf16[16,2048]{1,0:T(8,128)(2,1)S(1)}, bf16[16,2048]{1,0:T(8,128)(2,1)S(1)}, u32[]{:S(2)}, u32[]{:S(2)}) %collective-permute-start.10) | collective-permute-done | bytes 65568 | tf_op jit(solution)/shard_map/ppermute | solution.py:351
  55.1 3.1 %collective-permute-start.12 = (bf16[8,2048]{1,0:T(8,128)(2,1)S(1)}, bf16[8,2048]{1,0:T(8,128)(2,1)S(1)}, u32[]{:S(2)}, u32[]{:S(2)}) collective-permute-start(bf16[8,2048]{1,0:T(8,128)(2,1)S(1)} %get-tuple-element.44), channel_id=1, source_target_pairs={{0,8},{8,0},{16,24},{24,16},{1,9},{9,1},{17,25},{25,17},{2,10},{10... | collective-permute-start | bytes 98312 | tf_op jit(solution)/shard_map/ppermute | solution.py:351
  58.1 1.1 %hidden.4.rest_0_ = bf16[256,512]{1,0:T(8,128)(2,1)S(1)} custom-call(s32[3]{0:T(128)S(1)} %pad_add_fusion.place_ref, bf16[1,256,2048]{2,1,0:T(8,128)(2,1)S(1)} %get-tuple-element.32.q_ref, f32[256,16]{1,0:T(8,128)S(1)} %get-tuple-element.35.col_ref, f32[256,2048]{1,0:T(8,128)S(1)} %get-tuple-element.45.local_ref, ...), custom_call_target="tpu_custom_call" | custom-call | flops 33554432 | bytes 1048576 | tf_op jit(solution)/shard_map/hidden/pallas_call | solution.py:591
  59.3 1.1 %hidden.5.rest_1_ = bf16[256,512]{1,0:T(8,128)(2,1)S(1)} custom-call(s32[3]{0:T(128)S(1)} %pad_add_fusion.place_ref, bf16[1,256,2048]{2,1,0:T(8,128)(2,1)S(1)} %get-tuple-element.32.q_ref, f32[256,16]{1,0:T(8,128)S(1)} %get-tuple-element.35.col_ref, f32[256,2048]{1,0:T(8,128)S(1)} %get-tuple-element.45.local_ref, ...), custom_call_target="tpu_custom_call" | custom-call | flops 33554432 | bytes 1048576 | tf_op jit(solution)/shard_map/hidden/pallas_call | solution.py:591
  60.4 1.1 %hidden.6.rest_2_ = bf16[256,512]{1,0:T(8,128)(2,1)S(1)} custom-call(s32[3]{0:T(128)S(1)} %pad_add_fusion.place_ref, bf16[1,256,2048]{2,1,0:T(8,128)(2,1)S(1)} %get-tuple-element.32.q_ref, f32[256,16]{1,0:T(8,128)S(1)} %get-tuple-element.35.col_ref, f32[256,2048]{1,0:T(8,128)S(1)} %get-tuple-element.45.local_ref, ...), custom_call_target="tpu_custom_call" | custom-call | flops 33554432 | bytes 1048576 | tf_op jit(solution)/shard_map/hidden/pallas_call | solution.py:591
  61.5 0.8 decode_rows.1.decode_ref
  62.4 1.1 %hidden.7.rest_3_ = bf16[256,512]{1,0:T(8,128)(2,1)S(1)} custom-call(s32[3]{0:T(128)S(1)} %pad_add_fusion.place_ref, bf16[1,256,2048]{2,1,0:T(8,128)(2,1)S(1)} %get-tuple-element.32.q_ref, f32[256,16]{1,0:T(8,128)S(1)} %get-tuple-element.35.col_ref, f32[256,2048]{1,0:T(8,128)S(1)} %get-tuple-element.45.local_ref, ...), custom_call_target="tpu_custom_call" | custom-call | flops 33554432 | bytes 1048576 | tf_op jit(solution)/shard_map/hidden/pallas_call | solution.py:591
  63.5 1.6 %project.10 = bf16[272,768]{1,0:T(8,128)(2,1)S(1)} custom-call(s32[3]{0:T(128)S(1)} %pad_add_fusion.place_ref, bf16[16,2048]{1,0:T(8,128)(2,1)S(1)} %decode_rows.1.decode_ref, bf16[256,512]{1,0:T(8,128)(2,1)S(1)} %hidden.4.rest_0_, bf16[256,512]{1,0:T(8,128)(2,1)S(1)} %hidden.5.rest_1_, bf16[256,512]{1,0:T(8,128)(2,1)S(1)} %hidden.6.rest_2_, ...), custom_call_target="tpu_custom_call" | custom-call | flops 855638016 | bytes 3145728 | tf_op jit(solution)/shard_map/project/pallas_call | solution.py:621
  65.1 1.6 %collective-permute-start.17 = (bf16[272,768]{1,0:T(8,128)(2,1)S(1)}, bf16[272,768]{1,0:T(8,128)(2,1)S(1)}, u32[]{:S(2)}, u32[]{:S(2)}) collective-permute-start(bf16[272,768]{1,0:T(8,128)(2,1)S(1)} %project.10), channel_id=1, source_target_pairs={{0,4},{2,6},{4,0},{6,2},{1,5},{3,7},{5,1},{7,3},{8,12},{10,14},{12... | collective-permute-start | bytes 1253384 | tf_op jit(solution)/shard_map/ppermute | solution.py:351
  66.7 1.6 %project.9 = bf16[272,768]{1,0:T(8,128)(2,1)S(1)} custom-call(s32[3]{0:T(128)S(1)} %pad_add_fusion.place_ref, bf16[16,2048]{1,0:T(8,128)(2,1)S(1)} %decode_rows.1.decode_ref, bf16[256,512]{1,0:T(8,128)(2,1)S(1)} %hidden.4.rest_0_, bf16[256,512]{1,0:T(8,128)(2,1)S(1)} %hidden.5.rest_1_, bf16[256,512]{1,0:T(8,128)(2,1)S(1)} %hidden.6.rest_2_, ...), custom_call_target="tpu_custom_call" | custom-call | flops 855638016 | bytes 3145728 | tf_op jit(solution)/shard_map/project/pallas_call | solution.py:621
  68.4 1.6 %collective-permute-start.15 = (bf16[272,768]{1,0:T(8,128)(2,1)S(1)}, bf16[272,768]{1,0:T(8,128)(2,1)S(1)}, u32[]{:S(2)}, u32[]{:S(2)}) collective-permute-start(bf16[272,768]{1,0:T(8,128)(2,1)S(1)} %project.9), channel_id=1, source_target_pairs={{0,2},{2,0},{4,6},{6,4},{1,3},{3,1},{5,7},{7,5},{8,10},{10,8},{12,... | collective-permute-start | bytes 1253384 | tf_op jit(solution)/shard_map/ppermute | solution.py:351
  69.9 1.6 %project.7 = bf16[272,768]{1,0:T(8,128)(2,1)S(1)} custom-call(s32[3]{0:T(128)S(1)} %pad_add_fusion.place_ref, bf16[16,2048]{1,0:T(8,128)(2,1)S(1)} %decode_rows.1.decode_ref, bf16[256,512]{1,0:T(8,128)(2,1)S(1)} %hidden.4.rest_0_, bf16[256,512]{1,0:T(8,128)(2,1)S(1)} %hidden.5.rest_1_, bf16[256,512]{1,0:T(8,128)(2,1)S(1)} %hidden.6.rest_2_, ...), custom_call_target="tpu_custom_call" | custom-call | flops 855638016 | bytes 3145728 | tf_op jit(solution)/shard_map/project/pallas_call | solution.py:621
  71.6 0.6 collective-permute-start.14
  72.2 1.6 %project.11 = bf16[272,768]{1,0:T(8,128)(2,1)S(1)} custom-call(s32[3]{0:T(128)S(1)} %pad_add_fusion.place_ref, bf16[16,2048]{1,0:T(8,128)(2,1)S(1)} %decode_rows.1.decode_ref, bf16[256,512]{1,0:T(8,128)(2,1)S(1)} %hidden.4.rest_0_, bf16[256,512]{1,0:T(8,128)(2,1)S(1)} %hidden.5.rest_1_, bf16[256,512]{1,0:T(8,128)(2,1)S(1)} %hidden.6.rest_2_, ...), custom_call_target="tpu_custom_call" | custom-call | flops 855638016 | bytes 3145728 | tf_op jit(solution)/shard_map/project/pallas_call | solution.py:621
  73.8 0.6 collective-permute-start.19
  74.4 2.5 %project.8 = (f32[272,768]{1,0:T(8,128)S(1)}, f32[272,768]{1,0:T(8,128)S(1)}) custom-call(s32[3]{0:T(128)S(1)} %pad_add_fusion.place_ref, bf16[16,2048]{1,0:T(8,128)(2,1)S(1)} %decode_rows.1.decode_ref, bf16[256,512]{1,0:T(8,128)(2,1)S(1)} %hidden.4.rest_0_, bf16[256,512]{1,0:T(8,128)(2,1)S(1)} %hidden.5.rest_1_, bf16[256,512]{1,0:T(8,128)(2,1)S(1)} %hidden.6.rest_2_, ...), custom_call_target="tpu_custom_call" | custom-call | flops 1711276032 | bytes 6291456 | tf_op jit(solution)/shard_map/project/pallas_call | solution.py:621
  76.8 0.2 collective-permute-done.17.got_ref
  77.0 0.1 relay.3
  77.1 1.5 %collective-permute-start.18 = (bf16[272,768]{1,0:T(8,128)(2,1)S(1)}, bf16[272,768]{1,0:T(8,128)(2,1)S(1)}, u32[]{:S(2)}, u32[]{:S(2)}) collective-permute-start(bf16[272,768]{1,0:T(8,128)(2,1)S(1)} %relay.3), channel_id=1, source_target_pairs={{0,2},{2,0},{4,6},{6,4},{1,3},{3,1},{5,7},{7,5},{8,10},{10,8},{12,... | collective-permute-start | bytes 1253384 | tf_op jit(solution)/shard_map/ppermute | solution.py:351
  78.6 2.4 %collective-permute-done.15.got_ref = bf16[272,768]{1,0:T(8,128)(2,1)S(1)} collective-permute-done((bf16[272,768]{1,0:T(8,128)(2,1)S(1)}, bf16[272,768]{1,0:T(8,128)(2,1)S(1)}, u32[]{:S(2)}, u32[]{:S(2)}) %collective-permute-start.15) | collective-permute-done | bytes 417824 | tf_op jit(solution)/shard_map/ppermute | solution.py:351
  81.0 0.1 relay.2
  81.1 0.6 collective-permute-start.16
  81.7 2.5 %project.6 = (f32[272,768]{1,0:T(8,128)S(1)}, f32[272,768]{1,0:T(8,128)S(1)}) custom-call(s32[3]{0:T(128)S(1)} %pad_add_fusion.place_ref, bf16[16,2048]{1,0:T(8,128)(2,1)S(1)} %decode_rows.1.decode_ref, bf16[256,512]{1,0:T(8,128)(2,1)S(1)} %hidden.4.rest_0_, bf16[256,512]{1,0:T(8,128)(2,1)S(1)} %hidden.5.rest_1_, bf16[256,512]{1,0:T(8,128)(2,1)S(1)} %hidden.6.rest_2_, ...), custom_call_target="tpu_custom_call" | custom-call | flops 1711276032 | bytes 6291456 | tf_op jit(solution)/shard_map/project/pallas_call | solution.py:621
  84.2 5.8 %collective-permute-done.14.ax = bf16[272,768]{1,0:T(8,128)(2,1)S(1)} collective-permute-done((bf16[272,768]{1,0:T(8,128)(2,1)S(1)}, bf16[272,768]{1,0:T(8,128)(2,1)S(1)}, u32[]{:S(2)}, u32[]{:S(2)}) %collective-permute-start.14) | collective-permute-done | bytes 417824 | tf_op jit(solution)/shard_map/ppermute | solution.py:351
  90.0 6.7 %collective-permute-done.18.bx = bf16[272,768]{1,0:T(8,128)(2,1)S(1)} collective-permute-done((bf16[272,768]{1,0:T(8,128)(2,1)S(1)}, bf16[272,768]{1,0:T(8,128)(2,1)S(1)}, u32[]{:S(2)}, u32[]{:S(2)}) %collective-permute-start.18) | collective-permute-done | bytes 417824 | tf_op jit(solution)/shard_map/ppermute | solution.py:351
  96.7 0.0 collective-permute-done.16.ay
  96.7 1.6 %finish.1 = (bf16[1,256,1536]{2,1,0:T(8,128)(2,1)}, bf16[4,2,1536]{2,1,0:T(2,128)(2,1)}) custom-call(f32[272,768]{1,0:T(8,128)S(1)} %get-tuple-element.46.own_a, f32[272,768]{1,0:T(8,128)S(1)} %get-tuple-element.47.own_b, bf16[272,768]{1,0:T(8,128)(2,1)S(1)} %collective-permute-done.14.ax, bf16[272,768]{1,0:T(8,128)(2,1)S(1)} %collective-permute-done.16.ay, ...), custom_call_target="tpu_custom_call" | custom-call | flops 1253376 | bytes 4177920 | tf_op jit(solution)/shard_map/finish/pallas_call | solution.py:649
  (11 shorter events, 0.1 us)
Async XLA Ops:
  0.6 60.9 %copy-start.1 = (f32[4,16,2]{1,2,0:T(2,128)S(1)}, f32[4,16,2]{1,2,0:T(2,128)}, u32[]{:S(2)}) copy-start(f32[4,16,2]{1,2,0:T(2,128)} %param.18) | copy-start | bytes 1540
  0.6 62.9 %copy-start = (bf16[2048,6144]{1,0:T(8,128)(2,1)S(1)}, bf16[2048,6144]{1,0:T(8,128)(2,1)}, u32[]{:S(2)}) copy-start(bf16[2048,6144]{1,0:T(8,128)(2,1)} %rest_4_.11) | copy-start | bytes 75497472
  5.5 10.3 %collective-permute-start = (bf16[4,128,128]{2,1,0:T(8,128)(2,1)S(1)}, bf16[4,128,128]{2,1,0:T(8,128)(2,1)S(1)}, u32[]{:S(2)}, u32[]{:S(2)}) collective-permute-start(bf16[4,128,128]{2,1,0:T(8,128)(2,1)S(1)} %get-tuple-element.31), channel_id=1, source_target_pairs={{0,8},{8,16},{16,24},{1,9},{9,17},{17,25},{2,10},{10,18},{18,26},{... | collective-permute-start | bytes 393224 | tf_op jit(solution)/shard_map/ppermute | solution.py:582
  10.7 9.2 %collective-permute-start.1 = (bf16[4,128,128]{2,1,0:T(8,128)(2,1)S(1)}, bf16[4,128,128]{2,1,0:T(8,128)(2,1)S(1)}, u32[]{:S(2)}, u32[]{:S(2)}) collective-permute-start(bf16[4,128,128]{2,1,0:T(8,128)(2,1)S(1)} %get-tuple-element.38), channel_id=1, source_target_pairs={{0,8},{8,16},{16,24},{1,9},{9,17},{17,25},{2,10},{10,18},{18,26},{... | collective-permute-start | bytes 393224 | tf_op jit(solution)/shard_map/ppermute | solution.py:582
  16.4 9.4 %collective-permute-start.3 = (bf16[4,128,128]{2,1,0:T(8,128)(2,1)S(1)}, bf16[4,128,128]{2,1,0:T(8,128)(2,1)S(1)}, u32[]{:S(2)}, u32[]{:S(2)}) collective-permute-start(bf16[4,128,128]{2,1,0:T(8,128)(2,1)S(1)} %chain.6.rest_0_), channel_id=1, source_target_pairs={{0,8},{8,16},{16,24},{1,9},{9,17},{17,25},{2,10},{10,18},{18,26},{... | collective-permute-start | bytes 393224 | tf_op jit(solution)/shard_map/ppermute | solution.py:582
  19.9 0.7 copy-start.2
  21.2 4.6 %collective-permute-start.2 = (bf16[16,2048]{1,0:T(8,128)(2,1)S(1)}, bf16[16,2048]{1,0:T(8,128)(2,1)S(1)}, u32[]{:S(2)}, u32[]{:S(2)}) collective-permute-start(bf16[16,2048]{1,0:T(8,128)(2,1)S(1)} %decode_message.1.rest_0_.first_ref), channel_id=1, source_target_pairs={{0,8},{8,0},{16,24},{24,16},{1,9},{9,1},{17,25},{25,17},{2,10},{10... | collective-permute-start | bytes 196616 | tf_op jit(solution)/shard_map/ppermute | solution.py:351
  22.1 6.8 %collective-permute-start.5 = (bf16[4,128,128]{2,1,0:T(8,128)(2,1)S(1)}, bf16[4,128,128]{2,1,0:T(8,128)(2,1)S(1)}, u32[]{:S(2)}, u32[]{:S(2)}) collective-permute-start(bf16[4,128,128]{2,1,0:T(8,128)(2,1)S(1)} %chain.7.rest_0_), channel_id=1, source_target_pairs={{0,8},{8,16},{16,24},{1,9},{9,17},{17,25},{2,10},{10,18},{18,26},{... | collective-permute-start | bytes 393224 | tf_op jit(solution)/shard_map/ppermute | solution.py:582
  25.8 7.3 %collective-permute-start.4 = (bf16[32,2048]{1,0:T(8,128)(2,1)S(1)}, bf16[32,2048]{1,0:T(8,128)(2,1)S(1)}, u32[]{:S(2)}, u32[]{:S(2)}) collective-permute-start(bf16[32,2048]{1,0:T(8,128)(2,1)S(1)} %decode_join.2.rest_0_.first_ref), channel_id=1, source_target_pairs={{0,16},{8,24},{16,0},{24,8},{1,17},{9,25},{17,1},{25,9},{2,18},{10... | collective-permute-start | bytes 393224 | tf_op jit(solution)/shard_map/ppermute | solution.py:351
  33.2 5.9 %collective-permute-start.6 = (bf16[64,2048]{1,0:T(8,128)(2,1)S(1)}, bf16[64,2048]{1,0:T(8,128)(2,1)S(1)}, u32[]{:S(2)}, u32[]{:S(2)}) collective-permute-start(bf16[64,2048]{1,0:T(8,128)(2,1)S(1)} %decode_join.3.rest_0_.near_ref), channel_id=1, source_target_pairs={{0,1},{1,0},{2,3},{3,2},{4,5},{5,4},{6,7},{7,6},{8,9},{9,8},{10,11... | collective-permute-start | bytes 786440 | tf_op jit(solution)/shard_map/ppermute | solution.py:351
  33.3 5.8 %collective-permute-start.7 = (bf16[4,128,128]{2,1,0:T(8,128)(2,1)S(1)}, bf16[4,128,128]{2,1,0:T(8,128)(2,1)S(1)}, u32[]{:S(2)}, u32[]{:S(2)}) collective-permute-start(bf16[4,128,128]{2,1,0:T(8,128)(2,1)S(1)} %chain.8.rest_0_), channel_id=1, source_target_pairs={{0,8},{8,16},{16,24},{1,9},{9,17},{17,25},{2,10},{10,18},{18,26},{... | collective-permute-start | bytes 393224 | tf_op jit(solution)/shard_map/ppermute | solution.py:582
  35.9 9.5 %collective-permute-start.9 = (bf16[4,128,128]{2,1,0:T(8,128)(2,1)S(1)}, bf16[4,128,128]{2,1,0:T(8,128)(2,1)S(1)}, u32[]{:S(2)}, u32[]{:S(2)}) collective-permute-start(bf16[4,128,128]{2,1,0:T(8,128)(2,1)S(1)} %chain.9.rest_0_), channel_id=1, source_target_pairs={{0,8},{8,16},{16,24},{1,9},{9,17},{17,25},{2,10},{10,18},{18,26},{... | collective-permute-start | bytes 393224 | tf_op jit(solution)/shard_map/ppermute | solution.py:582
  40.1 5.3 %collective-permute-start.8 = (bf16[32,2048]{1,0:T(8,128)(2,1)S(1)}, bf16[32,2048]{1,0:T(8,128)(2,1)S(1)}, u32[]{:S(2)}, u32[]{:S(2)}) collective-permute-start(bf16[32,2048]{1,0:T(8,128)(2,1)S(1)} %get-tuple-element.40), channel_id=1, source_target_pairs={{0,1},{1,0},{2,3},{3,2},{4,5},{5,4},{6,7},{7,6},{8,9},{9,8},{10,11... | collective-permute-start | bytes 393224 | tf_op jit(solution)/shard_map/ppermute | solution.py:351
  40.8 11.0 %collective-permute-start.11 = (bf16[4,128,128]{2,1,0:T(8,128)(2,1)S(1)}, bf16[4,128,128]{2,1,0:T(8,128)(2,1)S(1)}, u32[]{:S(2)}, u32[]{:S(2)}) collective-permute-start(bf16[4,128,128]{2,1,0:T(8,128)(2,1)S(1)} %chain.10.rest_0_), channel_id=1, source_target_pairs={{0,8},{8,16},{16,24},{1,9},{9,17},{17,25},{2,10},{10,18},{18,26},{... | collective-permute-start | bytes 393224 | tf_op jit(solution)/shard_map/ppermute | solution.py:582
  46.7 15.7 %collective-permute-start.13 = (bf16[4,128,128]{2,1,0:T(8,128)(2,1)S(1)}, bf16[4,128,128]{2,1,0:T(8,128)(2,1)S(1)}, u32[]{:S(2)}, u32[]{:S(2)}) collective-permute-start(bf16[4,128,128]{2,1,0:T(8,128)(2,1)S(1)} %chain.11.rest_0_), channel_id=1, source_target_pairs={{0,8},{8,16},{16,24},{1,9},{9,17},{17,25},{2,10},{10,18},{18,26},{... | collective-permute-start | bytes 393224 | tf_op jit(solution)/shard_map/ppermute | solution.py:582
  49.8 5.2 %collective-permute-start.10 = (bf16[16,2048]{1,0:T(8,128)(2,1)S(1)}, bf16[16,2048]{1,0:T(8,128)(2,1)S(1)}, u32[]{:S(2)}, u32[]{:S(2)}) collective-permute-start(bf16[16,2048]{1,0:T(8,128)(2,1)S(1)} %get-tuple-element.42), channel_id=1, source_target_pairs={{0,16},{8,24},{16,0},{24,8},{1,17},{9,25},{17,1},{25,9},{2,18},{10... | collective-permute-start | bytes 196616 | tf_op jit(solution)/shard_map/ppermute | solution.py:351
  55.1 6.4 %collective-permute-start.12 = (bf16[8,2048]{1,0:T(8,128)(2,1)S(1)}, bf16[8,2048]{1,0:T(8,128)(2,1)S(1)}, u32[]{:S(2)}, u32[]{:S(2)}) collective-permute-start(bf16[8,2048]{1,0:T(8,128)(2,1)S(1)} %get-tuple-element.44), channel_id=1, source_target_pairs={{0,8},{8,0},{16,24},{24,16},{1,9},{9,1},{17,25},{25,17},{2,10},{10... | collective-permute-start | bytes 98312 | tf_op jit(solution)/shard_map/ppermute | solution.py:351
  65.1 11.8 %collective-permute-start.17 = (bf16[272,768]{1,0:T(8,128)(2,1)S(1)}, bf16[272,768]{1,0:T(8,128)(2,1)S(1)}, u32[]{:S(2)}, u32[]{:S(2)}) collective-permute-start(bf16[272,768]{1,0:T(8,128)(2,1)S(1)} %project.10), channel_id=1, source_target_pairs={{0,4},{2,6},{4,0},{6,2},{1,5},{3,7},{5,1},{7,3},{8,12},{10,14},{12... | collective-permute-start | bytes 1253384 | tf_op jit(solution)/shard_map/ppermute | solution.py:351
  68.4 12.6 %collective-permute-start.15 = (bf16[272,768]{1,0:T(8,128)(2,1)S(1)}, bf16[272,768]{1,0:T(8,128)(2,1)S(1)}, u32[]{:S(2)}, u32[]{:S(2)}) collective-permute-start(bf16[272,768]{1,0:T(8,128)(2,1)S(1)} %project.9), channel_id=1, source_target_pairs={{0,2},{2,0},{4,6},{6,4},{1,3},{3,1},{5,7},{7,5},{8,10},{10,8},{12,... | collective-permute-start | bytes 1253384 | tf_op jit(solution)/shard_map/ppermute | solution.py:351
  71.6 18.4 %collective-permute-start.14 = (bf16[272,768]{1,0:T(8,128)(2,1)S(1)}, bf16[272,768]{1,0:T(8,128)(2,1)S(1)}, u32[]{:S(2)}, u32[]{:S(2)}) collective-permute-start(bf16[272,768]{1,0:T(8,128)(2,1)S(1)} %project.7), channel_id=1, source_target_pairs={{0,2},{2,0},{4,6},{6,4},{1,3},{3,1},{5,7},{7,5},{8,10},{10,8},{12,... | collective-permute-start | bytes 1253384 | tf_op jit(solution)/shard_map/ppermute | solution.py:351
  73.8 16.2 %collective-permute-start.19 = (bf16[272,768]{1,0:T(8,128)(2,1)S(1)}, bf16[272,768]{1,0:T(8,128)(2,1)S(1)}, u32[]{:S(2)}, u32[]{:S(2)}) collective-permute-start(bf16[272,768]{1,0:T(8,128)(2,1)S(1)} %project.11), channel_id=1, source_target_pairs={{0,4},{2,6},{4,0},{6,2},{1,5},{3,7},{5,1},{7,3},{8,12},{10,14},{12... | collective-permute-start | bytes 1253384 | tf_op jit(solution)/shard_map/ppermute | solution.py:351
  77.1 19.6 %collective-permute-start.18 = (bf16[272,768]{1,0:T(8,128)(2,1)S(1)}, bf16[272,768]{1,0:T(8,128)(2,1)S(1)}, u32[]{:S(2)}, u32[]{:S(2)}) collective-permute-start(bf16[272,768]{1,0:T(8,128)(2,1)S(1)} %relay.3), channel_id=1, source_target_pairs={{0,2},{2,0},{4,6},{6,4},{1,3},{3,1},{5,7},{7,5},{8,10},{10,8},{12,... | collective-permute-start | bytes 1253384 | tf_op jit(solution)/shard_map/ppermute | solution.py:351
  81.1 15.6 %collective-permute-start.16 = (bf16[272,768]{1,0:T(8,128)(2,1)S(1)}, bf16[272,768]{1,0:T(8,128)(2,1)S(1)}, u32[]{:S(2)}, u32[]{:S(2)}) collective-permute-start(bf16[272,768]{1,0:T(8,128)(2,1)S(1)} %relay.2), channel_id=1, source_target_pairs={{0,4},{2,6},{4,0},{6,2},{1,5},{3,7},{5,1},{7,3},{8,12},{10,14},{12... | collective-permute-start | bytes 1253384 | tf_op jit(solution)/shard_map/ppermute | solution.py:351

commit v5 on v0

v5 whole, which is shorter than its diff:
```python
import functools

import jax
import jax.numpy as jnp
from jax import lax
from jax.experimental import pallas as pl
from jax.experimental.pallas import tpu as pltpu
from jax.sharding import PartitionSpec as P

HEAD_DIM = 128
EPSILON = 1e-06
NEGATIVE = -1e30
HIGH = lax.Precision.HIGHEST
CHUNKS = 2
WEIGHT_PARTS = 4
EARLY_PARTS = 3
VMEM_BYTES = 8 * 2**20
F32 = jnp.float32
BF16 = jnp.bfloat16
NT = (((1,), (1,)), ((), ()))
TN = (((0,), (0,)), ((), ()))


def params():
    return pltpu.CompilerParams(vmem_limit_bytes=VMEM_BYTES)


def cost(flops, moved, exps=0):
    return pl.CostEstimate(flops=int(flops), bytes_accessed=int(moved), transcendentals=int(exps))


def normalize(array):
    return array * lax.rsqrt(jnp.mean(array * array, axis=-1, keepdims=True) + EPSILON)


def lower_ones(length):
    rows = lax.broadcasted_iota(jnp.int32, (length, length), 0)
    cols = lax.broadcasted_iota(jnp.int32, (length, length), 1)
    return rows >= cols


def decay_columns(rate, lower):
    return -lax.dot_general(lower.astype(F32), rate, NT, precision=HIGH, preferred_element_type=F32)


def decay_rows(rate, lower):
    return -lax.dot_general(rate, lower.astype(F32), NT, precision=HIGH, preferred_element_type=F32)


def identity(size):
    rows = lax.broadcasted_iota(jnp.int32, (size, size), 0)
    cols = lax.broadcasted_iota(jnp.int32, (size, size), 1)
    return rows, cols


def head_slice(index):
    return slice(index * HEAD_DIM, (index + 1) * HEAD_DIM)


def halves(array):
    top = array.astype(BF16)
    return top, (array - top.astype(F32)).astype(BF16)

VMEM = pl.BlockSpec(memory_space=pltpu.VMEM)
SMEM = pl.BlockSpec(memory_space=pltpu.SMEM)
ANY = pl.BlockSpec(memory_space=pl.ANY)
HBM = pl.BlockSpec(memory_space=pltpu.HBM)


def call(kernel, name, in_specs, out_shape, scratch=(), estimate=None, out_specs=None):
    if out_specs is None:
        out_specs = jax.tree.map(lambda _: VMEM, out_shape)
    return pl.pallas_call(
        kernel,
        in_specs=in_specs,
        out_specs=out_specs,
        out_shape=out_shape,
        scratch_shapes=list(scratch),
        compiler_params=params(),
        cost_estimate=estimate,
        name=name,
    )


def sds(shape, dtype):
    return jax.ShapeDtypeStruct(shape, dtype)


LOG_ROWS = 16


def log_rows(log):
    top = log.astype(BF16).astype(F32)
    mid = (log - top).astype(BF16).astype(F32)
    row = lax.broadcasted_iota(jnp.int32, (LOG_ROWS, HEAD_DIM), 0)
    rest = jnp.where(row == 2, log - top - mid, 0.0)
    return jnp.where(row == 0, top, jnp.where(row == 1, mid, rest)).astype(BF16)


def read_log(message_ref):
    rows = message_ref.shape[0]
    facts = message_ref[rows - LOG_ROWS :, :].astype(F32)
    return facts[0:1] + facts[1:2] + facts[2:3]


def state_rows(message_ref, index):
    return message_ref[index * HEAD_DIM : (index + 1) * HEAD_DIM, :]


def state_kernel(chunks, place_ref, *refs):
    k_hbm, v_hbm, rate_hbm, q_hbm, dq_hbm, dk_hbm, dv_hbm = refs[:7]
    own_ref, log_ref, col_ref, row_ref = refs[7:11]
    k_ref, v_ref, q_ref, dq_ref, dk_ref, dv_ref = refs[11:17]
    messages = refs[17 : 17 + len(chunks)]
    rate_ref, sems = refs[17 + len(chunks) :]
    heads = own_ref.shape[0]
    pairs = (
        (rate_hbm, rate_ref),
        (k_hbm.at[0], k_ref),
        (v_hbm.at[0], v_ref),
        (dq_hbm, dq_ref),
        (dk_hbm, dk_ref),
        (dv_hbm, dv_ref),
        (q_hbm, q_ref),
    )
    copies = [
        pltpu.make_async_copy(source, target, sems.at[i]) for i, (source, target) in enumerate(pairs)
    ]
    for copy in copies:
        copy.start()
    length = k_ref.shape[0]
    lower = lower_ones(length)
    copies[0].wait()
    rate = rate_ref[0]
    columns = decay_columns(rate, lower)
    col_ref[...] = columns
    row_ref[...] = decay_rows(rate, lower)
    total = columns[length - 1 :, :]
    factor = jnp.exp(total - columns)
    log_ref[...] = jnp.zeros_like(log_ref)
    log_ref[:, :heads] = total
    facts = log_rows(log_ref[...])
    copies[1].wait()
    copies[2].wait()
    for (first, size), message_ref in zip(chunks, messages):
        for i in range(size):
            h = first + i
            at = head_slice(h)
            weighted = k_ref[:, at].astype(F32) * factor[:, h : h + 1]
            top, rest = halves(weighted)
            both = lax.dot_general(
                jnp.concatenate([top, rest], axis=1), v_ref[:, at], TN, preferred_element_type=F32
            )
            state = both[:HEAD_DIM] + both[HEAD_DIM:]
            own_ref[h] = state
            message_ref[i * HEAD_DIM : (i + 1) * HEAD_DIM, :] = state.astype(BF16)
        message_ref[size * HEAD_DIM :, :] = facts
    for copy in copies[3:]:
        copy.wait()


def chain_kernel(phase, first, place_ref, own_ref, log_ref, got_ref, *rest):
    out_ref = rest[-1]
    size = (out_ref.shape[0] - LOG_ROWS) // HEAD_DIM
    right = place_ref[0] == phase
    log = log_ref[...]
    later = read_log(got_ref)
    own_factor = jnp.where(right, 1.0, jnp.exp(later))
    got_factor = jnp.where(right, jnp.exp(log), 1.0)
    for i in range(size):
        h = first + i
        value = (
            own_factor[:, h : h + 1] * own_ref[h]
            + got_factor[:, h : h + 1] * state_rows(got_ref, i).astype(F32)
        )
        out_ref[i * HEAD_DIM : (i + 1) * HEAD_DIM, :] = value.astype(BF16)
    out_ref[size * HEAD_DIM :, :] = log_rows(log + later)


def entering_state(group, got, index):
    state = state_rows(got[0], index)
    for phase in range(1, len(got)):
        state = jnp.where(group == phase + 1, state_rows(got[phase], index), state)
    return jnp.where(group == 0, jnp.zeros_like(state), state)


def weight_copies(places, weight_hbm, weights, sems):
    copies = []
    for i, (index, ref) in enumerate(zip(places, weights)):
        depth = ref.shape[0]
        copies.append(
            pltpu.make_async_copy(weight_hbm.at[pl.ds(index * depth, depth)], ref, sems.at[i])
        )
    for copy in copies:
        copy.start()
    return copies


def load_kernel(index, weight_hbm, *rest):
    weight_ref, token_ref, sems = rest[-3:]
    copies = weight_copies([index], weight_hbm, [weight_ref], sems)
    token_ref[...] = jnp.zeros_like(token_ref)
    for copy in copies:
        copy.wait()


def local_kernel(first, q_ref, k_ref, v_ref, col_ref, row_ref, weight_hbm, *rest):
    local_ref, token_ref = rest[:2]
    weights, sems = rest[2:-1], rest[-1]
    copies = weight_copies(range(len(weights)), weight_hbm, weights, sems)
    token_ref[...] = jnp.zeros_like(token_ref)
    lower = lower_ones(q_ref.shape[1])
    for i in range(local_ref.shape[1] // HEAD_DIM):
        h = first + i
        at = head_slice(h)
        scores = lax.dot_general(q_ref[0, :, at], k_ref[:, at], NT, preferred_element_type=F32)
        decay = jnp.exp(
            jnp.where(lower, col_ref[:, h : h + 1] - row_ref[h : h + 1, :], NEGATIVE)
        )
        narrow = (scores * decay).astype(BF16)
        local_ref[:, head_slice(i)] = jnp.dot(narrow, v_ref[:, at], preferred_element_type=F32)
    for copy in copies:
        copy.wait()


def hidden_kernel(phases, first, place_ref, q_ref, col_ref, local_ref, *rest):
    got, hidden_ref = rest[:phases], rest[-1]
    for i in range(hidden_ref.shape[1] // HEAD_DIM):
        h = first + i
        whole = head_slice(h)
        state = entering_state(place_ref[0], got, i)
        inter = jnp.dot(q_ref[0, :, whole], state, preferred_element_type=F32)
        attended = local_ref[:, whole] + inter * jnp.exp(col_ref[:, h : h + 1])
        hidden_ref[:, head_slice(i)] = normalize(attended).astype(BF16)


def final_kernel(chunks, phases, place_ref, own_ref, log_ref, *rest):
    out_ref = rest[-1]
    group = place_ref[0]
    keep = jnp.exp(log_ref[...])
    for c, (first, size) in enumerate(chunks):
        got = [rest[phase * len(chunks) + c] for phase in range(phases)]
        later = jnp.zeros((1, HEAD_DIM), F32)
        for phase in range(phases):
            later = jnp.where(group == phases - 1 - phase, read_log(got[phase]), later)
        later = jnp.exp(later)
        for i in range(size):
            h = first + i
            suffix = jnp.zeros((HEAD_DIM, HEAD_DIM), F32)
            for phase in range(phases):
                there = state_rows(got[phase], i).astype(F32)
                suffix = jnp.where(group == phases - 1 - phase, there, suffix)
            prefix = entering_state(group, got, i).astype(F32)
            here = own_ref[h] + keep[:, h : h + 1] * prefix
            out_ref[h] = suffix + later[:, h : h + 1] * here


def flat_rows(ref, rows_ref):
    rows, steps = ref.shape[0], ref.shape[1]
    for r in range(rows):
        rows_ref[r * steps : (r + 1) * steps, :] = ref[r].astype(F32)


def decode_kernel(place_ref, prompt_ref, q_ref, k_ref, v_ref, rate_ref, near_ref, far_ref, *rest):
    out_ref, q_rows, k_rows, v_rows, rate_rows = rest[-5:]
    rows_here, steps = q_ref.shape[0], q_ref.shape[1]
    d_rows = q_rows.shape[0]
    flat_rows(q_ref, q_rows)
    flat_rows(k_ref, k_rows)
    flat_rows(v_ref, v_rows)
    flat_rows(rate_ref, rate_rows)
    rows, cols = identity(d_rows)
    seen = (rows // steps == cols // steps) & (rows >= cols)
    ones = seen.astype(F32)
    rates = rate_rows[...]
    down = -jnp.dot(ones, rates, precision=HIGH, preferred_element_type=F32)
    across = -lax.dot_general(
        rates, ones, (((0,), (1,)), ((), ())), precision=HIGH, preferred_element_type=F32
    )
    grow = jnp.exp(down)
    row_of = lax.broadcasted_iota(jnp.int32, (d_rows, HEAD_DIM), 0) // steps
    prompt = jnp.zeros((d_rows, HEAD_DIM), jnp.int32)
    for r in range(rows_here):
        prompt = jnp.where(row_of == r, prompt_ref[r], prompt)
    mine = prompt == place_ref[1]
    for i in range(rates.shape[1]):
        at = head_slice(i)
        query = q_rows[:, at]
        narrow = query.astype(BF16)
        terms = []
        for ref in (near_ref, far_ref):
            top, low = halves(ref[i])
            both = jnp.dot(
                narrow, jnp.concatenate([top, low], axis=1), preferred_element_type=F32
            )
            terms.append(both[:, :HEAD_DIM] + both[:, HEAD_DIM:])
        base = jnp.where(mine, terms[0], terms[1])
        scores = lax.dot_general(
            query, k_rows[:, at], NT, precision=HIGH, preferred_element_type=F32
        )
        decay = jnp.exp(jnp.where(seen, down[:, i : i + 1] - across[i : i + 1, :], NEGATIVE))
        intra = jnp.dot(scores * decay, v_rows[:, at], precision=HIGH, preferred_element_type=F32)
        q_rows[:, at] = normalize(base * grow[:, i : i + 1] + intra)
    pad = out_ref.shape[0] - d_rows
    value = q_rows[...]
    if pad:
        value = jnp.concatenate([value, jnp.zeros((pad, value.shape[1]), F32)], axis=0)
    out_ref[...] = value.astype(BF16)


def times_weight(rows, weights, column, width):
    total = None
    for i, ref in enumerate(weights):
        depth = ref.shape[0]
        term = jnp.dot(
            rows[:, i * depth : (i + 1) * depth],
            ref[:, pl.ds(column, width)],
            preferred_element_type=F32,
        )
        total = term if total is None else total + term
    return total


def project_kernel(pieces, chunks, place_ref, *rest):
    hidden, weights = rest[:chunks], rest[chunks : chunks + WEIGHT_PARTS]
    outs = rest[-len(pieces) :]
    half = outs[0].shape[1]
    rows = jnp.concatenate([ref[...] for ref in hidden], axis=1)
    for (bits, side), out_ref in zip(pieces, outs):
        column = pl.multiple_of(((place_ref[2] ^ bits) * 2 + side) * half, HEAD_DIM)
        out_ref[...] = times_weight(rows, weights, column, half).astype(out_ref.dtype)


def decode_project_kernel(place_ref, rows_ref, *rest):
    weights, outs = rest[:WEIGHT_PARTS], rest[-4:]
    width = outs[0].shape[1]
    rows = rows_ref[...]
    for bits, out_ref in enumerate(outs):
        column = pl.multiple_of((place_ref[2] ^ bits) * width, HEAD_DIM)
        out_ref[...] = times_weight(rows, weights, column, width).astype(out_ref.dtype)


def decode_finish_kernel(own_ref, x_ref, y_ref, far_ref, out_ref):
    rows, steps = out_ref.shape[0], out_ref.shape[1]
    total = own_ref[...] + x_ref[...].astype(F32) + y_ref[...].astype(F32) + far_ref[...].astype(F32)
    for r in range(rows):
        out_ref[r] = total[r * steps : (r + 1) * steps].astype(BF16)


def relay_kernel(own_ref, got_ref, *rest):
    out_ref = rest[-1]
    out_ref[...] = (own_ref[...] + got_ref[...].astype(F32)).astype(BF16)


def finish_kernel(own_a, own_b, ax, ay, bx, by, prefill_hbm, out_ref, sems):
    width = own_a.shape[1]
    count = sems.shape[0]
    size = out_ref.shape[0] // count
    copies = []
    for c in range(count):
        at = slice(c * size, (c + 1) * size)
        for at_cols, own, x_ref, y_ref in ((0, own_a, ax, ay), (width, own_b, bx, by)):
            total = own[at] + x_ref[at].astype(F32) + y_ref[at].astype(F32)
            out_ref[at, at_cols : at_cols + width] = total.astype(BF16)
        copy = pltpu.make_async_copy(
            out_ref.at[pl.ds(c * size, size)], prefill_hbm.at[0, pl.ds(c * size, size)], sems.at[c]
        )
        copy.start()
        copies.append(copy)
    for copy in copies:
        copy.wait()


def swap(array, axis, size, bit):
    return lax.ppermute(array, axis, [(i, i ^ bit) for i in range(size)])


def body(
    prefill_query,
    prefill_key,
    prefill_value,
    prefill_rate,
    out_weight,
    decode_query,
    decode_key,
    decode_value,
    decode_rate,
    prompt_of_row,
    *,
    groups,
    reps,
    parts,
):
    length = prefill_query.shape[1]
    features = prefill_query.shape[2]
    heads = prefill_rate.shape[1]
    rows_here, steps = decode_query.shape[0], decode_query.shape[1]
    d_rows = rows_here * steps
    d_pad = -(-d_rows // 16) * 16
    place = jnp.stack([lax.axis_index("ctx"), lax.axis_index("rep"), lax.axis_index("head")])
    place = place.astype(jnp.int32)
    count = min(CHUNKS, heads)
    edges = [heads * c // count for c in range(count + 1)]
    chunks = [(a, b - a) for a, b in zip(edges[:-1], edges[1:])]
    phases = groups - 1
    state_elements = heads * HEAD_DIM * HEAD_DIM

    def in_hbm(array):
        return pltpu.with_memory_space_constraint(array, pltpu.HBM)

    def in_vmem(array):
        return pltpu.with_memory_space_constraint(array, pltpu.VMEM)

    def message_shape(size):
        return sds((size * HEAD_DIM + LOG_ROWS, HEAD_DIM), BF16)

    decode_shape = (rows_here, steps, features)
    made = call(
        functools.partial(state_kernel, chunks),
        "own_state",
        [SMEM] + [HBM] * 7,
        [
            pltpu.VMEM((heads, HEAD_DIM, HEAD_DIM), F32),
            pltpu.VMEM((1, HEAD_DIM), F32),
            pltpu.VMEM((length, heads), F32),
            pltpu.VMEM((heads, length), F32),
            pltpu.VMEM((length, features), BF16),
            pltpu.VMEM((length, features), BF16),
            pltpu.VMEM((1, length, features), BF16),
            pltpu.VMEM(decode_shape, BF16),
            pltpu.VMEM(decode_shape, BF16),
            pltpu.VMEM(decode_shape, BF16),
        ]
        + [message_shape(size) for _, size in chunks],
        [pltpu.VMEM((1, heads, length), F32), pltpu.SemaphoreType.DMA((7,))],
        cost(4 * length * features * HEAD_DIM, 34 * length * features),
    )(
        place,
        *[
            in_hbm(array)
            for array in (
                prefill_key,
                prefill_value,
                prefill_rate,
                prefill_query,
                decode_query,
                decode_key,
                decode_value,
            )
        ],
    )
    own, log_row, columns, rows, keys, values, queries, d_query, d_key, d_value = map(
        in_vmem, made[:10]
    )

    weight_hbm = in_hbm(out_weight)
    weight_part = pltpu.VMEM((features // WEIGHT_PARTS, out_weight.shape[1]), BF16)
    token = sds((8, HEAD_DIM), F32)
    local, local_token, *weights = call(
        functools.partial(local_kernel, 0),
        "local_attention",
        [VMEM] * 5 + [HBM],
        [pltpu.VMEM((length, features), F32), token] + [weight_part] * EARLY_PARTS,
        [pltpu.SemaphoreType.DMA((EARLY_PARTS,))],
        cost(4 * length * length * features, 12 * length * features, heads * length * length),
    )(queries, keys, values, columns, rows, weight_hbm)
    local = in_vmem(local)

    def load_weight(*after):
        if len(weights) == WEIGHT_PARTS:
            return []
        part, done = call(
            functools.partial(load_kernel, len(weights)),
            "load_weight",
            [HBM] + [ANY] * len(after),
            [weight_part, token],
            [pltpu.SemaphoreType.DMA((1,))],
            cost(1, features // WEIGHT_PARTS * out_weight.shape[1] * 2),
        )(weight_hbm, *after)
        weights.append(part)
        return [done]

    values_out = list(made[10:])
    received = []
    after = [local_token]
    for phase in range(phases):
        pairs = {(phase, phase + 1), (groups - 2 - phase, groups - 1 - phase)}
        pairs = sorted(pairs | {(b, a) for a, b in pairs})
        if phase > 0:
            values_out = []
            for c, (first, size) in enumerate(chunks):
                value = call(
                    functools.partial(chain_kernel, phase, first),
                    "chain",
                    [SMEM, VMEM, VMEM, VMEM] + [ANY] * len(after),
                    message_shape(size),
                    (),
                    cost(2 * size * HEAD_DIM * HEAD_DIM, 24 * size * HEAD_DIM * HEAD_DIM),
                )(place, own, log_row, received[-1][c], *after)
                values_out.append(value)
                after = []
        received.append([lax.ppermute(value, "ctx", pairs) for value in values_out])
    loaded = []
    while len(weights) < WEIGHT_PARTS:
        loaded = load_weight(values_out[-1], *loaded)
    weights = [in_vmem(part) for part in weights]

    after = loaded
    hidden = [
        call(
            functools.partial(hidden_kernel, phases, first),
            "hidden",
            [SMEM] + [VMEM] * (3 + phases) + [ANY] * len(after),
            sds((length, size * HEAD_DIM), BF16),
            (),
            cost(2 * length * size * HEAD_DIM * HEAD_DIM, 20 * length * size * HEAD_DIM),
        )(place, queries, columns, local, *[received[phase][c] for phase in range(phases)], *after)
        for c, (first, size) in enumerate(chunks)
    ]

    def final_states(*after):
        final = call(
            functools.partial(final_kernel, chunks, phases),
            "final_state",
            [SMEM, VMEM, VMEM] + [VMEM] * (phases * count) + [ANY] * len(after),
            sds((heads, HEAD_DIM, HEAD_DIM), F32),
            (),
            cost(4 * state_elements, state_elements * 4 * phases),
        )(place, own, log_row, *[got for phase in received for got in phase], *after)
        return final, swap(final, "rep", reps, 1)

    def decode_rows(final, other, *after):
        flat = pltpu.VMEM((d_rows, features), F32)
        return call(
            decode_kernel,
            "decode_rows",
            [SMEM, SMEM] + [VMEM] * 6 + [ANY] * len(after),
            sds((d_pad, features), BF16),
            [flat, flat, flat, pltpu.VMEM((d_rows, heads), F32)],
            cost(16 * d_rows * features * HEAD_DIM, state_elements),
        )(
            place,
            prompt_of_row,
            d_query,
            d_key,
            d_value,
            jnp.transpose(decode_rate, (0, 2, 1)),
            final,
            other,
            *after,
        )

    out_columns = out_weight.shape[1]
    if parts != 4 or (out_columns // parts) % 256 != 0 or length % 64 != 0:
        rows_all = jnp.concatenate([jnp.concatenate(hidden, axis=1), decode_rows(*final_states())], axis=0)
        terms = jnp.dot(rows_all, out_weight, preferred_element_type=F32)
        summed = lax.psum_scatter(terms, "head", scatter_dimension=1, tiled=True)
        prefill_out = summed[:length].astype(BF16)[None]
        decode_out = summed[length : length + d_rows].astype(BF16)
        return prefill_out, decode_out.reshape(rows_here, steps, -1)

    width = out_columns // parts
    half = width // 2

    def project(pieces, dtype, *after):
        return call(
            functools.partial(project_kernel, pieces, count),
            "project",
            [SMEM] + [VMEM] * (count + WEIGHT_PARTS) + [ANY] * len(after),
            [sds((length, half), dtype) for _ in pieces],
            (),
            cost(2 * length * features * half * len(pieces), features * half * 2 * len(pieces)),
        )(place, *hidden, *weights, *after)

    def relay(own_term, got, *after):
        return call(
            relay_kernel,
            "relay",
            [VMEM, VMEM] + [ANY] * len(after),
            sds((length, half), BF16),
            (),
            cost(length * half, length * half * 8),
        )(own_term, got, *after)

    far_a = swap(project([(3, 0)], BF16)[0], "head", parts, 1)
    to_y, = project([(3, 1)], BF16)
    far_b = swap(to_y, "head", parts, 2)
    x_a = swap(project([(1, 0)], BF16)[0], "head", parts, 1)
    y_b = swap(project([(2, 1)], BF16)[0], "head", parts, 2)
    pass_a, pass_b = project([(2, 0), (1, 1)], F32)
    own_a, own_b = project([(0, 0), (0, 1)], F32)
    sent_a, sent_b = relay(pass_a, far_a), relay(pass_b, far_b)
    y_a = swap(sent_a, "head", parts, 2)
    x_b = swap(sent_b, "head", parts, 1)

    d_hidden = decode_rows(*final_states(to_y), sent_a, sent_b)
    d_own, d_x, d_y, d_far = call(
        decode_project_kernel,
        "decode_project",
        [SMEM] + [VMEM] * (1 + WEIGHT_PARTS),
        [sds((d_pad, width), F32)] + [sds((d_pad, width), BF16)] * 3,
        (),
        cost(2 * d_pad * features * out_columns, features * out_columns // 8),
    )(place, d_hidden, *weights)
    decode_out = call(
        decode_finish_kernel,
        "decode_finish",
        [VMEM] * 4,
        sds((rows_here, steps, width), BF16),
        (),
        cost(4 * d_pad * width, 10 * d_pad * width),
    )(
        d_own,
        swap(d_x, "head", parts, 1),
        swap(d_y, "head", parts, 2),
        swap(d_far, "head", parts, 3),
    )

    prefill_out = call(
        finish_kernel,
        "finish",
        [VMEM] * 6,
        sds((1, length, width), BF16),
        [pltpu.VMEM((length, width), BF16), pltpu.SemaphoreType.DMA((4,))],
        cost(6 * length * half, 20 * length * half),
        out_specs=HBM,
    )(own_a, own_b, x_a, y_a, x_b, y_b)
    return prefill_out, decode_out


def solution(mesh):
    return jax.shard_map(
        functools.partial(
            body, groups=mesh.shape["ctx"], reps=mesh.shape["rep"], parts=mesh.shape["head"]
        ),
        mesh=mesh,
        in_specs=(
            P("rep", "ctx", "head"),
            P("rep", "ctx", "head"),
            P("rep", "ctx", "head"),
            P("rep", "head", "ctx"),
            P("head", None),
            P(("ctx", "rep"), None, "head"),
            P(("ctx", "rep"), None, "head"),
            P(("ctx", "rep"), None, "head"),
            P(("ctx", "rep"), "head", None),
            P(("ctx", "rep")),
        ),
        out_specs=(P("rep", "ctx", "head"), P(("ctx", "rep"), None, "head")),
        check_vma=False,
    )
```

time: 242 us -> 76.9 us (0.32)
  waiting for transfers between devices: 148 us -> 11.1 us
  matrix products: 52.4 us -> 0 us
  Pallas kernels: 0 us -> 39 us
  starting transfers between devices: 0.56 us -> 25.6 us
  between operations: 14.7 us -> 0.84 us
  blocking collectives: 13.5 us -> 0 us
  other arithmetic: 7.12 us -> 0.08 us
  local copies, waits for them, and re-layouts: 5.24 us -> 0.01 us
    reduce_scatter x2 -> x0, waiting for transfers between devices: 80.3 us -> none  [the longest x1 71.7 us: body(): lax.psum_scatter(token_terms, 'head', scatter_dimension=1, tiled=True)]
    all_gather x2 -> x0, waiting for transfers between devices: 67.4 us -> none  [the longest x1 67.4 us: body(): piece = lax.all_gather(own_state[None], 'ctx', axis=0, tiled=True)]
    dot_general x12 -> x0, matrix products: 52.4 us -> none  [the longest x1 14.4 us: body(): jnp.dot(hidden, out_weight, preferred_element_type=jnp.float32)]
    pallas_call x0 -> x22, Pallas kernels: none -> 39 us  [the longest x6 10.9 us: project(): call(functools.partial(project_kernel, pieces, count), 'project', [SMEM]...]
    ppermute x0 -> x16, starting transfers between devices: none -> 25.6 us  [the longest x6 14.7 us: body(): received.append([lax.ppermute(value, 'ctx', pairs) for value in values_out])]
    unnamed x1 -> x0, blocking collectives: 13.5 us -> none
    ppermute x0 -> x16, waiting for transfers between devices: none -> 11.1 us  [the longest x10 6.18 us: swap(): return lax.ppermute(array, axis, [(i, i ^ bit) for i in range(size)])]
    dot_general x1 -> x0, other arithmetic: 3.21 us -> none  [body(): entering = jnp.einsum('ch,chde->hde', weight_in, piece, precision=HIGH)]
  transfers between devices with their start and end apart: 4 -> 16, of which waited for: 3 -> 8; matrix products, arithmetic and copies ran while one was open for 12% -> 0% of each run, Pallas kernels for 0% -> 39%
where the time goes in v5:
time: 76.9 us; the launch traced here: 76.7 us
  Pallas kernels  39 us (51%)
  starting transfers between devices  25.6 us (33%)
  waiting for transfers between devices  11.1 us (14%)
  between operations  0.84 us (1%)
    ppermute x6, starting transfers between devices, body(): received.append([lax.ppermute(value, 'ctx', pairs) for value in values_out])  14.7 us
    pallas_call x6, Pallas kernels, project(): call(functools.partial(project_kernel, pieces, count), 'project', [SMEM]...  10.9 us
    ppermute x10, starting transfers between devices, swap(): return lax.ppermute(array, axis, [(i, i ^ bit) for i in range(size)])  10.9 us
    pallas_call x1, Pallas kernels, body(): call(functools.partial(local_kernel, 0), 'local_attention', [VMEM] * 5 +...  6.42 us
    ppermute x10, waiting for transfers between devices, swap(): return lax.ppermute(array, axis, [(i, i ^ bit) for i in range(size)])  6.18 us
    ppermute x6, waiting for transfers between devices, body(): received.append([lax.ppermute(value, 'ctx', pairs) for value in values_out])  4.97 us
    pallas_call x1, Pallas kernels, body(): call(functools.partial(state_kernel, chunks), 'own_state', [SMEM] + [HBM]...  4.17 us
    pallas_call x1, Pallas kernels, body(): call(decode_project_kernel, 'decode_project', [SMEM] + [VMEM] * (1 + WEIG...  3.92 us
  transfers between devices with their start and end apart: 16, of which 8 were waited for; matrix products, arithmetic and copies ran while one was open for 0% of the time, Pallas kernels for 39%

profile of v5, /device:TPU:0, one launch (start us, length us, event | category | flops | bytes accessed | tf_op | source)
XLA Modules:
  0.0 76.7 jit_solution(1488217108165908469)
XLA Ops:
  0.6 0.1 pad_add_fusion.place_ref
  0.7 4.2 %own_state.1 = (f32[16,128,128]{2,1,0:T(8,128)S(1)}, f32[1,128]{1,0:T(1,128)S(1)}, f32[256,16]{1,0:T(8,128)S(1)}, f32[16,256]{1,0:T(8,128)S(1)}, bf16[256,2048]{...) custom-call(s32[3]{0:T(128)S(1)} %pad_add_fusion.place_ref, ...), custom_call_target="tpu_custom_call" | custom-call | flops 268435456 | bytes 17825792 | tf_op jit(solution)/shard_map/own_state/pallas_call | solution.py:418
  4.9 3.1 %collective-permute-start = (bf16[1040,128]{1,0:T(8,128)(2,1)S(1)}, bf16[1040,128]{1,0:T(8,128)(2,1)S(1)}, u32[]{:S(2)}, u32[]{:S(2)}) collective-permute-start(bf16[1040,128]{1,0:T(8,128)(2,1)S(1)} %get-tuple-element.35), channel_id=1, source_target_pairs={{0,8},{8,0},{16,24},{24,16},{1,9},{9,1},{17,25},{25,17},{2,10},{10... | collective-permute-start | bytes 798728 | tf_op jit(solution)/shard_map/ppermute | solution.py:502
  8.0 0.1 collective-permute-start.3
  8.1 6.4 %local_attention.1 = (f32[256,2048]{1,0:T(8,128)S(1)}, f32[8,128]{1,0:T(8,128)S(1)}, bf16[512,6144]{1,0:T(8,128)(2,1)S(1)}, bf16[512,6144]{1,0:T(8,128)(2,1)S(1)}, bf16[512,6144]{1,0:T(8,128)(2,1)S(1)}) custom-call(bf16[1,256,2048]{2,1,0:T(8,128)(2,1)S(1)} %get-tuple-element.29.q_ref, bf16[256,2048]{1,0:T(8,128)(2,1)S(1)} %get-tuple-element.31.k_ref, ...), custom_call_target="tpu_custom_call" | custom-call | flops 536870912 | bytes 6291456 | tf_op jit(solution)/shard_map/local_attention/pallas_call | solution.py:459
  14.5 0.7 collective-permute-done.got_ref.rest_0_
  15.2 0.7 chain.4
  15.9 0.7 collective-permute-start.1
  16.6 3.5 %collective-permute-done.3.got_ref.rest_0_.rest_1_ = bf16[1040,128]{1,0:T(8,128)(2,1)S(1)} collective-permute-done((bf16[1040,128]{1,0:T(8,128)(2,1)S(1)}, bf16[1040,128]{1,0:T(8,128)(2,1)S(1)}, u32[]{:S(2)}, u32[]{:S(2)}) %collective-permute-start.3) | collective-permute-done | bytes 266272 | tf_op jit(solution)/shard_map/ppermute | solution.py:502
  20.1 0.7 chain.6
  20.8 0.9 %collective-permute-start.4 = (bf16[1040,128]{1,0:T(8,128)(2,1)S(1)}, bf16[1040,128]{1,0:T(8,128)(2,1)S(1)}, u32[]{:S(2)}, u32[]{:S(2)}) collective-permute-start(bf16[1040,128]{1,0:T(8,128)(2,1)S(1)} %chain.6), channel_id=1, source_target_pairs={{8,16},{16,8},{9,17},{17,9},{10,18},{18,10},{11,19},{19,11},{12,20... | collective-permute-start | bytes 798728 | tf_op jit(solution)/shard_map/ppermute | solution.py:502
  21.7 0.0 collective-permute-done.1.got_ref.rest_1_.rest_2_
  21.7 0.7 chain.5
  22.4 5.6 %collective-permute-start.2 = (bf16[1040,128]{1,0:T(8,128)(2,1)S(1)}, bf16[1040,128]{1,0:T(8,128)(2,1)S(1)}, u32[]{:S(2)}, u32[]{:S(2)}) collective-permute-start(bf16[1040,128]{1,0:T(8,128)(2,1)S(1)} %chain.5), channel_id=1, source_target_pairs={{0,8},{8,0},{16,24},{24,16},{1,9},{9,1},{17,25},{25,17},{2,10},{10... | collective-permute-start | bytes 798728 | tf_op jit(solution)/shard_map/ppermute | solution.py:502
  28.0 0.0 collective-permute-done.4.got_ref.rest_1_.rest_3_
  28.0 0.7 chain.7.rest_0_
  28.7 4.4 %collective-permute-start.5 = (bf16[1040,128]{1,0:T(8,128)(2,1)S(1)}, bf16[1040,128]{1,0:T(8,128)(2,1)S(1)}, u32[]{:S(2)}, u32[]{:S(2)}) collective-permute-start(bf16[1040,128]{1,0:T(8,128)(2,1)S(1)} %chain.7.rest_0_), channel_id=1, source_target_pairs={{0,8},{8,0},{16,24},{24,16},{1,9},{9,1},{17,25},{25,17},{2,10},{10... | collective-permute-start | bytes 798728 | tf_op jit(solution)/shard_map/ppermute | solution.py:502
  33.2 2.8 %load_weight.1 = (bf16[512,6144]{1,0:T(8,128)(2,1)S(1)}, f32[8,128]{1,0:T(8,128)S(1)}) custom-call(bf16[2048,6144]{1,0:T(8,128)(2,1)} %weight_hbm.3, bf16[1040,128]{1,0:T(8,128)(2,1)S(1)} %chain.7.rest_0_), custom_call_target="tpu_custom_call" | custom-call | flops 1 | bytes 6291456 | tf_op jit(solution)/shard_map/load_weight/pallas_call | solution.py:472
  36.0 0.0 collective-permute-done.2.rest_2_.rest_4_
  36.0 1.6 %hidden.2.rest_0_ = bf16[256,1024]{1,0:T(8,128)(2,1)S(1)} custom-call(s32[3]{0:T(128)S(1)} %pad_add_fusion.place_ref, bf16[1,256,2048]{2,1,0:T(8,128)(2,1)S(1)} %get-tuple-element.29.q_ref, f32[256,16]{1,0:T(8,128)S(1)} %get-tuple-element.30.col_ref, f32[256,2048]{1,0:T(8,128)S(1)} %get-tuple-element.34.local_ref, ...), custom_call_target="tpu_custom_call" | custom-call | flops 67108864 | bytes 5242880 | tf_op jit(solution)/shard_map/hidden/pallas_call | solution.py:510
  37.6 0.8 %collective-permute-done.5.rest_2_.rest_5_ = bf16[1040,128]{1,0:T(8,128)(2,1)S(1)} collective-permute-done((bf16[1040,128]{1,0:T(8,128)(2,1)S(1)}, bf16[1040,128]{1,0:T(8,128)(2,1)S(1)}, u32[]{:S(2)}, u32[]{:S(2)}) %collective-permute-start.5) | collective-permute-done | bytes 266272 | tf_op jit(solution)/shard_map/ppermute | solution.py:502
  38.4 1.6 %hidden.3.rest_1_ = bf16[256,1024]{1,0:T(8,128)(2,1)S(1)} custom-call(s32[3]{0:T(128)S(1)} %pad_add_fusion.place_ref, bf16[1,256,2048]{2,1,0:T(8,128)(2,1)S(1)} %get-tuple-element.29.q_ref, f32[256,16]{1,0:T(8,128)S(1)} %get-tuple-element.30.col_ref, f32[256,2048]{1,0:T(8,128)S(1)} %get-tuple-element.34.local_ref, ...), custom_call_target="tpu_custom_call" | custom-call | flops 67108864 | bytes 5242880 | tf_op jit(solution)/shard_map/hidden/pallas_call | solution.py:510
  40.0 1.6 %project.10.rest_6_ = bf16[256,768]{1,0:T(8,128)(2,1)S(1)} custom-call(s32[3]{0:T(128)S(1)} %pad_add_fusion.place_ref, bf16[256,1024]{1,0:T(8,128)(2,1)S(1)} %hidden.2.rest_0_, bf16[256,1024]{1,0:T(8,128)(2,1)S(1)} %hidden.3.rest_1_, bf16[512,6144]{1,0:T(8,128)(2,1)S(1)} %get-tuple-element.41.rest_2_.rest_0_, ...), custom_call_target="tpu_custom_call" | custom-call | flops 805306368 | bytes 3145728 | tf_op jit(solution)/shard_map/project/pallas_call | solution.py:566
  41.6 1.1 %final_state.1.near_ref = f32[16,128,128]{2,1,0:T(8,128)S(1)} custom-call(s32[3]{0:T(128)S(1)} %pad_add_fusion.place_ref, f32[16,128,128]{2,1,0:T(8,128)S(1)} %get-tuple-element.36.own_ref, f32[1,128]{1,0:T(1,128)S(1)} %get-tuple-element.37.log_ref, bf16[1040,128]{1,0:T(8,128)(2,1)S(1)} %collective-permute-done.got_ref.rest_0_, ...), custom_call_target="tpu_custom_call" | custom-call | flops 1048576 | bytes 3145728 | tf_op jit(solution)/shard_map/final_state/pallas_call | solution.py:522
  42.7 0.1 collective-permute-start.12
  42.8 1.6 %collective-permute-start.9 = (bf16[256,768]{1,0:T(8,128)(2,1)S(1)}, bf16[256,768]{1,0:T(8,128)(2,1)S(1)}, u32[]{:S(2)}, u32[]{:S(2)}) collective-permute-start(bf16[256,768]{1,0:T(8,128)(2,1)S(1)} %project.10.rest_6_), channel_id=1, source_target_pairs={{0,4},{2,6},{4,0},{6,2},{1,5},{3,7},{5,1},{7,3},{8,12},{10,14},{12... | collective-permute-start | bytes 1179656 | tf_op jit(solution)/shard_map/ppermute | solution.py:375
  44.3 1.6 %project.9 = bf16[256,768]{1,0:T(8,128)(2,1)S(1)} custom-call(s32[3]{0:T(128)S(1)} %pad_add_fusion.place_ref, bf16[256,1024]{1,0:T(8,128)(2,1)S(1)} %hidden.2.rest_0_, bf16[256,1024]{1,0:T(8,128)(2,1)S(1)} %hidden.3.rest_1_, bf16[512,6144]{1,0:T(8,128)(2,1)S(1)} %get-tuple-element.41.rest_2_.rest_0_, ...), custom_call_target="tpu_custom_call" | custom-call | flops 805306368 | bytes 3145728 | tf_op jit(solution)/shard_map/project/pallas_call | solution.py:566
  45.9 1.5 %collective-permute-start.7 = (bf16[256,768]{1,0:T(8,128)(2,1)S(1)}, bf16[256,768]{1,0:T(8,128)(2,1)S(1)}, u32[]{:S(2)}, u32[]{:S(2)}) collective-permute-start(bf16[256,768]{1,0:T(8,128)(2,1)S(1)} %project.9), channel_id=1, source_target_pairs={{0,2},{2,0},{4,6},{6,4},{1,3},{3,1},{5,7},{7,5},{8,10},{10,8},{12,... | collective-permute-start | bytes 1179656 | tf_op jit(solution)/shard_map/ppermute | solution.py:375
  47.5 1.6 %project.7 = bf16[256,768]{1,0:T(8,128)(2,1)S(1)} custom-call(s32[3]{0:T(128)S(1)} %pad_add_fusion.place_ref, bf16[256,1024]{1,0:T(8,128)(2,1)S(1)} %hidden.2.rest_0_, bf16[256,1024]{1,0:T(8,128)(2,1)S(1)} %hidden.3.rest_1_, bf16[512,6144]{1,0:T(8,128)(2,1)S(1)} %get-tuple-element.41.rest_2_.rest_0_, ...), custom_call_target="tpu_custom_call" | custom-call | flops 805306368 | bytes 3145728 | tf_op jit(solution)/shard_map/project/pallas_call | solution.py:566
  49.0 0.6 collective-permute-start.6
  49.6 1.6 %project.11 = bf16[256,768]{1,0:T(8,128)(2,1)S(1)} custom-call(s32[3]{0:T(128)S(1)} %pad_add_fusion.place_ref, bf16[256,1024]{1,0:T(8,128)(2,1)S(1)} %hidden.2.rest_0_, bf16[256,1024]{1,0:T(8,128)(2,1)S(1)} %hidden.3.rest_1_, bf16[512,6144]{1,0:T(8,128)(2,1)S(1)} %get-tuple-element.41.rest_2_.rest_0_, ...), custom_call_target="tpu_custom_call" | custom-call | flops 805306368 | bytes 3145728 | tf_op jit(solution)/shard_map/project/pallas_call | solution.py:566
  51.2 0.0 copy-start
  51.2 0.0 copy-start.1
  51.2 0.6 collective-permute-start.11
  51.8 2.4 %project.8 = (f32[256,768]{1,0:T(8,128)S(1)}, f32[256,768]{1,0:T(8,128)S(1)}) custom-call(s32[3]{0:T(128)S(1)} %pad_add_fusion.place_ref, bf16[256,1024]{1,0:T(8,128)(2,1)S(1)} %hidden.2.rest_0_, bf16[256,1024]{1,0:T(8,128)(2,1)S(1)} %hidden.3.rest_1_, bf16[512,6144]{1,0:T(8,128)(2,1)S(1)} %get-tuple-element.41.rest_2_.rest_0_, ...), custom_call_target="tpu_custom_call" | custom-call | flops 1610612736 | bytes 6291456 | tf_op jit(solution)/shard_map/project/pallas_call | solution.py:566
  54.1 0.6 collective-permute-done.9.got_ref
  54.7 0.1 relay.3.rest_1_
  54.8 1.5 %collective-permute-start.10 = (bf16[256,768]{1,0:T(8,128)(2,1)S(1)}, bf16[256,768]{1,0:T(8,128)(2,1)S(1)}, u32[]{:S(2)}, u32[]{:S(2)}) collective-permute-start(bf16[256,768]{1,0:T(8,128)(2,1)S(1)} %relay.3.rest_1_), channel_id=1, source_target_pairs={{0,2},{2,0},{4,6},{6,4},{1,3},{3,1},{5,7},{7,5},{8,10},{10,8},{12,... | collective-permute-start | bytes 1179656 | tf_op jit(solution)/shard_map/ppermute | solution.py:375
  56.4 1.6 %collective-permute-done.7.got_ref = bf16[256,768]{1,0:T(8,128)(2,1)S(1)} collective-permute-done((bf16[256,768]{1,0:T(8,128)(2,1)S(1)}, bf16[256,768]{1,0:T(8,128)(2,1)S(1)}, u32[]{:S(2)}, u32[]{:S(2)}) %collective-permute-start.7) | collective-permute-done | bytes 393248 | tf_op jit(solution)/shard_map/ppermute | solution.py:375
  57.9 0.1 relay.2.rest_0_
  58.0 0.6 collective-permute-start.8
  58.6 0.0 collective-permute-done.12.far_ref
  58.6 0.0 copy-done
  58.6 0.0 copy-done.1
  58.6 1.7 %decode_rows.1.rows_ref = bf16[16,2048]{1,0:T(8,128)(2,1)S(1)} custom-call(s32[3]{0:T(128)S(1)} %pad_add_fusion.place_ref, s32[4]{0:T(128)S(1)} %copy-done.1, bf16[4,2,2048]{2,1,0:T(2,128)(2,1)S(1)} %get-tuple-element.49.q_ref, bf16[4,2,2048]{2,1,0:T(2,128)(2,1)S(1)} %get-tuple-element.50.k_ref, bf16[4,2,2048]{2,1,0:T(2,128)(2,1)S(1)} %get-tuple-element.51.v_ref, ...), custom_call_target="tpu_custom_call" | custom-call | flops 33554432 | bytes 262144 | tf_op jit(solution)/shard_map/decode_rows/pallas_call | solution.py:534
  60.3 3.9 %decode_project.1 = (f32[16,1536]{1,0:T(8,128)S(1)}, bf16[16,1536]{1,0:T(8,128)(2,1)S(1)}, bf16[16,1536]{1,0:T(8,128)(2,1)S(1)}, bf16[16,1536]{1,0:T(8,128)(2,1)S(1)}) custom-call(s32[3]{0:T(128)S(1)} %pad_add_fusion.place_ref, bf16[16,2048]{1,0:T(8,128)(2,1)S(1)} %decode_rows.1.rows_ref, bf16[512,6144]{1,0:T(8,128)(2,1)S(1)} %get-tuple-element.41.rest_2_.rest_0_, ...), custom_call_target="tpu_custom_call" | custom-call | flops 402653184 | bytes 1572864 | tf_op jit(solution)/shard_map/decode_project/pallas_call | solution.py:597
  64.2 1.5 %collective-permute-start.13 = (bf16[16,1536]{1,0:T(8,128)(2,1)S(1)}, bf16[16,1536]{1,0:T(8,128)(2,1)S(1)}, u32[]{:S(2)}, u32[]{:S(2)}) collective-permute-start(bf16[16,1536]{1,0:T(8,128)(2,1)S(1)} %get-tuple-element.53), channel_id=1, source_target_pairs={{0,2},{2,0},{4,6},{6,4},{1,3},{3,1},{5,7},{7,5},{8,10},{10,8},{12,... | collective-permute-start | bytes 147464 | tf_op jit(solution)/shard_map/ppermute | solution.py:375
  65.7 0.6 collective-permute-done.6.ax
  66.4 0.9 %collective-permute-start.14 = (bf16[16,1536]{1,0:T(8,128)(2,1)S(1)}, bf16[16,1536]{1,0:T(8,128)(2,1)S(1)}, u32[]{:S(2)}, u32[]{:S(2)}) collective-permute-start(bf16[16,1536]{1,0:T(8,128)(2,1)S(1)} %get-tuple-element.54), channel_id=1, source_target_pairs={{0,4},{2,6},{4,0},{6,2},{1,5},{3,7},{5,1},{7,3},{8,12},{10,14},{12... | collective-permute-start | bytes 147464 | tf_op jit(solution)/shard_map/ppermute | solution.py:375
  67.3 0.0 collective-permute-done.11.by
  67.3 2.0 %collective-permute-start.15 = (bf16[16,1536]{1,0:T(8,128)(2,1)S(1)}, bf16[16,1536]{1,0:T(8,128)(2,1)S(1)}, u32[]{:S(2)}, u32[]{:S(2)}) collective-permute-start(bf16[16,1536]{1,0:T(8,128)(2,1)S(1)} %get-tuple-element.55), channel_id=1, source_target_pairs={{0,6},{2,4},{4,2},{6,0},{1,7},{3,5},{5,3},{7,1},{8,14},{10,12},{12... | collective-permute-start | bytes 147464 | tf_op jit(solution)/shard_map/ppermute | solution.py:375
  69.3 2.3 %project.6 = (f32[256,768]{1,0:T(8,128)S(1)}, f32[256,768]{1,0:T(8,128)S(1)}) custom-call(s32[3]{0:T(128)S(1)} %pad_add_fusion.place_ref, bf16[256,1024]{1,0:T(8,128)(2,1)S(1)} %hidden.2.rest_0_, bf16[256,1024]{1,0:T(8,128)(2,1)S(1)} %hidden.3.rest_1_, bf16[512,6144]{1,0:T(8,128)(2,1)S(1)} %get-tuple-element.41.rest_2_.rest_0_, ...), custom_call_target="tpu_custom_call" | custom-call | flops 1610612736 | bytes 6291456 | tf_op jit(solution)/shard_map/project/pallas_call | solution.py:566
  71.7 3.1 %collective-permute-done.10.bx = bf16[256,768]{1,0:T(8,128)(2,1)S(1)} collective-permute-done((bf16[256,768]{1,0:T(8,128)(2,1)S(1)}, bf16[256,768]{1,0:T(8,128)(2,1)S(1)}, u32[]{:S(2)}, u32[]{:S(2)}) %collective-permute-start.10) | collective-permute-done | bytes 393248 | tf_op jit(solution)/shard_map/ppermute | solution.py:375
  74.8 0.0 collective-permute-done.8.ay
  74.8 1.0 %finish.1 = bf16[1,256,1536]{2,1,0:T(8,128)(2,1)} custom-call(f32[256,768]{1,0:T(8,128)S(1)} %get-tuple-element.45.own_a, f32[256,768]{1,0:T(8,128)S(1)} %get-tuple-element.46.own_b, bf16[256,768]{1,0:T(8,128)(2,1)S(1)} %collective-permute-done.6.ax, bf16[256,768]{1,0:T(8,128)(2,1)S(1)} %collective-permute-done.8.ay, ...), custom_call_target="tpu_custom_call" | custom-call | flops 1179648 | bytes 3932160 | tf_op jit(solution)/shard_map/finish/pallas_call | solution.py:619
  75.8 0.0 collective-permute-done.13.x_ref
  75.8 0.0 collective-permute-done.14.y_ref
  75.8 0.3 collective-permute-done.15.far_ref
  76.1 0.6 decode_finish.1
Async XLA Ops:
  4.9 10.3 %collective-permute-start = (bf16[1040,128]{1,0:T(8,128)(2,1)S(1)}, bf16[1040,128]{1,0:T(8,128)(2,1)S(1)}, u32[]{:S(2)}, u32[]{:S(2)}) collective-permute-start(bf16[1040,128]{1,0:T(8,128)(2,1)S(1)} %get-tuple-element.35), channel_id=1, source_target_pairs={{0,8},{8,0},{16,24},{24,16},{1,9},{9,1},{17,25},{25,17},{2,10},{10... | collective-permute-start | bytes 798728 | tf_op jit(solution)/shard_map/ppermute | solution.py:502
  8.0 12.1 %collective-permute-start.3 = (bf16[1040,128]{1,0:T(8,128)(2,1)S(1)}, bf16[1040,128]{1,0:T(8,128)(2,1)S(1)}, u32[]{:S(2)}, u32[]{:S(2)}) collective-permute-start(bf16[1040,128]{1,0:T(8,128)(2,1)S(1)} %get-tuple-element.39), channel_id=1, source_target_pairs={{0,8},{8,0},{16,24},{24,16},{1,9},{9,1},{17,25},{25,17},{2,10},{10... | collective-permute-start | bytes 798728 | tf_op jit(solution)/shard_map/ppermute | solution.py:502
  15.9 5.8 %collective-permute-start.1 = (bf16[1040,128]{1,0:T(8,128)(2,1)S(1)}, bf16[1040,128]{1,0:T(8,128)(2,1)S(1)}, u32[]{:S(2)}, u32[]{:S(2)}) collective-permute-start(bf16[1040,128]{1,0:T(8,128)(2,1)S(1)} %chain.4), channel_id=1, source_target_pairs={{8,16},{16,8},{9,17},{17,9},{10,18},{18,10},{11,19},{19,11},{12,20... | collective-permute-start | bytes 798728 | tf_op jit(solution)/shard_map/ppermute | solution.py:502
  20.8 7.2 %collective-permute-start.4 = (bf16[1040,128]{1,0:T(8,128)(2,1)S(1)}, bf16[1040,128]{1,0:T(8,128)(2,1)S(1)}, u32[]{:S(2)}, u32[]{:S(2)}) collective-permute-start(bf16[1040,128]{1,0:T(8,128)(2,1)S(1)} %chain.6), channel_id=1, source_target_pairs={{8,16},{16,8},{9,17},{17,9},{10,18},{18,10},{11,19},{19,11},{12,20... | collective-permute-start | bytes 798728 | tf_op jit(solution)/shard_map/ppermute | solution.py:502
  22.4 13.5 %collective-permute-start.2 = (bf16[1040,128]{1,0:T(8,128)(2,1)S(1)}, bf16[1040,128]{1,0:T(8,128)(2,1)S(1)}, u32[]{:S(2)}, u32[]{:S(2)}) collective-permute-start(bf16[1040,128]{1,0:T(8,128)(2,1)S(1)} %chain.5), channel_id=1, source_target_pairs={{0,8},{8,0},{16,24},{24,16},{1,9},{9,1},{17,25},{25,17},{2,10},{10... | collective-permute-start | bytes 798728 | tf_op jit(solution)/shard_map/ppermute | solution.py:502
  28.7 9.6 %collective-permute-start.5 = (bf16[1040,128]{1,0:T(8,128)(2,1)S(1)}, bf16[1040,128]{1,0:T(8,128)(2,1)S(1)}, u32[]{:S(2)}, u32[]{:S(2)}) collective-permute-start(bf16[1040,128]{1,0:T(8,128)(2,1)S(1)} %chain.7.rest_0_), channel_id=1, source_target_pairs={{0,8},{8,0},{16,24},{24,16},{1,9},{9,1},{17,25},{25,17},{2,10},{10... | collective-permute-start | bytes 798728 | tf_op jit(solution)/shard_map/ppermute | solution.py:502
  42.7 15.9 %collective-permute-start.12 = (f32[16,128,128]{2,1,0:T(8,128)S(1)}, f32[16,128,128]{2,1,0:T(8,128)S(1)}, u32[]{:S(2)}, u32[]{:S(2)}) collective-permute-start(f32[16,128,128]{2,1,0:T(8,128)S(1)} %final_state.1.near_ref), channel_id=1, source_target_pairs={{0,1},{1,0},{2,3},{3,2},{4,5},{5,4},{6,7},{7,6},{8,9},{9,8},{10,11... | collective-permute-start | bytes 3145736 | tf_op jit(solution)/shard_map/ppermute | solution.py:375
  42.8 12.0 %collective-permute-start.9 = (bf16[256,768]{1,0:T(8,128)(2,1)S(1)}, bf16[256,768]{1,0:T(8,128)(2,1)S(1)}, u32[]{:S(2)}, u32[]{:S(2)}) collective-permute-start(bf16[256,768]{1,0:T(8,128)(2,1)S(1)} %project.10.rest_6_), channel_id=1, source_target_pairs={{0,4},{2,6},{4,0},{6,2},{1,5},{3,7},{5,1},{7,3},{8,12},{10,14},{12... | collective-permute-start | bytes 1179656 | tf_op jit(solution)/shard_map/ppermute | solution.py:375
  45.9 12.0 %collective-permute-start.7 = (bf16[256,768]{1,0:T(8,128)(2,1)S(1)}, bf16[256,768]{1,0:T(8,128)(2,1)S(1)}, u32[]{:S(2)}, u32[]{:S(2)}) collective-permute-start(bf16[256,768]{1,0:T(8,128)(2,1)S(1)} %project.9), channel_id=1, source_target_pairs={{0,2},{2,0},{4,6},{6,4},{1,3},{3,1},{5,7},{7,5},{8,10},{10,8},{12,... | collective-permute-start | bytes 1179656 | tf_op jit(solution)/shard_map/ppermute | solution.py:375
  49.0 17.3 %collective-permute-start.6 = (bf16[256,768]{1,0:T(8,128)(2,1)S(1)}, bf16[256,768]{1,0:T(8,128)(2,1)S(1)}, u32[]{:S(2)}, u32[]{:S(2)}) collective-permute-start(bf16[256,768]{1,0:T(8,128)(2,1)S(1)} %project.7), channel_id=1, source_target_pairs={{0,2},{2,0},{4,6},{6,4},{1,3},{3,1},{5,7},{7,5},{8,10},{10,8},{12,... | collective-permute-start | bytes 1179656 | tf_op jit(solution)/shard_map/ppermute | solution.py:375
  51.2 7.4 %copy-start = (f32[4,16,2]{1,2,0:T(2,128)S(1)}, f32[4,16,2]{1,2,0:T(2,128)}, u32[]{:S(2)}) copy-start(f32[4,16,2]{1,2,0:T(2,128)} %param.18) | copy-start | bytes 1540
  51.2 7.4 %copy-start.1 = (s32[4]{0:T(128)S(1)}, s32[4]{0:T(128)}, u32[]{:S(2)}) copy-start(s32[4]{0:T(128)} %prompt_ref.1) | copy-start | bytes 52
  51.2 16.1 %collective-permute-start.11 = (bf16[256,768]{1,0:T(8,128)(2,1)S(1)}, bf16[256,768]{1,0:T(8,128)(2,1)S(1)}, u32[]{:S(2)}, u32[]{:S(2)}) collective-permute-start(bf16[256,768]{1,0:T(8,128)(2,1)S(1)} %project.11), channel_id=1, source_target_pairs={{0,4},{2,6},{4,0},{6,2},{1,5},{3,7},{5,1},{7,3},{8,12},{10,14},{12... | collective-permute-start | bytes 1179656 | tf_op jit(solution)/shard_map/ppermute | solution.py:375
  54.8 20.0 %collective-permute-start.10 = (bf16[256,768]{1,0:T(8,128)(2,1)S(1)}, bf16[256,768]{1,0:T(8,128)(2,1)S(1)}, u32[]{:S(2)}, u32[]{:S(2)}) collective-permute-start(bf16[256,768]{1,0:T(8,128)(2,1)S(1)} %relay.3.rest_1_), channel_id=1, source_target_pairs={{0,2},{2,0},{4,6},{6,4},{1,3},{3,1},{5,7},{7,5},{8,10},{10,8},{12,... | collective-permute-start | bytes 1179656 | tf_op jit(solution)/shard_map/ppermute | solution.py:375
  58.0 16.8 %collective-permute-start.8 = (bf16[256,768]{1,0:T(8,128)(2,1)S(1)}, bf16[256,768]{1,0:T(8,128)(2,1)S(1)}, u32[]{:S(2)}, u32[]{:S(2)}) collective-permute-start(bf16[256,768]{1,0:T(8,128)(2,1)S(1)} %relay.2.rest_0_), channel_id=1, source_target_pairs={{0,4},{2,6},{4,0},{6,2},{1,5},{3,7},{5,1},{7,3},{8,12},{10,14},{12... | collective-permute-start | bytes 1179656 | tf_op jit(solution)/shard_map/ppermute | solution.py:375
  64.2 11.5 %collective-permute-start.13 = (bf16[16,1536]{1,0:T(8,128)(2,1)S(1)}, bf16[16,1536]{1,0:T(8,128)(2,1)S(1)}, u32[]{:S(2)}, u32[]{:S(2)}) collective-permute-start(bf16[16,1536]{1,0:T(8,128)(2,1)S(1)} %get-tuple-element.53), channel_id=1, source_target_pairs={{0,2},{2,0},{4,6},{6,4},{1,3},{3,1},{5,7},{7,5},{8,10},{10,8},{12,... | collective-permute-start | bytes 147464 | tf_op jit(solution)/shard_map/ppermute | solution.py:375
  66.4 9.4 %collective-permute-start.14 = (bf16[16,1536]{1,0:T(8,128)(2,1)S(1)}, bf16[16,1536]{1,0:T(8,128)(2,1)S(1)}, u32[]{:S(2)}, u32[]{:S(2)}) collective-permute-start(bf16[16,1536]{1,0:T(8,128)(2,1)S(1)} %get-tuple-element.54), channel_id=1, source_target_pairs={{0,4},{2,6},{4,0},{6,2},{1,5},{3,7},{5,1},{7,3},{8,12},{10,14},{12... | collective-permute-start | bytes 147464 | tf_op jit(solution)/shard_map/ppermute | solution.py:375
  67.3 8.8 %collective-permute-start.15 = (bf16[16,1536]{1,0:T(8,128)(2,1)S(1)}, bf16[16,1536]{1,0:T(8,128)(2,1)S(1)}, u32[]{:S(2)}, u32[]{:S(2)}) collective-permute-start(bf16[16,1536]{1,0:T(8,128)(2,1)S(1)} %get-tuple-element.55), channel_id=1, source_target_pairs={{0,6},{2,4},{4,2},{6,0},{1,7},{3,5},{5,3},{7,1},{8,14},{10,12},{12... | collective-permute-start | bytes 147464 | tf_op jit(solution)/shard_map/ppermute | solution.py:375

commit v6 on v5

--- a/solution.py
+++ b/solution.py
@@ -107,55 +107,56 @@
     return message_ref[index * HEAD_DIM : (index + 1) * HEAD_DIM, :]
 
 
-def state_kernel(chunks, place_ref, *refs):
-    k_hbm, v_hbm, rate_hbm, q_hbm, dq_hbm, dk_hbm, dv_hbm = refs[:7]
-    own_ref, log_ref, col_ref, row_ref = refs[7:11]
-    k_ref, v_ref, q_ref, dq_ref, dk_ref, dv_ref = refs[11:17]
-    messages = refs[17 : 17 + len(chunks)]
-    rate_ref, sems = refs[17 + len(chunks) :]
-    heads = own_ref.shape[0]
-    pairs = (
-        (rate_hbm, rate_ref),
-        (k_hbm.at[0], k_ref),
-        (v_hbm.at[0], v_ref),
-        (dq_hbm, dq_ref),
-        (dk_hbm, dk_ref),
-        (dv_hbm, dv_ref),
-        (q_hbm, q_ref),
-    )
+def own_states(first, k_ref, v_ref, columns, own_ref, message_ref):
+    length = columns.shape[0]
+    factor = jnp.exp(columns[length - 1 :, :] - columns)
+    for i in range(own_ref.shape[0]):
+        h = first + i
+        at = head_slice(h)
+        weighted = k_ref[:, at].astype(F32) * factor[:, h : h + 1]
+        top, rest = halves(weighted)
+        both = lax.dot_general(
+            jnp.concatenate([top, rest], axis=1), v_ref[:, at], TN, preferred_element_type=F32
+        )
+        state = both[:HEAD_DIM] + both[HEAD_DIM:]
+        own_ref[i] = state
+        message_ref[i * HEAD_DIM : (i + 1) * HEAD_DIM, :] = state.astype(BF16)
+
+
+def started(pairs, sems):
     copies = [
         pltpu.make_async_copy(source, target, sems.at[i]) for i, (source, target) in enumerate(pairs)
     ]
     for copy in copies:
         copy.start()
+    return copies
+
+
+def first_state_kernel(place_ref, k_hbm, v_hbm, rate_hbm, *refs):
+    own_ref, log_ref, col_ref, rate_ref, k_ref, v_ref, message_ref, sems = refs
+    copies = started(((rate_hbm, rate_ref), (k_hbm.at[0], k_ref), (v_hbm.at[0], v_ref)), sems)
     length = k_ref.shape[0]
-    lower = lower_ones(length)
     copies[0].wait()
     rate = rate_ref[0]
-    columns = decay_columns(rate, lower)
+    columns = decay_columns(rate, lower_ones(length))
     col_ref[...] = columns
-    row_ref[...] = decay_rows(rate, lower)
-    total = columns[length - 1 :, :]
-    factor = jnp.exp(total - columns)
     log_ref[...] = jnp.zeros_like(log_ref)
-    log_ref[:, :heads] = total
-    facts = log_rows(log_ref[...])
+    log_ref[:, : rate.shape[0]] = columns[length - 1 :, :]
+    message_ref[message_ref.shape[0] - LOG_ROWS :, :] = log_rows(log_ref[...])
     copies[1].wait()
     copies[2].wait()
-    for (first, size), message_ref in zip(chunks, messages):
-        for i in range(size):
-            h = first + i
-            at = head_slice(h)
-            weighted = k_ref[:, at].astype(F32) * factor[:, h : h + 1]
-            top, rest = halves(weighted)
-            both = lax.dot_general(
-                jnp.concatenate([top, rest], axis=1), v_ref[:, at], TN, preferred_element_type=F32
-            )
-            state = both[:HEAD_DIM] + both[HEAD_DIM:]
-            own_ref[h] = state
-            message_ref[i * HEAD_DIM : (i + 1) * HEAD_DIM, :] = state.astype(BF16)
-        message_ref[size * HEAD_DIM :, :] = facts
-    for copy in copies[3:]:
+    own_states(0, k_ref, v_ref, columns, own_ref, message_ref)
+
+
+def more_state_kernel(first, copied, k_ref, v_ref, col_ref, rate_ref, log_ref, *refs):
+    sources, refs = refs[:copied], refs[copied:]
+    own_ref, message_ref, row_ref = refs[:3]
+    targets, sems = refs[3 : 3 + copied], refs[3 + copied]
+    copies = started(tuple(zip(sources, targets)), sems) if copied else []
+    row_ref[...] = decay_rows(rate_ref[0], lower_ones(k_ref.shape[0]))
+    message_ref[message_ref.shape[0] - LOG_ROWS :, :] = log_rows(log_ref[...])
+    own_states(first, k_ref, v_ref, col_ref[...], own_ref, message_ref)
+    for copy in copies:
         copy.wait()
 
 
@@ -170,7 +171,7 @@
     for i in range(size):
         h = first + i
         value = (
-            own_factor[:, h : h + 1] * own_ref[h]
+            own_factor[:, h : h + 1] * own_ref[i]
             + got_factor[:, h : h + 1] * state_rows(got_ref, i).astype(F32)
         )
         out_ref[i * HEAD_DIM : (i + 1) * HEAD_DIM, :] = value.astype(BF16)
@@ -234,25 +235,23 @@
         hidden_ref[:, head_slice(i)] = normalize(attended).astype(BF16)
 
 
-def final_kernel(chunks, phases, place_ref, own_ref, log_ref, *rest):
-    out_ref = rest[-1]
+def final_kernel(first, phases, place_ref, own_ref, log_ref, *rest):
+    got, out_ref = rest[:phases], rest[-1]
     group = place_ref[0]
     keep = jnp.exp(log_ref[...])
-    for c, (first, size) in enumerate(chunks):
-        got = [rest[phase * len(chunks) + c] for phase in range(phases)]
-        later = jnp.zeros((1, HEAD_DIM), F32)
+    later = jnp.zeros((1, HEAD_DIM), F32)
+    for phase in range(phases):
+        later = jnp.where(group == phases - 1 - phase, read_log(got[phase]), later)
+    later = jnp.exp(later)
+    for i in range(out_ref.shape[0]):
+        h = first + i
+        suffix = jnp.zeros((HEAD_DIM, HEAD_DIM), F32)
         for phase in range(phases):
-            later = jnp.where(group == phases - 1 - phase, read_log(got[phase]), later)
-        later = jnp.exp(later)
-        for i in range(size):
-            h = first + i
-            suffix = jnp.zeros((HEAD_DIM, HEAD_DIM), F32)
-            for phase in range(phases):
-                there = state_rows(got[phase], i).astype(F32)
-                suffix = jnp.where(group == phases - 1 - phase, there, suffix)
-            prefix = entering_state(group, got, i).astype(F32)
-            here = own_ref[h] + keep[:, h : h + 1] * prefix
-            out_ref[h] = suffix + later[:, h : h + 1] * here
+            there = state_rows(got[phase], i).astype(F32)
+            suffix = jnp.where(group == phases - 1 - phase, there, suffix)
+        prefix = entering_state(group, got, i).astype(F32)
+        here = own_ref[i] + keep[:, h : h + 1] * prefix
+        out_ref[i] = suffix + later[:, h : h + 1] * here
 
 
 def flat_rows(ref, rows_ref):
@@ -261,7 +260,9 @@
         rows_ref[r * steps : (r + 1) * steps, :] = ref[r].astype(F32)
 
 
-def decode_kernel(place_ref, prompt_ref, q_ref, k_ref, v_ref, rate_ref, near_ref, far_ref, *rest):
+def decode_kernel(count, place_ref, prompt_ref, q_ref, k_ref, v_ref, rate_ref, *rest):
+    near, far = rest[:count], rest[count : 2 * count]
+    finals = [(c, i) for c, ref in enumerate(near) for i in range(ref.shape[0])]
     out_ref, q_rows, k_rows, v_rows, rate_rows = rest[-5:]
     rows_here, steps = q_ref.shape[0], q_ref.shape[1]
     d_rows = q_rows.shape[0]
@@ -288,8 +289,9 @@
         query = q_rows[:, at]
         narrow = query.astype(BF16)
         terms = []
-        for ref in (near_ref, far_ref):
-            top, low = halves(ref[i])
+        c, slot = finals[i]
+        for ref in (near[c], far[c]):
+            top, low = halves(ref[slot])
             both = jnp.dot(
                 narrow, jnp.concatenate([top, low], axis=1), preferred_element_type=F32
             )
@@ -340,19 +342,13 @@
         out_ref[...] = times_weight(rows, weights, column, width).astype(out_ref.dtype)
 
 
-def decode_finish_kernel(own_ref, x_ref, y_ref, far_ref, out_ref):
-    rows, steps = out_ref.shape[0], out_ref.shape[1]
-    total = own_ref[...] + x_ref[...].astype(F32) + y_ref[...].astype(F32) + far_ref[...].astype(F32)
-    for r in range(rows):
-        out_ref[r] = total[r * steps : (r + 1) * steps].astype(BF16)
-
-
 def relay_kernel(own_ref, got_ref, *rest):
     out_ref = rest[-1]
     out_ref[...] = (own_ref[...] + got_ref[...].astype(F32)).astype(BF16)
 
 
-def finish_kernel(own_a, own_b, ax, ay, bx, by, prefill_hbm, out_ref, sems):
+def finish_kernel(own_a, own_b, ax, ay, bx, by, d_own, d_x, d_y, d_far, *rest):
+    prefill_hbm, decode_ref, out_ref, sems = rest
     width = own_a.shape[1]
     count = sems.shape[0]
     size = out_ref.shape[0] // count
@@ -367,6 +363,10 @@
         )
         copy.start()
         copies.append(copy)
+    rows, steps = decode_ref.shape[0], decode_ref.shape[1]
+    total = d_own[...] + d_x[...].astype(F32) + d_y[...].astype(F32) + d_far[...].astype(F32)
+    for r in range(rows):
+        decode_ref[r] = total[r * steps : (r + 1) * steps].astype(BF16)
     for copy in copies:
         copy.wait()
 
@@ -416,42 +416,42 @@
 
     decode_shape = (rows_here, steps, features)
     made = call(
-        functools.partial(state_kernel, chunks),
+        first_state_kernel,
         "own_state",
-        [SMEM] + [HBM] * 7,
+        [SMEM] + [HBM] * 3,
         [
-            pltpu.VMEM((heads, HEAD_DIM, HEAD_DIM), F32),
+            pltpu.VMEM((chunks[0][1], HEAD_DIM, HEAD_DIM), F32),
             pltpu.VMEM((1, HEAD_DIM), F32),
             pltpu.VMEM((length, heads), F32),
-            pltpu.VMEM((heads, length), F32),
+            pltpu.VMEM((1, heads, length), F32),
             pltpu.VMEM((length, features), BF16),
             pltpu.VMEM((length, features), BF16),
-            pltpu.VMEM((1, length, features), BF16),
-            pltpu.VMEM(decode_shape, BF16),
-            pltpu.VMEM(decode_shape, BF16),
-            pltpu.VMEM(decode_shape, BF16),
-        ]
-        + [message_shape(size) for _, size in chunks],
-        [pltpu.VMEM((1, heads, length), F32), pltpu.SemaphoreType.DMA((7,))],
-        cost(4 * length * features * HEAD_DIM, 34 * length * features),
-    )(
-        place,
-        *[
-            in_hbm(array)
-            for array in (
-                prefill_key,
-                prefill_value,
-                prefill_rate,
-                prefill_query,
-                decode_query,
-                decode_key,
-                decode_value,
-            )
+            message_shape(chunks[0][1]),
         ],
-    )
-    own, log_row, columns, rows, keys, values, queries, d_query, d_key, d_value = map(
-        in_vmem, made[:10]
-    )
+        [pltpu.SemaphoreType.DMA((3,))],
+        cost(4 * length * features * HEAD_DIM, 16 * length * features),
+    )(place, in_hbm(prefill_key), in_hbm(prefill_value), in_hbm(prefill_rate))
+    own, log_row, columns, rate, keys, values = map(in_vmem, made[:6])
+    owns, values_out = [own], [made[6]]
+    for c, (first, size) in enumerate(chunks[1:]):
+        arrays = (prefill_query, decode_query, decode_key, decode_value) if c == 0 else ()
+        made = call(
+            functools.partial(more_state_kernel, first, len(arrays)),
+            "more_state",
+            [VMEM] * 5 + [HBM] * len(arrays),
+            [
+                pltpu.VMEM((size, HEAD_DIM, HEAD_DIM), F32),
+                message_shape(size),
+                pltpu.VMEM((heads, length), F32),
+            ]
+            + [pltpu.VMEM(array.shape, BF16) for array in arrays],
+            [pltpu.SemaphoreType.DMA((max(len(arrays), 1),))],
+            cost(4 * length * size * HEAD_DIM * HEAD_DIM, 8 * length * features),
+        )(keys, values, columns, rate, log_row, *map(in_hbm, arrays))
+        owns.append(in_vmem(made[0]))
+        values_out.append(made[1])
+        if c == 0:
+            rows, queries, d_query, d_key, d_value = map(in_vmem, made[2:])
 
     weight_hbm = in_hbm(out_weight)
     weight_part = pltpu.VMEM((features // WEIGHT_PARTS, out_weight.shape[1]), BF16)
@@ -480,12 +480,10 @@
         weights.append(part)
         return [done]
 
-    values_out = list(made[10:])
     received = []
     after = [local_token]
     for phase in range(phases):
-        pairs = {(phase, phase + 1), (groups - 2 - phase, groups - 1 - phase)}
-        pairs = sorted(pairs | {(b, a) for a, b in pairs})
+        pairs = [(phase, phase + 1), (groups - 1 - phase, groups - 2 - phase)]
         if phase > 0:
             values_out = []
             for c, (first, size) in enumerate(chunks):
@@ -496,7 +494,7 @@
                     message_shape(size),
                     (),
                     cost(2 * size * HEAD_DIM * HEAD_DIM, 24 * size * HEAD_DIM * HEAD_DIM),
-                )(place, own, log_row, received[-1][c], *after)
+                )(place, owns[c], log_row, received[-1][c], *after)
                 values_out.append(value)
                 after = []
         received.append([lax.ppermute(value, "ctx", pairs) for value in values_out])
@@ -519,22 +517,27 @@
     ]
 
     def final_states(*after):
-        final = call(
-            functools.partial(final_kernel, chunks, phases),
-            "final_state",
-            [SMEM, VMEM, VMEM] + [VMEM] * (phases * count) + [ANY] * len(after),
-            sds((heads, HEAD_DIM, HEAD_DIM), F32),
-            (),
-            cost(4 * state_elements, state_elements * 4 * phases),
-        )(place, own, log_row, *[got for phase in received for got in phase], *after)
-        return final, swap(final, "rep", reps, 1)
-
-    def decode_rows(final, other, *after):
+        finals = []
+        for c, (first, size) in enumerate(chunks):
+            gate = after if c == count - 1 else ()
+            finals.append(
+                call(
+                    functools.partial(final_kernel, first, phases),
+                    "final_state",
+                    [SMEM, VMEM, VMEM] + [VMEM] * phases + [ANY] * len(gate),
+                    sds((size, HEAD_DIM, HEAD_DIM), F32),
+                    (),
+                    cost(4 * state_elements // count, state_elements * 4),
+                )(place, owns[c], log_row, *[got[c] for got in received], *gate)
+            )
+        return finals, [swap(final, "rep", reps, 1) for final in finals]
+
+    def decode_rows(finals, others, *after):
         flat = pltpu.VMEM((d_rows, features), F32)
         return call(
-            decode_kernel,
+            functools.partial(decode_kernel, count),
             "decode_rows",
-            [SMEM, SMEM] + [VMEM] * 6 + [ANY] * len(after),
+            [SMEM, SMEM] + [VMEM] * (4 + 2 * count) + [ANY] * len(after),
             sds((d_pad, features), BF16),
             [flat, flat, flat, pltpu.VMEM((d_rows, heads), F32)],
             cost(16 * d_rows * features * HEAD_DIM, state_elements),
@@ -545,8 +548,8 @@
             d_key,
             d_value,
             jnp.transpose(decode_rate, (0, 2, 1)),
-            final,
-            other,
+            *finals,
+            *others,
             *after,
         )
 
@@ -602,29 +605,26 @@
         (),
         cost(2 * d_pad * features * out_columns, features * out_columns // 8),
     )(place, d_hidden, *weights)
-    decode_out = call(
-        decode_finish_kernel,
-        "decode_finish",
-        [VMEM] * 4,
-        sds((rows_here, steps, width), BF16),
-        (),
-        cost(4 * d_pad * width, 10 * d_pad * width),
+    prefill_out, decode_out = call(
+        finish_kernel,
+        "finish",
+        [VMEM] * 10,
+        [sds((1, length, width), BF16), sds((rows_here, steps, width), BF16)],
+        [pltpu.VMEM((length, width), BF16), pltpu.SemaphoreType.DMA((4,))],
+        cost(6 * length * half, 20 * length * half),
+        out_specs=[HBM, VMEM],
     )(
+        own_a,
+        own_b,
+        x_a,
+        y_a,
+        x_b,
+        y_b,
         d_own,
         swap(d_x, "head", parts, 1),
         swap(d_y, "head", parts, 2),
         swap(d_far, "head", parts, 3),
     )
-
-    prefill_out = call(
-        finish_kernel,
-        "finish",
-        [VMEM] * 6,
-        sds((1, length, width), BF16),
-        [pltpu.VMEM((length, width), BF16), pltpu.SemaphoreType.DMA((4,))],
-        cost(6 * length * half, 20 * length * half),
-        out_specs=HBM,
-    )(own_a, own_b, x_a, y_a, x_b, y_b)
     return prefill_out, decode_out
 
 

time: 76.9 us -> 81.2 us (1.056)
  waiting for transfers between devices: 11.1 us -> 19.3 us
  starting transfers between devices: 25.6 us -> 20.5 us
  Pallas kernels: 39 us -> 39.9 us
    ppermute x6, waiting for transfers between devices: 4.97 us -> 11.9 us  [body(): received.append([lax.ppermute(value, 'ctx', pairs) for value in values_out])]
    ppermute x6, starting transfers between devices: 14.7 us -> 10.4 us  [body(): received.append([lax.ppermute(value, 'ctx', pairs) for value in values_out])]
    ppermute x10 -> x11, waiting for transfers between devices: 6.18 us -> 7.42 us  [swap(): return lax.ppermute(array, axis, [(i, i ^ bit) for i in range(size)])]
    pallas_call x5 -> x6, Pallas kernels: 8.63 us -> 9.51 us  [the longest x1 3.24 us: body(): call(first_state_kernel, 'own_state', [SMEM] + [HBM] * 3, [pltpu.VMEM((ch...]
    ppermute x10 -> x11, starting transfers between devices: 10.9 us -> 10.1 us  [swap(): return lax.ppermute(array, axis, [(i, i ^ bit) for i in range(size)])]
  transfers between devices with their start and end apart: 16 -> 17, of which waited for: 8 -> 7; matrix products, arithmetic and copies ran while one was open for 0% -> 0% of each run, Pallas kernels for 39% -> 39%
where the time goes in v6:
time: 81.2 us; the launch traced here: 80.9 us
  Pallas kernels  39.9 us (49%)
  starting transfers between devices  20.5 us (25%)
  waiting for transfers between devices  19.3 us (24%)
  between operations  1.04 us (1%)
    ppermute x6, waiting for transfers between devices, body(): received.append([lax.ppermute(value, 'ctx', pairs) for value in values_out])  11.9 us
    pallas_call x6, Pallas kernels, project(): call(functools.partial(project_kernel, pieces, count), 'project', [SMEM]...  10.9 us
    ppermute x6, starting transfers between devices, body(): received.append([lax.ppermute(value, 'ctx', pairs) for value in values_out])  10.4 us
    ppermute x11, starting transfers between devices, swap(): return lax.ppermute(array, axis, [(i, i ^ bit) for i in range(size)])  10.1 us
    ppermute x11, waiting for transfers between devices, swap(): return lax.ppermute(array, axis, [(i, i ^ bit) for i in range(size)])  7.42 us
    pallas_call x1, Pallas kernels, body(): call(functools.partial(local_kernel, 0), 'local_attention', [VMEM] * 5 +...  6.43 us
    pallas_call x1, Pallas kernels, body(): call(decode_project_kernel, 'decode_project', [SMEM] + [VMEM] * (1 + WEIG...  3.92 us
    pallas_call x1, Pallas kernels, body(): call(first_state_kernel, 'own_state', [SMEM] + [HBM] * 3, [pltpu.VMEM((ch...  3.24 us
  transfers between devices with their start and end apart: 17, of which 7 were waited for; matrix products, arithmetic and copies ran while one was open for 0% of the time, Pallas kernels for 39%

profile of v6, /device:TPU:0, one launch (start us, length us, event | category | flops | bytes accessed | tf_op | source)
XLA Modules:
  0.0 80.9 jit_solution(3475005455125936006)
XLA Ops:
  0.6 0.1 pad_add_fusion.place_ref
  0.7 3.2 %own_state.1 = (f32[8,128,128]{2,1,0:T(8,128)S(1)}, f32[1,128]{1,0:T(1,128)S(1)}, f32[256,16]{1,0:T(8,128)S(1)}, f32[1,16,256]{2,1,0:T(8,128)S(1)}, bf16[256,204...) custom-call(s32[3]{0:T(128)S(1)} %pad_add_fusion.place_ref, ...), custom_call_target="tpu_custom_call" | custom-call | flops 268435456 | bytes 8388608 | tf_op jit(solution)/shard_map/own_state/pallas_call | solution.py:418
  4.0 4.9 %collective-permute-start = (bf16[1040,128]{1,0:T(8,128)(2,1)S(1)}, bf16[1040,128]{1,0:T(8,128)(2,1)S(1)}, u32[]{:S(2)}, u32[]{:S(2)}) collective-permute-start(bf16[1040,128]{1,0:T(8,128)(2,1)S(1)} %get-tuple-element.39), channel_id=1, source_target_pairs={{0,8},{24,16},{1,9},{25,17},{2,10},{26,18},{3,11},{27,19},{4,12},{... | collective-permute-start | bytes 798728 | tf_op jit(solution)/shard_map/ppermute | solution.py:500
  8.9 1.3 %more_state.1 = (f32[8,128,128]{2,1,0:T(8,128)S(1)}, bf16[1040,128]{1,0:T(8,128)(2,1)S(1)}, f32[16,256]{1,0:T(8,128)S(1)}, bf16[1,256,2048]{2,1,0:T(8,128)(2,1)S...) custom-call(bf16[256,2048]{1,0:T(8,128)(2,1)S(1)} %get-tuple-element.31.k_ref, ...), custom_call_target="tpu_custom_call" | custom-call | flops 134217728 | bytes 4194304 | tf_op jit(solution)/shard_map/more_state/pallas_call | solution.py:438
  10.2 1.3 %collective-permute-start.3 = (bf16[1040,128]{1,0:T(8,128)(2,1)S(1)}, bf16[1040,128]{1,0:T(8,128)(2,1)S(1)}, u32[]{:S(2)}, u32[]{:S(2)}) collective-permute-start(bf16[1040,128]{1,0:T(8,128)(2,1)S(1)} %get-tuple-element.43), channel_id=1, source_target_pairs={{0,8},{24,16},{1,9},{25,17},{2,10},{26,18},{3,11},{27,19},{4,12},{... | collective-permute-start | bytes 798728 | tf_op jit(solution)/shard_map/ppermute | solution.py:500
  11.5 6.4 %local_attention.1 = (f32[256,2048]{1,0:T(8,128)S(1)}, f32[8,128]{1,0:T(8,128)S(1)}, bf16[512,6144]{1,0:T(8,128)(2,1)S(1)}, bf16[512,6144]{1,0:T(8,128)(2,1)S(1)}, bf16[512,6144]{1,0:T(8,128)(2,1)S(1)}) custom-call(bf16[1,256,2048]{2,1,0:T(8,128)(2,1)S(1)} %get-tuple-element.36.q_ref, bf16[256,2048]{1,0:T(8,128)(2,1)S(1)} %get-tuple-element.31.k_ref, ...), custom_call_target="tpu_custom_call" | custom-call | flops 536870912 | bytes 6291456 | tf_op jit(solution)/shard_map/local_attention/pallas_call | solution.py:459
  17.9 0.0 collective-permute-done.got_ref.rest_0_
  18.0 0.7 chain.4
  18.7 0.7 collective-permute-start.1
  19.4 0.9 %collective-permute-done.3.got_ref.rest_0_ = bf16[1040,128]{1,0:T(8,128)(2,1)S(1)} collective-permute-done((bf16[1040,128]{1,0:T(8,128)(2,1)S(1)}, bf16[1040,128]{1,0:T(8,128)(2,1)S(1)}, u32[]{:S(2)}, u32[]{:S(2)}) %collective-permute-start.3) | collective-permute-done | bytes 266272 | tf_op jit(solution)/shard_map/ppermute | solution.py:500
  20.2 0.7 chain.6
  21.0 0.7 collective-permute-start.4
  21.7 0.0 collective-permute-done.1.got_ref.rest_1_
  21.7 0.7 chain.5
  22.4 1.3 %collective-permute-start.2 = (bf16[1040,128]{1,0:T(8,128)(2,1)S(1)}, bf16[1040,128]{1,0:T(8,128)(2,1)S(1)}, u32[]{:S(2)}, u32[]{:S(2)}) collective-permute-start(bf16[1040,128]{1,0:T(8,128)(2,1)S(1)} %chain.5), channel_id=1, source_target_pairs={{16,24},{8,0},{17,25},{9,1},{18,26},{10,2},{19,27},{11,3},{20,28},... | collective-permute-start | bytes 798728 | tf_op jit(solution)/shard_map/ppermute | solution.py:500
  23.7 0.0 collective-permute-done.4.got_ref.rest_1_
  23.7 0.7 chain.7.rest_0_
  24.4 1.5 %collective-permute-start.5 = (bf16[1040,128]{1,0:T(8,128)(2,1)S(1)}, bf16[1040,128]{1,0:T(8,128)(2,1)S(1)}, u32[]{:S(2)}, u32[]{:S(2)}) collective-permute-start(bf16[1040,128]{1,0:T(8,128)(2,1)S(1)} %chain.7.rest_0_), channel_id=1, source_target_pairs={{16,24},{8,0},{17,25},{9,1},{18,26},{10,2},{19,27},{11,3},{20,28},... | collective-permute-start | bytes 798728 | tf_op jit(solution)/shard_map/ppermute | solution.py:500
  25.9 2.8 %load_weight.1 = (bf16[512,6144]{1,0:T(8,128)(2,1)S(1)}, f32[8,128]{1,0:T(8,128)S(1)}) custom-call(bf16[2048,6144]{1,0:T(8,128)(2,1)} %weight_hbm.3, bf16[1040,128]{1,0:T(8,128)(2,1)S(1)} %chain.7.rest_0_), custom_call_target="tpu_custom_call" | custom-call | flops 1 | bytes 6291456 | tf_op jit(solution)/shard_map/load_weight/pallas_call | solution.py:472
  28.7 6.8 %collective-permute-done.2.rest_2_ = bf16[1040,128]{1,0:T(8,128)(2,1)S(1)} collective-permute-done((bf16[1040,128]{1,0:T(8,128)(2,1)S(1)}, bf16[1040,128]{1,0:T(8,128)(2,1)S(1)}, u32[]{:S(2)}, u32[]{:S(2)}) %collective-permute-start.2) | collective-permute-done | bytes 266272 | tf_op jit(solution)/shard_map/ppermute | solution.py:500
  35.6 1.6 %hidden.2.rest_0_ = bf16[256,1024]{1,0:T(8,128)(2,1)S(1)} custom-call(s32[3]{0:T(128)S(1)} %pad_add_fusion.place_ref, bf16[1,256,2048]{2,1,0:T(8,128)(2,1)S(1)} %get-tuple-element.36.q_ref, f32[256,16]{1,0:T(8,128)S(1)} %get-tuple-element.33.col_ref, f32[256,2048]{1,0:T(8,128)S(1)} %get-tuple-element.38.local_ref, ...), custom_call_target="tpu_custom_call" | custom-call | flops 67108864 | bytes 5242880 | tf_op jit(solution)/shard_map/hidden/pallas_call | solution.py:508
  37.2 4.2 %collective-permute-done.5.rest_2_ = bf16[1040,128]{1,0:T(8,128)(2,1)S(1)} collective-permute-done((bf16[1040,128]{1,0:T(8,128)(2,1)S(1)}, bf16[1040,128]{1,0:T(8,128)(2,1)S(1)}, u32[]{:S(2)}, u32[]{:S(2)}) %collective-permute-start.5) | collective-permute-done | bytes 266272 | tf_op jit(solution)/shard_map/ppermute | solution.py:500
  41.3 1.6 %hidden.3.rest_1_ = bf16[256,1024]{1,0:T(8,128)(2,1)S(1)} custom-call(s32[3]{0:T(128)S(1)} %pad_add_fusion.place_ref, bf16[1,256,2048]{2,1,0:T(8,128)(2,1)S(1)} %get-tuple-element.36.q_ref, f32[256,16]{1,0:T(8,128)S(1)} %get-tuple-element.33.col_ref, f32[256,2048]{1,0:T(8,128)S(1)} %get-tuple-element.38.local_ref, ...), custom_call_target="tpu_custom_call" | custom-call | flops 67108864 | bytes 5242880 | tf_op jit(solution)/shard_map/hidden/pallas_call | solution.py:508
  43.0 1.6 %project.10.rest_3_ = bf16[256,768]{1,0:T(8,128)(2,1)S(1)} custom-call(s32[3]{0:T(128)S(1)} %pad_add_fusion.place_ref, bf16[256,1024]{1,0:T(8,128)(2,1)S(1)} %hidden.2.rest_0_, bf16[256,1024]{1,0:T(8,128)(2,1)S(1)} %hidden.3.rest_1_, bf16[512,6144]{1,0:T(8,128)(2,1)S(1)} %get-tuple-element.45.rest_2_.rest_0_, ...), custom_call_target="tpu_custom_call" | custom-call | flops 805306368 | bytes 3145728 | tf_op jit(solution)/shard_map/project/pallas_call | solution.py:569
  44.5 1.6 %collective-permute-start.9 = (bf16[256,768]{1,0:T(8,128)(2,1)S(1)}, bf16[256,768]{1,0:T(8,128)(2,1)S(1)}, u32[]{:S(2)}, u32[]{:S(2)}) collective-permute-start(bf16[256,768]{1,0:T(8,128)(2,1)S(1)} %project.10.rest_3_), channel_id=1, source_target_pairs={{0,4},{2,6},{4,0},{6,2},{1,5},{3,7},{5,1},{7,3},{8,12},{10,14},{12... | collective-permute-start | bytes 1179656 | tf_op jit(solution)/shard_map/ppermute | solution.py:375
  46.1 0.8 %final_state.3.rest_1_ = f32[8,128,128]{2,1,0:T(8,128)S(1)} custom-call(s32[3]{0:T(128)S(1)} %pad_add_fusion.place_ref, f32[8,128,128]{2,1,0:T(8,128)S(1)} %get-tuple-element.42.own_ref, f32[1,128]{1,0:T(1,128)S(1)} %get-tuple-element.35.log_ref, bf16[1040,128]{1,0:T(8,128)(2,1)S(1)} %collective-permute-done.3.got_ref.rest_0_, ...), custom_call_target="tpu_custom_call" | custom-call | flops 524288 | bytes 1048576 | tf_op jit(solution)/shard_map/final_state/pallas_call | solution.py:524
  47.0 0.1 collective-permute-start.13
  47.1 1.6 %project.9 = bf16[256,768]{1,0:T(8,128)(2,1)S(1)} custom-call(s32[3]{0:T(128)S(1)} %pad_add_fusion.place_ref, bf16[256,1024]{1,0:T(8,128)(2,1)S(1)} %hidden.2.rest_0_, bf16[256,1024]{1,0:T(8,128)(2,1)S(1)} %hidden.3.rest_1_, bf16[512,6144]{1,0:T(8,128)(2,1)S(1)} %get-tuple-element.45.rest_2_.rest_0_, ...), custom_call_target="tpu_custom_call" | custom-call | flops 805306368 | bytes 3145728 | tf_op jit(solution)/shard_map/project/pallas_call | solution.py:569
  48.6 1.5 %collective-permute-start.7 = (bf16[256,768]{1,0:T(8,128)(2,1)S(1)}, bf16[256,768]{1,0:T(8,128)(2,1)S(1)}, u32[]{:S(2)}, u32[]{:S(2)}) collective-permute-start(bf16[256,768]{1,0:T(8,128)(2,1)S(1)} %project.9), channel_id=1, source_target_pairs={{0,2},{2,0},{4,6},{6,4},{1,3},{3,1},{5,7},{7,5},{8,10},{10,8},{12,... | collective-permute-start | bytes 1179656 | tf_op jit(solution)/shard_map/ppermute | solution.py:375
  50.2 0.8 %final_state.2.rest_0_ = f32[8,128,128]{2,1,0:T(8,128)S(1)} custom-call(s32[3]{0:T(128)S(1)} %pad_add_fusion.place_ref, f32[8,128,128]{2,1,0:T(8,128)S(1)} %get-tuple-element.40.own_ref, f32[1,128]{1,0:T(1,128)S(1)} %get-tuple-element.35.log_ref, bf16[1040,128]{1,0:T(8,128)(2,1)S(1)} %collective-permute-done.got_ref.rest_0_, ...), custom_call_target="tpu_custom_call" | custom-call | flops 524288 | bytes 1048576 | tf_op jit(solution)/shard_map/final_state/pallas_call | solution.py:524
  51.0 0.3 collective-permute-start.12
  51.3 1.5 %project.11 = bf16[256,768]{1,0:T(8,128)(2,1)S(1)} custom-call(s32[3]{0:T(128)S(1)} %pad_add_fusion.place_ref, bf16[256,1024]{1,0:T(8,128)(2,1)S(1)} %hidden.2.rest_0_, bf16[256,1024]{1,0:T(8,128)(2,1)S(1)} %hidden.3.rest_1_, bf16[512,6144]{1,0:T(8,128)(2,1)S(1)} %get-tuple-element.45.rest_2_.rest_0_, ...), custom_call_target="tpu_custom_call" | custom-call | flops 805306368 | bytes 3145728 | tf_op jit(solution)/shard_map/project/pallas_call | solution.py:569
  52.9 1.6 %project.7 = bf16[256,768]{1,0:T(8,128)(2,1)S(1)} custom-call(s32[3]{0:T(128)S(1)} %pad_add_fusion.place_ref, bf16[256,1024]{1,0:T(8,128)(2,1)S(1)} %hidden.2.rest_0_, bf16[256,1024]{1,0:T(8,128)(2,1)S(1)} %hidden.3.rest_1_, bf16[512,6144]{1,0:T(8,128)(2,1)S(1)} %get-tuple-element.45.rest_2_.rest_0_, ...), custom_call_target="tpu_custom_call" | custom-call | flops 805306368 | bytes 3145728 | tf_op jit(solution)/shard_map/project/pallas_call | solution.py:569
  54.4 0.0 copy-start
  54.4 0.0 copy-start.1
  54.4 0.6 collective-permute-start.6
  55.1 0.0 collective-permute-done.9.got_ref
  55.1 0.5 collective-permute-start.11
  55.6 2.4 %project.8 = (f32[256,768]{1,0:T(8,128)S(1)}, f32[256,768]{1,0:T(8,128)S(1)}) custom-call(s32[3]{0:T(128)S(1)} %pad_add_fusion.place_ref, bf16[256,1024]{1,0:T(8,128)(2,1)S(1)} %hidden.2.rest_0_, bf16[256,1024]{1,0:T(8,128)(2,1)S(1)} %hidden.3.rest_1_, bf16[512,6144]{1,0:T(8,128)(2,1)S(1)} %get-tuple-element.45.rest_2_.rest_0_, ...), custom_call_target="tpu_custom_call" | custom-call | flops 1610612736 | bytes 6291456 | tf_op jit(solution)/shard_map/project/pallas_call | solution.py:569
  57.9 0.1 relay.3.rest_5_
  58.0 2.6 %collective-permute-done.7.got_ref = bf16[256,768]{1,0:T(8,128)(2,1)S(1)} collective-permute-done((bf16[256,768]{1,0:T(8,128)(2,1)S(1)}, bf16[256,768]{1,0:T(8,128)(2,1)S(1)}, u32[]{:S(2)}, u32[]{:S(2)}) %collective-permute-start.7) | collective-permute-done | bytes 393248 | tf_op jit(solution)/shard_map/ppermute | solution.py:375
  60.6 1.5 %collective-permute-start.10 = (bf16[256,768]{1,0:T(8,128)(2,1)S(1)}, bf16[256,768]{1,0:T(8,128)(2,1)S(1)}, u32[]{:S(2)}, u32[]{:S(2)}) collective-permute-start(bf16[256,768]{1,0:T(8,128)(2,1)S(1)} %relay.3.rest_5_), channel_id=1, source_target_pairs={{0,2},{2,0},{4,6},{6,4},{1,3},{3,1},{5,7},{7,5},{8,10},{10,8},{12,... | collective-permute-start | bytes 1179656 | tf_op jit(solution)/shard_map/ppermute | solution.py:375
  62.1 0.1 relay.2.rest_4_
  62.2 0.0 collective-permute-done.13.rest_3_
  62.2 0.6 collective-permute-start.8
  62.7 0.0 collective-permute-done.12.rest_2_
  62.7 0.0 copy-done
  62.7 0.0 copy-done.1
  62.8 1.7 %decode_rows.1.rows_ref = bf16[16,2048]{1,0:T(8,128)(2,1)S(1)} custom-call(s32[3]{0:T(128)S(1)} %pad_add_fusion.place_ref, s32[4]{0:T(128)S(1)} %copy-done.1, bf16[4,2,2048]{2,1,0:T(2,128)(2,1)S(1)} %get-tuple-element.53.q_ref, bf16[4,2,2048]{2,1,0:T(2,128)(2,1)S(1)} %get-tuple-element.54.k_ref, bf16[4,2,2048]{2,1,0:T(2,128)(2,1)S(1)} %get-tuple-element.55.v_ref, ...), custom_call_target="tpu_custom_call" | custom-call | flops 33554432 | bytes 262144 | tf_op jit(solution)/shard_map/decode_rows/pallas_call | solution.py:537
  64.5 3.9 %decode_project.1 = (f32[16,1536]{1,0:T(8,128)S(1)}, bf16[16,1536]{1,0:T(8,128)(2,1)S(1)}, bf16[16,1536]{1,0:T(8,128)(2,1)S(1)}, bf16[16,1536]{1,0:T(8,128)(2,1)S(1)}) custom-call(s32[3]{0:T(128)S(1)} %pad_add_fusion.place_ref, bf16[16,2048]{1,0:T(8,128)(2,1)S(1)} %decode_rows.1.rows_ref, bf16[512,6144]{1,0:T(8,128)(2,1)S(1)} %get-tuple-element.45.rest_2_.rest_0_, ...), custom_call_target="tpu_custom_call" | custom-call | flops 402653184 | bytes 1572864 | tf_op jit(solution)/shard_map/decode_project/pallas_call | solution.py:600
  68.4 0.6 collective-permute-start.14
  69.0 0.1 collective-permute-done.6.ax
  69.0 1.5 %collective-permute-start.15 = (bf16[16,1536]{1,0:T(8,128)(2,1)S(1)}, bf16[16,1536]{1,0:T(8,128)(2,1)S(1)}, u32[]{:S(2)}, u32[]{:S(2)}) collective-permute-start(bf16[16,1536]{1,0:T(8,128)(2,1)S(1)} %get-tuple-element.58), channel_id=1, source_target_pairs={{0,4},{2,6},{4,0},{6,2},{1,5},{3,7},{5,1},{7,3},{8,12},{10,14},{12... | collective-permute-start | bytes 147464 | tf_op jit(solution)/shard_map/ppermute | solution.py:375
  70.5 0.0 collective-permute-done.11.by
  70.5 1.5 %collective-permute-start.16 = (bf16[16,1536]{1,0:T(8,128)(2,1)S(1)}, bf16[16,1536]{1,0:T(8,128)(2,1)S(1)}, u32[]{:S(2)}, u32[]{:S(2)}) collective-permute-start(bf16[16,1536]{1,0:T(8,128)(2,1)S(1)} %get-tuple-element.59), channel_id=1, source_target_pairs={{0,6},{2,4},{4,2},{6,0},{1,7},{3,5},{5,3},{7,1},{8,14},{10,12},{12... | collective-permute-start | bytes 147464 | tf_op jit(solution)/shard_map/ppermute | solution.py:375
  72.0 2.3 %project.6 = (f32[256,768]{1,0:T(8,128)S(1)}, f32[256,768]{1,0:T(8,128)S(1)}) custom-call(s32[3]{0:T(128)S(1)} %pad_add_fusion.place_ref, bf16[256,1024]{1,0:T(8,128)(2,1)S(1)} %hidden.2.rest_0_, bf16[256,1024]{1,0:T(8,128)(2,1)S(1)} %hidden.3.rest_1_, bf16[512,6144]{1,0:T(8,128)(2,1)S(1)} %get-tuple-element.45.rest_2_.rest_0_, ...), custom_call_target="tpu_custom_call" | custom-call | flops 1610612736 | bytes 6291456 | tf_op jit(solution)/shard_map/project/pallas_call | solution.py:569
  74.3 4.2 %collective-permute-done.14.d_x = bf16[16,1536]{1,0:T(8,128)(2,1)S(1)} collective-permute-done((bf16[16,1536]{1,0:T(8,128)(2,1)S(1)}, bf16[16,1536]{1,0:T(8,128)(2,1)S(1)}, u32[]{:S(2)}, u32[]{:S(2)}) %collective-permute-start.14) | collective-permute-done | bytes 49184 | tf_op jit(solution)/shard_map/ppermute | solution.py:375
  78.5 0.0 collective-permute-done.15.d_y
  78.5 0.6 collective-permute-done.16.d_far
  79.1 0.0 collective-permute-done.10.bx
  79.1 0.0 collective-permute-done.8.ay
  79.1 1.6 %finish.1 = (bf16[1,256,1536]{2,1,0:T(8,128)(2,1)}, bf16[4,2,1536]{2,1,0:T(2,128)(2,1)}) custom-call(f32[256,768]{1,0:T(8,128)S(1)} %get-tuple-element.49.own_a, f32[256,768]{1,0:T(8,128)S(1)} %get-tuple-element.50.own_b, bf16[256,768]{1,0:T(8,128)(2,1)S(1)} %collective-permute-done.6.ax, bf16[256,768]{1,0:T(8,128)(2,1)S(1)} %collective-permute-done.8.ay, ...), custom_call_target="tpu_custom_call" | custom-call | flops 1179648 | bytes 3932160 | tf_op jit(solution)/shard_map/finish/pallas_call | solution.py:608
Async XLA Ops:
  4.0 14.0 %collective-permute-start = (bf16[1040,128]{1,0:T(8,128)(2,1)S(1)}, bf16[1040,128]{1,0:T(8,128)(2,1)S(1)}, u32[]{:S(2)}, u32[]{:S(2)}) collective-permute-start(bf16[1040,128]{1,0:T(8,128)(2,1)S(1)} %get-tuple-element.39), channel_id=1, source_target_pairs={{0,8},{24,16},{1,9},{25,17},{2,10},{26,18},{3,11},{27,19},{4,12},{... | collective-permute-start | bytes 798728 | tf_op jit(solution)/shard_map/ppermute | solution.py:500
  10.2 10.0 %collective-permute-start.3 = (bf16[1040,128]{1,0:T(8,128)(2,1)S(1)}, bf16[1040,128]{1,0:T(8,128)(2,1)S(1)}, u32[]{:S(2)}, u32[]{:S(2)}) collective-permute-start(bf16[1040,128]{1,0:T(8,128)(2,1)S(1)} %get-tuple-element.43), channel_id=1, source_target_pairs={{0,8},{24,16},{1,9},{25,17},{2,10},{26,18},{3,11},{27,19},{4,12},{... | collective-permute-start | bytes 798728 | tf_op jit(solution)/shard_map/ppermute | solution.py:500
  18.7 3.0 %collective-permute-start.1 = (bf16[1040,128]{1,0:T(8,128)(2,1)S(1)}, bf16[1040,128]{1,0:T(8,128)(2,1)S(1)}, u32[]{:S(2)}, u32[]{:S(2)}) collective-permute-start(bf16[1040,128]{1,0:T(8,128)(2,1)S(1)} %chain.4), channel_id=1, source_target_pairs={{8,16},{16,8},{9,17},{17,9},{10,18},{18,10},{11,19},{19,11},{12,20... | collective-permute-start | bytes 798728 | tf_op jit(solution)/shard_map/ppermute | solution.py:500
  21.0 2.7 %collective-permute-start.4 = (bf16[1040,128]{1,0:T(8,128)(2,1)S(1)}, bf16[1040,128]{1,0:T(8,128)(2,1)S(1)}, u32[]{:S(2)}, u32[]{:S(2)}) collective-permute-start(bf16[1040,128]{1,0:T(8,128)(2,1)S(1)} %chain.6), channel_id=1, source_target_pairs={{8,16},{16,8},{9,17},{17,9},{10,18},{18,10},{11,19},{19,11},{12,20... | collective-permute-start | bytes 798728 | tf_op jit(solution)/shard_map/ppermute | solution.py:500
  22.4 13.2 %collective-permute-start.2 = (bf16[1040,128]{1,0:T(8,128)(2,1)S(1)}, bf16[1040,128]{1,0:T(8,128)(2,1)S(1)}, u32[]{:S(2)}, u32[]{:S(2)}) collective-permute-start(bf16[1040,128]{1,0:T(8,128)(2,1)S(1)} %chain.5), channel_id=1, source_target_pairs={{16,24},{8,0},{17,25},{9,1},{18,26},{10,2},{19,27},{11,3},{20,28},... | collective-permute-start | bytes 798728 | tf_op jit(solution)/shard_map/ppermute | solution.py:500
  24.4 16.9 %collective-permute-start.5 = (bf16[1040,128]{1,0:T(8,128)(2,1)S(1)}, bf16[1040,128]{1,0:T(8,128)(2,1)S(1)}, u32[]{:S(2)}, u32[]{:S(2)}) collective-permute-start(bf16[1040,128]{1,0:T(8,128)(2,1)S(1)} %chain.7.rest_0_), channel_id=1, source_target_pairs={{16,24},{8,0},{17,25},{9,1},{18,26},{10,2},{19,27},{11,3},{20,28},... | collective-permute-start | bytes 798728 | tf_op jit(solution)/shard_map/ppermute | solution.py:500
  44.5 10.5 %collective-permute-start.9 = (bf16[256,768]{1,0:T(8,128)(2,1)S(1)}, bf16[256,768]{1,0:T(8,128)(2,1)S(1)}, u32[]{:S(2)}, u32[]{:S(2)}) collective-permute-start(bf16[256,768]{1,0:T(8,128)(2,1)S(1)} %project.10.rest_3_), channel_id=1, source_target_pairs={{0,4},{2,6},{4,0},{6,2},{1,5},{3,7},{5,1},{7,3},{8,12},{10,14},{12... | collective-permute-start | bytes 1179656 | tf_op jit(solution)/shard_map/ppermute | solution.py:375
  47.0 15.2 %collective-permute-start.13 = (f32[8,128,128]{2,1,0:T(8,128)S(1)}, f32[8,128,128]{2,1,0:T(8,128)S(1)}, u32[]{:S(2)}, u32[]{:S(2)}) collective-permute-start(f32[8,128,128]{2,1,0:T(8,128)S(1)} %final_state.3.rest_1_), channel_id=1, source_target_pairs={{0,1},{1,0},{2,3},{3,2},{4,5},{5,4},{6,7},{7,6},{8,9},{9,8},{10,11... | collective-permute-start | bytes 1572872 | tf_op jit(solution)/shard_map/ppermute | solution.py:375
  48.6 12.0 %collective-permute-start.7 = (bf16[256,768]{1,0:T(8,128)(2,1)S(1)}, bf16[256,768]{1,0:T(8,128)(2,1)S(1)}, u32[]{:S(2)}, u32[]{:S(2)}) collective-permute-start(bf16[256,768]{1,0:T(8,128)(2,1)S(1)} %project.9), channel_id=1, source_target_pairs={{0,2},{2,0},{4,6},{6,4},{1,3},{3,1},{5,7},{7,5},{8,10},{10,8},{12,... | collective-permute-start | bytes 1179656 | tf_op jit(solution)/shard_map/ppermute | solution.py:375
  51.0 11.7 %collective-permute-start.12 = (f32[8,128,128]{2,1,0:T(8,128)S(1)}, f32[8,128,128]{2,1,0:T(8,128)S(1)}, u32[]{:S(2)}, u32[]{:S(2)}) collective-permute-start(f32[8,128,128]{2,1,0:T(8,128)S(1)} %final_state.2.rest_0_), channel_id=1, source_target_pairs={{0,1},{1,0},{2,3},{3,2},{4,5},{5,4},{6,7},{7,6},{8,9},{9,8},{10,11... | collective-permute-start | bytes 1572872 | tf_op jit(solution)/shard_map/ppermute | solution.py:375
  54.4 8.3 %copy-start = (f32[4,16,2]{1,2,0:T(2,128)S(1)}, f32[4,16,2]{1,2,0:T(2,128)}, u32[]{:S(2)}) copy-start(f32[4,16,2]{1,2,0:T(2,128)} %param.18) | copy-start | bytes 1540
  54.4 8.3 %copy-start.1 = (s32[4]{0:T(128)S(1)}, s32[4]{0:T(128)}, u32[]{:S(2)}) copy-start(s32[4]{0:T(128)} %prompt_ref.1) | copy-start | bytes 52
  54.4 14.6 %collective-permute-start.6 = (bf16[256,768]{1,0:T(8,128)(2,1)S(1)}, bf16[256,768]{1,0:T(8,128)(2,1)S(1)}, u32[]{:S(2)}, u32[]{:S(2)}) collective-permute-start(bf16[256,768]{1,0:T(8,128)(2,1)S(1)} %project.7), channel_id=1, source_target_pairs={{0,2},{2,0},{4,6},{6,4},{1,3},{3,1},{5,7},{7,5},{8,10},{10,8},{12,... | collective-permute-start | bytes 1179656 | tf_op jit(solution)/shard_map/ppermute | solution.py:375
  55.1 15.4 %collective-permute-start.11 = (bf16[256,768]{1,0:T(8,128)(2,1)S(1)}, bf16[256,768]{1,0:T(8,128)(2,1)S(1)}, u32[]{:S(2)}, u32[]{:S(2)}) collective-permute-start(bf16[256,768]{1,0:T(8,128)(2,1)S(1)} %project.11), channel_id=1, source_target_pairs={{0,4},{2,6},{4,0},{6,2},{1,5},{3,7},{5,1},{7,3},{8,12},{10,14},{12... | collective-permute-start | bytes 1179656 | tf_op jit(solution)/shard_map/ppermute | solution.py:375
  60.6 18.5 %collective-permute-start.10 = (bf16[256,768]{1,0:T(8,128)(2,1)S(1)}, bf16[256,768]{1,0:T(8,128)(2,1)S(1)}, u32[]{:S(2)}, u32[]{:S(2)}) collective-permute-start(bf16[256,768]{1,0:T(8,128)(2,1)S(1)} %relay.3.rest_5_), channel_id=1, source_target_pairs={{0,2},{2,0},{4,6},{6,4},{1,3},{3,1},{5,7},{7,5},{8,10},{10,8},{12,... | collective-permute-start | bytes 1179656 | tf_op jit(solution)/shard_map/ppermute | solution.py:375
  62.2 16.9 %collective-permute-start.8 = (bf16[256,768]{1,0:T(8,128)(2,1)S(1)}, bf16[256,768]{1,0:T(8,128)(2,1)S(1)}, u32[]{:S(2)}, u32[]{:S(2)}) collective-permute-start(bf16[256,768]{1,0:T(8,128)(2,1)S(1)} %relay.2.rest_4_), channel_id=1, source_target_pairs={{0,4},{2,6},{4,0},{6,2},{1,5},{3,7},{5,1},{7,3},{8,12},{10,14},{12... | collective-permute-start | bytes 1179656 | tf_op jit(solution)/shard_map/ppermute | solution.py:375
  68.4 10.1 %collective-permute-start.14 = (bf16[16,1536]{1,0:T(8,128)(2,1)S(1)}, bf16[16,1536]{1,0:T(8,128)(2,1)S(1)}, u32[]{:S(2)}, u32[]{:S(2)}) collective-permute-start(bf16[16,1536]{1,0:T(8,128)(2,1)S(1)} %get-tuple-element.57), channel_id=1, source_target_pairs={{0,2},{2,0},{4,6},{6,4},{1,3},{3,1},{5,7},{7,5},{8,10},{10,8},{12,... | collective-permute-start | bytes 147464 | tf_op jit(solution)/shard_map/ppermute | solution.py:375
  69.0 9.5 %collective-permute-start.15 = (bf16[16,1536]{1,0:T(8,128)(2,1)S(1)}, bf16[16,1536]{1,0:T(8,128)(2,1)S(1)}, u32[]{:S(2)}, u32[]{:S(2)}) collective-permute-start(bf16[16,1536]{1,0:T(8,128)(2,1)S(1)} %get-tuple-element.58), channel_id=1, source_target_pairs={{0,4},{2,6},{4,0},{6,2},{1,5},{3,7},{5,1},{7,3},{8,12},{10,14},{12... | collective-permute-start | bytes 147464 | tf_op jit(solution)/shard_map/ppermute | solution.py:375
  70.5 8.6 %collective-permute-start.16 = (bf16[16,1536]{1,0:T(8,128)(2,1)S(1)}, bf16[16,1536]{1,0:T(8,128)(2,1)S(1)}, u32[]{:S(2)}, u32[]{:S(2)}) collective-permute-start(bf16[16,1536]{1,0:T(8,128)(2,1)S(1)} %get-tuple-element.59), channel_id=1, source_target_pairs={{0,6},{2,4},{4,2},{6,0},{1,7},{3,5},{5,3},{7,1},{8,14},{10,12},{12... | collective-permute-start | bytes 147464 | tf_op jit(solution)/shard_map/ppermute | solution.py:375

commit v7 on v6

--- a/solution.py
+++ b/solution.py
@@ -483,7 +483,10 @@
     received = []
     after = [local_token]
     for phase in range(phases):
-        pairs = [(phase, phase + 1), (groups - 1 - phase, groups - 2 - phase)]
+        target = list(range(groups))
+        for low in (phase, groups - 2 - phase):
+            target[low], target[low + 1] = low + 1, low
+        pairs = list(enumerate(target))
         if phase > 0:
             values_out = []
             for c, (first, size) in enumerate(chunks):
@@ -585,8 +588,8 @@
             cost(length * half, length * half * 8),
         )(own_term, got, *after)
 
-    far_a = swap(project([(3, 0)], BF16)[0], "head", parts, 1)
-    to_y, = project([(3, 1)], BF16)
+    to_x, to_y = project([(3, 0), (3, 1)], BF16)
+    far_a = swap(to_x, "head", parts, 1)
     far_b = swap(to_y, "head", parts, 2)
     x_a = swap(project([(1, 0)], BF16)[0], "head", parts, 1)
     y_b = swap(project([(2, 1)], BF16)[0], "head", parts, 2)

time: 81.2 us -> 78.6 us (0.968)
  waiting for transfers between devices: 19.3 us -> 10.9 us
  starting transfers between devices: 20.5 us -> 27.1 us
    ppermute x6, waiting for transfers between devices: 11.9 us -> 4.52 us  [body(): received.append([lax.ppermute(value, 'ctx', pairs) for value in values_out])]
    ppermute x6, starting transfers between devices: 10.4 us -> 16 us  [body(): received.append([lax.ppermute(value, 'ctx', pairs) for value in values_out])]
    ppermute x11, waiting for transfers between devices: 7.42 us -> 6.38 us  [swap(): return lax.ppermute(array, axis, [(i, i ^ bit) for i in range(size)])]
    ppermute x11, starting transfers between devices: 10.1 us -> 11.1 us  [swap(): return lax.ppermute(array, axis, [(i, i ^ bit) for i in range(size)])]
    pallas_call x6 -> x5, Pallas kernels: 10.9 us -> 10.2 us  [project(): call(functools.partial(project_kernel, pieces, count), 'project', [SMEM]...]
  transfers between devices with their start and end apart: 17 -> 17, of which waited for: 7 -> 6; matrix products, arithmetic and copies ran while one was open for 0% -> 0% of each run, Pallas kernels for 39% -> 39%
where the time goes in v7:
time: 78.6 us; the launch traced here: 78.4 us
  Pallas kernels  39.2 us (50%)
  starting transfers between devices  27.1 us (34%)
  waiting for transfers between devices  10.9 us (14%)
  between operations  1 us (1%)
    ppermute x6, starting transfers between devices, body(): received.append([lax.ppermute(value, 'ctx', pairs) for value in values_out])  16 us
    ppermute x11, starting transfers between devices, swap(): return lax.ppermute(array, axis, [(i, i ^ bit) for i in range(size)])  11.1 us
    pallas_call x5, Pallas kernels, project(): call(functools.partial(project_kernel, pieces, count), 'project', [SMEM]...  10.2 us
    pallas_call x1, Pallas kernels, body(): call(functools.partial(local_kernel, 0), 'local_attention', [VMEM] * 5 +...  6.42 us
    ppermute x11, waiting for transfers between devices, swap(): return lax.ppermute(array, axis, [(i, i ^ bit) for i in range(size)])  6.38 us
    ppermute x6, waiting for transfers between devices, body(): received.append([lax.ppermute(value, 'ctx', pairs) for value in values_out])  4.52 us
    pallas_call x1, Pallas kernels, body(): call(decode_project_kernel, 'decode_project', [SMEM] + [VMEM] * (1 + WEIG...  3.92 us
    pallas_call x2, Pallas kernels, body(): call(functools.partial(hidden_kernel, phases, first), 'hidden', [SMEM] +...  3.25 us
  transfers between devices with their start and end apart: 17, of which 6 were waited for; matrix products, arithmetic and copies ran while one was open for 0% of the time, Pallas kernels for 39%

profile of v7, /device:TPU:0, one launch (start us, length us, event | category | flops | bytes accessed | tf_op | source)
XLA Modules:
  0.0 78.4 jit_solution(10201367615712403835)
XLA Ops:
  0.6 0.1 pad_add_fusion.place_ref
  0.7 3.2 %own_state.1 = (f32[8,128,128]{2,1,0:T(8,128)S(1)}, f32[1,128]{1,0:T(1,128)S(1)}, f32[256,16]{1,0:T(8,128)S(1)}, f32[1,16,256]{2,1,0:T(8,128)S(1)}, bf16[256,204...) custom-call(s32[3]{0:T(128)S(1)} %pad_add_fusion.place_ref, ...), custom_call_target="tpu_custom_call" | custom-call | flops 268435456 | bytes 8388608 | tf_op jit(solution)/shard_map/own_state/pallas_call | solution.py:418
  4.0 3.1 %collective-permute-start = (bf16[1040,128]{1,0:T(8,128)(2,1)S(1)}, bf16[1040,128]{1,0:T(8,128)(2,1)S(1)}, u32[]{:S(2)}, u32[]{:S(2)}) collective-permute-start(bf16[1040,128]{1,0:T(8,128)(2,1)S(1)} %get-tuple-element.41), channel_id=1, source_target_pairs={{0,8},{8,0},{16,24},{24,16},{1,9},{9,1},{17,25},{25,17},{2,10},{10... | collective-permute-start | bytes 798728 | tf_op jit(solution)/shard_map/ppermute | solution.py:503
  7.0 1.3 %more_state.1 = (f32[8,128,128]{2,1,0:T(8,128)S(1)}, bf16[1040,128]{1,0:T(8,128)(2,1)S(1)}, f32[16,256]{1,0:T(8,128)S(1)}, bf16[1,256,2048]{2,1,0:T(8,128)(2,1)S...) custom-call(bf16[256,2048]{1,0:T(8,128)(2,1)S(1)} %get-tuple-element.33.k_ref, ...), custom_call_target="tpu_custom_call" | custom-call | flops 134217728 | bytes 4194304 | tf_op jit(solution)/shard_map/more_state/pallas_call | solution.py:438
  8.3 0.1 collective-permute-start.3
  8.4 6.4 %local_attention.1 = (f32[256,2048]{1,0:T(8,128)S(1)}, f32[8,128]{1,0:T(8,128)S(1)}, bf16[512,6144]{1,0:T(8,128)(2,1)S(1)}, bf16[512,6144]{1,0:T(8,128)(2,1)S(1)}, bf16[512,6144]{1,0:T(8,128)(2,1)S(1)}) custom-call(bf16[1,256,2048]{2,1,0:T(8,128)(2,1)S(1)} %get-tuple-element.38.q_ref, bf16[256,2048]{1,0:T(8,128)(2,1)S(1)} %get-tuple-element.33.k_ref, ...), custom_call_target="tpu_custom_call" | custom-call | flops 536870912 | bytes 6291456 | tf_op jit(solution)/shard_map/local_attention/pallas_call | solution.py:459
  14.8 0.0 collective-permute-done.got_ref.rest_0_
  14.8 0.7 chain.4
  15.6 0.7 collective-permute-start.1
  16.3 2.9 %collective-permute-done.3.got_ref.rest_0_ = bf16[1040,128]{1,0:T(8,128)(2,1)S(1)} collective-permute-done((bf16[1040,128]{1,0:T(8,128)(2,1)S(1)}, bf16[1040,128]{1,0:T(8,128)(2,1)S(1)}, u32[]{:S(2)}, u32[]{:S(2)}) %collective-permute-start.3) | collective-permute-done | bytes 266272 | tf_op jit(solution)/shard_map/ppermute | solution.py:503
  19.1 0.7 chain.6
  19.9 0.9 %collective-permute-start.4 = (bf16[1040,128]{1,0:T(8,128)(2,1)S(1)}, bf16[1040,128]{1,0:T(8,128)(2,1)S(1)}, u32[]{:S(2)}, u32[]{:S(2)}) collective-permute-start(bf16[1040,128]{1,0:T(8,128)(2,1)S(1)} %chain.6), channel_id=1, source_target_pairs={{0,0},{8,16},{16,8},{24,24},{1,1},{9,17},{17,9},{25,25},{2,2},{10,... | collective-permute-start | bytes 798728 | tf_op jit(solution)/shard_map/ppermute | solution.py:503
  20.7 0.0 collective-permute-done.1.got_ref.rest_1_
  20.8 0.7 chain.5
  21.5 8.0 %collective-permute-start.2 = (bf16[1040,128]{1,0:T(8,128)(2,1)S(1)}, bf16[1040,128]{1,0:T(8,128)(2,1)S(1)}, u32[]{:S(2)}, u32[]{:S(2)}) collective-permute-start(bf16[1040,128]{1,0:T(8,128)(2,1)S(1)} %chain.5), channel_id=1, source_target_pairs={{0,8},{8,0},{16,24},{24,16},{1,9},{9,1},{17,25},{25,17},{2,10},{10... | collective-permute-start | bytes 798728 | tf_op jit(solution)/shard_map/ppermute | solution.py:503
  29.5 0.0 collective-permute-done.4.got_ref.rest_1_
  29.5 0.7 chain.7.rest_0_
  30.3 3.3 %collective-permute-start.5 = (bf16[1040,128]{1,0:T(8,128)(2,1)S(1)}, bf16[1040,128]{1,0:T(8,128)(2,1)S(1)}, u32[]{:S(2)}, u32[]{:S(2)}) collective-permute-start(bf16[1040,128]{1,0:T(8,128)(2,1)S(1)} %chain.7.rest_0_), channel_id=1, source_target_pairs={{0,8},{8,0},{16,24},{24,16},{1,9},{9,1},{17,25},{25,17},{2,10},{10... | collective-permute-start | bytes 798728 | tf_op jit(solution)/shard_map/ppermute | solution.py:503
  33.6 2.8 %load_weight.1 = (bf16[512,6144]{1,0:T(8,128)(2,1)S(1)}, f32[8,128]{1,0:T(8,128)S(1)}) custom-call(bf16[2048,6144]{1,0:T(8,128)(2,1)} %weight_hbm.3, bf16[1040,128]{1,0:T(8,128)(2,1)S(1)} %chain.7.rest_0_), custom_call_target="tpu_custom_call" | custom-call | flops 1 | bytes 6291456 | tf_op jit(solution)/shard_map/load_weight/pallas_call | solution.py:472
  36.4 0.0 collective-permute-done.2.rest_2_
  36.4 1.6 %hidden.2.rest_0_ = bf16[256,1024]{1,0:T(8,128)(2,1)S(1)} custom-call(s32[3]{0:T(128)S(1)} %pad_add_fusion.place_ref, bf16[1,256,2048]{2,1,0:T(8,128)(2,1)S(1)} %get-tuple-element.38.q_ref, f32[256,16]{1,0:T(8,128)S(1)} %get-tuple-element.35.col_ref, f32[256,2048]{1,0:T(8,128)S(1)} %get-tuple-element.40.local_ref, ...), custom_call_target="tpu_custom_call" | custom-call | flops 67108864 | bytes 5242880 | tf_op jit(solution)/shard_map/hidden/pallas_call | solution.py:511
  38.0 1.6 %collective-permute-done.5.rest_2_ = bf16[1040,128]{1,0:T(8,128)(2,1)S(1)} collective-permute-done((bf16[1040,128]{1,0:T(8,128)(2,1)S(1)}, bf16[1040,128]{1,0:T(8,128)(2,1)S(1)}, u32[]{:S(2)}, u32[]{:S(2)}) %collective-permute-start.5) | collective-permute-done | bytes 266272 | tf_op jit(solution)/shard_map/ppermute | solution.py:503
  39.6 1.6 %hidden.3.rest_1_ = bf16[256,1024]{1,0:T(8,128)(2,1)S(1)} custom-call(s32[3]{0:T(128)S(1)} %pad_add_fusion.place_ref, bf16[1,256,2048]{2,1,0:T(8,128)(2,1)S(1)} %get-tuple-element.38.q_ref, f32[256,16]{1,0:T(8,128)S(1)} %get-tuple-element.35.col_ref, f32[256,2048]{1,0:T(8,128)S(1)} %get-tuple-element.40.local_ref, ...), custom_call_target="tpu_custom_call" | custom-call | flops 67108864 | bytes 5242880 | tf_op jit(solution)/shard_map/hidden/pallas_call | solution.py:511
  41.3 2.4 %project.8 = (bf16[256,768]{1,0:T(8,128)(2,1)S(1)}, bf16[256,768]{1,0:T(8,128)(2,1)S(1)}) custom-call(s32[3]{0:T(128)S(1)} %pad_add_fusion.place_ref, bf16[256,1024]{1,0:T(8,128)(2,1)S(1)} %hidden.2.rest_0_, bf16[256,1024]{1,0:T(8,128)(2,1)S(1)} %hidden.3.rest_1_, bf16[512,6144]{1,0:T(8,128)(2,1)S(1)} %get-tuple-element.47.rest_2_.rest_0_, ...), custom_call_target="tpu_custom_call" | custom-call | flops 1610612736 | bytes 6291456 | tf_op jit(solution)/shard_map/project/pallas_call | solution.py:572
  43.6 1.6 %collective-permute-start.9 = (bf16[256,768]{1,0:T(8,128)(2,1)S(1)}, bf16[256,768]{1,0:T(8,128)(2,1)S(1)}, u32[]{:S(2)}, u32[]{:S(2)}) collective-permute-start(bf16[256,768]{1,0:T(8,128)(2,1)S(1)} %get-tuple-element.56.rest_3_), channel_id=1, source_target_pairs={{0,4},{2,6},{4,0},{6,2},{1,5},{3,7},{5,1},{7,3},{8,12},{10,14},{12... | collective-permute-start | bytes 1179656 | tf_op jit(solution)/shard_map/ppermute | solution.py:375
  45.2 0.8 %final_state.2.rest_0_ = f32[8,128,128]{2,1,0:T(8,128)S(1)} custom-call(s32[3]{0:T(128)S(1)} %pad_add_fusion.place_ref, f32[8,128,128]{2,1,0:T(8,128)S(1)} %get-tuple-element.42.own_ref, f32[1,128]{1,0:T(1,128)S(1)} %get-tuple-element.37.log_ref, bf16[1040,128]{1,0:T(8,128)(2,1)S(1)} %collective-permute-done.got_ref.rest_0_, ...), custom_call_target="tpu_custom_call" | custom-call | flops 524288 | bytes 1048576 | tf_op jit(solution)/shard_map/final_state/pallas_call | solution.py:527
  46.1 0.1 collective-permute-start.12
  46.1 1.5 %collective-permute-start.7 = (bf16[256,768]{1,0:T(8,128)(2,1)S(1)}, bf16[256,768]{1,0:T(8,128)(2,1)S(1)}, u32[]{:S(2)}, u32[]{:S(2)}) collective-permute-start(bf16[256,768]{1,0:T(8,128)(2,1)S(1)} %get-tuple-element.54), channel_id=1, source_target_pairs={{0,2},{2,0},{4,6},{6,4},{1,3},{3,1},{5,7},{7,5},{8,10},{10,8},{12,... | collective-permute-start | bytes 1179656 | tf_op jit(solution)/shard_map/ppermute | solution.py:375
  47.7 0.9 %final_state.3.rest_1_ = f32[8,128,128]{2,1,0:T(8,128)S(1)} custom-call(s32[3]{0:T(128)S(1)} %pad_add_fusion.place_ref, f32[8,128,128]{2,1,0:T(8,128)S(1)} %get-tuple-element.44.own_ref, f32[1,128]{1,0:T(1,128)S(1)} %get-tuple-element.37.log_ref, bf16[1040,128]{1,0:T(8,128)(2,1)S(1)} %collective-permute-done.3.got_ref.rest_0_, ...), custom_call_target="tpu_custom_call" | custom-call | flops 524288 | bytes 1048576 | tf_op jit(solution)/shard_map/final_state/pallas_call | solution.py:527
  48.5 0.2 collective-permute-start.13
  48.8 1.5 %project.9 = bf16[256,768]{1,0:T(8,128)(2,1)S(1)} custom-call(s32[3]{0:T(128)S(1)} %pad_add_fusion.place_ref, bf16[256,1024]{1,0:T(8,128)(2,1)S(1)} %hidden.2.rest_0_, bf16[256,1024]{1,0:T(8,128)(2,1)S(1)} %hidden.3.rest_1_, bf16[512,6144]{1,0:T(8,128)(2,1)S(1)} %get-tuple-element.47.rest_2_.rest_0_, ...), custom_call_target="tpu_custom_call" | custom-call | flops 805306368 | bytes 3145728 | tf_op jit(solution)/shard_map/project/pallas_call | solution.py:572
  50.3 1.6 %project.6 = bf16[256,768]{1,0:T(8,128)(2,1)S(1)} custom-call(s32[3]{0:T(128)S(1)} %pad_add_fusion.place_ref, bf16[256,1024]{1,0:T(8,128)(2,1)S(1)} %hidden.2.rest_0_, bf16[256,1024]{1,0:T(8,128)(2,1)S(1)} %hidden.3.rest_1_, bf16[512,6144]{1,0:T(8,128)(2,1)S(1)} %get-tuple-element.47.rest_2_.rest_0_, ...), custom_call_target="tpu_custom_call" | custom-call | flops 805306368 | bytes 3145728 | tf_op jit(solution)/shard_map/project/pallas_call | solution.py:572
  51.9 0.0 copy-start
  51.9 0.0 copy-start.1
  51.9 0.6 collective-permute-start.6
  52.5 1.1 %collective-permute-done.9.got_ref = bf16[256,768]{1,0:T(8,128)(2,1)S(1)} collective-permute-done((bf16[256,768]{1,0:T(8,128)(2,1)S(1)}, bf16[256,768]{1,0:T(8,128)(2,1)S(1)}, u32[]{:S(2)}, u32[]{:S(2)}) %collective-permute-start.9) | collective-permute-done | bytes 393248 | tf_op jit(solution)/shard_map/ppermute | solution.py:375
  53.6 1.5 %collective-permute-start.11 = (bf16[256,768]{1,0:T(8,128)(2,1)S(1)}, bf16[256,768]{1,0:T(8,128)(2,1)S(1)}, u32[]{:S(2)}, u32[]{:S(2)}) collective-permute-start(bf16[256,768]{1,0:T(8,128)(2,1)S(1)} %project.9), channel_id=1, source_target_pairs={{0,4},{2,6},{4,0},{6,2},{1,5},{3,7},{5,1},{7,3},{8,12},{10,14},{12... | collective-permute-start | bytes 1179656 | tf_op jit(solution)/shard_map/ppermute | solution.py:375
  55.1 2.4 %project.7 = (f32[256,768]{1,0:T(8,128)S(1)}, f32[256,768]{1,0:T(8,128)S(1)}) custom-call(s32[3]{0:T(128)S(1)} %pad_add_fusion.place_ref, bf16[256,1024]{1,0:T(8,128)(2,1)S(1)} %hidden.2.rest_0_, bf16[256,1024]{1,0:T(8,128)(2,1)S(1)} %hidden.3.rest_1_, bf16[512,6144]{1,0:T(8,128)(2,1)S(1)} %get-tuple-element.47.rest_2_.rest_0_, ...), custom_call_target="tpu_custom_call" | custom-call | flops 1610612736 | bytes 6291456 | tf_op jit(solution)/shard_map/project/pallas_call | solution.py:572
  57.5 0.1 relay.3.rest_5_
  57.6 0.5 collective-permute-done.7.got_ref
  58.1 1.5 %collective-permute-start.10 = (bf16[256,768]{1,0:T(8,128)(2,1)S(1)}, bf16[256,768]{1,0:T(8,128)(2,1)S(1)}, u32[]{:S(2)}, u32[]{:S(2)}) collective-permute-start(bf16[256,768]{1,0:T(8,128)(2,1)S(1)} %relay.3.rest_5_), channel_id=1, source_target_pairs={{0,2},{2,0},{4,6},{6,4},{1,3},{3,1},{5,7},{7,5},{8,10},{10,8},{12,... | collective-permute-start | bytes 1179656 | tf_op jit(solution)/shard_map/ppermute | solution.py:375
  59.6 0.1 relay.2.rest_4_
  59.7 0.0 collective-permute-done.12.rest_2_
  59.7 0.6 collective-permute-start.8
  60.3 0.0 collective-permute-done.13.rest_3_
  60.3 0.0 copy-done
  60.3 0.0 copy-done.1
  60.3 1.7 %decode_rows.1.rows_ref = bf16[16,2048]{1,0:T(8,128)(2,1)S(1)} custom-call(s32[3]{0:T(128)S(1)} %pad_add_fusion.place_ref, s32[4]{0:T(128)S(1)} %copy-done.1, bf16[4,2,2048]{2,1,0:T(2,128)(2,1)S(1)} %get-tuple-element.57.q_ref, bf16[4,2,2048]{2,1,0:T(2,128)(2,1)S(1)} %get-tuple-element.58.k_ref, bf16[4,2,2048]{2,1,0:T(2,128)(2,1)S(1)} %get-tuple-element.59.v_ref, ...), custom_call_target="tpu_custom_call" | custom-call | flops 33554432 | bytes 262144 | tf_op jit(solution)/shard_map/decode_rows/pallas_call | solution.py:540
  62.0 3.9 %decode_project.1 = (f32[16,1536]{1,0:T(8,128)S(1)}, bf16[16,1536]{1,0:T(8,128)(2,1)S(1)}, bf16[16,1536]{1,0:T(8,128)(2,1)S(1)}, bf16[16,1536]{1,0:T(8,128)(2,1)S(1)}) custom-call(s32[3]{0:T(128)S(1)} %pad_add_fusion.place_ref, bf16[16,2048]{1,0:T(8,128)(2,1)S(1)} %decode_rows.1.rows_ref, bf16[512,6144]{1,0:T(8,128)(2,1)S(1)} %get-tuple-element.47.rest_2_.rest_0_, ...), custom_call_target="tpu_custom_call" | custom-call | flops 402653184 | bytes 1572864 | tf_op jit(solution)/shard_map/decode_project/pallas_call | solution.py:603
  65.9 0.6 collective-permute-start.14
  66.5 0.0 collective-permute-done.6.ax
  66.6 1.5 %collective-permute-start.15 = (bf16[16,1536]{1,0:T(8,128)(2,1)S(1)}, bf16[16,1536]{1,0:T(8,128)(2,1)S(1)}, u32[]{:S(2)}, u32[]{:S(2)}) collective-permute-start(bf16[16,1536]{1,0:T(8,128)(2,1)S(1)} %get-tuple-element.62), channel_id=1, source_target_pairs={{0,4},{2,6},{4,0},{6,2},{1,5},{3,7},{5,1},{7,3},{8,12},{10,14},{12... | collective-permute-start | bytes 147464 | tf_op jit(solution)/shard_map/ppermute | solution.py:375
  68.0 0.0 collective-permute-done.11.by
  68.0 1.4 %collective-permute-start.16 = (bf16[16,1536]{1,0:T(8,128)(2,1)S(1)}, bf16[16,1536]{1,0:T(8,128)(2,1)S(1)}, u32[]{:S(2)}, u32[]{:S(2)}) collective-permute-start(bf16[16,1536]{1,0:T(8,128)(2,1)S(1)} %get-tuple-element.63), channel_id=1, source_target_pairs={{0,6},{2,4},{4,2},{6,0},{1,7},{3,5},{5,3},{7,1},{8,14},{10,12},{12... | collective-permute-start | bytes 147464 | tf_op jit(solution)/shard_map/ppermute | solution.py:375
  69.5 2.4 %project.5 = (f32[256,768]{1,0:T(8,128)S(1)}, f32[256,768]{1,0:T(8,128)S(1)}) custom-call(s32[3]{0:T(128)S(1)} %pad_add_fusion.place_ref, bf16[256,1024]{1,0:T(8,128)(2,1)S(1)} %hidden.2.rest_0_, bf16[256,1024]{1,0:T(8,128)(2,1)S(1)} %hidden.3.rest_1_, bf16[512,6144]{1,0:T(8,128)(2,1)S(1)} %get-tuple-element.47.rest_2_.rest_0_, ...), custom_call_target="tpu_custom_call" | custom-call | flops 1610612736 | bytes 6291456 | tf_op jit(solution)/shard_map/project/pallas_call | solution.py:572
  71.8 4.2 %collective-permute-done.14.d_x = bf16[16,1536]{1,0:T(8,128)(2,1)S(1)} collective-permute-done((bf16[16,1536]{1,0:T(8,128)(2,1)S(1)}, bf16[16,1536]{1,0:T(8,128)(2,1)S(1)}, u32[]{:S(2)}, u32[]{:S(2)}) %collective-permute-start.14) | collective-permute-done | bytes 49184 | tf_op jit(solution)/shard_map/ppermute | solution.py:375
  76.0 0.0 collective-permute-done.15.d_y
  76.0 0.5 collective-permute-done.16.d_far
  76.6 0.0 collective-permute-done.10.bx
  76.6 0.0 collective-permute-done.8.ay
  76.6 1.6 %finish.1 = (bf16[1,256,1536]{2,1,0:T(8,128)(2,1)}, bf16[4,2,1536]{2,1,0:T(2,128)(2,1)}) custom-call(f32[256,768]{1,0:T(8,128)S(1)} %get-tuple-element.51.own_a, f32[256,768]{1,0:T(8,128)S(1)} %get-tuple-element.52.own_b, bf16[256,768]{1,0:T(8,128)(2,1)S(1)} %collective-permute-done.6.ax, bf16[256,768]{1,0:T(8,128)(2,1)S(1)} %collective-permute-done.8.ay, ...), custom_call_target="tpu_custom_call" | custom-call | flops 1179648 | bytes 3932160 | tf_op jit(solution)/shard_map/finish/pallas_call | solution.py:611
Async XLA Ops:
  4.0 10.9 %collective-permute-start = (bf16[1040,128]{1,0:T(8,128)(2,1)S(1)}, bf16[1040,128]{1,0:T(8,128)(2,1)S(1)}, u32[]{:S(2)}, u32[]{:S(2)}) collective-permute-start(bf16[1040,128]{1,0:T(8,128)(2,1)S(1)} %get-tuple-element.41), channel_id=1, source_target_pairs={{0,8},{8,0},{16,24},{24,16},{1,9},{9,1},{17,25},{25,17},{2,10},{10... | collective-permute-start | bytes 798728 | tf_op jit(solution)/shard_map/ppermute | solution.py:503
  8.3 10.8 %collective-permute-start.3 = (bf16[1040,128]{1,0:T(8,128)(2,1)S(1)}, bf16[1040,128]{1,0:T(8,128)(2,1)S(1)}, u32[]{:S(2)}, u32[]{:S(2)}) collective-permute-start(bf16[1040,128]{1,0:T(8,128)(2,1)S(1)} %get-tuple-element.45), channel_id=1, source_target_pairs={{0,8},{8,0},{16,24},{24,16},{1,9},{9,1},{17,25},{25,17},{2,10},{10... | collective-permute-start | bytes 798728 | tf_op jit(solution)/shard_map/ppermute | solution.py:503
  15.6 5.2 %collective-permute-start.1 = (bf16[1040,128]{1,0:T(8,128)(2,1)S(1)}, bf16[1040,128]{1,0:T(8,128)(2,1)S(1)}, u32[]{:S(2)}, u32[]{:S(2)}) collective-permute-start(bf16[1040,128]{1,0:T(8,128)(2,1)S(1)} %chain.4), channel_id=1, source_target_pairs={{0,0},{8,16},{16,8},{24,24},{1,1},{9,17},{17,9},{25,25},{2,2},{10,... | collective-permute-start | bytes 798728 | tf_op jit(solution)/shard_map/ppermute | solution.py:503
  19.9 9.6 %collective-permute-start.4 = (bf16[1040,128]{1,0:T(8,128)(2,1)S(1)}, bf16[1040,128]{1,0:T(8,128)(2,1)S(1)}, u32[]{:S(2)}, u32[]{:S(2)}) collective-permute-start(bf16[1040,128]{1,0:T(8,128)(2,1)S(1)} %chain.6), channel_id=1, source_target_pairs={{0,0},{8,16},{16,8},{24,24},{1,1},{9,17},{17,9},{25,25},{2,2},{10,... | collective-permute-start | bytes 798728 | tf_op jit(solution)/shard_map/ppermute | solution.py:503
  21.5 14.9 %collective-permute-start.2 = (bf16[1040,128]{1,0:T(8,128)(2,1)S(1)}, bf16[1040,128]{1,0:T(8,128)(2,1)S(1)}, u32[]{:S(2)}, u32[]{:S(2)}) collective-permute-start(bf16[1040,128]{1,0:T(8,128)(2,1)S(1)} %chain.5), channel_id=1, source_target_pairs={{0,8},{8,0},{16,24},{24,16},{1,9},{9,1},{17,25},{25,17},{2,10},{10... | collective-permute-start | bytes 798728 | tf_op jit(solution)/shard_map/ppermute | solution.py:503
  30.3 9.4 %collective-permute-start.5 = (bf16[1040,128]{1,0:T(8,128)(2,1)S(1)}, bf16[1040,128]{1,0:T(8,128)(2,1)S(1)}, u32[]{:S(2)}, u32[]{:S(2)}) collective-permute-start(bf16[1040,128]{1,0:T(8,128)(2,1)S(1)} %chain.7.rest_0_), channel_id=1, source_target_pairs={{0,8},{8,0},{16,24},{24,16},{1,9},{9,1},{17,25},{25,17},{2,10},{10... | collective-permute-start | bytes 798728 | tf_op jit(solution)/shard_map/ppermute | solution.py:503
  43.6 10.0 %collective-permute-start.9 = (bf16[256,768]{1,0:T(8,128)(2,1)S(1)}, bf16[256,768]{1,0:T(8,128)(2,1)S(1)}, u32[]{:S(2)}, u32[]{:S(2)}) collective-permute-start(bf16[256,768]{1,0:T(8,128)(2,1)S(1)} %get-tuple-element.56.rest_3_), channel_id=1, source_target_pairs={{0,4},{2,6},{4,0},{6,2},{1,5},{3,7},{5,1},{7,3},{8,12},{10,14},{12... | collective-permute-start | bytes 1179656 | tf_op jit(solution)/shard_map/ppermute | solution.py:375
  46.1 13.6 %collective-permute-start.12 = (f32[8,128,128]{2,1,0:T(8,128)S(1)}, f32[8,128,128]{2,1,0:T(8,128)S(1)}, u32[]{:S(2)}, u32[]{:S(2)}) collective-permute-start(f32[8,128,128]{2,1,0:T(8,128)S(1)} %final_state.2.rest_0_), channel_id=1, source_target_pairs={{0,1},{1,0},{2,3},{3,2},{4,5},{5,4},{6,7},{7,6},{8,9},{9,8},{10,11... | collective-permute-start | bytes 1572872 | tf_op jit(solution)/shard_map/ppermute | solution.py:375
  46.1 12.0 %collective-permute-start.7 = (bf16[256,768]{1,0:T(8,128)(2,1)S(1)}, bf16[256,768]{1,0:T(8,128)(2,1)S(1)}, u32[]{:S(2)}, u32[]{:S(2)}) collective-permute-start(bf16[256,768]{1,0:T(8,128)(2,1)S(1)} %get-tuple-element.54), channel_id=1, source_target_pairs={{0,2},{2,0},{4,6},{6,4},{1,3},{3,1},{5,7},{7,5},{8,10},{10,8},{12,... | collective-permute-start | bytes 1179656 | tf_op jit(solution)/shard_map/ppermute | solution.py:375
  48.5 11.8 %collective-permute-start.13 = (f32[8,128,128]{2,1,0:T(8,128)S(1)}, f32[8,128,128]{2,1,0:T(8,128)S(1)}, u32[]{:S(2)}, u32[]{:S(2)}) collective-permute-start(f32[8,128,128]{2,1,0:T(8,128)S(1)} %final_state.3.rest_1_), channel_id=1, source_target_pairs={{0,1},{1,0},{2,3},{3,2},{4,5},{5,4},{6,7},{7,6},{8,9},{9,8},{10,11... | collective-permute-start | bytes 1572872 | tf_op jit(solution)/shard_map/ppermute | solution.py:375
  51.9 8.4 %copy-start = (f32[4,16,2]{1,2,0:T(2,128)S(1)}, f32[4,16,2]{1,2,0:T(2,128)}, u32[]{:S(2)}) copy-start(f32[4,16,2]{1,2,0:T(2,128)} %param.18) | copy-start | bytes 1540
  51.9 8.4 %copy-start.1 = (s32[4]{0:T(128)S(1)}, s32[4]{0:T(128)}, u32[]{:S(2)}) copy-start(s32[4]{0:T(128)} %prompt_ref.1) | copy-start | bytes 52
  51.9 14.7 %collective-permute-start.6 = (bf16[256,768]{1,0:T(8,128)(2,1)S(1)}, bf16[256,768]{1,0:T(8,128)(2,1)S(1)}, u32[]{:S(2)}, u32[]{:S(2)}) collective-permute-start(bf16[256,768]{1,0:T(8,128)(2,1)S(1)} %project.6), channel_id=1, source_target_pairs={{0,2},{2,0},{4,6},{6,4},{1,3},{3,1},{5,7},{7,5},{8,10},{10,8},{12,... | collective-permute-start | bytes 1179656 | tf_op jit(solution)/shard_map/ppermute | solution.py:375
  53.6 14.5 %collective-permute-start.11 = (bf16[256,768]{1,0:T(8,128)(2,1)S(1)}, bf16[256,768]{1,0:T(8,128)(2,1)S(1)}, u32[]{:S(2)}, u32[]{:S(2)}) collective-permute-start(bf16[256,768]{1,0:T(8,128)(2,1)S(1)} %project.9), channel_id=1, source_target_pairs={{0,4},{2,6},{4,0},{6,2},{1,5},{3,7},{5,1},{7,3},{8,12},{10,14},{12... | collective-permute-start | bytes 1179656 | tf_op jit(solution)/shard_map/ppermute | solution.py:375
  58.1 18.5 %collective-permute-start.10 = (bf16[256,768]{1,0:T(8,128)(2,1)S(1)}, bf16[256,768]{1,0:T(8,128)(2,1)S(1)}, u32[]{:S(2)}, u32[]{:S(2)}) collective-permute-start(bf16[256,768]{1,0:T(8,128)(2,1)S(1)} %relay.3.rest_5_), channel_id=1, source_target_pairs={{0,2},{2,0},{4,6},{6,4},{1,3},{3,1},{5,7},{7,5},{8,10},{10,8},{12,... | collective-permute-start | bytes 1179656 | tf_op jit(solution)/shard_map/ppermute | solution.py:375
  59.7 16.9 %collective-permute-start.8 = (bf16[256,768]{1,0:T(8,128)(2,1)S(1)}, bf16[256,768]{1,0:T(8,128)(2,1)S(1)}, u32[]{:S(2)}, u32[]{:S(2)}) collective-permute-start(bf16[256,768]{1,0:T(8,128)(2,1)S(1)} %relay.2.rest_4_), channel_id=1, source_target_pairs={{0,4},{2,6},{4,0},{6,2},{1,5},{3,7},{5,1},{7,3},{8,12},{10,14},{12... | collective-permute-start | bytes 1179656 | tf_op jit(solution)/shard_map/ppermute | solution.py:375
  65.9 10.1 %collective-permute-start.14 = (bf16[16,1536]{1,0:T(8,128)(2,1)S(1)}, bf16[16,1536]{1,0:T(8,128)(2,1)S(1)}, u32[]{:S(2)}, u32[]{:S(2)}) collective-permute-start(bf16[16,1536]{1,0:T(8,128)(2,1)S(1)} %get-tuple-element.61), channel_id=1, source_target_pairs={{0,2},{2,0},{4,6},{6,4},{1,3},{3,1},{5,7},{7,5},{8,10},{10,8},{12,... | collective-permute-start | bytes 147464 | tf_op jit(solution)/shard_map/ppermute | solution.py:375
  66.6 9.5 %collective-permute-start.15 = (bf16[16,1536]{1,0:T(8,128)(2,1)S(1)}, bf16[16,1536]{1,0:T(8,128)(2,1)S(1)}, u32[]{:S(2)}, u32[]{:S(2)}) collective-permute-start(bf16[16,1536]{1,0:T(8,128)(2,1)S(1)} %get-tuple-element.62), channel_id=1, source_target_pairs={{0,4},{2,6},{4,0},{6,2},{1,5},{3,7},{5,1},{7,3},{8,12},{10,14},{12... | collective-permute-start | bytes 147464 | tf_op jit(solution)/shard_map/ppermute | solution.py:375
  68.0 8.5 %collective-permute-start.16 = (bf16[16,1536]{1,0:T(8,128)(2,1)S(1)}, bf16[16,1536]{1,0:T(8,128)(2,1)S(1)}, u32[]{:S(2)}, u32[]{:S(2)}) collective-permute-start(bf16[16,1536]{1,0:T(8,128)(2,1)S(1)} %get-tuple-element.63), channel_id=1, source_target_pairs={{0,6},{2,4},{4,2},{6,0},{1,7},{3,5},{5,3},{7,1},{8,14},{10,12},{12... | collective-permute-start | bytes 147464 | tf_op jit(solution)/shard_map/ppermute | solution.py:375

commit v8 on v7

--- a/solution.py
+++ b/solution.py
@@ -13,7 +13,7 @@
 HIGH = lax.Precision.HIGHEST
 CHUNKS = 2
 WEIGHT_PARTS = 4
-EARLY_PARTS = 3
+EARLY_PARTS = 2
 VMEM_BYTES = 8 * 2**20
 F32 = jnp.float32
 BF16 = jnp.bfloat16
@@ -148,16 +148,10 @@
     own_states(0, k_ref, v_ref, columns, own_ref, message_ref)
 
 
-def more_state_kernel(first, copied, k_ref, v_ref, col_ref, rate_ref, log_ref, *refs):
-    sources, refs = refs[:copied], refs[copied:]
-    own_ref, message_ref, row_ref = refs[:3]
-    targets, sems = refs[3 : 3 + copied], refs[3 + copied]
-    copies = started(tuple(zip(sources, targets)), sems) if copied else []
-    row_ref[...] = decay_rows(rate_ref[0], lower_ones(k_ref.shape[0]))
+def more_state_kernel(first, k_ref, v_ref, col_ref, log_ref, *rest):
+    own_ref, message_ref = rest[-2:]
     message_ref[message_ref.shape[0] - LOG_ROWS :, :] = log_rows(log_ref[...])
     own_states(first, k_ref, v_ref, col_ref[...], own_ref, message_ref)
-    for copy in copies:
-        copy.wait()
 
 
 def chain_kernel(phase, first, place_ref, own_ref, log_ref, got_ref, *rest):
@@ -205,22 +199,25 @@
         copy.wait()
 
 
-def local_kernel(first, q_ref, k_ref, v_ref, col_ref, row_ref, weight_hbm, *rest):
+def local_kernel(copied, k_ref, v_ref, col_ref, rate_ref, weight_hbm, *rest):
+    sources, rest = rest[:copied], rest[copied:]
+    targets, rest = rest[:copied], rest[copied:]
     local_ref, token_ref = rest[:2]
-    weights, sems = rest[2:-1], rest[-1]
+    weights, sems, more = rest[2:-2], rest[-2], rest[-1]
+    loads = started(tuple(zip(sources, targets)), more)
     copies = weight_copies(range(len(weights)), weight_hbm, weights, sems)
     token_ref[...] = jnp.zeros_like(token_ref)
-    lower = lower_ones(q_ref.shape[1])
-    for i in range(local_ref.shape[1] // HEAD_DIM):
-        h = first + i
+    q_ref = targets[0]
+    lower = lower_ones(k_ref.shape[0])
+    rows = decay_rows(rate_ref[0], lower)
+    loads[0].wait()
+    for h in range(local_ref.shape[1] // HEAD_DIM):
         at = head_slice(h)
         scores = lax.dot_general(q_ref[0, :, at], k_ref[:, at], NT, preferred_element_type=F32)
-        decay = jnp.exp(
-            jnp.where(lower, col_ref[:, h : h + 1] - row_ref[h : h + 1, :], NEGATIVE)
-        )
+        decay = jnp.exp(jnp.where(lower, col_ref[:, h : h + 1] - rows[h : h + 1, :], NEGATIVE))
         narrow = (scores * decay).astype(BF16)
-        local_ref[:, head_slice(i)] = jnp.dot(narrow, v_ref[:, at], preferred_element_type=F32)
-    for copy in copies:
+        local_ref[:, at] = jnp.dot(narrow, v_ref[:, at], preferred_element_type=F32)
+    for copy in loads[1:] + copies:
         copy.wait()
 
 
@@ -433,38 +430,34 @@
     )(place, in_hbm(prefill_key), in_hbm(prefill_value), in_hbm(prefill_rate))
     own, log_row, columns, rate, keys, values = map(in_vmem, made[:6])
     owns, values_out = [own], [made[6]]
-    for c, (first, size) in enumerate(chunks[1:]):
-        arrays = (prefill_query, decode_query, decode_key, decode_value) if c == 0 else ()
-        made = call(
-            functools.partial(more_state_kernel, first, len(arrays)),
-            "more_state",
-            [VMEM] * 5 + [HBM] * len(arrays),
-            [
-                pltpu.VMEM((size, HEAD_DIM, HEAD_DIM), F32),
-                message_shape(size),
-                pltpu.VMEM((heads, length), F32),
-            ]
-            + [pltpu.VMEM(array.shape, BF16) for array in arrays],
-            [pltpu.SemaphoreType.DMA((max(len(arrays), 1),))],
-            cost(4 * length * size * HEAD_DIM * HEAD_DIM, 8 * length * features),
-        )(keys, values, columns, rate, log_row, *map(in_hbm, arrays))
-        owns.append(in_vmem(made[0]))
-        values_out.append(made[1])
-        if c == 0:
-            rows, queries, d_query, d_key, d_value = map(in_vmem, made[2:])
-
     weight_hbm = in_hbm(out_weight)
     weight_part = pltpu.VMEM((features // WEIGHT_PARTS, out_weight.shape[1]), BF16)
     token = sds((8, HEAD_DIM), F32)
-    local, local_token, *weights = call(
-        functools.partial(local_kernel, 0),
+    arrays = (prefill_query, decode_query, decode_key, decode_value)
+    queries, d_query, d_key, d_value, local, local_token, *weights = call(
+        functools.partial(local_kernel, len(arrays)),
         "local_attention",
-        [VMEM] * 5 + [HBM],
-        [pltpu.VMEM((length, features), F32), token] + [weight_part] * EARLY_PARTS,
-        [pltpu.SemaphoreType.DMA((EARLY_PARTS,))],
+        [VMEM] * 4 + [HBM] * (1 + len(arrays)),
+        [pltpu.VMEM(array.shape, BF16) for array in arrays]
+        + [pltpu.VMEM((length, features), F32), token]
+        + [weight_part] * EARLY_PARTS,
+        [pltpu.SemaphoreType.DMA((EARLY_PARTS,)), pltpu.SemaphoreType.DMA((len(arrays),))],
         cost(4 * length * length * features, 12 * length * features, heads * length * length),
-    )(queries, keys, values, columns, rows, weight_hbm)
-    local = in_vmem(local)
+    )(keys, values, columns, rate, weight_hbm, *map(in_hbm, arrays))
+    queries, d_query, d_key, d_value, local = map(
+        in_vmem, (queries, d_query, d_key, d_value, local)
+    )
+    for first, size in chunks[1:]:
+        made = call(
+            functools.partial(more_state_kernel, first),
+            "more_state",
+            [VMEM] * 4 + [ANY],
+            [pltpu.VMEM((size, HEAD_DIM, HEAD_DIM), F32), message_shape(size)],
+            (),
+            cost(4 * length * size * HEAD_DIM * HEAD_DIM, 8 * length * features),
+        )(keys, values, columns, log_row, local_token)
+        owns.append(in_vmem(made[0]))
+        values_out.append(made[1])
 
     def load_weight(*after):
         if len(weights) == WEIGHT_PARTS:
@@ -481,12 +474,18 @@
         return [done]
 
     received = []
-    after = [local_token]
+    after = values_out[-1:]
     for phase in range(phases):
-        target = list(range(groups))
-        for low in (phase, groups - 2 - phase):
-            target[low], target[low + 1] = low + 1, low
-        pairs = list(enumerate(target))
+        pairs = []
+        for g in range(groups):
+            for r in range(reps):
+                if g in (phase, groups - 2 - phase):
+                    other = (g + 1, r)
+                elif g in (phase + 1, groups - 1 - phase):
+                    other = (g - 1, r)
+                else:
+                    other = (g, r ^ 1)
+                pairs.append((g * reps + r, other[0] * reps + other[1]))
         if phase > 0:
             values_out = []
             for c, (first, size) in enumerate(chunks):
@@ -500,7 +499,7 @@
                 )(place, owns[c], log_row, received[-1][c], *after)
                 values_out.append(value)
                 after = []
-        received.append([lax.ppermute(value, "ctx", pairs) for value in values_out])
+        received.append([lax.ppermute(value, ("ctx", "rep"), pairs) for value in values_out])
     loaded = []
     while len(weights) < WEIGHT_PARTS:
         loaded = load_weight(values_out[-1], *loaded)

time: 78.6 us -> 77.3 us (0.983)
  starting transfers between devices: 27.1 us -> 22 us
  waiting for transfers between devices: 10.9 us -> 13.3 us
  Pallas kernels: 39.2 us -> 40.6 us
    ppermute x6, starting transfers between devices: 16 us -> 11 us  [body(): lax.ppermute(value, ('ctx', 'rep'), pairs)]
    pallas_call x1 -> x2, Pallas kernels: 2.79 us -> 5.59 us  [load_weight(): call(functools.partial(load_kernel, len(weights)), 'load_weight', [HBM] +...]
    ppermute x6, waiting for transfers between devices: 4.52 us -> 7.04 us  [body(): lax.ppermute(value, ('ctx', 'rep'), pairs)]
    pallas_call x2, Pallas kernels: 7.69 us -> 6.18 us  [the longest x1 5.01 us: body(): call(functools.partial(local_kernel, len(arrays)), 'local_attention', [VM...]
  transfers between devices with their start and end apart: 17 -> 17, of which waited for: 6 -> 6; matrix products, arithmetic and copies ran while one was open for 0% -> 0% of each run, Pallas kernels for 39% -> 41%
where the time goes in v8:
time: 77.3 us; the launch traced here: 77.1 us
  Pallas kernels  40.6 us (53%)
  starting transfers between devices  22 us (28%)
  waiting for transfers between devices  13.3 us (17%)
  between operations  1.01 us (1%)
    ppermute x11, starting transfers between devices, swap(): return lax.ppermute(array, axis, [(i, i ^ bit) for i in range(size)])  11 us
    ppermute x6, starting transfers between devices, body(): lax.ppermute(value, ('ctx', 'rep'), pairs)  11 us
    pallas_call x5, Pallas kernels, project(): call(functools.partial(project_kernel, pieces, count), 'project', [SMEM]...  10.4 us
    ppermute x6, waiting for transfers between devices, body(): lax.ppermute(value, ('ctx', 'rep'), pairs)  7.04 us
    ppermute x11, waiting for transfers between devices, swap(): return lax.ppermute(array, axis, [(i, i ^ bit) for i in range(size)])  6.29 us
    pallas_call x2, Pallas kernels, load_weight(): call(functools.partial(load_kernel, len(weights)), 'load_weight', [HBM] +...  5.59 us
    pallas_call x1, Pallas kernels, body(): call(functools.partial(local_kernel, len(arrays)), 'local_attention', [VM...  5.01 us
    pallas_call x1, Pallas kernels, body(): call(decode_project_kernel, 'decode_project', [SMEM] + [VMEM] * (1 + WEIG...  3.92 us
  transfers between devices with their start and end apart: 17, of which 6 were waited for; matrix products, arithmetic and copies ran while one was open for 0% of the time, Pallas kernels for 41%

profile of v8, /device:TPU:0, one launch (start us, length us, event | category | flops | bytes accessed | tf_op | source)
XLA Modules:
  0.0 77.1 jit_solution(13745938716246960093)
XLA Ops:
  0.6 0.1 pad_add_fusion.place_ref
  0.7 3.2 %own_state.1 = (f32[8,128,128]{2,1,0:T(8,128)S(1)}, f32[1,128]{1,0:T(1,128)S(1)}, f32[256,16]{1,0:T(8,128)S(1)}, f32[1,16,256]{2,1,0:T(8,128)S(1)}, bf16[256,204...) custom-call(s32[3]{0:T(128)S(1)} %pad_add_fusion.place_ref, ...), custom_call_target="tpu_custom_call" | custom-call | flops 268435456 | bytes 8388608 | tf_op jit(solution)/shard_map/own_state/pallas_call | solution.py:415
  4.0 3.1 %collective-permute-start = (bf16[1040,128]{1,0:T(8,128)(2,1)S(1)}, bf16[1040,128]{1,0:T(8,128)(2,1)S(1)}, u32[]{:S(2)}, u32[]{:S(2)}) collective-permute-start(bf16[1040,128]{1,0:T(8,128)(2,1)S(1)} %get-tuple-element.39), channel_id=1, source_target_pairs={{0,8},{1,9},{8,0},{9,1},{16,24},{17,25},{24,16},{25,17},{2,10},{3,... | collective-permute-start | bytes 798728 | tf_op jit(solution)/shard_map/ppermute | solution.py:502
  7.0 5.0 %local_attention.1 = (bf16[1,256,2048]{2,1,0:T(8,128)(2,1)S(1)}, bf16[4,2,2048]{2,1,0:T(2,128)(2,1)S(1)}, bf16[4,2,2048]{2,1,0:T(2,128)(2,1)S(1)}, bf16[4,2,2048...) custom-call(bf16[256,2048]{1,0:T(8,128)(2,1)S(1)} %get-tuple-element, ...), custom_call_target="tpu_custom_call" | custom-call | flops 536870912 | bytes 6291456 | tf_op jit(solution)/shard_map/local_attention/pallas_call | solution.py:437
  12.1 1.2 %more_state.1 = (f32[8,128,128]{2,1,0:T(8,128)S(1)}, bf16[1040,128]{1,0:T(8,128)(2,1)S(1)}) custom-call(bf16[256,2048]{1,0:T(8,128)(2,1)S(1)} %get-tuple-element.33.k_ref, bf16[256,2048]{1,0:T(8,128)(2,1)S(1)} %get-tuple-element.34.v_ref, f32[256,16]{1,0:T(8,128)S(1)} %get-tuple-element.35.col_ref, f32[1,128]{1,0:T(1,128)S(1)} %get-tuple-element.41.log_ref, ...), custom_call_target="tpu_custom_call" | custom-call | flops 134217728 | bytes 4194304 | tf_op jit(solution)/shard_map/more_state/pallas_call | solution.py:451
  13.2 0.1 collective-permute-start.3
  13.3 0.1 collective-permute-done.got_ref.rest_0_
  13.4 0.7 chain.4
  14.2 0.1 collective-permute-start.1
  14.2 6.9 %collective-permute-done.3.got_ref.rest_0_ = bf16[1040,128]{1,0:T(8,128)(2,1)S(1)} collective-permute-done((bf16[1040,128]{1,0:T(8,128)(2,1)S(1)}, bf16[1040,128]{1,0:T(8,128)(2,1)S(1)}, u32[]{:S(2)}, u32[]{:S(2)}) %collective-permute-start.3) | collective-permute-done | bytes 266272 | tf_op jit(solution)/shard_map/ppermute | solution.py:502
  21.2 0.7 chain.6
  21.9 0.1 collective-permute-start.4
  22.0 0.0 collective-permute-done.1.got_ref.rest_1_
  22.0 0.7 chain.5
  22.7 3.2 %collective-permute-start.2 = (bf16[1040,128]{1,0:T(8,128)(2,1)S(1)}, bf16[1040,128]{1,0:T(8,128)(2,1)S(1)}, u32[]{:S(2)}, u32[]{:S(2)}) collective-permute-start(bf16[1040,128]{1,0:T(8,128)(2,1)S(1)} %chain.5), channel_id=1, source_target_pairs={{0,8},{1,9},{8,0},{9,1},{16,24},{17,25},{24,16},{25,17},{2,10},{3,... | collective-permute-start | bytes 798728 | tf_op jit(solution)/shard_map/ppermute | solution.py:502
  25.9 0.0 collective-permute-done.4.got_ref.rest_1_
  25.9 0.7 chain.7.rest_0_
  26.6 4.5 %collective-permute-start.5 = (bf16[1040,128]{1,0:T(8,128)(2,1)S(1)}, bf16[1040,128]{1,0:T(8,128)(2,1)S(1)}, u32[]{:S(2)}, u32[]{:S(2)}) collective-permute-start(bf16[1040,128]{1,0:T(8,128)(2,1)S(1)} %chain.7.rest_0_), channel_id=1, source_target_pairs={{0,8},{1,9},{8,0},{9,1},{16,24},{17,25},{24,16},{25,17},{2,10},{3,... | collective-permute-start | bytes 798728 | tf_op jit(solution)/shard_map/ppermute | solution.py:502
  31.1 2.8 %load_weight.2 = (bf16[512,6144]{1,0:T(8,128)(2,1)S(1)}, f32[8,128]{1,0:T(8,128)S(1)}) custom-call(bf16[2048,6144]{1,0:T(8,128)(2,1)} %weight_hbm.5, bf16[1040,128]{1,0:T(8,128)(2,1)S(1)} %chain.7.rest_0_), custom_call_target="tpu_custom_call" | custom-call | flops 1 | bytes 6291456 | tf_op jit(solution)/shard_map/load_weight/pallas_call | solution.py:465
  33.9 2.8 %load_weight.3 = (bf16[512,6144]{1,0:T(8,128)(2,1)S(1)}, f32[8,128]{1,0:T(8,128)S(1)}) custom-call(bf16[2048,6144]{1,0:T(8,128)(2,1)} %weight_hbm.5, bf16[1040,128]{1,0:T(8,128)(2,1)S(1)} %chain.7.rest_0_, f32[8,128]{1,0:T(8,128)S(1)} %get-tuple-element.45.rest_1_), custom_call_target="tpu_custom_call" | custom-call | flops 1 | bytes 6291456 | tf_op jit(solution)/shard_map/load_weight/pallas_call | solution.py:465
  36.7 0.0 collective-permute-done.2.rest_2_
  36.7 1.6 %hidden.2.rest_0_ = bf16[256,1024]{1,0:T(8,128)(2,1)S(1)} custom-call(s32[3]{0:T(128)S(1)} %pad_add_fusion.place_ref, bf16[1,256,2048]{2,1,0:T(8,128)(2,1)S(1)} %get-tuple-element.37.q_ref, f32[256,16]{1,0:T(8,128)S(1)} %get-tuple-element.35.col_ref, f32[256,2048]{1,0:T(8,128)S(1)} %get-tuple-element.38.local_ref, ...), custom_call_target="tpu_custom_call" | custom-call | flops 67108864 | bytes 5242880 | tf_op jit(solution)/shard_map/hidden/pallas_call | solution.py:510
  38.4 0.0 collective-permute-done.5.rest_2_
  38.4 1.6 %hidden.3.rest_1_ = bf16[256,1024]{1,0:T(8,128)(2,1)S(1)} custom-call(s32[3]{0:T(128)S(1)} %pad_add_fusion.place_ref, bf16[1,256,2048]{2,1,0:T(8,128)(2,1)S(1)} %get-tuple-element.37.q_ref, f32[256,16]{1,0:T(8,128)S(1)} %get-tuple-element.35.col_ref, f32[256,2048]{1,0:T(8,128)S(1)} %get-tuple-element.38.local_ref, ...), custom_call_target="tpu_custom_call" | custom-call | flops 67108864 | bytes 5242880 | tf_op jit(solution)/shard_map/hidden/pallas_call | solution.py:510
  40.0 2.4 %project.8 = (bf16[256,768]{1,0:T(8,128)(2,1)S(1)}, bf16[256,768]{1,0:T(8,128)(2,1)S(1)}) custom-call(s32[3]{0:T(128)S(1)} %pad_add_fusion.place_ref, bf16[256,1024]{1,0:T(8,128)(2,1)S(1)} %hidden.2.rest_0_, bf16[256,1024]{1,0:T(8,128)(2,1)S(1)} %hidden.3.rest_1_, bf16[512,6144]{1,0:T(8,128)(2,1)S(1)} %get-tuple-element.47.rest_2_.rest_0_, ...), custom_call_target="tpu_custom_call" | custom-call | flops 1610612736 | bytes 6291456 | tf_op jit(solution)/shard_map/project/pallas_call | solution.py:571
  42.4 1.6 %collective-permute-start.9 = (bf16[256,768]{1,0:T(8,128)(2,1)S(1)}, bf16[256,768]{1,0:T(8,128)(2,1)S(1)}, u32[]{:S(2)}, u32[]{:S(2)}) collective-permute-start(bf16[256,768]{1,0:T(8,128)(2,1)S(1)} %get-tuple-element.56.rest_3_), channel_id=1, source_target_pairs={{0,4},{2,6},{4,0},{6,2},{1,5},{3,7},{5,1},{7,3},{8,12},{10,14},{12... | collective-permute-start | bytes 1179656 | tf_op jit(solution)/shard_map/ppermute | solution.py:372
  44.0 0.8 %final_state.2.rest_0_ = f32[8,128,128]{2,1,0:T(8,128)S(1)} custom-call(s32[3]{0:T(128)S(1)} %pad_add_fusion.place_ref, f32[8,128,128]{2,1,0:T(8,128)S(1)} %get-tuple-element.40.own_ref, f32[1,128]{1,0:T(1,128)S(1)} %get-tuple-element.41.log_ref, bf16[1040,128]{1,0:T(8,128)(2,1)S(1)} %collective-permute-done.got_ref.rest_0_, ...), custom_call_target="tpu_custom_call" | custom-call | flops 524288 | bytes 1048576 | tf_op jit(solution)/shard_map/final_state/pallas_call | solution.py:526
  44.8 0.1 collective-permute-start.12
  44.9 1.6 %collective-permute-start.7 = (bf16[256,768]{1,0:T(8,128)(2,1)S(1)}, bf16[256,768]{1,0:T(8,128)(2,1)S(1)}, u32[]{:S(2)}, u32[]{:S(2)}) collective-permute-start(bf16[256,768]{1,0:T(8,128)(2,1)S(1)} %get-tuple-element.54), channel_id=1, source_target_pairs={{0,2},{2,0},{4,6},{6,4},{1,3},{3,1},{5,7},{7,5},{8,10},{10,8},{12,... | collective-permute-start | bytes 1179656 | tf_op jit(solution)/shard_map/ppermute | solution.py:372
  46.5 0.8 %final_state.3.rest_1_ = f32[8,128,128]{2,1,0:T(8,128)S(1)} custom-call(s32[3]{0:T(128)S(1)} %pad_add_fusion.place_ref, f32[8,128,128]{2,1,0:T(8,128)S(1)} %get-tuple-element.44.own_ref, f32[1,128]{1,0:T(1,128)S(1)} %get-tuple-element.41.log_ref, bf16[1040,128]{1,0:T(8,128)(2,1)S(1)} %collective-permute-done.3.got_ref.rest_0_, ...), custom_call_target="tpu_custom_call" | custom-call | flops 524288 | bytes 1048576 | tf_op jit(solution)/shard_map/final_state/pallas_call | solution.py:526
  47.3 0.2 collective-permute-start.13
  47.5 1.5 %project.9 = bf16[256,768]{1,0:T(8,128)(2,1)S(1)} custom-call(s32[3]{0:T(128)S(1)} %pad_add_fusion.place_ref, bf16[256,1024]{1,0:T(8,128)(2,1)S(1)} %hidden.2.rest_0_, bf16[256,1024]{1,0:T(8,128)(2,1)S(1)} %hidden.3.rest_1_, bf16[512,6144]{1,0:T(8,128)(2,1)S(1)} %get-tuple-element.47.rest_2_.rest_0_, ...), custom_call_target="tpu_custom_call" | custom-call | flops 805306368 | bytes 3145728 | tf_op jit(solution)/shard_map/project/pallas_call | solution.py:571
  49.1 1.6 %project.6 = bf16[256,768]{1,0:T(8,128)(2,1)S(1)} custom-call(s32[3]{0:T(128)S(1)} %pad_add_fusion.place_ref, bf16[256,1024]{1,0:T(8,128)(2,1)S(1)} %hidden.2.rest_0_, bf16[256,1024]{1,0:T(8,128)(2,1)S(1)} %hidden.3.rest_1_, bf16[512,6144]{1,0:T(8,128)(2,1)S(1)} %get-tuple-element.47.rest_2_.rest_0_, ...), custom_call_target="tpu_custom_call" | custom-call | flops 805306368 | bytes 3145728 | tf_op jit(solution)/shard_map/project/pallas_call | solution.py:571
  50.6 0.0 copy-start
  50.7 0.0 copy-start.1
  50.7 0.6 collective-permute-start.6
  51.3 0.0 collective-permute-done.9.got_ref
  51.3 1.4 %collective-permute-start.11 = (bf16[256,768]{1,0:T(8,128)(2,1)S(1)}, bf16[256,768]{1,0:T(8,128)(2,1)S(1)}, u32[]{:S(2)}, u32[]{:S(2)}) collective-permute-start(bf16[256,768]{1,0:T(8,128)(2,1)S(1)} %project.9), channel_id=1, source_target_pairs={{0,4},{2,6},{4,0},{6,2},{1,5},{3,7},{5,1},{7,3},{8,12},{10,14},{12... | collective-permute-start | bytes 1179656 | tf_op jit(solution)/shard_map/ppermute | solution.py:372
  52.7 2.6 %project.7 = (f32[256,768]{1,0:T(8,128)S(1)}, f32[256,768]{1,0:T(8,128)S(1)}) custom-call(s32[3]{0:T(128)S(1)} %pad_add_fusion.place_ref, bf16[256,1024]{1,0:T(8,128)(2,1)S(1)} %hidden.2.rest_0_, bf16[256,1024]{1,0:T(8,128)(2,1)S(1)} %hidden.3.rest_1_, bf16[512,6144]{1,0:T(8,128)(2,1)S(1)} %get-tuple-element.47.rest_2_.rest_0_, ...), custom_call_target="tpu_custom_call" | custom-call | flops 1610612736 | bytes 6291456 | tf_op jit(solution)/shard_map/project/pallas_call | solution.py:571
  55.3 0.1 relay.3.rest_5_
  55.4 1.5 %collective-permute-done.7.got_ref = bf16[256,768]{1,0:T(8,128)(2,1)S(1)} collective-permute-done((bf16[256,768]{1,0:T(8,128)(2,1)S(1)}, bf16[256,768]{1,0:T(8,128)(2,1)S(1)}, u32[]{:S(2)}, u32[]{:S(2)}) %collective-permute-start.7) | collective-permute-done | bytes 393248 | tf_op jit(solution)/shard_map/ppermute | solution.py:372
  56.9 1.5 %collective-permute-start.10 = (bf16[256,768]{1,0:T(8,128)(2,1)S(1)}, bf16[256,768]{1,0:T(8,128)(2,1)S(1)}, u32[]{:S(2)}, u32[]{:S(2)}) collective-permute-start(bf16[256,768]{1,0:T(8,128)(2,1)S(1)} %relay.3.rest_5_), channel_id=1, source_target_pairs={{0,2},{2,0},{4,6},{6,4},{1,3},{3,1},{5,7},{7,5},{8,10},{10,8},{12,... | collective-permute-start | bytes 1179656 | tf_op jit(solution)/shard_map/ppermute | solution.py:372
  58.4 0.1 relay.2.rest_4_
  58.5 0.0 collective-permute-done.12.rest_2_
  58.5 0.6 collective-permute-start.8
  59.0 0.0 collective-permute-done.13.rest_3_
  59.0 0.0 copy-done
  59.0 0.0 copy-done.1
  59.0 1.7 %decode_rows.1.rows_ref = bf16[16,2048]{1,0:T(8,128)(2,1)S(1)} custom-call(s32[3]{0:T(128)S(1)} %pad_add_fusion.place_ref, s32[4]{0:T(128)S(1)} %copy-done.1, bf16[4,2,2048]{2,1,0:T(2,128)(2,1)S(1)} %get-tuple-element.57.q_ref, bf16[4,2,2048]{2,1,0:T(2,128)(2,1)S(1)} %get-tuple-element.58.k_ref, bf16[4,2,2048]{2,1,0:T(2,128)(2,1)S(1)} %get-tuple-element.59.v_ref, ...), custom_call_target="tpu_custom_call" | custom-call | flops 33554432 | bytes 262144 | tf_op jit(solution)/shard_map/decode_rows/pallas_call | solution.py:539
  60.8 3.9 %decode_project.1 = (f32[16,1536]{1,0:T(8,128)S(1)}, bf16[16,1536]{1,0:T(8,128)(2,1)S(1)}, bf16[16,1536]{1,0:T(8,128)(2,1)S(1)}, bf16[16,1536]{1,0:T(8,128)(2,1)S(1)}) custom-call(s32[3]{0:T(128)S(1)} %pad_add_fusion.place_ref, bf16[16,2048]{1,0:T(8,128)(2,1)S(1)} %decode_rows.1.rows_ref, bf16[512,6144]{1,0:T(8,128)(2,1)S(1)} %get-tuple-element.47.rest_2_.rest_0_, ...), custom_call_target="tpu_custom_call" | custom-call | flops 402653184 | bytes 1572864 | tf_op jit(solution)/shard_map/decode_project/pallas_call | solution.py:602
  64.7 0.6 collective-permute-start.14
  65.2 0.1 collective-permute-done.6.ax
  65.3 1.5 %collective-permute-start.15 = (bf16[16,1536]{1,0:T(8,128)(2,1)S(1)}, bf16[16,1536]{1,0:T(8,128)(2,1)S(1)}, u32[]{:S(2)}, u32[]{:S(2)}) collective-permute-start(bf16[16,1536]{1,0:T(8,128)(2,1)S(1)} %get-tuple-element.62), channel_id=1, source_target_pairs={{0,4},{2,6},{4,0},{6,2},{1,5},{3,7},{5,1},{7,3},{8,12},{10,14},{12... | collective-permute-start | bytes 147464 | tf_op jit(solution)/shard_map/ppermute | solution.py:372
  66.8 0.0 collective-permute-done.11.by
  66.8 1.5 %collective-permute-start.16 = (bf16[16,1536]{1,0:T(8,128)(2,1)S(1)}, bf16[16,1536]{1,0:T(8,128)(2,1)S(1)}, u32[]{:S(2)}, u32[]{:S(2)}) collective-permute-start(bf16[16,1536]{1,0:T(8,128)(2,1)S(1)} %get-tuple-element.63), channel_id=1, source_target_pairs={{0,6},{2,4},{4,2},{6,0},{1,7},{3,5},{5,3},{7,1},{8,14},{10,12},{12... | collective-permute-start | bytes 147464 | tf_op jit(solution)/shard_map/ppermute | solution.py:372
  68.3 2.4 %project.5 = (f32[256,768]{1,0:T(8,128)S(1)}, f32[256,768]{1,0:T(8,128)S(1)}) custom-call(s32[3]{0:T(128)S(1)} %pad_add_fusion.place_ref, bf16[256,1024]{1,0:T(8,128)(2,1)S(1)} %hidden.2.rest_0_, bf16[256,1024]{1,0:T(8,128)(2,1)S(1)} %hidden.3.rest_1_, bf16[512,6144]{1,0:T(8,128)(2,1)S(1)} %get-tuple-element.47.rest_2_.rest_0_, ...), custom_call_target="tpu_custom_call" | custom-call | flops 1610612736 | bytes 6291456 | tf_op jit(solution)/shard_map/project/pallas_call | solution.py:571
  70.6 4.2 %collective-permute-done.14.d_x = bf16[16,1536]{1,0:T(8,128)(2,1)S(1)} collective-permute-done((bf16[16,1536]{1,0:T(8,128)(2,1)S(1)}, bf16[16,1536]{1,0:T(8,128)(2,1)S(1)}, u32[]{:S(2)}, u32[]{:S(2)}) %collective-permute-start.14) | collective-permute-done | bytes 49184 | tf_op jit(solution)/shard_map/ppermute | solution.py:372
  74.8 0.0 collective-permute-done.15.d_y
  74.8 0.5 collective-permute-done.16.d_far
  75.3 0.0 collective-permute-done.10.bx
  75.3 0.0 collective-permute-done.8.ay
  75.3 1.6 %finish.1 = (bf16[1,256,1536]{2,1,0:T(8,128)(2,1)}, bf16[4,2,1536]{2,1,0:T(2,128)(2,1)}) custom-call(f32[256,768]{1,0:T(8,128)S(1)} %get-tuple-element.51.own_a, f32[256,768]{1,0:T(8,128)S(1)} %get-tuple-element.52.own_b, bf16[256,768]{1,0:T(8,128)(2,1)S(1)} %collective-permute-done.6.ax, bf16[256,768]{1,0:T(8,128)(2,1)S(1)} %collective-permute-done.8.ay, ...), custom_call_target="tpu_custom_call" | custom-call | flops 1179648 | bytes 3932160 | tf_op jit(solution)/shard_map/finish/pallas_call | solution.py:610
Async XLA Ops:
  4.0 9.5 %collective-permute-start = (bf16[1040,128]{1,0:T(8,128)(2,1)S(1)}, bf16[1040,128]{1,0:T(8,128)(2,1)S(1)}, u32[]{:S(2)}, u32[]{:S(2)}) collective-permute-start(bf16[1040,128]{1,0:T(8,128)(2,1)S(1)} %get-tuple-element.39), channel_id=1, source_target_pairs={{0,8},{1,9},{8,0},{9,1},{16,24},{17,25},{24,16},{25,17},{2,10},{3,... | collective-permute-start | bytes 798728 | tf_op jit(solution)/shard_map/ppermute | solution.py:502
  13.2 7.9 %collective-permute-start.3 = (bf16[1040,128]{1,0:T(8,128)(2,1)S(1)}, bf16[1040,128]{1,0:T(8,128)(2,1)S(1)}, u32[]{:S(2)}, u32[]{:S(2)}) collective-permute-start(bf16[1040,128]{1,0:T(8,128)(2,1)S(1)} %get-tuple-element.43.rest_0_), channel_id=1, source_target_pairs={{0,8},{1,9},{8,0},{9,1},{16,24},{17,25},{24,16},{25,17},{2,10},{3,... | collective-permute-start | bytes 798728 | tf_op jit(solution)/shard_map/ppermute | solution.py:502
  14.2 7.8 %collective-permute-start.1 = (bf16[1040,128]{1,0:T(8,128)(2,1)S(1)}, bf16[1040,128]{1,0:T(8,128)(2,1)S(1)}, u32[]{:S(2)}, u32[]{:S(2)}) collective-permute-start(bf16[1040,128]{1,0:T(8,128)(2,1)S(1)} %chain.4), channel_id=1, source_target_pairs={{0,1},{1,0},{8,16},{9,17},{16,8},{17,9},{24,25},{25,24},{2,3},{3,2... | collective-permute-start | bytes 798728 | tf_op jit(solution)/shard_map/ppermute | solution.py:502
  21.9 4.0 %collective-permute-start.4 = (bf16[1040,128]{1,0:T(8,128)(2,1)S(1)}, bf16[1040,128]{1,0:T(8,128)(2,1)S(1)}, u32[]{:S(2)}, u32[]{:S(2)}) collective-permute-start(bf16[1040,128]{1,0:T(8,128)(2,1)S(1)} %chain.6), channel_id=1, source_target_pairs={{0,1},{1,0},{8,16},{9,17},{16,8},{17,9},{24,25},{25,24},{2,3},{3,2... | collective-permute-start | bytes 798728 | tf_op jit(solution)/shard_map/ppermute | solution.py:502
  22.7 14.0 %collective-permute-start.2 = (bf16[1040,128]{1,0:T(8,128)(2,1)S(1)}, bf16[1040,128]{1,0:T(8,128)(2,1)S(1)}, u32[]{:S(2)}, u32[]{:S(2)}) collective-permute-start(bf16[1040,128]{1,0:T(8,128)(2,1)S(1)} %chain.5), channel_id=1, source_target_pairs={{0,8},{1,9},{8,0},{9,1},{16,24},{17,25},{24,16},{25,17},{2,10},{3,... | collective-permute-start | bytes 798728 | tf_op jit(solution)/shard_map/ppermute | solution.py:502
  26.6 11.7 %collective-permute-start.5 = (bf16[1040,128]{1,0:T(8,128)(2,1)S(1)}, bf16[1040,128]{1,0:T(8,128)(2,1)S(1)}, u32[]{:S(2)}, u32[]{:S(2)}) collective-permute-start(bf16[1040,128]{1,0:T(8,128)(2,1)S(1)} %chain.7.rest_0_), channel_id=1, source_target_pairs={{0,8},{1,9},{8,0},{9,1},{16,24},{17,25},{24,16},{25,17},{2,10},{3,... | collective-permute-start | bytes 798728 | tf_op jit(solution)/shard_map/ppermute | solution.py:502
  42.4 8.9 %collective-permute-start.9 = (bf16[256,768]{1,0:T(8,128)(2,1)S(1)}, bf16[256,768]{1,0:T(8,128)(2,1)S(1)}, u32[]{:S(2)}, u32[]{:S(2)}) collective-permute-start(bf16[256,768]{1,0:T(8,128)(2,1)S(1)} %get-tuple-element.56.rest_3_), channel_id=1, source_target_pairs={{0,4},{2,6},{4,0},{6,2},{1,5},{3,7},{5,1},{7,3},{8,12},{10,14},{12... | collective-permute-start | bytes 1179656 | tf_op jit(solution)/shard_map/ppermute | solution.py:372
  44.8 13.6 %collective-permute-start.12 = (f32[8,128,128]{2,1,0:T(8,128)S(1)}, f32[8,128,128]{2,1,0:T(8,128)S(1)}, u32[]{:S(2)}, u32[]{:S(2)}) collective-permute-start(f32[8,128,128]{2,1,0:T(8,128)S(1)} %final_state.2.rest_0_), channel_id=1, source_target_pairs={{0,1},{1,0},{2,3},{3,2},{4,5},{5,4},{6,7},{7,6},{8,9},{9,8},{10,11... | collective-permute-start | bytes 1572872 | tf_op jit(solution)/shard_map/ppermute | solution.py:372
  44.9 12.0 %collective-permute-start.7 = (bf16[256,768]{1,0:T(8,128)(2,1)S(1)}, bf16[256,768]{1,0:T(8,128)(2,1)S(1)}, u32[]{:S(2)}, u32[]{:S(2)}) collective-permute-start(bf16[256,768]{1,0:T(8,128)(2,1)S(1)} %get-tuple-element.54), channel_id=1, source_target_pairs={{0,2},{2,0},{4,6},{6,4},{1,3},{3,1},{5,7},{7,5},{8,10},{10,8},{12,... | collective-permute-start | bytes 1179656 | tf_op jit(solution)/shard_map/ppermute | solution.py:372
  47.3 11.7 %collective-permute-start.13 = (f32[8,128,128]{2,1,0:T(8,128)S(1)}, f32[8,128,128]{2,1,0:T(8,128)S(1)}, u32[]{:S(2)}, u32[]{:S(2)}) collective-permute-start(f32[8,128,128]{2,1,0:T(8,128)S(1)} %final_state.3.rest_1_), channel_id=1, source_target_pairs={{0,1},{1,0},{2,3},{3,2},{4,5},{5,4},{6,7},{7,6},{8,9},{9,8},{10,11... | collective-permute-start | bytes 1572872 | tf_op jit(solution)/shard_map/ppermute | solution.py:372
  50.6 8.4 %copy-start = (f32[4,16,2]{1,2,0:T(2,128)S(1)}, f32[4,16,2]{1,2,0:T(2,128)}, u32[]{:S(2)}) copy-start(f32[4,16,2]{1,2,0:T(2,128)} %param.18) | copy-start | bytes 1540
  50.7 8.4 %copy-start.1 = (s32[4]{0:T(128)S(1)}, s32[4]{0:T(128)}, u32[]{:S(2)}) copy-start(s32[4]{0:T(128)} %prompt_ref.1) | copy-start | bytes 52
  50.7 14.6 %collective-permute-start.6 = (bf16[256,768]{1,0:T(8,128)(2,1)S(1)}, bf16[256,768]{1,0:T(8,128)(2,1)S(1)}, u32[]{:S(2)}, u32[]{:S(2)}) collective-permute-start(bf16[256,768]{1,0:T(8,128)(2,1)S(1)} %project.6), channel_id=1, source_target_pairs={{0,2},{2,0},{4,6},{6,4},{1,3},{3,1},{5,7},{7,5},{8,10},{10,8},{12,... | collective-permute-start | bytes 1179656 | tf_op jit(solution)/shard_map/ppermute | solution.py:372
  51.3 15.5 %collective-permute-start.11 = (bf16[256,768]{1,0:T(8,128)(2,1)S(1)}, bf16[256,768]{1,0:T(8,128)(2,1)S(1)}, u32[]{:S(2)}, u32[]{:S(2)}) collective-permute-start(bf16[256,768]{1,0:T(8,128)(2,1)S(1)} %project.9), channel_id=1, source_target_pairs={{0,4},{2,6},{4,0},{6,2},{1,5},{3,7},{5,1},{7,3},{8,12},{10,14},{12... | collective-permute-start | bytes 1179656 | tf_op jit(solution)/shard_map/ppermute | solution.py:372
  56.9 18.5 %collective-permute-start.10 = (bf16[256,768]{1,0:T(8,128)(2,1)S(1)}, bf16[256,768]{1,0:T(8,128)(2,1)S(1)}, u32[]{:S(2)}, u32[]{:S(2)}) collective-permute-start(bf16[256,768]{1,0:T(8,128)(2,1)S(1)} %relay.3.rest_5_), channel_id=1, source_target_pairs={{0,2},{2,0},{4,6},{6,4},{1,3},{3,1},{5,7},{7,5},{8,10},{10,8},{12,... | collective-permute-start | bytes 1179656 | tf_op jit(solution)/shard_map/ppermute | solution.py:372
  58.5 16.9 %collective-permute-start.8 = (bf16[256,768]{1,0:T(8,128)(2,1)S(1)}, bf16[256,768]{1,0:T(8,128)(2,1)S(1)}, u32[]{:S(2)}, u32[]{:S(2)}) collective-permute-start(bf16[256,768]{1,0:T(8,128)(2,1)S(1)} %relay.2.rest_4_), channel_id=1, source_target_pairs={{0,4},{2,6},{4,0},{6,2},{1,5},{3,7},{5,1},{7,3},{8,12},{10,14},{12... | collective-permute-start | bytes 1179656 | tf_op jit(solution)/shard_map/ppermute | solution.py:372
  64.7 10.1 %collective-permute-start.14 = (bf16[16,1536]{1,0:T(8,128)(2,1)S(1)}, bf16[16,1536]{1,0:T(8,128)(2,1)S(1)}, u32[]{:S(2)}, u32[]{:S(2)}) collective-permute-start(bf16[16,1536]{1,0:T(8,128)(2,1)S(1)} %get-tuple-element.61), channel_id=1, source_target_pairs={{0,2},{2,0},{4,6},{6,4},{1,3},{3,1},{5,7},{7,5},{8,10},{10,8},{12,... | collective-permute-start | bytes 147464 | tf_op jit(solution)/shard_map/ppermute | solution.py:372
  65.3 9.5 %collective-permute-start.15 = (bf16[16,1536]{1,0:T(8,128)(2,1)S(1)}, bf16[16,1536]{1,0:T(8,128)(2,1)S(1)}, u32[]{:S(2)}, u32[]{:S(2)}) collective-permute-start(bf16[16,1536]{1,0:T(8,128)(2,1)S(1)} %get-tuple-element.62), channel_id=1, source_target_pairs={{0,4},{2,6},{4,0},{6,2},{1,5},{3,7},{5,1},{7,3},{8,12},{10,14},{12... | collective-permute-start | bytes 147464 | tf_op jit(solution)/shard_map/ppermute | solution.py:372
  66.8 8.6 %collective-permute-start.16 = (bf16[16,1536]{1,0:T(8,128)(2,1)S(1)}, bf16[16,1536]{1,0:T(8,128)(2,1)S(1)}, u32[]{:S(2)}, u32[]{:S(2)}) collective-permute-start(bf16[16,1536]{1,0:T(8,128)(2,1)S(1)} %get-tuple-element.63), channel_id=1, source_target_pairs={{0,6},{2,4},{4,2},{6,0},{1,7},{3,5},{5,3},{7,1},{8,14},{10,12},{12... | collective-permute-start | bytes 147464 | tf_op jit(solution)/shard_map/ppermute | solution.py:372

commit v9 on v8

--- a/solution.py
+++ b/solution.py
@@ -320,14 +320,17 @@
     return total
 
 
-def project_kernel(pieces, chunks, place_ref, *rest):
-    hidden, weights = rest[:chunks], rest[chunks : chunks + WEIGHT_PARTS]
+def project_kernel(pieces, width, chunks, added, place_ref, *rest):
+    hidden, rest = rest[:chunks], rest[chunks:]
+    addends, weights = rest[:added], rest[added : -len(pieces)]
     outs = rest[-len(pieces) :]
-    half = outs[0].shape[1]
     rows = jnp.concatenate([ref[...] for ref in hidden], axis=1)
-    for (bits, side), out_ref in zip(pieces, outs):
-        column = pl.multiple_of(((place_ref[2] ^ bits) * 2 + side) * half, HEAD_DIM)
-        out_ref[...] = times_weight(rows, weights, column, half).astype(out_ref.dtype)
+    for n, ((bits, first, columns), out_ref) in enumerate(zip(pieces, outs)):
+        column = pl.multiple_of((place_ref[2] ^ bits) * width + first, HEAD_DIM)
+        total = times_weight(rows, weights, column, columns)
+        if added:
+            total = total + addends[n][...]
+        out_ref[...] = total.astype(out_ref.dtype)
 
 
 def decode_project_kernel(place_ref, rows_ref, *rest):
@@ -336,7 +339,8 @@
     rows = rows_ref[...]
     for bits, out_ref in enumerate(outs):
         column = pl.multiple_of((place_ref[2] ^ bits) * width, HEAD_DIM)
-        out_ref[...] = times_weight(rows, weights, column, width).astype(out_ref.dtype)
+        terms = times_weight(rows, weights, column, width)
+        out_ref[...] = terms[: out_ref.shape[0]].astype(out_ref.dtype)
 
 
 def relay_kernel(own_ref, got_ref, *rest):
@@ -346,15 +350,15 @@
 
 def finish_kernel(own_a, own_b, ax, ay, bx, by, d_own, d_x, d_y, d_far, *rest):
     prefill_hbm, decode_ref, out_ref, sems = rest
-    width = own_a.shape[1]
+    split = own_a.shape[1]
     count = sems.shape[0]
     size = out_ref.shape[0] // count
     copies = []
     for c in range(count):
         at = slice(c * size, (c + 1) * size)
-        for at_cols, own, x_ref, y_ref in ((0, own_a, ax, ay), (width, own_b, bx, by)):
+        for first, own, x_ref, y_ref in ((0, own_a, ax, ay), (split, own_b, bx, by)):
             total = own[at] + x_ref[at].astype(F32) + y_ref[at].astype(F32)
-            out_ref[at, at_cols : at_cols + width] = total.astype(BF16)
+            out_ref[at, first : first + own.shape[1]] = total.astype(BF16)
         copy = pltpu.make_async_copy(
             out_ref.at[pl.ds(c * size, size)], prefill_hbm.at[0, pl.ds(c * size, size)], sems.at[c]
         )
@@ -468,7 +472,7 @@
             [HBM] + [ANY] * len(after),
             [weight_part, token],
             [pltpu.SemaphoreType.DMA((1,))],
-            cost(1, features // WEIGHT_PARTS * out_weight.shape[1] * 2),
+            cost(1, 1),
         )(weight_hbm, *after)
         weights.append(part)
         return [done]
@@ -498,7 +502,7 @@
                     cost(2 * size * HEAD_DIM * HEAD_DIM, 24 * size * HEAD_DIM * HEAD_DIM),
                 )(place, owns[c], log_row, received[-1][c], *after)
                 values_out.append(value)
-                after = []
+                after = load_weight(value) if c == 0 else []
         received.append([lax.ppermute(value, ("ctx", "rep"), pairs) for value in values_out])
     loaded = []
     while len(weights) < WEIGHT_PARTS:
@@ -565,35 +569,47 @@
         return prefill_out, decode_out.reshape(rows_here, steps, -1)
 
     width = out_columns // parts
-    half = width // 2
-
-    def project(pieces, dtype, *after):
+    split = (width * 5 // 12) // HEAD_DIM * HEAD_DIM
+    side_x, side_y = (0, split), (split, width - split)
+
+    def project(pieces, dtype, inputs=None, parts_used=None, addends=()):
+        inputs = hidden if inputs is None else inputs
+        used = weights if parts_used is None else weights[parts_used]
+        moved = sum(columns for _, _, columns in pieces)
+        depth = sum(array.shape[1] for array in inputs)
         return call(
-            functools.partial(project_kernel, pieces, count),
+            functools.partial(project_kernel, pieces, width, len(inputs), len(addends)),
             "project",
-            [SMEM] + [VMEM] * (count + WEIGHT_PARTS) + [ANY] * len(after),
-            [sds((length, half), dtype) for _ in pieces],
+            [SMEM] + [VMEM] * (len(inputs) + len(addends) + len(used)),
+            [sds((length, columns), dtype) for _, _, columns in pieces],
             (),
-            cost(2 * length * features * half * len(pieces), features * half * 2 * len(pieces)),
-        )(place, *hidden, *weights, *after)
-
-    def relay(own_term, got, *after):
+            cost(2 * length * depth * moved, depth * moved * 2),
+        )(place, *inputs, *addends, *used)
+
+    def relay(own_term, got):
         return call(
             relay_kernel,
             "relay",
-            [VMEM, VMEM] + [ANY] * len(after),
-            sds((length, half), BF16),
+            [VMEM, VMEM],
+            sds(own_term.shape, BF16),
             (),
-            cost(length * half, length * half * 8),
-        )(own_term, got, *after)
-
-    to_x, to_y = project([(3, 0), (3, 1)], BF16)
+            cost(own_term.size, own_term.size * 8),
+        )(own_term, got)
+
+    far = [(3, *side_x), (3, *side_y)]
+    if count == 2 and chunks[0][1] * HEAD_DIM * 2 == features and WEIGHT_PARTS % 2 == 0:
+        early = slice(0, WEIGHT_PARTS // 2)
+        late = slice(WEIGHT_PARTS // 2, WEIGHT_PARTS)
+        begun = project(far, F32, hidden[:1], early)
+        to_x, to_y = project(far, BF16, hidden[1:], late, begun)
+    else:
+        to_x, to_y = project(far, BF16)
     far_a = swap(to_x, "head", parts, 1)
     far_b = swap(to_y, "head", parts, 2)
-    x_a = swap(project([(1, 0)], BF16)[0], "head", parts, 1)
-    y_b = swap(project([(2, 1)], BF16)[0], "head", parts, 2)
-    pass_a, pass_b = project([(2, 0), (1, 1)], F32)
-    own_a, own_b = project([(0, 0), (0, 1)], F32)
+    x_a = swap(project([(1, *side_x)], BF16)[0], "head", parts, 1)
+    y_b = swap(project([(2, *side_y)], BF16)[0], "head", parts, 2)
+    pass_a, pass_b = project([(2, *side_x), (1, *side_y)], F32)
+    own_a, own_b = project([(0, *side_x), (0, *side_y)], F32)
     sent_a, sent_b = relay(pass_a, far_a), relay(pass_b, far_b)
     y_a = swap(sent_a, "head", parts, 2)
     x_b = swap(sent_b, "head", parts, 1)
@@ -603,7 +619,7 @@
         decode_project_kernel,
         "decode_project",
         [SMEM] + [VMEM] * (1 + WEIGHT_PARTS),
-        [sds((d_pad, width), F32)] + [sds((d_pad, width), BF16)] * 3,
+        [sds((d_rows, width), F32)] + [sds((d_rows, width), BF16)] * 3,
         (),
         cost(2 * d_pad * features * out_columns, features * out_columns // 8),
     )(place, d_hidden, *weights)
@@ -613,7 +629,7 @@
         [VMEM] * 10,
         [sds((1, length, width), BF16), sds((rows_here, steps, width), BF16)],
         [pltpu.VMEM((length, width), BF16), pltpu.SemaphoreType.DMA((4,))],
-        cost(6 * length * half, 20 * length * half),
+        cost(3 * length * width, 10 * length * width),
         out_specs=[HBM, VMEM],
     )(
         own_a,

time: 77.3 us -> 74.8 us (0.968)
  waiting for transfers between devices: 13.3 us -> 10.5 us
  Pallas kernels: 40.6 us -> 42.6 us
  starting transfers between devices: 22 us -> 20.4 us
    ppermute x11, waiting for transfers between devices: 6.29 us -> 3.46 us  [swap(): return lax.ppermute(array, axis, [(i, i ^ bit) for i in range(size)])]
    ppermute x6, starting transfers between devices: 11 us -> 8.16 us  [body(): lax.ppermute(value, ('ctx', 'rep'), pairs)]
    pallas_call x7 -> x8, Pallas kernels: 10.6 us -> 12.5 us  [the longest x6 12.4 us: project(): call(functools.partial(project_kernel, pieces, width, len(inputs), len(ad...]
    ppermute x11, starting transfers between devices: 11 us -> 12.2 us  [swap(): return lax.ppermute(array, axis, [(i, i ^ bit) for i in range(size)])]
  transfers between devices with their start and end apart: 17 -> 17, of which waited for: 6 -> 6; matrix products, arithmetic and copies ran while one was open for 0% -> 0% of each run, Pallas kernels for 41% -> 46%
where the time goes in v9:
time: 74.8 us; the launch traced here: 74.6 us
  Pallas kernels  42.6 us (57%)
  starting transfers between devices  20.4 us (27%)
  waiting for transfers between devices  10.5 us (14%)
  between operations  1.03 us (1%)
    pallas_call x6, Pallas kernels, project(): call(functools.partial(project_kernel, pieces, width, len(inputs), len(ad...  12.4 us
    ppermute x11, starting transfers between devices, swap(): return lax.ppermute(array, axis, [(i, i ^ bit) for i in range(size)])  12.2 us
    ppermute x6, starting transfers between devices, body(): lax.ppermute(value, ('ctx', 'rep'), pairs)  8.16 us
    ppermute x6, waiting for transfers between devices, body(): lax.ppermute(value, ('ctx', 'rep'), pairs)  7.07 us
    pallas_call x2, Pallas kernels, load_weight(): call(functools.partial(load_kernel, len(weights)), 'load_weight', [HBM] +...  5.59 us
    pallas_call x1, Pallas kernels, body(): call(functools.partial(local_kernel, len(arrays)), 'local_attention', [VM...  5.01 us
    pallas_call x1, Pallas kernels, body(): call(decode_project_kernel, 'decode_project', [SMEM] + [VMEM] * (1 + WEIG...  3.91 us
    ppermute x11, waiting for transfers between devices, swap(): return lax.ppermute(array, axis, [(i, i ^ bit) for i in range(size)])  3.46 us
  transfers between devices with their start and end apart: 17, of which 6 were waited for; matrix products, arithmetic and copies ran while one was open for 0% of the time, Pallas kernels for 46%

profile of v9, /device:TPU:0, one launch (start us, length us, event | category | flops | bytes accessed | tf_op | source)
XLA Modules:
  0.0 74.6 jit_solution(11488568061031240185)
XLA Ops:
  0.6 0.1 pad_add_fusion.place_ref
  0.7 3.2 %own_state.1 = (f32[8,128,128]{2,1,0:T(8,128)S(1)}, f32[1,128]{1,0:T(1,128)S(1)}, f32[256,16]{1,0:T(8,128)S(1)}, f32[1,16,256]{2,1,0:T(8,128)S(1)}, bf16[256,204...) custom-call(s32[3]{0:T(128)S(1)} %pad_add_fusion.place_ref, ...), custom_call_target="tpu_custom_call" | custom-call | flops 268435456 | bytes 8388608 | tf_op jit(solution)/shard_map/own_state/pallas_call | solution.py:419
  4.0 3.1 %collective-permute-start = (bf16[1040,128]{1,0:T(8,128)(2,1)S(1)}, bf16[1040,128]{1,0:T(8,128)(2,1)S(1)}, u32[]{:S(2)}, u32[]{:S(2)}) collective-permute-start(bf16[1040,128]{1,0:T(8,128)(2,1)S(1)} %get-tuple-element.41), channel_id=1, source_target_pairs={{0,8},{1,9},{8,0},{9,1},{16,24},{17,25},{24,16},{25,17},{2,10},{3,... | collective-permute-start | bytes 798728 | tf_op jit(solution)/shard_map/ppermute | solution.py:506
  7.0 5.0 %local_attention.1 = (bf16[1,256,2048]{2,1,0:T(8,128)(2,1)S(1)}, bf16[4,2,2048]{2,1,0:T(2,128)(2,1)S(1)}, bf16[4,2,2048]{2,1,0:T(2,128)(2,1)S(1)}, bf16[4,2,2048...) custom-call(bf16[256,2048]{1,0:T(8,128)(2,1)S(1)} %get-tuple-element, ...), custom_call_target="tpu_custom_call" | custom-call | flops 536870912 | bytes 6291456 | tf_op jit(solution)/shard_map/local_attention/pallas_call | solution.py:441
  12.1 1.2 %more_state.1 = (f32[8,128,128]{2,1,0:T(8,128)S(1)}, bf16[1040,128]{1,0:T(8,128)(2,1)S(1)}) custom-call(bf16[256,2048]{1,0:T(8,128)(2,1)S(1)} %get-tuple-element.35.k_ref, bf16[256,2048]{1,0:T(8,128)(2,1)S(1)} %get-tuple-element.36.v_ref, f32[256,16]{1,0:T(8,128)S(1)} %get-tuple-element.37.col_ref, f32[1,128]{1,0:T(1,128)S(1)} %get-tuple-element.43.log_ref, ...), custom_call_target="tpu_custom_call" | custom-call | flops 134217728 | bytes 4194304 | tf_op jit(solution)/shard_map/more_state/pallas_call | solution.py:455
  13.2 0.1 collective-permute-start.3
  13.3 0.1 collective-permute-done.got_ref.rest_0_
  13.4 0.7 chain.4.rest_0_
  14.2 0.1 collective-permute-start.1
  14.2 2.8 %load_weight.2 = (bf16[512,6144]{1,0:T(8,128)(2,1)S(1)}, f32[8,128]{1,0:T(8,128)S(1)}) custom-call(bf16[2048,6144]{1,0:T(8,128)(2,1)} %weight_hbm.5, bf16[1040,128]{1,0:T(8,128)(2,1)S(1)} %chain.4.rest_0_), custom_call_target="tpu_custom_call" | custom-call | flops 1 | bytes 1 | tf_op jit(solution)/shard_map/load_weight/pallas_call | solution.py:469
  17.1 4.1 %collective-permute-done.3.got_ref.rest_0_ = bf16[1040,128]{1,0:T(8,128)(2,1)S(1)} collective-permute-done((bf16[1040,128]{1,0:T(8,128)(2,1)S(1)}, bf16[1040,128]{1,0:T(8,128)(2,1)S(1)}, u32[]{:S(2)}, u32[]{:S(2)}) %collective-permute-start.3) | collective-permute-done | bytes 266272 | tf_op jit(solution)/shard_map/ppermute | solution.py:506
  21.2 0.7 chain.6
  21.9 0.1 collective-permute-start.4
  22.0 0.0 collective-permute-done.1.got_ref.rest_1_
  22.0 0.7 chain.5.rest_0_
  22.7 3.2 %collective-permute-start.2 = (bf16[1040,128]{1,0:T(8,128)(2,1)S(1)}, bf16[1040,128]{1,0:T(8,128)(2,1)S(1)}, u32[]{:S(2)}, u32[]{:S(2)}) collective-permute-start(bf16[1040,128]{1,0:T(8,128)(2,1)S(1)} %chain.5.rest_0_), channel_id=1, source_target_pairs={{0,8},{1,9},{8,0},{9,1},{16,24},{17,25},{24,16},{25,17},{2,10},{3,... | collective-permute-start | bytes 798728 | tf_op jit(solution)/shard_map/ppermute | solution.py:506
  25.9 2.8 %load_weight.3 = (bf16[512,6144]{1,0:T(8,128)(2,1)S(1)}, f32[8,128]{1,0:T(8,128)S(1)}) custom-call(bf16[2048,6144]{1,0:T(8,128)(2,1)} %weight_hbm.5, bf16[1040,128]{1,0:T(8,128)(2,1)S(1)} %chain.5.rest_0_), custom_call_target="tpu_custom_call" | custom-call | flops 1 | bytes 1 | tf_op jit(solution)/shard_map/load_weight/pallas_call | solution.py:469
  28.7 0.0 collective-permute-done.4.got_ref.rest_1_
  28.7 0.7 chain.7
  29.4 1.7 %collective-permute-start.5 = (bf16[1040,128]{1,0:T(8,128)(2,1)S(1)}, bf16[1040,128]{1,0:T(8,128)(2,1)S(1)}, u32[]{:S(2)}, u32[]{:S(2)}) collective-permute-start(bf16[1040,128]{1,0:T(8,128)(2,1)S(1)} %chain.7), channel_id=1, source_target_pairs={{0,8},{1,9},{8,0},{9,1},{16,24},{17,25},{24,16},{25,17},{2,10},{3,... | collective-permute-start | bytes 798728 | tf_op jit(solution)/shard_map/ppermute | solution.py:506
  31.1 1.8 %collective-permute-done.2.rest_2_ = bf16[1040,128]{1,0:T(8,128)(2,1)S(1)} collective-permute-done((bf16[1040,128]{1,0:T(8,128)(2,1)S(1)}, bf16[1040,128]{1,0:T(8,128)(2,1)S(1)}, u32[]{:S(2)}, u32[]{:S(2)}) %collective-permute-start.2) | collective-permute-done | bytes 266272 | tf_op jit(solution)/shard_map/ppermute | solution.py:506
  32.9 1.6 %hidden.2.rest_0_ = bf16[256,1024]{1,0:T(8,128)(2,1)S(1)} custom-call(s32[3]{0:T(128)S(1)} %pad_add_fusion.place_ref, bf16[1,256,2048]{2,1,0:T(8,128)(2,1)S(1)} %get-tuple-element.39.q_ref, f32[256,16]{1,0:T(8,128)S(1)} %get-tuple-element.37.col_ref, f32[256,2048]{1,0:T(8,128)S(1)} %get-tuple-element.40.local_ref, ...), custom_call_target="tpu_custom_call" | custom-call | flops 67108864 | bytes 5242880 | tf_op jit(solution)/shard_map/hidden/pallas_call | solution.py:514
  34.5 1.7 %project.9 = (f32[256,640]{1,0:T(8,128)S(1)}, f32[256,896]{1,0:T(8,128)S(1)}) custom-call(s32[3]{0:T(128)S(1)} %pad_add_fusion.place_ref, bf16[256,1024]{1,0:T(8,128)(2,1)S(1)} %hidden.2.rest_0_, bf16[512,6144]{1,0:T(8,128)(2,1)S(1)} %get-tuple-element.49.rest_2_.rest_1_.rest_0_, bf16[512,6144]{1,0:T(8,128)(2,1)S(1)} %get-tuple-element.50.rest_3_.rest_2_.rest_1_), custom_call_target="tpu_custom_call" | custom-call | flops 805306368 | bytes 3145728 | tf_op jit(solution)/shard_map/project/pallas_call | solution.py:580
  36.2 1.1 %collective-permute-done.5.rest_2_ = bf16[1040,128]{1,0:T(8,128)(2,1)S(1)} collective-permute-done((bf16[1040,128]{1,0:T(8,128)(2,1)S(1)}, bf16[1040,128]{1,0:T(8,128)(2,1)S(1)}, u32[]{:S(2)}, u32[]{:S(2)}) %collective-permute-start.5) | collective-permute-done | bytes 266272 | tf_op jit(solution)/shard_map/ppermute | solution.py:506
  37.3 1.6 %hidden.3.rest_1_.rest_0_ = bf16[256,1024]{1,0:T(8,128)(2,1)S(1)} custom-call(s32[3]{0:T(128)S(1)} %pad_add_fusion.place_ref, bf16[1,256,2048]{2,1,0:T(8,128)(2,1)S(1)} %get-tuple-element.39.q_ref, f32[256,16]{1,0:T(8,128)S(1)} %get-tuple-element.37.col_ref, f32[256,2048]{1,0:T(8,128)S(1)} %get-tuple-element.40.local_ref, ...), custom_call_target="tpu_custom_call" | custom-call | flops 67108864 | bytes 5242880 | tf_op jit(solution)/shard_map/hidden/pallas_call | solution.py:514
  38.9 1.7 %project.10 = (bf16[256,640]{1,0:T(8,128)(2,1)S(1)}, bf16[256,896]{1,0:T(8,128)(2,1)S(1)}) custom-call(s32[3]{0:T(128)S(1)} %pad_add_fusion.place_ref, bf16[256,1024]{1,0:T(8,128)(2,1)S(1)} %hidden.3.rest_1_.rest_0_, f32[256,640]{1,0:T(8,128)S(1)} %get-tuple-element.56.rest_1_, f32[256,896]{1,0:T(8,128)S(1)} %get-tuple-element.57.rest_2_, ...), custom_call_target="tpu_custom_call" | custom-call | flops 805306368 | bytes 3145728 | tf_op jit(solution)/shard_map/project/pallas_call | solution.py:580
  40.6 1.6 %collective-permute-start.9 = (bf16[256,896]{1,0:T(8,128)(2,1)S(1)}, bf16[256,896]{1,0:T(8,128)(2,1)S(1)}, u32[]{:S(2)}, u32[]{:S(2)}) collective-permute-start(bf16[256,896]{1,0:T(8,128)(2,1)S(1)} %get-tuple-element.60.rest_3_), channel_id=1, source_target_pairs={{0,4},{2,6},{4,0},{6,2},{1,5},{3,7},{5,1},{7,3},{8,12},{10,14},{12... | collective-permute-start | bytes 1376264 | tf_op jit(solution)/shard_map/ppermute | solution.py:376
  42.2 0.8 %final_state.2.rest_0_ = f32[8,128,128]{2,1,0:T(8,128)S(1)} custom-call(s32[3]{0:T(128)S(1)} %pad_add_fusion.place_ref, f32[8,128,128]{2,1,0:T(8,128)S(1)} %get-tuple-element.42.own_ref, f32[1,128]{1,0:T(1,128)S(1)} %get-tuple-element.43.log_ref, bf16[1040,128]{1,0:T(8,128)(2,1)S(1)} %collective-permute-done.got_ref.rest_0_, ...), custom_call_target="tpu_custom_call" | custom-call | flops 524288 | bytes 1048576 | tf_op jit(solution)/shard_map/final_state/pallas_call | solution.py:530
  43.1 0.1 collective-permute-start.12
  43.1 1.5 %collective-permute-start.7 = (bf16[256,640]{1,0:T(8,128)(2,1)S(1)}, bf16[256,640]{1,0:T(8,128)(2,1)S(1)}, u32[]{:S(2)}, u32[]{:S(2)}) collective-permute-start(bf16[256,640]{1,0:T(8,128)(2,1)S(1)} %get-tuple-element.58), channel_id=1, source_target_pairs={{0,2},{2,0},{4,6},{6,4},{1,3},{3,1},{5,7},{7,5},{8,10},{10,8},{12,... | collective-permute-start | bytes 983048 | tf_op jit(solution)/shard_map/ppermute | solution.py:376
  44.7 0.9 %final_state.3.rest_1_ = f32[8,128,128]{2,1,0:T(8,128)S(1)} custom-call(s32[3]{0:T(128)S(1)} %pad_add_fusion.place_ref, f32[8,128,128]{2,1,0:T(8,128)S(1)} %get-tuple-element.46.own_ref, f32[1,128]{1,0:T(1,128)S(1)} %get-tuple-element.43.log_ref, bf16[1040,128]{1,0:T(8,128)(2,1)S(1)} %collective-permute-done.3.got_ref.rest_0_, ...), custom_call_target="tpu_custom_call" | custom-call | flops 524288 | bytes 1048576 | tf_op jit(solution)/shard_map/final_state/pallas_call | solution.py:530
  45.5 0.2 collective-permute-start.13
  45.8 1.8 %project.11 = bf16[256,896]{1,0:T(8,128)(2,1)S(1)} custom-call(s32[3]{0:T(128)S(1)} %pad_add_fusion.place_ref, bf16[256,1024]{1,0:T(8,128)(2,1)S(1)} %hidden.2.rest_0_, bf16[256,1024]{1,0:T(8,128)(2,1)S(1)} %hidden.3.rest_1_.rest_0_, bf16[512,6144]{1,0:T(8,128)(2,1)S(1)} %get-tuple-element.49.rest_2_.rest_1_.rest_0_, ...), custom_call_target="tpu_custom_call" | custom-call | flops 939524096 | bytes 3670016 | tf_op jit(solution)/shard_map/project/pallas_call | solution.py:580
  47.6 0.6 collective-permute-start.11
  48.2 1.6 %project.7 = bf16[256,640]{1,0:T(8,128)(2,1)S(1)} custom-call(s32[3]{0:T(128)S(1)} %pad_add_fusion.place_ref, bf16[256,1024]{1,0:T(8,128)(2,1)S(1)} %hidden.2.rest_0_, bf16[256,1024]{1,0:T(8,128)(2,1)S(1)} %hidden.3.rest_1_.rest_0_, bf16[512,6144]{1,0:T(8,128)(2,1)S(1)} %get-tuple-element.49.rest_2_.rest_1_.rest_0_, ...), custom_call_target="tpu_custom_call" | custom-call | flops 671088640 | bytes 2621440 | tf_op jit(solution)/shard_map/project/pallas_call | solution.py:580
  49.7 0.0 copy-start
  49.8 0.0 copy-start.1
  49.8 2.9 %collective-permute-done.9.got_ref = bf16[256,896]{1,0:T(8,128)(2,1)S(1)} collective-permute-done((bf16[256,896]{1,0:T(8,128)(2,1)S(1)}, bf16[256,896]{1,0:T(8,128)(2,1)S(1)}, u32[]{:S(2)}, u32[]{:S(2)}) %collective-permute-start.9) | collective-permute-done | bytes 458784 | tf_op jit(solution)/shard_map/ppermute | solution.py:376
  52.7 2.4 %collective-permute-start.6 = (bf16[256,640]{1,0:T(8,128)(2,1)S(1)}, bf16[256,640]{1,0:T(8,128)(2,1)S(1)}, u32[]{:S(2)}, u32[]{:S(2)}) collective-permute-start(bf16[256,640]{1,0:T(8,128)(2,1)S(1)} %project.7), channel_id=1, source_target_pairs={{0,2},{2,0},{4,6},{6,4},{1,3},{3,1},{5,7},{7,5},{8,10},{10,8},{12,... | collective-permute-start | bytes 983048 | tf_op jit(solution)/shard_map/ppermute | solution.py:376
  55.0 2.9 %project.8 = (f32[256,640]{1,0:T(8,128)S(1)}, f32[256,896]{1,0:T(8,128)S(1)}) custom-call(s32[3]{0:T(128)S(1)} %pad_add_fusion.place_ref, bf16[256,1024]{1,0:T(8,128)(2,1)S(1)} %hidden.2.rest_0_, bf16[256,1024]{1,0:T(8,128)(2,1)S(1)} %hidden.3.rest_1_.rest_0_, bf16[512,6144]{1,0:T(8,128)(2,1)S(1)} %get-tuple-element.49.rest_2_.rest_1_.rest_0_, ...), custom_call_target="tpu_custom_call" | custom-call | flops 1610612736 | bytes 6291456 | tf_op jit(solution)/shard_map/project/pallas_call | solution.py:580
  57.9 0.1 relay.3.rest_5_
  58.0 0.0 collective-permute-done.7.got_ref
  58.0 0.1 collective-permute-start.10
  58.1 0.1 relay.2.rest_4_
  58.1 0.0 collective-permute-done.12.rest_2_
  58.2 2.2 %collective-permute-start.8 = (bf16[256,640]{1,0:T(8,128)(2,1)S(1)}, bf16[256,640]{1,0:T(8,128)(2,1)S(1)}, u32[]{:S(2)}, u32[]{:S(2)}) collective-permute-start(bf16[256,640]{1,0:T(8,128)(2,1)S(1)} %relay.2.rest_4_), channel_id=1, source_target_pairs={{0,4},{2,6},{4,0},{6,2},{1,5},{3,7},{5,1},{7,3},{8,12},{10,14},{12... | collective-permute-start | bytes 983048 | tf_op jit(solution)/shard_map/ppermute | solution.py:376
  60.4 0.0 collective-permute-done.13.rest_3_
  60.4 0.0 copy-done
  60.4 0.0 copy-done.1
  60.4 1.7 %decode_rows.1.rows_ref = bf16[16,2048]{1,0:T(8,128)(2,1)S(1)} custom-call(s32[3]{0:T(128)S(1)} %pad_add_fusion.place_ref, s32[4]{0:T(128)S(1)} %copy-done.1, bf16[4,2,2048]{2,1,0:T(2,128)(2,1)S(1)} %get-tuple-element.61.q_ref, bf16[4,2,2048]{2,1,0:T(2,128)(2,1)S(1)} %get-tuple-element.62.k_ref, bf16[4,2,2048]{2,1,0:T(2,128)(2,1)S(1)} %get-tuple-element.63.v_ref, ...), custom_call_target="tpu_custom_call" | custom-call | flops 33554432 | bytes 262144 | tf_op jit(solution)/shard_map/decode_rows/pallas_call | solution.py:543
  62.1 3.9 %decode_project.1 = (f32[8,1536]{1,0:T(8,128)S(1)}, bf16[8,1536]{1,0:T(8,128)(2,1)S(1)}, bf16[8,1536]{1,0:T(8,128)(2,1)S(1)}, bf16[8,1536]{1,0:T(8,128)(2,1)S(1)}) custom-call(s32[3]{0:T(128)S(1)} %pad_add_fusion.place_ref, bf16[16,2048]{1,0:T(8,128)(2,1)S(1)} %decode_rows.1.rows_ref, bf16[512,6144]{1,0:T(8,128)(2,1)S(1)} %get-tuple-element.49.rest_2_.rest_1_.rest_0_, ...), custom_call_target="tpu_custom_call" | custom-call | flops 402653184 | bytes 1572864 | tf_op jit(solution)/shard_map/decode_project/pallas_call | solution.py:618
  66.0 2.0 %collective-permute-start.14 = (bf16[8,1536]{1,0:T(8,128)(2,1)S(1)}, bf16[8,1536]{1,0:T(8,128)(2,1)S(1)}, u32[]{:S(2)}, u32[]{:S(2)}) collective-permute-start(bf16[8,1536]{1,0:T(8,128)(2,1)S(1)} %get-tuple-element.65), channel_id=1, source_target_pairs={{0,2},{2,0},{4,6},{6,4},{1,3},{3,1},{5,7},{7,5},{8,10},{10,8},{12,... | collective-permute-start | bytes 73736 | tf_op jit(solution)/shard_map/ppermute | solution.py:376
  68.0 0.0 collective-permute-done.6.ax
  68.0 0.0 collective-permute-start.15
  68.1 0.0 collective-permute-done.11.by
  68.1 1.5 %collective-permute-start.16 = (bf16[8,1536]{1,0:T(8,128)(2,1)S(1)}, bf16[8,1536]{1,0:T(8,128)(2,1)S(1)}, u32[]{:S(2)}, u32[]{:S(2)}) collective-permute-start(bf16[8,1536]{1,0:T(8,128)(2,1)S(1)} %get-tuple-element.67), channel_id=1, source_target_pairs={{0,6},{2,4},{4,2},{6,0},{1,7},{3,5},{5,3},{7,1},{8,14},{10,12},{12... | collective-permute-start | bytes 73736 | tf_op jit(solution)/shard_map/ppermute | solution.py:376
  69.6 2.7 %project.6 = (f32[256,640]{1,0:T(8,128)S(1)}, f32[256,896]{1,0:T(8,128)S(1)}) custom-call(s32[3]{0:T(128)S(1)} %pad_add_fusion.place_ref, bf16[256,1024]{1,0:T(8,128)(2,1)S(1)} %hidden.2.rest_0_, bf16[256,1024]{1,0:T(8,128)(2,1)S(1)} %hidden.3.rest_1_.rest_0_, bf16[512,6144]{1,0:T(8,128)(2,1)S(1)} %get-tuple-element.49.rest_2_.rest_1_.rest_0_, ...), custom_call_target="tpu_custom_call" | custom-call | flops 1610612736 | bytes 6291456 | tf_op jit(solution)/shard_map/project/pallas_call | solution.py:580
  72.3 0.0 collective-permute-done.14.d_x
  72.3 0.0 collective-permute-done.15.d_y
  72.3 0.6 collective-permute-done.16.d_far
  72.8 0.0 collective-permute-done.8.ay
  72.9 0.0 collective-permute-done.10.bx
  72.9 1.6 %finish.1 = (bf16[1,256,1536]{2,1,0:T(8,128)(2,1)}, bf16[4,2,1536]{2,1,0:T(2,128)(2,1)}) custom-call(f32[256,640]{1,0:T(8,128)S(1)} %get-tuple-element.53.own_a, f32[256,896]{1,0:T(8,128)S(1)} %get-tuple-element.54.own_b, bf16[256,640]{1,0:T(8,128)(2,1)S(1)} %collective-permute-done.6.ax, bf16[256,640]{1,0:T(8,128)(2,1)S(1)} %collective-permute-done.8.ay, ...), custom_call_target="tpu_custom_call" | custom-call | flops 1179648 | bytes 3932160 | tf_op jit(solution)/shard_map/finish/pallas_call | solution.py:626
Async XLA Ops:
  4.0 9.5 %collective-permute-start = (bf16[1040,128]{1,0:T(8,128)(2,1)S(1)}, bf16[1040,128]{1,0:T(8,128)(2,1)S(1)}, u32[]{:S(2)}, u32[]{:S(2)}) collective-permute-start(bf16[1040,128]{1,0:T(8,128)(2,1)S(1)} %get-tuple-element.41), channel_id=1, source_target_pairs={{0,8},{1,9},{8,0},{9,1},{16,24},{17,25},{24,16},{25,17},{2,10},{3,... | collective-permute-start | bytes 798728 | tf_op jit(solution)/shard_map/ppermute | solution.py:506
  13.2 7.9 %collective-permute-start.3 = (bf16[1040,128]{1,0:T(8,128)(2,1)S(1)}, bf16[1040,128]{1,0:T(8,128)(2,1)S(1)}, u32[]{:S(2)}, u32[]{:S(2)}) collective-permute-start(bf16[1040,128]{1,0:T(8,128)(2,1)S(1)} %get-tuple-element.45.rest_0_), channel_id=1, source_target_pairs={{0,8},{1,9},{8,0},{9,1},{16,24},{17,25},{24,16},{25,17},{2,10},{3,... | collective-permute-start | bytes 798728 | tf_op jit(solution)/shard_map/ppermute | solution.py:506
  14.2 7.8 %collective-permute-start.1 = (bf16[1040,128]{1,0:T(8,128)(2,1)S(1)}, bf16[1040,128]{1,0:T(8,128)(2,1)S(1)}, u32[]{:S(2)}, u32[]{:S(2)}) collective-permute-start(bf16[1040,128]{1,0:T(8,128)(2,1)S(1)} %chain.4.rest_0_), channel_id=1, source_target_pairs={{0,1},{1,0},{8,16},{9,17},{16,8},{17,9},{24,25},{25,24},{2,3},{3,2... | collective-permute-start | bytes 798728 | tf_op jit(solution)/shard_map/ppermute | solution.py:506
  21.9 6.8 %collective-permute-start.4 = (bf16[1040,128]{1,0:T(8,128)(2,1)S(1)}, bf16[1040,128]{1,0:T(8,128)(2,1)S(1)}, u32[]{:S(2)}, u32[]{:S(2)}) collective-permute-start(bf16[1040,128]{1,0:T(8,128)(2,1)S(1)} %chain.6), channel_id=1, source_target_pairs={{0,1},{1,0},{8,16},{9,17},{16,8},{17,9},{24,25},{25,24},{2,3},{3,2... | collective-permute-start | bytes 798728 | tf_op jit(solution)/shard_map/ppermute | solution.py:506
  22.7 10.2 %collective-permute-start.2 = (bf16[1040,128]{1,0:T(8,128)(2,1)S(1)}, bf16[1040,128]{1,0:T(8,128)(2,1)S(1)}, u32[]{:S(2)}, u32[]{:S(2)}) collective-permute-start(bf16[1040,128]{1,0:T(8,128)(2,1)S(1)} %chain.5.rest_0_), channel_id=1, source_target_pairs={{0,8},{1,9},{8,0},{9,1},{16,24},{17,25},{24,16},{25,17},{2,10},{3,... | collective-permute-start | bytes 798728 | tf_op jit(solution)/shard_map/ppermute | solution.py:506
  29.4 7.8 %collective-permute-start.5 = (bf16[1040,128]{1,0:T(8,128)(2,1)S(1)}, bf16[1040,128]{1,0:T(8,128)(2,1)S(1)}, u32[]{:S(2)}, u32[]{:S(2)}) collective-permute-start(bf16[1040,128]{1,0:T(8,128)(2,1)S(1)} %chain.7), channel_id=1, source_target_pairs={{0,8},{1,9},{8,0},{9,1},{16,24},{17,25},{24,16},{25,17},{2,10},{3,... | collective-permute-start | bytes 798728 | tf_op jit(solution)/shard_map/ppermute | solution.py:506
  40.6 12.0 %collective-permute-start.9 = (bf16[256,896]{1,0:T(8,128)(2,1)S(1)}, bf16[256,896]{1,0:T(8,128)(2,1)S(1)}, u32[]{:S(2)}, u32[]{:S(2)}) collective-permute-start(bf16[256,896]{1,0:T(8,128)(2,1)S(1)} %get-tuple-element.60.rest_3_), channel_id=1, source_target_pairs={{0,4},{2,6},{4,0},{6,2},{1,5},{3,7},{5,1},{7,3},{8,12},{10,14},{12... | collective-permute-start | bytes 1376264 | tf_op jit(solution)/shard_map/ppermute | solution.py:376
  43.1 15.1 %collective-permute-start.12 = (f32[8,128,128]{2,1,0:T(8,128)S(1)}, f32[8,128,128]{2,1,0:T(8,128)S(1)}, u32[]{:S(2)}, u32[]{:S(2)}) collective-permute-start(f32[8,128,128]{2,1,0:T(8,128)S(1)} %final_state.2.rest_0_), channel_id=1, source_target_pairs={{0,1},{1,0},{2,3},{3,2},{4,5},{5,4},{6,7},{7,6},{8,9},{9,8},{10,11... | collective-permute-start | bytes 1572872 | tf_op jit(solution)/shard_map/ppermute | solution.py:376
  43.1 14.8 %collective-permute-start.7 = (bf16[256,640]{1,0:T(8,128)(2,1)S(1)}, bf16[256,640]{1,0:T(8,128)(2,1)S(1)}, u32[]{:S(2)}, u32[]{:S(2)}) collective-permute-start(bf16[256,640]{1,0:T(8,128)(2,1)S(1)} %get-tuple-element.58), channel_id=1, source_target_pairs={{0,2},{2,0},{4,6},{6,4},{1,3},{3,1},{5,7},{7,5},{8,10},{10,8},{12,... | collective-permute-start | bytes 983048 | tf_op jit(solution)/shard_map/ppermute | solution.py:376
  45.5 14.8 %collective-permute-start.13 = (f32[8,128,128]{2,1,0:T(8,128)S(1)}, f32[8,128,128]{2,1,0:T(8,128)S(1)}, u32[]{:S(2)}, u32[]{:S(2)}) collective-permute-start(f32[8,128,128]{2,1,0:T(8,128)S(1)} %final_state.3.rest_1_), channel_id=1, source_target_pairs={{0,1},{1,0},{2,3},{3,2},{4,5},{5,4},{6,7},{7,6},{8,9},{9,8},{10,11... | collective-permute-start | bytes 1572872 | tf_op jit(solution)/shard_map/ppermute | solution.py:376
  47.6 20.5 %collective-permute-start.11 = (bf16[256,896]{1,0:T(8,128)(2,1)S(1)}, bf16[256,896]{1,0:T(8,128)(2,1)S(1)}, u32[]{:S(2)}, u32[]{:S(2)}) collective-permute-start(bf16[256,896]{1,0:T(8,128)(2,1)S(1)} %project.11), channel_id=1, source_target_pairs={{0,4},{2,6},{4,0},{6,2},{1,5},{3,7},{5,1},{7,3},{8,12},{10,14},{12... | collective-permute-start | bytes 1376264 | tf_op jit(solution)/shard_map/ppermute | solution.py:376
  49.7 10.6 %copy-start = (f32[4,16,2]{1,2,0:T(2,128)S(1)}, f32[4,16,2]{1,2,0:T(2,128)}, u32[]{:S(2)}) copy-start(f32[4,16,2]{1,2,0:T(2,128)} %param.18) | copy-start | bytes 1540
  49.8 10.6 %copy-start.1 = (s32[4]{0:T(128)S(1)}, s32[4]{0:T(128)}, u32[]{:S(2)}) copy-start(s32[4]{0:T(128)} %prompt_ref.1) | copy-start | bytes 52
  52.7 15.4 %collective-permute-start.6 = (bf16[256,640]{1,0:T(8,128)(2,1)S(1)}, bf16[256,640]{1,0:T(8,128)(2,1)S(1)}, u32[]{:S(2)}, u32[]{:S(2)}) collective-permute-start(bf16[256,640]{1,0:T(8,128)(2,1)S(1)} %project.7), channel_id=1, source_target_pairs={{0,2},{2,0},{4,6},{6,4},{1,3},{3,1},{5,7},{7,5},{8,10},{10,8},{12,... | collective-permute-start | bytes 983048 | tf_op jit(solution)/shard_map/ppermute | solution.py:376
  58.0 14.9 %collective-permute-start.10 = (bf16[256,896]{1,0:T(8,128)(2,1)S(1)}, bf16[256,896]{1,0:T(8,128)(2,1)S(1)}, u32[]{:S(2)}, u32[]{:S(2)}) collective-permute-start(bf16[256,896]{1,0:T(8,128)(2,1)S(1)} %relay.3.rest_5_), channel_id=1, source_target_pairs={{0,2},{2,0},{4,6},{6,4},{1,3},{3,1},{5,7},{7,5},{8,10},{10,8},{12,... | collective-permute-start | bytes 1376264 | tf_op jit(solution)/shard_map/ppermute | solution.py:376
  58.2 14.7 %collective-permute-start.8 = (bf16[256,640]{1,0:T(8,128)(2,1)S(1)}, bf16[256,640]{1,0:T(8,128)(2,1)S(1)}, u32[]{:S(2)}, u32[]{:S(2)}) collective-permute-start(bf16[256,640]{1,0:T(8,128)(2,1)S(1)} %relay.2.rest_4_), channel_id=1, source_target_pairs={{0,4},{2,6},{4,0},{6,2},{1,5},{3,7},{5,1},{7,3},{8,12},{10,14},{12... | collective-permute-start | bytes 983048 | tf_op jit(solution)/shard_map/ppermute | solution.py:376
  66.0 6.3 %collective-permute-start.14 = (bf16[8,1536]{1,0:T(8,128)(2,1)S(1)}, bf16[8,1536]{1,0:T(8,128)(2,1)S(1)}, u32[]{:S(2)}, u32[]{:S(2)}) collective-permute-start(bf16[8,1536]{1,0:T(8,128)(2,1)S(1)} %get-tuple-element.65), channel_id=1, source_target_pairs={{0,2},{2,0},{4,6},{6,4},{1,3},{3,1},{5,7},{7,5},{8,10},{10,8},{12,... | collective-permute-start | bytes 73736 | tf_op jit(solution)/shard_map/ppermute | solution.py:376
  68.0 4.2 %collective-permute-start.15 = (bf16[8,1536]{1,0:T(8,128)(2,1)S(1)}, bf16[8,1536]{1,0:T(8,128)(2,1)S(1)}, u32[]{:S(2)}, u32[]{:S(2)}) collective-permute-start(bf16[8,1536]{1,0:T(8,128)(2,1)S(1)} %get-tuple-element.66), channel_id=1, source_target_pairs={{0,4},{2,6},{4,0},{6,2},{1,5},{3,7},{5,1},{7,3},{8,12},{10,14},{12... | collective-permute-start | bytes 73736 | tf_op jit(solution)/shard_map/ppermute | solution.py:376
  68.1 4.8 %collective-permute-start.16 = (bf16[8,1536]{1,0:T(8,128)(2,1)S(1)}, bf16[8,1536]{1,0:T(8,128)(2,1)S(1)}, u32[]{:S(2)}, u32[]{:S(2)}) collective-permute-start(bf16[8,1536]{1,0:T(8,128)(2,1)S(1)} %get-tuple-element.67), channel_id=1, source_target_pairs={{0,6},{2,4},{4,2},{6,0},{1,7},{3,5},{5,3},{7,1},{8,14},{10,12},{12... | collective-permute-start | bytes 73736 | tf_op jit(solution)/shard_map/ppermute | solution.py:376

commit v10 on v9

--- a/solution.py
+++ b/solution.py
@@ -12,8 +12,9 @@
 NEGATIVE = -1e30
 HIGH = lax.Precision.HIGHEST
 CHUNKS = 2
-WEIGHT_PARTS = 4
-EARLY_PARTS = 2
+WEIGHT_PARTS = 8
+EARLY_PARTS = 3
+LATER_PARTS = (2, 2, 1)
 VMEM_BYTES = 8 * 2**20
 F32 = jnp.float32
 BF16 = jnp.bfloat16
@@ -191,9 +192,10 @@
     return copies
 
 
-def load_kernel(index, weight_hbm, *rest):
-    weight_ref, token_ref, sems = rest[-3:]
-    copies = weight_copies([index], weight_hbm, [weight_ref], sems)
+def load_kernel(places, weight_hbm, *rest):
+    token_ref, sems = rest[-2:]
+    weights = rest[-2 - len(places) : -2]
+    copies = weight_copies(places, weight_hbm, weights, sems)
     token_ref[...] = jnp.zeros_like(token_ref)
     for copy in copies:
         copy.wait()
@@ -234,21 +236,23 @@
 
 def final_kernel(first, phases, place_ref, own_ref, log_ref, *rest):
     got, out_ref = rest[:phases], rest[-1]
-    group = place_ref[0]
     keep = jnp.exp(log_ref[...])
-    later = jnp.zeros((1, HEAD_DIM), F32)
-    for phase in range(phases):
-        later = jnp.where(group == phases - 1 - phase, read_log(got[phase]), later)
-    later = jnp.exp(later)
-    for i in range(out_ref.shape[0]):
-        h = first + i
-        suffix = jnp.zeros((HEAD_DIM, HEAD_DIM), F32)
-        for phase in range(phases):
-            there = state_rows(got[phase], i).astype(F32)
-            suffix = jnp.where(group == phases - 1 - phase, there, suffix)
-        prefix = entering_state(group, got, i).astype(F32)
-        here = own_ref[i] + keep[:, h : h + 1] * prefix
-        out_ref[i] = suffix + later[:, h : h + 1] * here
+
+    def write(group):
+        prefix = got[group - 1] if group > 0 else None
+        suffix = got[phases - 1 - group] if group < phases else None
+        later = None if suffix is None else jnp.exp(read_log(suffix))
+        for i in range(out_ref.shape[0]):
+            h = first + i
+            value = own_ref[i]
+            if prefix is not None:
+                value = value + keep[:, h : h + 1] * state_rows(prefix, i).astype(F32)
+            if suffix is not None:
+                value = later[:, h : h + 1] * value + state_rows(suffix, i).astype(F32)
+            out_ref[i] = value
+
+    for group in range(phases + 1):
+        pl.when(place_ref[0] == group)(functools.partial(write, group))
 
 
 def flat_rows(ref, rows_ref):
@@ -320,9 +324,9 @@
     return total
 
 
-def project_kernel(pieces, width, chunks, added, place_ref, *rest):
+def project_kernel(pieces, width, chunks, added, used, place_ref, *rest):
     hidden, rest = rest[:chunks], rest[chunks:]
-    addends, weights = rest[:added], rest[added : -len(pieces)]
+    addends, weights = rest[:added], rest[added : added + used]
     outs = rest[-len(pieces) :]
     rows = jnp.concatenate([ref[...] for ref in hidden], axis=1)
     for n, ((bits, first, columns), out_ref) in enumerate(zip(pieces, outs)):
@@ -334,13 +338,21 @@
 
 
 def decode_project_kernel(place_ref, rows_ref, *rest):
-    weights, outs = rest[:WEIGHT_PARTS], rest[-4:]
-    width = outs[0].shape[1]
+    weights, (keep_ref, send_ref) = rest[:WEIGHT_PARTS], rest[-2:]
+    width = keep_ref.shape[1] // 2
     rows = rows_ref[...]
-    for bits, out_ref in enumerate(outs):
-        column = pl.multiple_of((place_ref[2] ^ bits) * width, HEAD_DIM)
-        terms = times_weight(rows, weights, column, width)
-        out_ref[...] = terms[: out_ref.shape[0]].astype(out_ref.dtype)
+    for out_ref, sides in ((keep_ref, (0, 2)), (send_ref, (1, 3))):
+        for n, bits in enumerate(sides):
+            column = pl.multiple_of((place_ref[2] ^ bits) * width, HEAD_DIM)
+            terms = times_weight(rows, weights, column, width)
+            out_ref[:, n * width : (n + 1) * width] = terms[: out_ref.shape[0]].astype(out_ref.dtype)
+
+
+def decode_relay_kernel(keep_ref, got_ref, own_ref, send_ref):
+    width = own_ref.shape[1]
+    total = keep_ref[...] + got_ref[...].astype(F32)
+    own_ref[...] = total[:, :width]
+    send_ref[...] = total[:, width:].astype(BF16)
 
 
 def relay_kernel(own_ref, got_ref, *rest):
@@ -348,7 +360,7 @@
     out_ref[...] = (own_ref[...] + got_ref[...].astype(F32)).astype(BF16)
 
 
-def finish_kernel(own_a, own_b, ax, ay, bx, by, d_own, d_x, d_y, d_far, *rest):
+def finish_kernel(own_a, own_b, ax, ay, bx, by, d_own, d_got, *rest):
     prefill_hbm, decode_ref, out_ref, sems = rest
     split = own_a.shape[1]
     count = sems.shape[0]
@@ -365,7 +377,7 @@
         copy.start()
         copies.append(copy)
     rows, steps = decode_ref.shape[0], decode_ref.shape[1]
-    total = d_own[...] + d_x[...].astype(F32) + d_y[...].astype(F32) + d_far[...].astype(F32)
+    total = d_own[...] + d_got[...].astype(F32)
     for r in range(rows):
         decode_ref[r] = total[r * steps : (r + 1) * steps].astype(BF16)
     for copy in copies:
@@ -463,18 +475,21 @@
         owns.append(in_vmem(made[0]))
         values_out.append(made[1])
 
+    todo = list(LATER_PARTS)
+
     def load_weight(*after):
-        if len(weights) == WEIGHT_PARTS:
+        if not todo:
             return []
-        part, done = call(
-            functools.partial(load_kernel, len(weights)),
+        places = range(len(weights), len(weights) + todo.pop(0))
+        *loaded, done = call(
+            functools.partial(load_kernel, places),
             "load_weight",
             [HBM] + [ANY] * len(after),
-            [weight_part, token],
-            [pltpu.SemaphoreType.DMA((1,))],
+            [weight_part] * len(places) + [token],
+            [pltpu.SemaphoreType.DMA((len(places),))],
             cost(1, 1),
         )(weight_hbm, *after)
-        weights.append(part)
+        weights.extend(loaded)
         return [done]
 
     received = []
@@ -505,7 +520,7 @@
                 after = load_weight(value) if c == 0 else []
         received.append([lax.ppermute(value, ("ctx", "rep"), pairs) for value in values_out])
     loaded = []
-    while len(weights) < WEIGHT_PARTS:
+    while todo:
         loaded = load_weight(values_out[-1], *loaded)
     weights = [in_vmem(part) for part in weights]
 
@@ -525,7 +540,7 @@
     def final_states(*after):
         finals = []
         for c, (first, size) in enumerate(chunks):
-            gate = after if c == count - 1 else ()
+            gate = after[c : c + 1]
             finals.append(
                 call(
                     functools.partial(final_kernel, first, phases),
@@ -533,7 +548,7 @@
                     [SMEM, VMEM, VMEM] + [VMEM] * phases + [ANY] * len(gate),
                     sds((size, HEAD_DIM, HEAD_DIM), F32),
                     (),
-                    cost(4 * state_elements // count, state_elements * 4),
+                    cost(1, 1),
                 )(place, owns[c], log_row, *[got[c] for got in received], *gate)
             )
         return finals, [swap(final, "rep", reps, 1) for final in finals]
@@ -546,7 +561,7 @@
             [SMEM, SMEM] + [VMEM] * (4 + 2 * count) + [ANY] * len(after),
             sds((d_pad, features), BF16),
             [flat, flat, flat, pltpu.VMEM((d_rows, heads), F32)],
-            cost(16 * d_rows * features * HEAD_DIM, state_elements),
+            cost(1, 1),
         )(
             place,
             prompt_of_row,
@@ -572,29 +587,29 @@
     split = (width * 5 // 12) // HEAD_DIM * HEAD_DIM
     side_x, side_y = (0, split), (split, width - split)
 
-    def project(pieces, dtype, inputs=None, parts_used=None, addends=()):
+    def project(pieces, dtype, inputs=None, parts_used=None, addends=(), after=()):
         inputs = hidden if inputs is None else inputs
         used = weights if parts_used is None else weights[parts_used]
         moved = sum(columns for _, _, columns in pieces)
         depth = sum(array.shape[1] for array in inputs)
         return call(
-            functools.partial(project_kernel, pieces, width, len(inputs), len(addends)),
+            functools.partial(project_kernel, pieces, width, len(inputs), len(addends), len(used)),
             "project",
-            [SMEM] + [VMEM] * (len(inputs) + len(addends) + len(used)),
+            [SMEM] + [VMEM] * (len(inputs) + len(addends) + len(used)) + [ANY] * len(after),
             [sds((length, columns), dtype) for _, _, columns in pieces],
             (),
-            cost(2 * length * depth * moved, depth * moved * 2),
-        )(place, *inputs, *addends, *used)
-
-    def relay(own_term, got):
+            cost(1, 1),
+        )(place, *inputs, *addends, *used, *after)
+
+    def relay(own_term, got, *after):
         return call(
             relay_kernel,
             "relay",
-            [VMEM, VMEM],
+            [VMEM, VMEM] + [ANY] * len(after),
             sds(own_term.shape, BF16),
             (),
-            cost(own_term.size, own_term.size * 8),
-        )(own_term, got)
+            cost(1, 1),
+        )(own_term, got, *after)
 
     far = [(3, *side_x), (3, *side_y)]
     if count == 2 and chunks[0][1] * HEAD_DIM * 2 == features and WEIGHT_PARTS % 2 == 0:
@@ -603,30 +618,44 @@
         begun = project(far, F32, hidden[:1], early)
         to_x, to_y = project(far, BF16, hidden[1:], late, begun)
     else:
+        begun = hidden[:1]
         to_x, to_y = project(far, BF16)
+    finals, others = final_states(*begun[:1], to_y)
     far_a = swap(to_x, "head", parts, 1)
     far_b = swap(to_y, "head", parts, 2)
-    x_a = swap(project([(1, *side_x)], BF16)[0], "head", parts, 1)
-    y_b = swap(project([(2, *side_y)], BF16)[0], "head", parts, 2)
-    pass_a, pass_b = project([(2, *side_x), (1, *side_y)], F32)
-    own_a, own_b = project([(0, *side_x), (0, *side_y)], F32)
-    sent_a, sent_b = relay(pass_a, far_a), relay(pass_b, far_b)
-    y_a = swap(sent_a, "head", parts, 2)
-    x_b = swap(sent_b, "head", parts, 1)
-
-    d_hidden = decode_rows(*final_states(to_y), sent_a, sent_b)
-    d_own, d_x, d_y, d_far = call(
+    near_x, = project([(1, *side_x)], BF16)
+    near_y, = project([(2, *side_y)], BF16)
+    x_a = swap(near_x, "head", parts, 1)
+    y_b = swap(near_y, "head", parts, 2)
+    pass_a, pass_b = project([(2, *side_x), (1, *side_y)], F32, after=(near_x, near_y))
+    d_hidden = decode_rows(finals, others, pass_a)
+    d_keep, d_send = call(
         decode_project_kernel,
         "decode_project",
         [SMEM] + [VMEM] * (1 + WEIGHT_PARTS),
-        [sds((d_rows, width), F32)] + [sds((d_rows, width), BF16)] * 3,
+        [sds((d_rows, 2 * width), F32), sds((d_rows, 2 * width), BF16)],
         (),
-        cost(2 * d_pad * features * out_columns, features * out_columns // 8),
+        cost(1, 1),
     )(place, d_hidden, *weights)
+    d_got = swap(d_send, "head", parts, 1)
+    own_a, own_b = project([(0, *side_x), (0, *side_y)], F32, after=(d_got,))
+    d_own, d_pass = call(
+        decode_relay_kernel,
+        "decode_relay",
+        [VMEM] * 2,
+        [sds((d_rows, width), F32), sds((d_rows, width), BF16)],
+        (),
+        cost(1, 1),
+    )(d_keep, d_got)
+
+    sent_a, sent_b = relay(pass_a, far_a), relay(pass_b, far_b, x_a, d_send)
+    y_a = swap(sent_a, "head", parts, 2)
+    x_b = swap(sent_b, "head", parts, 1)
+
     prefill_out, decode_out = call(
         finish_kernel,
         "finish",
-        [VMEM] * 10,
+        [VMEM] * 8,
         [sds((1, length, width), BF16), sds((rows_here, steps, width), BF16)],
         [pltpu.VMEM((length, width), BF16), pltpu.SemaphoreType.DMA((4,))],
         cost(3 * length * width, 10 * length * width),
@@ -639,9 +668,7 @@
         x_b,
         y_b,
         d_own,
-        swap(d_x, "head", parts, 1),
-        swap(d_y, "head", parts, 2),
-        swap(d_far, "head", parts, 3),
+        swap(d_pass, "head", parts, 2),
     )
     return prefill_out, decode_out
 

time: 74.8 us -> 77.5 us (1.036)
  waiting for transfers between devices: 10.5 us -> 16 us
  starting transfers between devices: 20.4 us -> 16.7 us
  Pallas kernels: 42.6 us -> 43.4 us
    ppermute x11 -> x10, waiting for transfers between devices: 3.46 us -> 11.8 us  [swap(): return lax.ppermute(array, axis, [(i, i ^ bit) for i in range(size)])]
    ppermute x11 -> x10, starting transfers between devices: 12.2 us -> 8.62 us  [swap(): return lax.ppermute(array, axis, [(i, i ^ bit) for i in range(size)])]
    ppermute x6, waiting for transfers between devices: 7.07 us -> 4.26 us  [body(): lax.ppermute(value, ('ctx', 'rep'), pairs)]
    pallas_call x5 -> x7, Pallas kernels: 7.34 us -> 9.41 us  [the longest x3 7.63 us: load_weight(): call(functools.partial(load_kernel, places), 'load_weight', [HBM] + [ANY]...]
    pallas_call x1, Pallas kernels: 5.01 us -> 4.17 us  [body(): call(functools.partial(local_kernel, len(arrays)), 'local_attention', [VM...]
  transfers between devices with their start and end apart: 17 -> 16, of which waited for: 6 -> 6; matrix products, arithmetic and copies ran while one was open for 0% -> 0% of each run, Pallas kernels for 46% -> 50%
where the time goes in v10:
time: 77.5 us; the launch traced here: 77.3 us
  Pallas kernels  43.4 us (56%)
  starting transfers between devices  16.7 us (22%)
  waiting for transfers between devices  16 us (21%)
  between operations  1.07 us (1%)
    pallas_call x6, Pallas kernels, project(): call(functools.partial(project_kernel, pieces, width, len(inputs), len(ad...  12 us
    ppermute x10, waiting for transfers between devices, swap(): return lax.ppermute(array, axis, [(i, i ^ bit) for i in range(size)])  11.8 us
    ppermute x10, starting transfers between devices, swap(): return lax.ppermute(array, axis, [(i, i ^ bit) for i in range(size)])  8.62 us
    ppermute x6, starting transfers between devices, body(): lax.ppermute(value, ('ctx', 'rep'), pairs)  8.1 us
    pallas_call x3, Pallas kernels, load_weight(): call(functools.partial(load_kernel, places), 'load_weight', [HBM] + [ANY]...  7.63 us
    ppermute x6, waiting for transfers between devices, body(): lax.ppermute(value, ('ctx', 'rep'), pairs)  4.26 us
    pallas_call x1, Pallas kernels, body(): call(functools.partial(local_kernel, len(arrays)), 'local_attention', [VM...  4.17 us
    pallas_call x1, Pallas kernels, body(): call(decode_project_kernel, 'decode_project', [SMEM] + [VMEM] * (1 + WEIG...  3.88 us
  transfers between devices with their start and end apart: 16, of which 6 were waited for; matrix products, arithmetic and copies ran while one was open for 0% of the time, Pallas kernels for 50%

profile of v10, /device:TPU:0, one launch (start us, length us, event | category | flops | bytes accessed | tf_op | source)
XLA Modules:
  0.0 77.3 jit_solution(17785804751458128780)
XLA Ops:
  0.6 0.1 pad_add_fusion.place_ref
  0.7 3.2 %own_state.1 = (f32[8,128,128]{2,1,0:T(8,128)S(1)}, f32[1,128]{1,0:T(1,128)S(1)}, f32[256,16]{1,0:T(8,128)S(1)}, f32[1,16,256]{2,1,0:T(8,128)S(1)}, bf16[256,204...) custom-call(s32[3]{0:T(128)S(1)} %pad_add_fusion.place_ref, ...), custom_call_target="tpu_custom_call" | custom-call | flops 268435456 | bytes 8388608 | tf_op jit(solution)/shard_map/own_state/pallas_call | solution.py:431
  4.0 3.1 %collective-permute-start = (bf16[1040,128]{1,0:T(8,128)(2,1)S(1)}, bf16[1040,128]{1,0:T(8,128)(2,1)S(1)}, u32[]{:S(2)}, u32[]{:S(2)}) collective-permute-start(bf16[1040,128]{1,0:T(8,128)(2,1)S(1)} %get-tuple-element.46), channel_id=1, source_target_pairs={{0,8},{1,9},{8,0},{9,1},{16,24},{17,25},{24,16},{25,17},{2,10},{3,... | collective-permute-start | bytes 798728 | tf_op jit(solution)/shard_map/ppermute | solution.py:521
  7.0 4.2 %local_attention.1 = (bf16[1,256,2048]{2,1,0:T(8,128)(2,1)S(1)}, bf16[4,2,2048]{2,1,0:T(2,128)(2,1)S(1)}, bf16[4,2,2048]{2,1,0:T(2,128)(2,1)S(1)}, bf16[4,2,2048...) custom-call(bf16[256,2048]{1,0:T(8,128)(2,1)S(1)} %get-tuple-element, ...), custom_call_target="tpu_custom_call" | custom-call | flops 536870912 | bytes 6291456 | tf_op jit(solution)/shard_map/local_attention/pallas_call | solution.py:453
  11.2 1.2 %more_state.1 = (f32[8,128,128]{2,1,0:T(8,128)S(1)}, bf16[1040,128]{1,0:T(8,128)(2,1)S(1)}) custom-call(bf16[256,2048]{1,0:T(8,128)(2,1)S(1)} %get-tuple-element.40.k_ref, bf16[256,2048]{1,0:T(8,128)(2,1)S(1)} %get-tuple-element.41.v_ref, f32[256,16]{1,0:T(8,128)S(1)} %get-tuple-element.42.col_ref, f32[1,128]{1,0:T(1,128)S(1)} %get-tuple-element.48.log_ref, ...), custom_call_target="tpu_custom_call" | custom-call | flops 134217728 | bytes 4194304 | tf_op jit(solution)/shard_map/more_state/pallas_call | solution.py:467
  12.4 0.1 collective-permute-start.3
  12.5 1.0 %collective-permute-done.got_ref.rest_0_ = bf16[1040,128]{1,0:T(8,128)(2,1)S(1)} collective-permute-done((bf16[1040,128]{1,0:T(8,128)(2,1)S(1)}, bf16[1040,128]{1,0:T(8,128)(2,1)S(1)}, u32[]{:S(2)}, u32[]{:S(2)}) %collective-permute-start) | collective-permute-done | bytes 266272 | tf_op jit(solution)/shard_map/ppermute | solution.py:521
  13.4 0.7 chain.4.rest_0_
  14.2 0.1 collective-permute-start.1
  14.3 2.9 %load_weight.3 = (bf16[256,6144]{1,0:T(8,128)(2,1)S(1)}, bf16[256,6144]{1,0:T(8,128)(2,1)S(1)}, f32[8,128]{1,0:T(8,128)S(1)}) custom-call(bf16[2048,6144]{1,0:T(8,128)(2,1)} %weight_hbm.7, bf16[1040,128]{1,0:T(8,128)(2,1)S(1)} %chain.4.rest_0_), custom_call_target="tpu_custom_call" | custom-call | flops 1 | bytes 1 | tf_op jit(solution)/shard_map/load_weight/pallas_call | solution.py:484
  17.1 3.2 %collective-permute-done.3.got_ref.rest_0_ = bf16[1040,128]{1,0:T(8,128)(2,1)S(1)} collective-permute-done((bf16[1040,128]{1,0:T(8,128)(2,1)S(1)}, bf16[1040,128]{1,0:T(8,128)(2,1)S(1)}, u32[]{:S(2)}, u32[]{:S(2)}) %collective-permute-start.3) | collective-permute-done | bytes 266272 | tf_op jit(solution)/shard_map/ppermute | solution.py:521
  20.3 0.7 chain.6
  21.1 0.1 collective-permute-start.4
  21.1 0.0 collective-permute-done.1.got_ref.rest_1_
  21.1 0.7 chain.5.rest_0_
  21.9 3.2 %collective-permute-start.2 = (bf16[1040,128]{1,0:T(8,128)(2,1)S(1)}, bf16[1040,128]{1,0:T(8,128)(2,1)S(1)}, u32[]{:S(2)}, u32[]{:S(2)}) collective-permute-start(bf16[1040,128]{1,0:T(8,128)(2,1)S(1)} %chain.5.rest_0_), channel_id=1, source_target_pairs={{0,8},{1,9},{8,0},{9,1},{16,24},{17,25},{24,16},{25,17},{2,10},{3,... | collective-permute-start | bytes 798728 | tf_op jit(solution)/shard_map/ppermute | solution.py:521
  25.1 2.9 %load_weight.4 = (bf16[256,6144]{1,0:T(8,128)(2,1)S(1)}, bf16[256,6144]{1,0:T(8,128)(2,1)S(1)}, f32[8,128]{1,0:T(8,128)S(1)}) custom-call(bf16[2048,6144]{1,0:T(8,128)(2,1)} %weight_hbm.7, bf16[1040,128]{1,0:T(8,128)(2,1)S(1)} %chain.5.rest_0_), custom_call_target="tpu_custom_call" | custom-call | flops 1 | bytes 1 | tf_op jit(solution)/shard_map/load_weight/pallas_call | solution.py:484
  27.9 0.0 collective-permute-done.4.got_ref.rest_1_
  28.0 0.7 chain.7.rest_0_
  28.7 1.6 %collective-permute-start.5 = (bf16[1040,128]{1,0:T(8,128)(2,1)S(1)}, bf16[1040,128]{1,0:T(8,128)(2,1)S(1)}, u32[]{:S(2)}, u32[]{:S(2)}) collective-permute-start(bf16[1040,128]{1,0:T(8,128)(2,1)S(1)} %chain.7.rest_0_), channel_id=1, source_target_pairs={{0,8},{1,9},{8,0},{9,1},{16,24},{17,25},{24,16},{25,17},{2,10},{3,... | collective-permute-start | bytes 798728 | tf_op jit(solution)/shard_map/ppermute | solution.py:521
  30.3 1.9 %load_weight.5 = (bf16[256,6144]{1,0:T(8,128)(2,1)S(1)}, f32[8,128]{1,0:T(8,128)S(1)}) custom-call(bf16[2048,6144]{1,0:T(8,128)(2,1)} %weight_hbm.7, bf16[1040,128]{1,0:T(8,128)(2,1)S(1)} %chain.7.rest_0_), custom_call_target="tpu_custom_call" | custom-call | flops 1 | bytes 1 | tf_op jit(solution)/shard_map/load_weight/pallas_call | solution.py:484
  32.2 0.0 collective-permute-done.2.rest_2_
  32.2 1.6 %hidden.2.rest_0_ = bf16[256,1024]{1,0:T(8,128)(2,1)S(1)} custom-call(s32[3]{0:T(128)S(1)} %pad_add_fusion.place_ref, bf16[1,256,2048]{2,1,0:T(8,128)(2,1)S(1)} %get-tuple-element.44.q_ref, f32[256,16]{1,0:T(8,128)S(1)} %get-tuple-element.42.col_ref, f32[256,2048]{1,0:T(8,128)S(1)} %get-tuple-element.45.local_ref, ...), custom_call_target="tpu_custom_call" | custom-call | flops 67108864 | bytes 5242880 | tf_op jit(solution)/shard_map/hidden/pallas_call | solution.py:529
  33.8 1.7 %project.6 = (f32[256,640]{1,0:T(8,128)S(1)}, f32[256,896]{1,0:T(8,128)S(1)}) custom-call(s32[3]{0:T(128)S(1)} %pad_add_fusion.place_ref, bf16[256,1024]{1,0:T(8,128)(2,1)S(1)} %hidden.2.rest_0_, bf16[256,6144]{1,0:T(8,128)(2,1)S(1)} %get-tuple-element.55.rest_1_.rest_2_.rest_0_, bf16[256,6144]{1,0:T(8,128)(2,1)S(1)} %get-tuple-element.56.rest_2_.rest_3_.rest_1_, ...), custom_call_target="tpu_custom_call" | custom-call | flops 1 | bytes 1 | tf_op jit(solution)/shard_map/project/pallas_call | solution.py:595
  35.5 0.7 final_state.2.rest_0_
  36.3 0.1 collective-permute-start.6
  36.3 0.1 collective-permute-done.5.rest_2_
  36.4 1.6 %hidden.3.rest_0_.rest_1_ = bf16[256,1024]{1,0:T(8,128)(2,1)S(1)} custom-call(s32[3]{0:T(128)S(1)} %pad_add_fusion.place_ref, bf16[1,256,2048]{2,1,0:T(8,128)(2,1)S(1)} %get-tuple-element.44.q_ref, f32[256,16]{1,0:T(8,128)S(1)} %get-tuple-element.42.col_ref, f32[256,2048]{1,0:T(8,128)S(1)} %get-tuple-element.45.local_ref, ...), custom_call_target="tpu_custom_call" | custom-call | flops 67108864 | bytes 5242880 | tf_op jit(solution)/shard_map/hidden/pallas_call | solution.py:529
  38.1 1.7 %project.7 = (bf16[256,640]{1,0:T(8,128)(2,1)S(1)}, bf16[256,896]{1,0:T(8,128)(2,1)S(1)}) custom-call(s32[3]{0:T(128)S(1)} %pad_add_fusion.place_ref, bf16[256,1024]{1,0:T(8,128)(2,1)S(1)} %hidden.3.rest_0_.rest_1_, f32[256,640]{1,0:T(8,128)S(1)} %get-tuple-element.66.rest_3_.rest_1_, f32[256,896]{1,0:T(8,128)S(1)} %get-tuple-element.67.rest_2_, ...), custom_call_target="tpu_custom_call" | custom-call | flops 1 | bytes 1 | tf_op jit(solution)/shard_map/project/pallas_call | solution.py:595
  39.8 0.9 %final_state.3.rest_1_ = f32[8,128,128]{2,1,0:T(8,128)S(1)} custom-call(s32[3]{0:T(128)S(1)} %pad_add_fusion.place_ref, f32[8,128,128]{2,1,0:T(8,128)S(1)} %get-tuple-element.51.own_ref, f32[1,128]{1,0:T(1,128)S(1)} %get-tuple-element.48.log_ref, bf16[1040,128]{1,0:T(8,128)(2,1)S(1)} %collective-permute-done.3.got_ref.rest_0_, ...), custom_call_target="tpu_custom_call" | custom-call | flops 1 | bytes 1 | tf_op jit(solution)/shard_map/final_state/pallas_call | solution.py:545
  40.7 0.5 collective-permute-start.7
  41.2 1.5 %collective-permute-start.12 = (bf16[256,896]{1,0:T(8,128)(2,1)S(1)}, bf16[256,896]{1,0:T(8,128)(2,1)S(1)}, u32[]{:S(2)}, u32[]{:S(2)}) collective-permute-start(bf16[256,896]{1,0:T(8,128)(2,1)S(1)} %get-tuple-element.68.rest_3_), channel_id=1, source_target_pairs={{0,4},{2,6},{4,0},{6,2},{1,5},{3,7},{5,1},{7,3},{8,12},{10,14},{12... | collective-permute-start | bytes 1376264 | tf_op jit(solution)/shard_map/ppermute | solution.py:388
  42.7 1.5 %project.8.rest_10_ = bf16[256,640]{1,0:T(8,128)(2,1)S(1)} custom-call(s32[3]{0:T(128)S(1)} %pad_add_fusion.place_ref, bf16[256,1024]{1,0:T(8,128)(2,1)S(1)} %hidden.2.rest_0_, bf16[256,1024]{1,0:T(8,128)(2,1)S(1)} %hidden.3.rest_0_.rest_1_, bf16[256,6144]{1,0:T(8,128)(2,1)S(1)} %get-tuple-element.55.rest_1_.rest_2_.rest_0_, ...), custom_call_target="tpu_custom_call" | custom-call | flops 1 | bytes 1 | tf_op jit(solution)/shard_map/project/pallas_call | solution.py:595
  44.2 1.6 %collective-permute-start.9 = (bf16[256,640]{1,0:T(8,128)(2,1)S(1)}, bf16[256,640]{1,0:T(8,128)(2,1)S(1)}, u32[]{:S(2)}, u32[]{:S(2)}) collective-permute-start(bf16[256,640]{1,0:T(8,128)(2,1)S(1)} %project.8.rest_10_), channel_id=1, source_target_pairs={{0,2},{2,0},{4,6},{6,4},{1,3},{3,1},{5,7},{7,5},{8,10},{10,8},{12,... | collective-permute-start | bytes 983048 | tf_op jit(solution)/shard_map/ppermute | solution.py:388
  45.8 0.5 collective-permute-start.10
  46.3 1.8 %project.9.rest_11_ = bf16[256,896]{1,0:T(8,128)(2,1)S(1)} custom-call(s32[3]{0:T(128)S(1)} %pad_add_fusion.place_ref, bf16[256,1024]{1,0:T(8,128)(2,1)S(1)} %hidden.2.rest_0_, bf16[256,1024]{1,0:T(8,128)(2,1)S(1)} %hidden.3.rest_0_.rest_1_, bf16[256,6144]{1,0:T(8,128)(2,1)S(1)} %get-tuple-element.55.rest_1_.rest_2_.rest_0_, ...), custom_call_target="tpu_custom_call" | custom-call | flops 1 | bytes 1 | tf_op jit(solution)/shard_map/project/pallas_call | solution.py:595
  48.1 0.0 copy-start
  48.1 0.0 copy-start.1
  48.2 2.6 %project.10 = (f32[256,640]{1,0:T(8,128)S(1)}, f32[256,896]{1,0:T(8,128)S(1)}) custom-call(s32[3]{0:T(128)S(1)} %pad_add_fusion.place_ref, bf16[256,1024]{1,0:T(8,128)(2,1)S(1)} %hidden.2.rest_0_, bf16[256,1024]{1,0:T(8,128)(2,1)S(1)} %hidden.3.rest_0_.rest_1_, bf16[256,6144]{1,0:T(8,128)(2,1)S(1)} %get-tuple-element.55.rest_1_.rest_2_.rest_0_, ...), custom_call_target="tpu_custom_call" | custom-call | flops 1 | bytes 1 | tf_op jit(solution)/shard_map/project/pallas_call | solution.py:595
  50.8 0.0 collective-permute-done.6.rest_2_
  50.8 0.0 collective-permute-done.7.rest_3_
  50.8 0.0 copy-done
  50.8 0.0 copy-done.1
  50.8 1.7 %decode_rows.1.rows_ref = bf16[16,2048]{1,0:T(8,128)(2,1)S(1)} custom-call(s32[3]{0:T(128)S(1)} %pad_add_fusion.place_ref, s32[4]{0:T(128)S(1)} %copy-done.1, bf16[4,2,2048]{2,1,0:T(2,128)(2,1)S(1)} %get-tuple-element.63.q_ref, bf16[4,2,2048]{2,1,0:T(2,128)(2,1)S(1)} %get-tuple-element.64.k_ref, bf16[4,2,2048]{2,1,0:T(2,128)(2,1)S(1)} %get-tuple-element.65.v_ref, ...), custom_call_target="tpu_custom_call" | custom-call | flops 1 | bytes 1 | tf_op jit(solution)/shard_map/decode_rows/pallas_call | solution.py:558
  52.6 0.5 collective-permute-start.14
  53.1 3.9 %decode_project.1 = (f32[8,3072]{1,0:T(8,128)S(1)}, bf16[8,3072]{1,0:T(8,128)(2,1)S(1)}) custom-call(s32[3]{0:T(128)S(1)} %pad_add_fusion.place_ref, bf16[16,2048]{1,0:T(8,128)(2,1)S(1)} %decode_rows.1.rows_ref, bf16[256,6144]{1,0:T(8,128)(2,1)S(1)} %get-tuple-element.55.rest_1_.rest_2_.rest_0_, ...), custom_call_target="tpu_custom_call" | custom-call | flops 1 | bytes 1 | tf_op jit(solution)/shard_map/decode_project/pallas_call | solution.py:632
  57.0 0.0 collective-permute-done.9.rest_0_.ax
  57.0 0.0 collective-permute-done.12.got_ref
  57.0 0.1 relay.3
  57.1 1.6 %collective-permute-start.13 = (bf16[256,896]{1,0:T(8,128)(2,1)S(1)}, bf16[256,896]{1,0:T(8,128)(2,1)S(1)}, u32[]{:S(2)}, u32[]{:S(2)}) collective-permute-start(bf16[256,896]{1,0:T(8,128)(2,1)S(1)} %relay.3), channel_id=1, source_target_pairs={{0,2},{2,0},{4,6},{6,4},{1,3},{3,1},{5,7},{7,5},{8,10},{10,8},{12,... | collective-permute-start | bytes 1376264 | tf_op jit(solution)/shard_map/ppermute | solution.py:388
  58.7 3.2 %collective-permute-done.10.got_ref = bf16[256,640]{1,0:T(8,128)(2,1)S(1)} collective-permute-done((bf16[256,640]{1,0:T(8,128)(2,1)S(1)}, bf16[256,640]{1,0:T(8,128)(2,1)S(1)}, u32[]{:S(2)}, u32[]{:S(2)}) %collective-permute-start.10) | collective-permute-done | bytes 327712 | tf_op jit(solution)/shard_map/ppermute | solution.py:388
  61.9 0.1 relay.2
  62.0 0.3 collective-permute-start.11
  62.3 1.5 %collective-permute-start.8 = (bf16[8,3072]{1,0:T(8,128)(2,1)S(1)}, bf16[8,3072]{1,0:T(8,128)(2,1)S(1)}, u32[]{:S(2)}, u32[]{:S(2)}) collective-permute-start(bf16[8,3072]{1,0:T(8,128)(2,1)S(1)} %get-tuple-element.70.rest_1_), channel_id=1, source_target_pairs={{0,2},{2,0},{4,6},{6,4},{1,3},{3,1},{5,7},{7,5},{8,10},{10,8},{12,... | collective-permute-start | bytes 147464 | tf_op jit(solution)/shard_map/ppermute | solution.py:388
  63.8 7.9 %collective-permute-done.8.rest_10_.got_ref = bf16[8,3072]{1,0:T(8,128)(2,1)S(1)} collective-permute-done((bf16[8,3072]{1,0:T(8,128)(2,1)S(1)}, bf16[8,3072]{1,0:T(8,128)(2,1)S(1)}, u32[]{:S(2)}, u32[]{:S(2)}) %collective-permute-start.8) | collective-permute-done | bytes 49184 | tf_op jit(solution)/shard_map/ppermute | solution.py:388
  71.7 0.6 collective-permute-start.15
  72.2 2.6 %project.11 = (f32[256,640]{1,0:T(8,128)S(1)}, f32[256,896]{1,0:T(8,128)S(1)}) custom-call(s32[3]{0:T(128)S(1)} %pad_add_fusion.place_ref, bf16[256,1024]{1,0:T(8,128)(2,1)S(1)} %hidden.2.rest_0_, bf16[256,1024]{1,0:T(8,128)(2,1)S(1)} %hidden.3.rest_0_.rest_1_, bf16[256,6144]{1,0:T(8,128)(2,1)S(1)} %get-tuple-element.55.rest_1_.rest_2_.rest_0_, ...), custom_call_target="tpu_custom_call" | custom-call | flops 1 | bytes 1 | tf_op jit(solution)/shard_map/project/pallas_call | solution.py:595
  74.9 0.0 collective-permute-done.14.by
  74.9 0.7 collective-permute-done.15.d_got
  75.5 0.0 collective-permute-done.11.ay
  75.5 0.0 collective-permute-done.13.bx
  75.5 1.6 %finish.1 = (bf16[1,256,1536]{2,1,0:T(8,128)(2,1)}, bf16[4,2,1536]{2,1,0:T(2,128)(2,1)}) custom-call(f32[256,640]{1,0:T(8,128)S(1)} %get-tuple-element.71.own_a, f32[256,896]{1,0:T(8,128)S(1)} %get-tuple-element.72.own_b, bf16[256,640]{1,0:T(8,128)(2,1)S(1)} %collective-permute-done.9.rest_0_.ax, bf16[256,640]{1,0:T(8,128)(2,1)S(1)} %collective-permute-done.11.ay, ...), custom_call_target="tpu_custom_call" | custom-call | flops 1179648 | bytes 3932160 | tf_op jit(solution)/shard_map/finish/pallas_call | solution.py:655
  (1 shorter events, 0.0 us)
Async XLA Ops:
  4.0 9.5 %collective-permute-start = (bf16[1040,128]{1,0:T(8,128)(2,1)S(1)}, bf16[1040,128]{1,0:T(8,128)(2,1)S(1)}, u32[]{:S(2)}, u32[]{:S(2)}) collective-permute-start(bf16[1040,128]{1,0:T(8,128)(2,1)S(1)} %get-tuple-element.46), channel_id=1, source_target_pairs={{0,8},{1,9},{8,0},{9,1},{16,24},{17,25},{24,16},{25,17},{2,10},{3,... | collective-permute-start | bytes 798728 | tf_op jit(solution)/shard_map/ppermute | solution.py:521
  12.4 7.9 %collective-permute-start.3 = (bf16[1040,128]{1,0:T(8,128)(2,1)S(1)}, bf16[1040,128]{1,0:T(8,128)(2,1)S(1)}, u32[]{:S(2)}, u32[]{:S(2)}) collective-permute-start(bf16[1040,128]{1,0:T(8,128)(2,1)S(1)} %get-tuple-element.50.rest_0_), channel_id=1, source_target_pairs={{0,8},{1,9},{8,0},{9,1},{16,24},{17,25},{24,16},{25,17},{2,10},{3,... | collective-permute-start | bytes 798728 | tf_op jit(solution)/shard_map/ppermute | solution.py:521
  14.2 7.0 %collective-permute-start.1 = (bf16[1040,128]{1,0:T(8,128)(2,1)S(1)}, bf16[1040,128]{1,0:T(8,128)(2,1)S(1)}, u32[]{:S(2)}, u32[]{:S(2)}) collective-permute-start(bf16[1040,128]{1,0:T(8,128)(2,1)S(1)} %chain.4.rest_0_), channel_id=1, source_target_pairs={{0,1},{1,0},{8,16},{9,17},{16,8},{17,9},{24,25},{25,24},{2,3},{3,2... | collective-permute-start | bytes 798728 | tf_op jit(solution)/shard_map/ppermute | solution.py:521
  21.1 6.9 %collective-permute-start.4 = (bf16[1040,128]{1,0:T(8,128)(2,1)S(1)}, bf16[1040,128]{1,0:T(8,128)(2,1)S(1)}, u32[]{:S(2)}, u32[]{:S(2)}) collective-permute-start(bf16[1040,128]{1,0:T(8,128)(2,1)S(1)} %chain.6), channel_id=1, source_target_pairs={{0,1},{1,0},{8,16},{9,17},{16,8},{17,9},{24,25},{25,24},{2,3},{3,2... | collective-permute-start | bytes 798728 | tf_op jit(solution)/shard_map/ppermute | solution.py:521
  21.9 10.3 %collective-permute-start.2 = (bf16[1040,128]{1,0:T(8,128)(2,1)S(1)}, bf16[1040,128]{1,0:T(8,128)(2,1)S(1)}, u32[]{:S(2)}, u32[]{:S(2)}) collective-permute-start(bf16[1040,128]{1,0:T(8,128)(2,1)S(1)} %chain.5.rest_0_), channel_id=1, source_target_pairs={{0,8},{1,9},{8,0},{9,1},{16,24},{17,25},{24,16},{25,17},{2,10},{3,... | collective-permute-start | bytes 798728 | tf_op jit(solution)/shard_map/ppermute | solution.py:521
  28.7 7.7 %collective-permute-start.5 = (bf16[1040,128]{1,0:T(8,128)(2,1)S(1)}, bf16[1040,128]{1,0:T(8,128)(2,1)S(1)}, u32[]{:S(2)}, u32[]{:S(2)}) collective-permute-start(bf16[1040,128]{1,0:T(8,128)(2,1)S(1)} %chain.7.rest_0_), channel_id=1, source_target_pairs={{0,8},{1,9},{8,0},{9,1},{16,24},{17,25},{24,16},{25,17},{2,10},{3,... | collective-permute-start | bytes 798728 | tf_op jit(solution)/shard_map/ppermute | solution.py:521
  36.3 14.6 %collective-permute-start.6 = (f32[8,128,128]{2,1,0:T(8,128)S(1)}, f32[8,128,128]{2,1,0:T(8,128)S(1)}, u32[]{:S(2)}, u32[]{:S(2)}) collective-permute-start(f32[8,128,128]{2,1,0:T(8,128)S(1)} %final_state.2.rest_0_), channel_id=1, source_target_pairs={{0,1},{1,0},{2,3},{3,2},{4,5},{5,4},{6,7},{7,6},{8,9},{9,8},{10,11... | collective-permute-start | bytes 1572872 | tf_op jit(solution)/shard_map/ppermute | solution.py:388
  40.7 10.1 %collective-permute-start.7 = (f32[8,128,128]{2,1,0:T(8,128)S(1)}, f32[8,128,128]{2,1,0:T(8,128)S(1)}, u32[]{:S(2)}, u32[]{:S(2)}) collective-permute-start(f32[8,128,128]{2,1,0:T(8,128)S(1)} %final_state.3.rest_1_), channel_id=1, source_target_pairs={{0,1},{1,0},{2,3},{3,2},{4,5},{5,4},{6,7},{7,6},{8,9},{9,8},{10,11... | collective-permute-start | bytes 1572872 | tf_op jit(solution)/shard_map/ppermute | solution.py:388
  41.2 15.8 %collective-permute-start.12 = (bf16[256,896]{1,0:T(8,128)(2,1)S(1)}, bf16[256,896]{1,0:T(8,128)(2,1)S(1)}, u32[]{:S(2)}, u32[]{:S(2)}) collective-permute-start(bf16[256,896]{1,0:T(8,128)(2,1)S(1)} %get-tuple-element.68.rest_3_), channel_id=1, source_target_pairs={{0,4},{2,6},{4,0},{6,2},{1,5},{3,7},{5,1},{7,3},{8,12},{10,14},{12... | collective-permute-start | bytes 1376264 | tf_op jit(solution)/shard_map/ppermute | solution.py:388
  44.2 12.8 %collective-permute-start.9 = (bf16[256,640]{1,0:T(8,128)(2,1)S(1)}, bf16[256,640]{1,0:T(8,128)(2,1)S(1)}, u32[]{:S(2)}, u32[]{:S(2)}) collective-permute-start(bf16[256,640]{1,0:T(8,128)(2,1)S(1)} %project.8.rest_10_), channel_id=1, source_target_pairs={{0,2},{2,0},{4,6},{6,4},{1,3},{3,1},{5,7},{7,5},{8,10},{10,8},{12,... | collective-permute-start | bytes 983048 | tf_op jit(solution)/shard_map/ppermute | solution.py:388
  45.8 16.1 %collective-permute-start.10 = (bf16[256,640]{1,0:T(8,128)(2,1)S(1)}, bf16[256,640]{1,0:T(8,128)(2,1)S(1)}, u32[]{:S(2)}, u32[]{:S(2)}) collective-permute-start(bf16[256,640]{1,0:T(8,128)(2,1)S(1)} %get-tuple-element.73), channel_id=1, source_target_pairs={{0,2},{2,0},{4,6},{6,4},{1,3},{3,1},{5,7},{7,5},{8,10},{10,8},{12,... | collective-permute-start | bytes 983048 | tf_op jit(solution)/shard_map/ppermute | solution.py:388
  48.1 2.7 %copy-start = (f32[4,16,2]{1,2,0:T(2,128)S(1)}, f32[4,16,2]{1,2,0:T(2,128)}, u32[]{:S(2)}) copy-start(f32[4,16,2]{1,2,0:T(2,128)} %param.18) | copy-start | bytes 1540
  48.1 2.7 %copy-start.1 = (s32[4]{0:T(128)S(1)}, s32[4]{0:T(128)}, u32[]{:S(2)}) copy-start(s32[4]{0:T(128)} %prompt_ref.1) | copy-start | bytes 52
  52.6 22.3 %collective-permute-start.14 = (bf16[256,896]{1,0:T(8,128)(2,1)S(1)}, bf16[256,896]{1,0:T(8,128)(2,1)S(1)}, u32[]{:S(2)}, u32[]{:S(2)}) collective-permute-start(bf16[256,896]{1,0:T(8,128)(2,1)S(1)} %project.9.rest_11_), channel_id=1, source_target_pairs={{0,4},{2,6},{4,0},{6,2},{1,5},{3,7},{5,1},{7,3},{8,12},{10,14},{12... | collective-permute-start | bytes 1376264 | tf_op jit(solution)/shard_map/ppermute | solution.py:388
  57.1 18.4 %collective-permute-start.13 = (bf16[256,896]{1,0:T(8,128)(2,1)S(1)}, bf16[256,896]{1,0:T(8,128)(2,1)S(1)}, u32[]{:S(2)}, u32[]{:S(2)}) collective-permute-start(bf16[256,896]{1,0:T(8,128)(2,1)S(1)} %relay.3), channel_id=1, source_target_pairs={{0,2},{2,0},{4,6},{6,4},{1,3},{3,1},{5,7},{7,5},{8,10},{10,8},{12,... | collective-permute-start | bytes 1376264 | tf_op jit(solution)/shard_map/ppermute | solution.py:388
  62.0 13.6 %collective-permute-start.11 = (bf16[256,640]{1,0:T(8,128)(2,1)S(1)}, bf16[256,640]{1,0:T(8,128)(2,1)S(1)}, u32[]{:S(2)}, u32[]{:S(2)}) collective-permute-start(bf16[256,640]{1,0:T(8,128)(2,1)S(1)} %relay.2), channel_id=1, source_target_pairs={{0,4},{2,6},{4,0},{6,2},{1,5},{3,7},{5,1},{7,3},{8,12},{10,14},{12... | collective-permute-start | bytes 983048 | tf_op jit(solution)/shard_map/ppermute | solution.py:388
  62.3 9.3 %collective-permute-start.8 = (bf16[8,3072]{1,0:T(8,128)(2,1)S(1)}, bf16[8,3072]{1,0:T(8,128)(2,1)S(1)}, u32[]{:S(2)}, u32[]{:S(2)}) collective-permute-start(bf16[8,3072]{1,0:T(8,128)(2,1)S(1)} %get-tuple-element.70.rest_1_), channel_id=1, source_target_pairs={{0,2},{2,0},{4,6},{6,4},{1,3},{3,1},{5,7},{7,5},{8,10},{10,8},{12,... | collective-permute-start | bytes 147464 | tf_op jit(solution)/shard_map/ppermute | solution.py:388
  71.7 3.9 %collective-permute-start.15 = (bf16[8,1536]{1,0:T(8,128)(2,1)S(1)}, bf16[8,1536]{1,0:T(8,128)(2,1)S(1)}, u32[]{:S(2)}, u32[]{:S(2)}) collective-permute-start(bf16[8,1536]{1,0:T(8,128)(2,1)S(1)} %get-tuple-element.77), channel_id=1, source_target_pairs={{0,4},{2,6},{4,0},{6,2},{1,5},{3,7},{5,1},{7,3},{8,12},{10,14},{12... | collective-permute-start | bytes 73736 | tf_op jit(solution)/shard_map/ppermute | solution.py:388

commit v11 on v9

--- a/solution.py
+++ b/solution.py
@@ -12,8 +12,9 @@
 NEGATIVE = -1e30
 HIGH = lax.Precision.HIGHEST
 CHUNKS = 2
-WEIGHT_PARTS = 4
-EARLY_PARTS = 2
+WEIGHT_PARTS = 8
+EARLY_PARTS = 3
+LATER_PARTS = (2, 3)
 VMEM_BYTES = 8 * 2**20
 F32 = jnp.float32
 BF16 = jnp.bfloat16
@@ -191,9 +192,10 @@
     return copies
 
 
-def load_kernel(index, weight_hbm, *rest):
-    weight_ref, token_ref, sems = rest[-3:]
-    copies = weight_copies([index], weight_hbm, [weight_ref], sems)
+def load_kernel(places, weight_hbm, *rest):
+    token_ref, sems = rest[-2:]
+    weights = rest[-2 - len(places) : -2]
+    copies = weight_copies(places, weight_hbm, weights, sems)
     token_ref[...] = jnp.zeros_like(token_ref)
     for copy in copies:
         copy.wait()
@@ -234,21 +236,23 @@
 
 def final_kernel(first, phases, place_ref, own_ref, log_ref, *rest):
     got, out_ref = rest[:phases], rest[-1]
-    group = place_ref[0]
     keep = jnp.exp(log_ref[...])
-    later = jnp.zeros((1, HEAD_DIM), F32)
-    for phase in range(phases):
-        later = jnp.where(group == phases - 1 - phase, read_log(got[phase]), later)
-    later = jnp.exp(later)
-    for i in range(out_ref.shape[0]):
-        h = first + i
-        suffix = jnp.zeros((HEAD_DIM, HEAD_DIM), F32)
-        for phase in range(phases):
-            there = state_rows(got[phase], i).astype(F32)
-            suffix = jnp.where(group == phases - 1 - phase, there, suffix)
-        prefix = entering_state(group, got, i).astype(F32)
-        here = own_ref[i] + keep[:, h : h + 1] * prefix
-        out_ref[i] = suffix + later[:, h : h + 1] * here
+
+    def write(group):
+        prefix = got[group - 1] if group > 0 else None
+        suffix = got[phases - 1 - group] if group < phases else None
+        later = None if suffix is None else jnp.exp(read_log(suffix))
+        for i in range(out_ref.shape[0]):
+            h = first + i
+            value = own_ref[i]
+            if prefix is not None:
+                value = value + keep[:, h : h + 1] * state_rows(prefix, i).astype(F32)
+            if suffix is not None:
+                value = later[:, h : h + 1] * value + state_rows(suffix, i).astype(F32)
+            out_ref[i] = value
+
+    for group in range(phases + 1):
+        pl.when(place_ref[0] == group)(functools.partial(write, group))
 
 
 def flat_rows(ref, rows_ref):
@@ -463,18 +467,21 @@
         owns.append(in_vmem(made[0]))
         values_out.append(made[1])
 
+    todo = list(LATER_PARTS)
+
     def load_weight(*after):
-        if len(weights) == WEIGHT_PARTS:
+        if not todo:
             return []
-        part, done = call(
-            functools.partial(load_kernel, len(weights)),
+        places = range(len(weights), len(weights) + todo.pop(0))
+        *loaded, done = call(
+            functools.partial(load_kernel, places),
             "load_weight",
             [HBM] + [ANY] * len(after),
-            [weight_part, token],
-            [pltpu.SemaphoreType.DMA((1,))],
+            [weight_part] * len(places) + [token],
+            [pltpu.SemaphoreType.DMA((len(places),))],
             cost(1, 1),
         )(weight_hbm, *after)
-        weights.append(part)
+        weights.extend(loaded)
         return [done]
 
     received = []
@@ -505,13 +512,13 @@
                 after = load_weight(value) if c == 0 else []
         received.append([lax.ppermute(value, ("ctx", "rep"), pairs) for value in values_out])
     loaded = []
-    while len(weights) < WEIGHT_PARTS:
+    while todo:
         loaded = load_weight(values_out[-1], *loaded)
     weights = [in_vmem(part) for part in weights]
 
-    after = loaded
-    hidden = [
-        call(
+    def make_hidden(c, *after):
+        first, size = chunks[c]
+        return call(
             functools.partial(hidden_kernel, phases, first),
             "hidden",
             [SMEM] + [VMEM] * (3 + phases) + [ANY] * len(after),
@@ -519,24 +526,23 @@
             (),
             cost(2 * length * size * HEAD_DIM * HEAD_DIM, 20 * length * size * HEAD_DIM),
         )(place, queries, columns, local, *[received[phase][c] for phase in range(phases)], *after)
-        for c, (first, size) in enumerate(chunks)
-    ]
-
-    def final_states(*after):
-        finals = []
-        for c, (first, size) in enumerate(chunks):
-            gate = after if c == count - 1 else ()
-            finals.append(
-                call(
-                    functools.partial(final_kernel, first, phases),
-                    "final_state",
-                    [SMEM, VMEM, VMEM] + [VMEM] * phases + [ANY] * len(gate),
-                    sds((size, HEAD_DIM, HEAD_DIM), F32),
-                    (),
-                    cost(4 * state_elements // count, state_elements * 4),
-                )(place, owns[c], log_row, *[got[c] for got in received], *gate)
-            )
-        return finals, [swap(final, "rep", reps, 1) for final in finals]
+
+    def make_final(c, *after):
+        first, size = chunks[c]
+        final = call(
+            functools.partial(final_kernel, first, phases),
+            "final_state",
+            [SMEM, VMEM, VMEM] + [VMEM] * phases + [ANY] * len(after),
+            sds((size, HEAD_DIM, HEAD_DIM), F32),
+            (),
+            cost(4 * state_elements // count, state_elements * 4),
+        )(place, owns[c], log_row, *[got[c] for got in received], *after)
+        return final, swap(final, "rep", reps, 1)
+
+    hidden, finals = [make_hidden(0, *loaded)], []
+    for c in range(1, count):
+        finals.append(make_final(c - 1, hidden[-1]))
+        hidden.append(make_hidden(c, finals[-1][0]))
 
     def decode_rows(finals, others, *after):
         flat = pltpu.VMEM((d_rows, features), F32)
@@ -561,7 +567,7 @@
 
     out_columns = out_weight.shape[1]
     if parts != 4 or (out_columns // parts) % 256 != 0 or length % 64 != 0:
-        rows_all = jnp.concatenate([jnp.concatenate(hidden, axis=1), decode_rows(*final_states())], axis=0)
+        rows_all = jnp.concatenate([jnp.concatenate(hidden, axis=1), decode_rows(*zip(*finals, make_final(count - 1)))], axis=0)
         terms = jnp.dot(rows_all, out_weight, preferred_element_type=F32)
         summed = lax.psum_scatter(terms, "head", scatter_dimension=1, tiled=True)
         prefill_out = summed[:length].astype(BF16)[None]
@@ -614,7 +620,8 @@
     y_a = swap(sent_a, "head", parts, 2)
     x_b = swap(sent_b, "head", parts, 1)
 
-    d_hidden = decode_rows(*final_states(to_y), sent_a, sent_b)
+    finals.append(make_final(count - 1, to_y))
+    d_hidden = decode_rows(*zip(*finals), sent_a, sent_b)
     d_own, d_x, d_y, d_far = call(
         decode_project_kernel,
         "decode_project",

time: 74.8 us -> 73.1 us (0.977)
  waiting for transfers between devices: 10.5 us -> 9.56 us
    pallas_call x6, Pallas kernels: 10.5 us -> 11.5 us  [the longest x2 6.65 us: load_weight(): call(functools.partial(load_kernel, places), 'load_weight', [HBM] + [ANY]...]
    ppermute x6, starting transfers between devices: 8.16 us -> 7.17 us  [body(): lax.ppermute(value, ('ctx', 'rep'), pairs)]
    pallas_call x1, Pallas kernels: 5.01 us -> 4.17 us  [body(): call(functools.partial(local_kernel, len(arrays)), 'local_attention', [VM...]
    ppermute x6, waiting for transfers between devices: 7.07 us -> 6.27 us  [body(): lax.ppermute(value, ('ctx', 'rep'), pairs)]
  transfers between devices with their start and end apart: 17 -> 17, of which waited for: 6 -> 6; matrix products, arithmetic and copies ran while one was open for 0% -> 0% of each run, Pallas kernels for 46% -> 47%
where the time goes in v11:
time: 73.1 us; the launch traced here: 72.8 us
  Pallas kernels  42.4 us (58%)
  starting transfers between devices  19.8 us (27%)
  waiting for transfers between devices  9.56 us (13%)
  between operations  1.05 us (1%)
    ppermute x11, starting transfers between devices, swap(): return lax.ppermute(array, axis, [(i, i ^ bit) for i in range(size)])  12.6 us
    pallas_call x6, Pallas kernels, project(): call(functools.partial(project_kernel, pieces, width, len(inputs), len(ad...  12 us
    ppermute x6, starting transfers between devices, body(): lax.ppermute(value, ('ctx', 'rep'), pairs)  7.17 us
    pallas_call x2, Pallas kernels, load_weight(): call(functools.partial(load_kernel, places), 'load_weight', [HBM] + [ANY]...  6.65 us
    ppermute x6, waiting for transfers between devices, body(): lax.ppermute(value, ('ctx', 'rep'), pairs)  6.27 us
    pallas_call x1, Pallas kernels, body(): call(functools.partial(local_kernel, len(arrays)), 'local_attention', [VM...  4.17 us
    pallas_call x1, Pallas kernels, body(): call(decode_project_kernel, 'decode_project', [SMEM] + [VMEM] * (1 + WEIG...  3.91 us
    ppermute x11, waiting for transfers between devices, swap(): return lax.ppermute(array, axis, [(i, i ^ bit) for i in range(size)])  3.28 us
  transfers between devices with their start and end apart: 17, of which 6 were waited for; matrix products, arithmetic and copies ran while one was open for 0% of the time, Pallas kernels for 47%

profile of v11, /device:TPU:0, one launch (start us, length us, event | category | flops | bytes accessed | tf_op | source)
XLA Modules:
  0.0 72.8 jit_solution(11962060960084278510)
XLA Ops:
  0.6 0.1 pad_add_fusion.place_ref
  0.7 3.2 %own_state.1 = (f32[8,128,128]{2,1,0:T(8,128)S(1)}, f32[1,128]{1,0:T(1,128)S(1)}, f32[256,16]{1,0:T(8,128)S(1)}, f32[1,16,256]{2,1,0:T(8,128)S(1)}, bf16[256,204...) custom-call(s32[3]{0:T(128)S(1)} %pad_add_fusion.place_ref, ...), custom_call_target="tpu_custom_call" | custom-call | flops 268435456 | bytes 8388608 | tf_op jit(solution)/shard_map/own_state/pallas_call | solution.py:423
  4.0 3.1 %collective-permute-start = (bf16[1040,128]{1,0:T(8,128)(2,1)S(1)}, bf16[1040,128]{1,0:T(8,128)(2,1)S(1)}, u32[]{:S(2)}, u32[]{:S(2)}) collective-permute-start(bf16[1040,128]{1,0:T(8,128)(2,1)S(1)} %get-tuple-element.45), channel_id=1, source_target_pairs={{0,8},{1,9},{8,0},{9,1},{16,24},{17,25},{24,16},{25,17},{2,10},{3,... | collective-permute-start | bytes 798728 | tf_op jit(solution)/shard_map/ppermute | solution.py:513
  7.0 4.2 %local_attention.1 = (bf16[1,256,2048]{2,1,0:T(8,128)(2,1)S(1)}, bf16[4,2,2048]{2,1,0:T(2,128)(2,1)S(1)}, bf16[4,2,2048]{2,1,0:T(2,128)(2,1)S(1)}, bf16[4,2,2048...) custom-call(bf16[256,2048]{1,0:T(8,128)(2,1)S(1)} %get-tuple-element, ...), custom_call_target="tpu_custom_call" | custom-call | flops 536870912 | bytes 6291456 | tf_op jit(solution)/shard_map/local_attention/pallas_call | solution.py:445
  11.2 1.2 %more_state.1 = (f32[8,128,128]{2,1,0:T(8,128)S(1)}, bf16[1040,128]{1,0:T(8,128)(2,1)S(1)}) custom-call(bf16[256,2048]{1,0:T(8,128)(2,1)S(1)} %get-tuple-element.39.k_ref, bf16[256,2048]{1,0:T(8,128)(2,1)S(1)} %get-tuple-element.40.v_ref, f32[256,16]{1,0:T(8,128)S(1)} %get-tuple-element.41.col_ref, f32[1,128]{1,0:T(1,128)S(1)} %get-tuple-element.47.log_ref, ...), custom_call_target="tpu_custom_call" | custom-call | flops 134217728 | bytes 4194304 | tf_op jit(solution)/shard_map/more_state/pallas_call | solution.py:459
  12.4 0.1 collective-permute-start.3
  12.5 1.0 %collective-permute-done.got_ref.rest_0_ = bf16[1040,128]{1,0:T(8,128)(2,1)S(1)} collective-permute-done((bf16[1040,128]{1,0:T(8,128)(2,1)S(1)}, bf16[1040,128]{1,0:T(8,128)(2,1)S(1)}, u32[]{:S(2)}, u32[]{:S(2)}) %collective-permute-start) | collective-permute-done | bytes 266272 | tf_op jit(solution)/shard_map/ppermute | solution.py:513
  13.4 0.7 chain.4.rest_0_
  14.2 0.1 collective-permute-start.1
  14.2 2.9 %load_weight.2 = (bf16[256,6144]{1,0:T(8,128)(2,1)S(1)}, bf16[256,6144]{1,0:T(8,128)(2,1)S(1)}, f32[8,128]{1,0:T(8,128)S(1)}) custom-call(bf16[2048,6144]{1,0:T(8,128)(2,1)} %weight_hbm.5, bf16[1040,128]{1,0:T(8,128)(2,1)S(1)} %chain.4.rest_0_), custom_call_target="tpu_custom_call" | custom-call | flops 1 | bytes 1 | tf_op jit(solution)/shard_map/load_weight/pallas_call | solution.py:476
  17.1 3.2 %collective-permute-done.3.got_ref.rest_0_ = bf16[1040,128]{1,0:T(8,128)(2,1)S(1)} collective-permute-done((bf16[1040,128]{1,0:T(8,128)(2,1)S(1)}, bf16[1040,128]{1,0:T(8,128)(2,1)S(1)}, u32[]{:S(2)}, u32[]{:S(2)}) %collective-permute-start.3) | collective-permute-done | bytes 266272 | tf_op jit(solution)/shard_map/ppermute | solution.py:513
  20.3 0.7 chain.6
  21.1 0.1 collective-permute-start.4
  21.1 0.0 collective-permute-done.1.got_ref.rest_1_
  21.1 0.7 chain.5.rest_0_
  21.9 3.2 %collective-permute-start.2 = (bf16[1040,128]{1,0:T(8,128)(2,1)S(1)}, bf16[1040,128]{1,0:T(8,128)(2,1)S(1)}, u32[]{:S(2)}, u32[]{:S(2)}) collective-permute-start(bf16[1040,128]{1,0:T(8,128)(2,1)S(1)} %chain.5.rest_0_), channel_id=1, source_target_pairs={{0,8},{1,9},{8,0},{9,1},{16,24},{17,25},{24,16},{25,17},{2,10},{3,... | collective-permute-start | bytes 798728 | tf_op jit(solution)/shard_map/ppermute | solution.py:513
  25.1 3.8 %load_weight.3 = (bf16[256,6144]{1,0:T(8,128)(2,1)S(1)}, bf16[256,6144]{1,0:T(8,128)(2,1)S(1)}, bf16[256,6144]{1,0:T(8,128)(2,1)S(1)}, f32[8,128]{1,0:T(8,128)S(1)}) custom-call(bf16[2048,6144]{1,0:T(8,128)(2,1)} %weight_hbm.5, bf16[1040,128]{1,0:T(8,128)(2,1)S(1)} %chain.5.rest_0_), custom_call_target="tpu_custom_call" | custom-call | flops 1 | bytes 1 | tf_op jit(solution)/shard_map/load_weight/pallas_call | solution.py:476
  28.9 0.0 collective-permute-done.4.got_ref.rest_1_
  28.9 0.7 chain.7
  29.6 0.7 collective-permute-start.5
  30.3 0.8 %collective-permute-done.2.rest_2_ = bf16[1040,128]{1,0:T(8,128)(2,1)S(1)} collective-permute-done((bf16[1040,128]{1,0:T(8,128)(2,1)S(1)}, bf16[1040,128]{1,0:T(8,128)(2,1)S(1)}, u32[]{:S(2)}, u32[]{:S(2)}) %collective-permute-start.2) | collective-permute-done | bytes 266272 | tf_op jit(solution)/shard_map/ppermute | solution.py:513
  31.0 1.6 %hidden.2.rest_3_.rest_0_ = bf16[256,1024]{1,0:T(8,128)(2,1)S(1)} custom-call(s32[3]{0:T(128)S(1)} %pad_add_fusion.place_ref, bf16[1,256,2048]{2,1,0:T(8,128)(2,1)S(1)} %get-tuple-element.43.q_ref, f32[256,16]{1,0:T(8,128)S(1)} %get-tuple-element.41.col_ref, f32[256,2048]{1,0:T(8,128)S(1)} %get-tuple-element.44.local_ref, ...), custom_call_target="tpu_custom_call" | custom-call | flops 67108864 | bytes 5242880 | tf_op jit(solution)/shard_map/hidden/pallas_call | solution.py:521
  32.7 0.7 %final_state.2.rest_3_.rest_0_ = f32[8,128,128]{2,1,0:T(8,128)S(1)} custom-call(s32[3]{0:T(128)S(1)} %pad_add_fusion.place_ref, f32[8,128,128]{2,1,0:T(8,128)S(1)} %get-tuple-element.46.own_ref, f32[1,128]{1,0:T(1,128)S(1)} %get-tuple-element.47.log_ref, bf16[1040,128]{1,0:T(8,128)(2,1)S(1)} %collective-permute-done.got_ref.rest_0_, ...), custom_call_target="tpu_custom_call" | custom-call | flops 524288 | bytes 1048576 | tf_op jit(solution)/shard_map/final_state/pallas_call | solution.py:532
  33.4 1.7 %project.9 = (f32[256,640]{1,0:T(8,128)S(1)}, f32[256,896]{1,0:T(8,128)S(1)}) custom-call(s32[3]{0:T(128)S(1)} %pad_add_fusion.place_ref, bf16[256,1024]{1,0:T(8,128)(2,1)S(1)} %hidden.2.rest_3_.rest_0_, bf16[256,6144]{1,0:T(8,128)(2,1)S(1)} %get-tuple-element.53.rest_2_.rest_1_.rest_0_, bf16[256,6144]{1,0:T(8,128)(2,1)S(1)} %get-tuple-element.54.rest_3_.rest_2_.rest_1_, ...), custom_call_target="tpu_custom_call" | custom-call | flops 805306368 | bytes 3145728 | tf_op jit(solution)/shard_map/project/pallas_call | solution.py:586
  35.1 1.3 %collective-permute-done.5.rest_2_ = bf16[1040,128]{1,0:T(8,128)(2,1)S(1)} collective-permute-done((bf16[1040,128]{1,0:T(8,128)(2,1)S(1)}, bf16[1040,128]{1,0:T(8,128)(2,1)S(1)}, u32[]{:S(2)}, u32[]{:S(2)}) %collective-permute-start.5) | collective-permute-done | bytes 266272 | tf_op jit(solution)/shard_map/ppermute | solution.py:513
  36.4 1.6 %hidden.3.rest_1_.rest_0_ = bf16[256,1024]{1,0:T(8,128)(2,1)S(1)} custom-call(s32[3]{0:T(128)S(1)} %pad_add_fusion.place_ref, bf16[1,256,2048]{2,1,0:T(8,128)(2,1)S(1)} %get-tuple-element.43.q_ref, f32[256,16]{1,0:T(8,128)S(1)} %get-tuple-element.41.col_ref, f32[256,2048]{1,0:T(8,128)S(1)} %get-tuple-element.44.local_ref, ...), custom_call_target="tpu_custom_call" | custom-call | flops 67108864 | bytes 5242880 | tf_op jit(solution)/shard_map/hidden/pallas_call | solution.py:521
  38.1 1.7 %project.10 = (bf16[256,640]{1,0:T(8,128)(2,1)S(1)}, bf16[256,896]{1,0:T(8,128)(2,1)S(1)}) custom-call(s32[3]{0:T(128)S(1)} %pad_add_fusion.place_ref, bf16[256,1024]{1,0:T(8,128)(2,1)S(1)} %hidden.3.rest_1_.rest_0_, f32[256,640]{1,0:T(8,128)S(1)} %get-tuple-element.64.rest_1_, f32[256,896]{1,0:T(8,128)S(1)} %get-tuple-element.65.rest_2_, ...), custom_call_target="tpu_custom_call" | custom-call | flops 805306368 | bytes 3145728 | tf_op jit(solution)/shard_map/project/pallas_call | solution.py:586
  39.8 1.6 %collective-permute-start.9 = (bf16[256,896]{1,0:T(8,128)(2,1)S(1)}, bf16[256,896]{1,0:T(8,128)(2,1)S(1)}, u32[]{:S(2)}, u32[]{:S(2)}) collective-permute-start(bf16[256,896]{1,0:T(8,128)(2,1)S(1)} %get-tuple-element.68.rest_3_), channel_id=1, source_target_pairs={{0,4},{2,6},{4,0},{6,2},{1,5},{3,7},{5,1},{7,3},{8,12},{10,14},{12... | collective-permute-start | bytes 1376264 | tf_op jit(solution)/shard_map/ppermute | solution.py:380
  41.3 0.9 %final_state.3.rest_1_ = f32[8,128,128]{2,1,0:T(8,128)S(1)} custom-call(s32[3]{0:T(128)S(1)} %pad_add_fusion.place_ref, f32[8,128,128]{2,1,0:T(8,128)S(1)} %get-tuple-element.50.own_ref, f32[1,128]{1,0:T(1,128)S(1)} %get-tuple-element.47.log_ref, bf16[1040,128]{1,0:T(8,128)(2,1)S(1)} %collective-permute-done.3.got_ref.rest_0_, ...), custom_call_target="tpu_custom_call" | custom-call | flops 524288 | bytes 1048576 | tf_op jit(solution)/shard_map/final_state/pallas_call | solution.py:532
  42.3 0.1 collective-permute-start.13
  42.4 1.6 %collective-permute-start.7 = (bf16[256,640]{1,0:T(8,128)(2,1)S(1)}, bf16[256,640]{1,0:T(8,128)(2,1)S(1)}, u32[]{:S(2)}, u32[]{:S(2)}) collective-permute-start(bf16[256,640]{1,0:T(8,128)(2,1)S(1)} %get-tuple-element.66), channel_id=1, source_target_pairs={{0,2},{2,0},{4,6},{6,4},{1,3},{3,1},{5,7},{7,5},{8,10},{10,8},{12,... | collective-permute-start | bytes 983048 | tf_op jit(solution)/shard_map/ppermute | solution.py:380
  43.9 0.2 collective-permute-start.12
  44.1 1.8 %project.11 = bf16[256,896]{1,0:T(8,128)(2,1)S(1)} custom-call(s32[3]{0:T(128)S(1)} %pad_add_fusion.place_ref, bf16[256,1024]{1,0:T(8,128)(2,1)S(1)} %hidden.2.rest_3_.rest_0_, bf16[256,1024]{1,0:T(8,128)(2,1)S(1)} %hidden.3.rest_1_.rest_0_, bf16[256,6144]{1,0:T(8,128)(2,1)S(1)} %get-tuple-element.53.rest_2_.rest_1_.rest_0_, ...), custom_call_target="tpu_custom_call" | custom-call | flops 939524096 | bytes 3670016 | tf_op jit(solution)/shard_map/project/pallas_call | solution.py:586
  45.9 0.6 collective-permute-start.11
  46.5 1.5 %project.7 = bf16[256,640]{1,0:T(8,128)(2,1)S(1)} custom-call(s32[3]{0:T(128)S(1)} %pad_add_fusion.place_ref, bf16[256,1024]{1,0:T(8,128)(2,1)S(1)} %hidden.2.rest_3_.rest_0_, bf16[256,1024]{1,0:T(8,128)(2,1)S(1)} %hidden.3.rest_1_.rest_0_, bf16[256,6144]{1,0:T(8,128)(2,1)S(1)} %get-tuple-element.53.rest_2_.rest_1_.rest_0_, ...), custom_call_target="tpu_custom_call" | custom-call | flops 671088640 | bytes 2621440 | tf_op jit(solution)/shard_map/project/pallas_call | solution.py:586
  48.0 2.6 %collective-permute-done.9.got_ref = bf16[256,896]{1,0:T(8,128)(2,1)S(1)} collective-permute-done((bf16[256,896]{1,0:T(8,128)(2,1)S(1)}, bf16[256,896]{1,0:T(8,128)(2,1)S(1)}, u32[]{:S(2)}, u32[]{:S(2)}) %collective-permute-start.9) | collective-permute-done | bytes 458784 | tf_op jit(solution)/shard_map/ppermute | solution.py:380
  50.7 2.5 %collective-permute-start.6 = (bf16[256,640]{1,0:T(8,128)(2,1)S(1)}, bf16[256,640]{1,0:T(8,128)(2,1)S(1)}, u32[]{:S(2)}, u32[]{:S(2)}) collective-permute-start(bf16[256,640]{1,0:T(8,128)(2,1)S(1)} %project.7), channel_id=1, source_target_pairs={{0,2},{2,0},{4,6},{6,4},{1,3},{3,1},{5,7},{7,5},{8,10},{10,8},{12,... | collective-permute-start | bytes 983048 | tf_op jit(solution)/shard_map/ppermute | solution.py:380
  53.1 2.6 %project.8 = (f32[256,640]{1,0:T(8,128)S(1)}, f32[256,896]{1,0:T(8,128)S(1)}) custom-call(s32[3]{0:T(128)S(1)} %pad_add_fusion.place_ref, bf16[256,1024]{1,0:T(8,128)(2,1)S(1)} %hidden.2.rest_3_.rest_0_, bf16[256,1024]{1,0:T(8,128)(2,1)S(1)} %hidden.3.rest_1_.rest_0_, bf16[256,6144]{1,0:T(8,128)(2,1)S(1)} %get-tuple-element.53.rest_2_.rest_1_.rest_0_, ...), custom_call_target="tpu_custom_call" | custom-call | flops 1610612736 | bytes 6291456 | tf_op jit(solution)/shard_map/project/pallas_call | solution.py:586
  55.8 0.0 copy-start
  55.8 0.0 copy-start.1
  55.8 0.1 relay.3.rest_5_
  55.9 0.0 collective-permute-done.7.got_ref
  55.9 0.1 collective-permute-start.10
  56.0 0.1 relay.2.rest_4_
  56.0 0.0 collective-permute-done.13.rest_3_
  56.0 2.5 %collective-permute-start.8 = (bf16[256,640]{1,0:T(8,128)(2,1)S(1)}, bf16[256,640]{1,0:T(8,128)(2,1)S(1)}, u32[]{:S(2)}, u32[]{:S(2)}) collective-permute-start(bf16[256,640]{1,0:T(8,128)(2,1)S(1)} %relay.2.rest_4_), channel_id=1, source_target_pairs={{0,4},{2,6},{4,0},{6,2},{1,5},{3,7},{5,1},{7,3},{8,12},{10,14},{12... | collective-permute-start | bytes 983048 | tf_op jit(solution)/shard_map/ppermute | solution.py:380
  58.6 0.0 collective-permute-done.12.rest_2_
  58.6 0.0 copy-done
  58.6 0.0 copy-done.1
  58.6 1.7 %decode_rows.1.rows_ref = bf16[16,2048]{1,0:T(8,128)(2,1)S(1)} custom-call(s32[3]{0:T(128)S(1)} %pad_add_fusion.place_ref, s32[4]{0:T(128)S(1)} %copy-done.1, bf16[4,2,2048]{2,1,0:T(2,128)(2,1)S(1)} %get-tuple-element.69.q_ref, bf16[4,2,2048]{2,1,0:T(2,128)(2,1)S(1)} %get-tuple-element.70.k_ref, bf16[4,2,2048]{2,1,0:T(2,128)(2,1)S(1)} %get-tuple-element.71.v_ref, ...), custom_call_target="tpu_custom_call" | custom-call | flops 33554432 | bytes 262144 | tf_op jit(solution)/shard_map/decode_rows/pallas_call | solution.py:549
  60.3 3.9 %decode_project.1 = (f32[8,1536]{1,0:T(8,128)S(1)}, bf16[8,1536]{1,0:T(8,128)(2,1)S(1)}, bf16[8,1536]{1,0:T(8,128)(2,1)S(1)}, bf16[8,1536]{1,0:T(8,128)(2,1)S(1)}) custom-call(s32[3]{0:T(128)S(1)} %pad_add_fusion.place_ref, bf16[16,2048]{1,0:T(8,128)(2,1)S(1)} %decode_rows.1.rows_ref, bf16[256,6144]{1,0:T(8,128)(2,1)S(1)} %get-tuple-element.53.rest_2_.rest_1_.rest_0_, ...), custom_call_target="tpu_custom_call" | custom-call | flops 402653184 | bytes 1572864 | tf_op jit(solution)/shard_map/decode_project/pallas_call | solution.py:625
  64.2 2.0 %collective-permute-start.14 = (bf16[8,1536]{1,0:T(8,128)(2,1)S(1)}, bf16[8,1536]{1,0:T(8,128)(2,1)S(1)}, u32[]{:S(2)}, u32[]{:S(2)}) collective-permute-start(bf16[8,1536]{1,0:T(8,128)(2,1)S(1)} %get-tuple-element.73), channel_id=1, source_target_pairs={{0,2},{2,0},{4,6},{6,4},{1,3},{3,1},{5,7},{7,5},{8,10},{10,8},{12,... | collective-permute-start | bytes 73736 | tf_op jit(solution)/shard_map/ppermute | solution.py:380
  66.3 0.0 collective-permute-done.6.ax
  66.3 0.0 collective-permute-start.15
  66.3 0.0 collective-permute-done.11.by
  66.3 1.5 %collective-permute-start.16 = (bf16[8,1536]{1,0:T(8,128)(2,1)S(1)}, bf16[8,1536]{1,0:T(8,128)(2,1)S(1)}, u32[]{:S(2)}, u32[]{:S(2)}) collective-permute-start(bf16[8,1536]{1,0:T(8,128)(2,1)S(1)} %get-tuple-element.75), channel_id=1, source_target_pairs={{0,6},{2,4},{4,2},{6,0},{1,7},{3,5},{5,3},{7,1},{8,14},{10,12},{12... | collective-permute-start | bytes 73736 | tf_op jit(solution)/shard_map/ppermute | solution.py:380
  67.8 2.6 %project.6 = (f32[256,640]{1,0:T(8,128)S(1)}, f32[256,896]{1,0:T(8,128)S(1)}) custom-call(s32[3]{0:T(128)S(1)} %pad_add_fusion.place_ref, bf16[256,1024]{1,0:T(8,128)(2,1)S(1)} %hidden.2.rest_3_.rest_0_, bf16[256,1024]{1,0:T(8,128)(2,1)S(1)} %hidden.3.rest_1_.rest_0_, bf16[256,6144]{1,0:T(8,128)(2,1)S(1)} %get-tuple-element.53.rest_2_.rest_1_.rest_0_, ...), custom_call_target="tpu_custom_call" | custom-call | flops 1610612736 | bytes 6291456 | tf_op jit(solution)/shard_map/project/pallas_call | solution.py:586
  70.4 0.0 collective-permute-done.14.d_x
  70.4 0.0 collective-permute-done.15.d_y
  70.5 0.6 collective-permute-done.16.d_far
  71.1 0.0 collective-permute-done.8.ay
  71.1 0.0 collective-permute-done.10.bx
  71.1 1.6 %finish.1 = (bf16[1,256,1536]{2,1,0:T(8,128)(2,1)}, bf16[4,2,1536]{2,1,0:T(2,128)(2,1)}) custom-call(f32[256,640]{1,0:T(8,128)S(1)} %get-tuple-element.61.own_a, f32[256,896]{1,0:T(8,128)S(1)} %get-tuple-element.62.own_b, bf16[256,640]{1,0:T(8,128)(2,1)S(1)} %collective-permute-done.6.ax, bf16[256,640]{1,0:T(8,128)(2,1)S(1)} %collective-permute-done.8.ay, ...), custom_call_target="tpu_custom_call" | custom-call | flops 1179648 | bytes 3932160 | tf_op jit(solution)/shard_map/finish/pallas_call | solution.py:633
Async XLA Ops:
  4.0 9.5 %collective-permute-start = (bf16[1040,128]{1,0:T(8,128)(2,1)S(1)}, bf16[1040,128]{1,0:T(8,128)(2,1)S(1)}, u32[]{:S(2)}, u32[]{:S(2)}) collective-permute-start(bf16[1040,128]{1,0:T(8,128)(2,1)S(1)} %get-tuple-element.45), channel_id=1, source_target_pairs={{0,8},{1,9},{8,0},{9,1},{16,24},{17,25},{24,16},{25,17},{2,10},{3,... | collective-permute-start | bytes 798728 | tf_op jit(solution)/shard_map/ppermute | solution.py:513
  12.4 7.9 %collective-permute-start.3 = (bf16[1040,128]{1,0:T(8,128)(2,1)S(1)}, bf16[1040,128]{1,0:T(8,128)(2,1)S(1)}, u32[]{:S(2)}, u32[]{:S(2)}) collective-permute-start(bf16[1040,128]{1,0:T(8,128)(2,1)S(1)} %get-tuple-element.49.rest_0_), channel_id=1, source_target_pairs={{0,8},{1,9},{8,0},{9,1},{16,24},{17,25},{24,16},{25,17},{2,10},{3,... | collective-permute-start | bytes 798728 | tf_op jit(solution)/shard_map/ppermute | solution.py:513
  14.2 7.0 %collective-permute-start.1 = (bf16[1040,128]{1,0:T(8,128)(2,1)S(1)}, bf16[1040,128]{1,0:T(8,128)(2,1)S(1)}, u32[]{:S(2)}, u32[]{:S(2)}) collective-permute-start(bf16[1040,128]{1,0:T(8,128)(2,1)S(1)} %chain.4.rest_0_), channel_id=1, source_target_pairs={{0,1},{1,0},{8,16},{9,17},{16,8},{17,9},{24,25},{25,24},{2,3},{3,2... | collective-permute-start | bytes 798728 | tf_op jit(solution)/shard_map/ppermute | solution.py:513
  21.1 7.8 %collective-permute-start.4 = (bf16[1040,128]{1,0:T(8,128)(2,1)S(1)}, bf16[1040,128]{1,0:T(8,128)(2,1)S(1)}, u32[]{:S(2)}, u32[]{:S(2)}) collective-permute-start(bf16[1040,128]{1,0:T(8,128)(2,1)S(1)} %chain.6), channel_id=1, source_target_pairs={{0,1},{1,0},{8,16},{9,17},{16,8},{17,9},{24,25},{25,24},{2,3},{3,2... | collective-permute-start | bytes 798728 | tf_op jit(solution)/shard_map/ppermute | solution.py:513
  21.9 9.2 %collective-permute-start.2 = (bf16[1040,128]{1,0:T(8,128)(2,1)S(1)}, bf16[1040,128]{1,0:T(8,128)(2,1)S(1)}, u32[]{:S(2)}, u32[]{:S(2)}) collective-permute-start(bf16[1040,128]{1,0:T(8,128)(2,1)S(1)} %chain.5.rest_0_), channel_id=1, source_target_pairs={{0,8},{1,9},{8,0},{9,1},{16,24},{17,25},{24,16},{25,17},{2,10},{3,... | collective-permute-start | bytes 798728 | tf_op jit(solution)/shard_map/ppermute | solution.py:513
  29.6 6.8 %collective-permute-start.5 = (bf16[1040,128]{1,0:T(8,128)(2,1)S(1)}, bf16[1040,128]{1,0:T(8,128)(2,1)S(1)}, u32[]{:S(2)}, u32[]{:S(2)}) collective-permute-start(bf16[1040,128]{1,0:T(8,128)(2,1)S(1)} %chain.7), channel_id=1, source_target_pairs={{0,8},{1,9},{8,0},{9,1},{16,24},{17,25},{24,16},{25,17},{2,10},{3,... | collective-permute-start | bytes 798728 | tf_op jit(solution)/shard_map/ppermute | solution.py:513
  39.8 10.9 %collective-permute-start.9 = (bf16[256,896]{1,0:T(8,128)(2,1)S(1)}, bf16[256,896]{1,0:T(8,128)(2,1)S(1)}, u32[]{:S(2)}, u32[]{:S(2)}) collective-permute-start(bf16[256,896]{1,0:T(8,128)(2,1)S(1)} %get-tuple-element.68.rest_3_), channel_id=1, source_target_pairs={{0,4},{2,6},{4,0},{6,2},{1,5},{3,7},{5,1},{7,3},{8,12},{10,14},{12... | collective-permute-start | bytes 1376264 | tf_op jit(solution)/shard_map/ppermute | solution.py:380
  42.3 13.8 %collective-permute-start.13 = (f32[8,128,128]{2,1,0:T(8,128)S(1)}, f32[8,128,128]{2,1,0:T(8,128)S(1)}, u32[]{:S(2)}, u32[]{:S(2)}) collective-permute-start(f32[8,128,128]{2,1,0:T(8,128)S(1)} %final_state.3.rest_1_), channel_id=1, source_target_pairs={{0,1},{1,0},{2,3},{3,2},{4,5},{5,4},{6,7},{7,6},{8,9},{9,8},{10,11... | collective-permute-start | bytes 1572872 | tf_op jit(solution)/shard_map/ppermute | solution.py:380
  42.4 13.5 %collective-permute-start.7 = (bf16[256,640]{1,0:T(8,128)(2,1)S(1)}, bf16[256,640]{1,0:T(8,128)(2,1)S(1)}, u32[]{:S(2)}, u32[]{:S(2)}) collective-permute-start(bf16[256,640]{1,0:T(8,128)(2,1)S(1)} %get-tuple-element.66), channel_id=1, source_target_pairs={{0,2},{2,0},{4,6},{6,4},{1,3},{3,1},{5,7},{7,5},{8,10},{10,8},{12,... | collective-permute-start | bytes 983048 | tf_op jit(solution)/shard_map/ppermute | solution.py:380
  43.9 14.7 %collective-permute-start.12 = (f32[8,128,128]{2,1,0:T(8,128)S(1)}, f32[8,128,128]{2,1,0:T(8,128)S(1)}, u32[]{:S(2)}, u32[]{:S(2)}) collective-permute-start(f32[8,128,128]{2,1,0:T(8,128)S(1)} %final_state.2.rest_3_.rest_0_), channel_id=1, source_target_pairs={{0,1},{1,0},{2,3},{3,2},{4,5},{5,4},{6,7},{7,6},{8,9},{9,8},{10,11... | collective-permute-start | bytes 1572872 | tf_op jit(solution)/shard_map/ppermute | solution.py:380
  45.9 20.4 %collective-permute-start.11 = (bf16[256,896]{1,0:T(8,128)(2,1)S(1)}, bf16[256,896]{1,0:T(8,128)(2,1)S(1)}, u32[]{:S(2)}, u32[]{:S(2)}) collective-permute-start(bf16[256,896]{1,0:T(8,128)(2,1)S(1)} %project.11), channel_id=1, source_target_pairs={{0,4},{2,6},{4,0},{6,2},{1,5},{3,7},{5,1},{7,3},{8,12},{10,14},{12... | collective-permute-start | bytes 1376264 | tf_op jit(solution)/shard_map/ppermute | solution.py:380
  50.7 15.6 %collective-permute-start.6 = (bf16[256,640]{1,0:T(8,128)(2,1)S(1)}, bf16[256,640]{1,0:T(8,128)(2,1)S(1)}, u32[]{:S(2)}, u32[]{:S(2)}) collective-permute-start(bf16[256,640]{1,0:T(8,128)(2,1)S(1)} %project.7), channel_id=1, source_target_pairs={{0,2},{2,0},{4,6},{6,4},{1,3},{3,1},{5,7},{7,5},{8,10},{10,8},{12,... | collective-permute-start | bytes 983048 | tf_op jit(solution)/shard_map/ppermute | solution.py:380
  55.8 2.8 %copy-start = (f32[4,16,2]{1,2,0:T(2,128)S(1)}, f32[4,16,2]{1,2,0:T(2,128)}, u32[]{:S(2)}) copy-start(f32[4,16,2]{1,2,0:T(2,128)} %param.18) | copy-start | bytes 1540
  55.8 2.8 %copy-start.1 = (s32[4]{0:T(128)S(1)}, s32[4]{0:T(128)}, u32[]{:S(2)}) copy-start(s32[4]{0:T(128)} %prompt_ref.1) | copy-start | bytes 52
  55.9 15.2 %collective-permute-start.10 = (bf16[256,896]{1,0:T(8,128)(2,1)S(1)}, bf16[256,896]{1,0:T(8,128)(2,1)S(1)}, u32[]{:S(2)}, u32[]{:S(2)}) collective-permute-start(bf16[256,896]{1,0:T(8,128)(2,1)S(1)} %relay.3.rest_5_), channel_id=1, source_target_pairs={{0,2},{2,0},{4,6},{6,4},{1,3},{3,1},{5,7},{7,5},{8,10},{10,8},{12,... | collective-permute-start | bytes 1376264 | tf_op jit(solution)/shard_map/ppermute | solution.py:380
  56.0 15.0 %collective-permute-start.8 = (bf16[256,640]{1,0:T(8,128)(2,1)S(1)}, bf16[256,640]{1,0:T(8,128)(2,1)S(1)}, u32[]{:S(2)}, u32[]{:S(2)}) collective-permute-start(bf16[256,640]{1,0:T(8,128)(2,1)S(1)} %relay.2.rest_4_), channel_id=1, source_target_pairs={{0,4},{2,6},{4,0},{6,2},{1,5},{3,7},{5,1},{7,3},{8,12},{10,14},{12... | collective-permute-start | bytes 983048 | tf_op jit(solution)/shard_map/ppermute | solution.py:380
  64.2 6.2 %collective-permute-start.14 = (bf16[8,1536]{1,0:T(8,128)(2,1)S(1)}, bf16[8,1536]{1,0:T(8,128)(2,1)S(1)}, u32[]{:S(2)}, u32[]{:S(2)}) collective-permute-start(bf16[8,1536]{1,0:T(8,128)(2,1)S(1)} %get-tuple-element.73), channel_id=1, source_target_pairs={{0,2},{2,0},{4,6},{6,4},{1,3},{3,1},{5,7},{7,5},{8,10},{10,8},{12,... | collective-permute-start | bytes 73736 | tf_op jit(solution)/shard_map/ppermute | solution.py:380
  66.3 4.2 %collective-permute-start.15 = (bf16[8,1536]{1,0:T(8,128)(2,1)S(1)}, bf16[8,1536]{1,0:T(8,128)(2,1)S(1)}, u32[]{:S(2)}, u32[]{:S(2)}) collective-permute-start(bf16[8,1536]{1,0:T(8,128)(2,1)S(1)} %get-tuple-element.74), channel_id=1, source_target_pairs={{0,4},{2,6},{4,0},{6,2},{1,5},{3,7},{5,1},{7,3},{8,12},{10,14},{12... | collective-permute-start | bytes 73736 | tf_op jit(solution)/shard_map/ppermute | solution.py:380
  66.3 4.8 %collective-permute-start.16 = (bf16[8,1536]{1,0:T(8,128)(2,1)S(1)}, bf16[8,1536]{1,0:T(8,128)(2,1)S(1)}, u32[]{:S(2)}, u32[]{:S(2)}) collective-permute-start(bf16[8,1536]{1,0:T(8,128)(2,1)S(1)} %get-tuple-element.75), channel_id=1, source_target_pairs={{0,6},{2,4},{4,2},{6,0},{1,7},{3,5},{5,3},{7,1},{8,14},{10,12},{12... | collective-permute-start | bytes 73736 | tf_op jit(solution)/shard_map/ppermute | solution.py:380

commit v12 on v11

--- a/solution.py
+++ b/solution.py
@@ -579,6 +579,7 @@
     side_x, side_y = (0, split), (split, width - split)
 
     def project(pieces, dtype, inputs=None, parts_used=None, addends=()):
+        dtypes = dtype if isinstance(dtype, tuple) else (dtype,) * len(pieces)
         inputs = hidden if inputs is None else inputs
         used = weights if parts_used is None else weights[parts_used]
         moved = sum(columns for _, _, columns in pieces)
@@ -587,7 +588,7 @@
             functools.partial(project_kernel, pieces, width, len(inputs), len(addends)),
             "project",
             [SMEM] + [VMEM] * (len(inputs) + len(addends) + len(used)),
-            [sds((length, columns), dtype) for _, _, columns in pieces],
+            [sds((length, columns), kind) for (_, _, columns), kind in zip(pieces, dtypes)],
             (),
             cost(2 * length * depth * moved, depth * moved * 2),
         )(place, *inputs, *addends, *used)
@@ -612,10 +613,10 @@
         to_x, to_y = project(far, BF16)
     far_a = swap(to_x, "head", parts, 1)
     far_b = swap(to_y, "head", parts, 2)
-    x_a = swap(project([(1, *side_x)], BF16)[0], "head", parts, 1)
+    near_x, own_a, own_b = project([(1, *side_x), (0, *side_x), (0, *side_y)], (BF16, F32, F32))
+    x_a = swap(near_x, "head", parts, 1)
     y_b = swap(project([(2, *side_y)], BF16)[0], "head", parts, 2)
     pass_a, pass_b = project([(2, *side_x), (1, *side_y)], F32)
-    own_a, own_b = project([(0, *side_x), (0, *side_y)], F32)
     sent_a, sent_b = relay(pass_a, far_a), relay(pass_b, far_b)
     y_a = swap(sent_a, "head", parts, 2)
     x_b = swap(sent_b, "head", parts, 1)

time: 73.1 us -> 77.4 us (1.059)
  waiting for transfers between devices: 9.56 us -> 14.8 us
    ppermute x11, waiting for transfers between devices: 3.28 us -> 8.58 us  [swap(): return lax.ppermute(array, axis, [(i, i ^ bit) for i in range(size)])]
    pallas_call x6 -> x5, Pallas kernels: 12 us -> 11.3 us  [project(): call(functools.partial(project_kernel, pieces, width, len(inputs), len(ad...]
  transfers between devices with their start and end apart: 17 -> 17, of which waited for: 6 -> 8; matrix products, arithmetic and copies ran while one was open for 0% -> 0% of each run, Pallas kernels for 47% -> 44%
where the time goes in v12:
time: 77.4 us; the launch traced here: 77.1 us
  Pallas kernels  41.7 us (54%)
  starting transfers between devices  19.5 us (25%)
  waiting for transfers between devices  14.8 us (19%)
  between operations  1.01 us (1%)
    ppermute x11, starting transfers between devices, swap(): return lax.ppermute(array, axis, [(i, i ^ bit) for i in range(size)])  12.3 us
    pallas_call x5, Pallas kernels, project(): call(functools.partial(project_kernel, pieces, width, len(inputs), len(ad...  11.3 us
    ppermute x11, waiting for transfers between devices, swap(): return lax.ppermute(array, axis, [(i, i ^ bit) for i in range(size)])  8.58 us
    ppermute x6, starting transfers between devices, body(): lax.ppermute(value, ('ctx', 'rep'), pairs)  7.17 us
    pallas_call x2, Pallas kernels, load_weight(): call(functools.partial(load_kernel, places), 'load_weight', [HBM] + [ANY]...  6.65 us
    ppermute x6, waiting for transfers between devices, body(): lax.ppermute(value, ('ctx', 'rep'), pairs)  6.27 us
    pallas_call x1, Pallas kernels, body(): call(functools.partial(local_kernel, len(arrays)), 'local_attention', [VM...  4.17 us
    pallas_call x1, Pallas kernels, body(): call(decode_project_kernel, 'decode_project', [SMEM] + [VMEM] * (1 + WEIG...  3.91 us
  transfers between devices with their start and end apart: 17, of which 8 were waited for; matrix products, arithmetic and copies ran while one was open for 0% of the time, Pallas kernels for 44%

profile of v12, /device:TPU:0, one launch (start us, length us, event | category | flops | bytes accessed | tf_op | source)
XLA Modules:
  0.0 77.1 jit_solution(4280012972784349917)
XLA Ops:
  0.6 0.1 pad_add_fusion.place_ref
  0.7 3.2 %own_state.1 = (f32[8,128,128]{2,1,0:T(8,128)S(1)}, f32[1,128]{1,0:T(1,128)S(1)}, f32[256,16]{1,0:T(8,128)S(1)}, f32[1,16,256]{2,1,0:T(8,128)S(1)}, bf16[256,204...) custom-call(s32[3]{0:T(128)S(1)} %pad_add_fusion.place_ref, ...), custom_call_target="tpu_custom_call" | custom-call | flops 268435456 | bytes 8388608 | tf_op jit(solution)/shard_map/own_state/pallas_call | solution.py:423
  4.0 3.1 %collective-permute-start = (bf16[1040,128]{1,0:T(8,128)(2,1)S(1)}, bf16[1040,128]{1,0:T(8,128)(2,1)S(1)}, u32[]{:S(2)}, u32[]{:S(2)}) collective-permute-start(bf16[1040,128]{1,0:T(8,128)(2,1)S(1)} %get-tuple-element.46), channel_id=1, source_target_pairs={{0,8},{1,9},{8,0},{9,1},{16,24},{17,25},{24,16},{25,17},{2,10},{3,... | collective-permute-start | bytes 798728 | tf_op jit(solution)/shard_map/ppermute | solution.py:513
  7.0 4.2 %local_attention.1 = (bf16[1,256,2048]{2,1,0:T(8,128)(2,1)S(1)}, bf16[4,2,2048]{2,1,0:T(2,128)(2,1)S(1)}, bf16[4,2,2048]{2,1,0:T(2,128)(2,1)S(1)}, bf16[4,2,2048...) custom-call(bf16[256,2048]{1,0:T(8,128)(2,1)S(1)} %get-tuple-element, ...), custom_call_target="tpu_custom_call" | custom-call | flops 536870912 | bytes 6291456 | tf_op jit(solution)/shard_map/local_attention/pallas_call | solution.py:445
  11.2 1.2 %more_state.1 = (f32[8,128,128]{2,1,0:T(8,128)S(1)}, bf16[1040,128]{1,0:T(8,128)(2,1)S(1)}) custom-call(bf16[256,2048]{1,0:T(8,128)(2,1)S(1)} %get-tuple-element.40.k_ref, bf16[256,2048]{1,0:T(8,128)(2,1)S(1)} %get-tuple-element.41.v_ref, f32[256,16]{1,0:T(8,128)S(1)} %get-tuple-element.42.col_ref, f32[1,128]{1,0:T(1,128)S(1)} %get-tuple-element.48.log_ref, ...), custom_call_target="tpu_custom_call" | custom-call | flops 134217728 | bytes 4194304 | tf_op jit(solution)/shard_map/more_state/pallas_call | solution.py:459
  12.4 0.1 collective-permute-start.3
  12.5 1.0 %collective-permute-done.got_ref.rest_0_ = bf16[1040,128]{1,0:T(8,128)(2,1)S(1)} collective-permute-done((bf16[1040,128]{1,0:T(8,128)(2,1)S(1)}, bf16[1040,128]{1,0:T(8,128)(2,1)S(1)}, u32[]{:S(2)}, u32[]{:S(2)}) %collective-permute-start) | collective-permute-done | bytes 266272 | tf_op jit(solution)/shard_map/ppermute | solution.py:513
  13.4 0.7 chain.4.rest_0_
  14.2 0.1 collective-permute-start.1
  14.2 2.9 %load_weight.2 = (bf16[256,6144]{1,0:T(8,128)(2,1)S(1)}, bf16[256,6144]{1,0:T(8,128)(2,1)S(1)}, f32[8,128]{1,0:T(8,128)S(1)}) custom-call(bf16[2048,6144]{1,0:T(8,128)(2,1)} %weight_hbm.5, bf16[1040,128]{1,0:T(8,128)(2,1)S(1)} %chain.4.rest_0_), custom_call_target="tpu_custom_call" | custom-call | flops 1 | bytes 1 | tf_op jit(solution)/shard_map/load_weight/pallas_call | solution.py:476
  17.1 3.2 %collective-permute-done.3.got_ref.rest_0_ = bf16[1040,128]{1,0:T(8,128)(2,1)S(1)} collective-permute-done((bf16[1040,128]{1,0:T(8,128)(2,1)S(1)}, bf16[1040,128]{1,0:T(8,128)(2,1)S(1)}, u32[]{:S(2)}, u32[]{:S(2)}) %collective-permute-start.3) | collective-permute-done | bytes 266272 | tf_op jit(solution)/shard_map/ppermute | solution.py:513
  20.3 0.7 chain.6
  21.1 0.1 collective-permute-start.4
  21.1 0.0 collective-permute-done.1.got_ref.rest_1_
  21.1 0.7 chain.5.rest_0_
  21.9 3.2 %collective-permute-start.2 = (bf16[1040,128]{1,0:T(8,128)(2,1)S(1)}, bf16[1040,128]{1,0:T(8,128)(2,1)S(1)}, u32[]{:S(2)}, u32[]{:S(2)}) collective-permute-start(bf16[1040,128]{1,0:T(8,128)(2,1)S(1)} %chain.5.rest_0_), channel_id=1, source_target_pairs={{0,8},{1,9},{8,0},{9,1},{16,24},{17,25},{24,16},{25,17},{2,10},{3,... | collective-permute-start | bytes 798728 | tf_op jit(solution)/shard_map/ppermute | solution.py:513
  25.1 3.8 %load_weight.3 = (bf16[256,6144]{1,0:T(8,128)(2,1)S(1)}, bf16[256,6144]{1,0:T(8,128)(2,1)S(1)}, bf16[256,6144]{1,0:T(8,128)(2,1)S(1)}, f32[8,128]{1,0:T(8,128)S(1)}) custom-call(bf16[2048,6144]{1,0:T(8,128)(2,1)} %weight_hbm.5, bf16[1040,128]{1,0:T(8,128)(2,1)S(1)} %chain.5.rest_0_), custom_call_target="tpu_custom_call" | custom-call | flops 1 | bytes 1 | tf_op jit(solution)/shard_map/load_weight/pallas_call | solution.py:476
  28.9 0.0 collective-permute-done.4.got_ref.rest_1_
  28.9 0.7 chain.7
  29.6 0.7 collective-permute-start.5
  30.3 0.8 %collective-permute-done.2.rest_2_ = bf16[1040,128]{1,0:T(8,128)(2,1)S(1)} collective-permute-done((bf16[1040,128]{1,0:T(8,128)(2,1)S(1)}, bf16[1040,128]{1,0:T(8,128)(2,1)S(1)}, u32[]{:S(2)}, u32[]{:S(2)}) %collective-permute-start.2) | collective-permute-done | bytes 266272 | tf_op jit(solution)/shard_map/ppermute | solution.py:513
  31.0 1.6 %hidden.2.rest_3_.rest_0_ = bf16[256,1024]{1,0:T(8,128)(2,1)S(1)} custom-call(s32[3]{0:T(128)S(1)} %pad_add_fusion.place_ref, bf16[1,256,2048]{2,1,0:T(8,128)(2,1)S(1)} %get-tuple-element.44.q_ref, f32[256,16]{1,0:T(8,128)S(1)} %get-tuple-element.42.col_ref, f32[256,2048]{1,0:T(8,128)S(1)} %get-tuple-element.45.local_ref, ...), custom_call_target="tpu_custom_call" | custom-call | flops 67108864 | bytes 5242880 | tf_op jit(solution)/shard_map/hidden/pallas_call | solution.py:521
  32.7 0.7 final_state.2.rest_3_.rest_0_
  33.4 1.7 %project.7 = (f32[256,640]{1,0:T(8,128)S(1)}, f32[256,896]{1,0:T(8,128)S(1)}) custom-call(s32[3]{0:T(128)S(1)} %pad_add_fusion.place_ref, bf16[256,1024]{1,0:T(8,128)(2,1)S(1)} %hidden.2.rest_3_.rest_0_, bf16[256,6144]{1,0:T(8,128)(2,1)S(1)} %get-tuple-element.54.rest_2_.rest_1_.rest_0_, bf16[256,6144]{1,0:T(8,128)(2,1)S(1)} %get-tuple-element.55.rest_3_.rest_2_.rest_1_, ...), custom_call_target="tpu_custom_call" | custom-call | flops 805306368 | bytes 3145728 | tf_op jit(solution)/shard_map/project/pallas_call | solution.py:587
  35.1 1.3 %collective-permute-done.5.rest_2_ = bf16[1040,128]{1,0:T(8,128)(2,1)S(1)} collective-permute-done((bf16[1040,128]{1,0:T(8,128)(2,1)S(1)}, bf16[1040,128]{1,0:T(8,128)(2,1)S(1)}, u32[]{:S(2)}, u32[]{:S(2)}) %collective-permute-start.5) | collective-permute-done | bytes 266272 | tf_op jit(solution)/shard_map/ppermute | solution.py:513
  36.4 1.6 %hidden.3.rest_1_.rest_0_ = bf16[256,1024]{1,0:T(8,128)(2,1)S(1)} custom-call(s32[3]{0:T(128)S(1)} %pad_add_fusion.place_ref, bf16[1,256,2048]{2,1,0:T(8,128)(2,1)S(1)} %get-tuple-element.44.q_ref, f32[256,16]{1,0:T(8,128)S(1)} %get-tuple-element.42.col_ref, f32[256,2048]{1,0:T(8,128)S(1)} %get-tuple-element.45.local_ref, ...), custom_call_target="tpu_custom_call" | custom-call | flops 67108864 | bytes 5242880 | tf_op jit(solution)/shard_map/hidden/pallas_call | solution.py:521
  38.1 1.7 %project.8 = (bf16[256,640]{1,0:T(8,128)(2,1)S(1)}, bf16[256,896]{1,0:T(8,128)(2,1)S(1)}) custom-call(s32[3]{0:T(128)S(1)} %pad_add_fusion.place_ref, bf16[256,1024]{1,0:T(8,128)(2,1)S(1)} %hidden.3.rest_1_.rest_0_, f32[256,640]{1,0:T(8,128)S(1)} %get-tuple-element.66.rest_1_, f32[256,896]{1,0:T(8,128)S(1)} %get-tuple-element.67.rest_2_, ...), custom_call_target="tpu_custom_call" | custom-call | flops 805306368 | bytes 3145728 | tf_op jit(solution)/shard_map/project/pallas_call | solution.py:587
  39.8 1.6 %collective-permute-start.9 = (bf16[256,896]{1,0:T(8,128)(2,1)S(1)}, bf16[256,896]{1,0:T(8,128)(2,1)S(1)}, u32[]{:S(2)}, u32[]{:S(2)}) collective-permute-start(bf16[256,896]{1,0:T(8,128)(2,1)S(1)} %get-tuple-element.70.rest_3_), channel_id=1, source_target_pairs={{0,4},{2,6},{4,0},{6,2},{1,5},{3,7},{5,1},{7,3},{8,12},{10,14},{12... | collective-permute-start | bytes 1376264 | tf_op jit(solution)/shard_map/ppermute | solution.py:380
  41.3 0.9 %final_state.3.rest_1_ = f32[8,128,128]{2,1,0:T(8,128)S(1)} custom-call(s32[3]{0:T(128)S(1)} %pad_add_fusion.place_ref, f32[8,128,128]{2,1,0:T(8,128)S(1)} %get-tuple-element.51.own_ref, f32[1,128]{1,0:T(1,128)S(1)} %get-tuple-element.48.log_ref, bf16[1040,128]{1,0:T(8,128)(2,1)S(1)} %collective-permute-done.3.got_ref.rest_0_, ...), custom_call_target="tpu_custom_call" | custom-call | flops 524288 | bytes 1048576 | tf_op jit(solution)/shard_map/final_state/pallas_call | solution.py:532
  42.3 0.1 collective-permute-start.13
  42.4 1.6 %collective-permute-start.7 = (bf16[256,640]{1,0:T(8,128)(2,1)S(1)}, bf16[256,640]{1,0:T(8,128)(2,1)S(1)}, u32[]{:S(2)}, u32[]{:S(2)}) collective-permute-start(bf16[256,640]{1,0:T(8,128)(2,1)S(1)} %get-tuple-element.68), channel_id=1, source_target_pairs={{0,2},{2,0},{4,6},{6,4},{1,3},{3,1},{5,7},{7,5},{8,10},{10,8},{12,... | collective-permute-start | bytes 983048 | tf_op jit(solution)/shard_map/ppermute | solution.py:380
  43.9 2.6 %project.6 = (f32[256,640]{1,0:T(8,128)S(1)}, f32[256,896]{1,0:T(8,128)S(1)}) custom-call(s32[3]{0:T(128)S(1)} %pad_add_fusion.place_ref, bf16[256,1024]{1,0:T(8,128)(2,1)S(1)} %hidden.2.rest_3_.rest_0_, bf16[256,1024]{1,0:T(8,128)(2,1)S(1)} %hidden.3.rest_1_.rest_0_, bf16[256,6144]{1,0:T(8,128)(2,1)S(1)} %get-tuple-element.54.rest_2_.rest_1_.rest_0_, ...), custom_call_target="tpu_custom_call" | custom-call | flops 1610612736 | bytes 6291456 | tf_op jit(solution)/shard_map/project/pallas_call | solution.py:587
  46.6 0.2 collective-permute-start.12
  46.8 1.8 %project.9 = bf16[256,896]{1,0:T(8,128)(2,1)S(1)} custom-call(s32[3]{0:T(128)S(1)} %pad_add_fusion.place_ref, bf16[256,1024]{1,0:T(8,128)(2,1)S(1)} %hidden.2.rest_3_.rest_0_, bf16[256,1024]{1,0:T(8,128)(2,1)S(1)} %hidden.3.rest_1_.rest_0_, bf16[256,6144]{1,0:T(8,128)(2,1)S(1)} %get-tuple-element.54.rest_2_.rest_1_.rest_0_, ...), custom_call_target="tpu_custom_call" | custom-call | flops 939524096 | bytes 3670016 | tf_op jit(solution)/shard_map/project/pallas_call | solution.py:587
  48.6 0.6 collective-permute-start.11
  49.2 0.6 collective-permute-done.9.got_ref
  49.8 0.1 relay.3.rest_5_
  49.9 0.0 copy-start
  49.9 0.0 copy-start.1
  49.9 1.6 %collective-permute-start.10 = (bf16[256,896]{1,0:T(8,128)(2,1)S(1)}, bf16[256,896]{1,0:T(8,128)(2,1)S(1)}, u32[]{:S(2)}, u32[]{:S(2)}) collective-permute-start(bf16[256,896]{1,0:T(8,128)(2,1)S(1)} %relay.3.rest_5_), channel_id=1, source_target_pairs={{0,2},{2,0},{4,6},{6,4},{1,3},{3,1},{5,7},{7,5},{8,10},{10,8},{12,... | collective-permute-start | bytes 1376264 | tf_op jit(solution)/shard_map/ppermute | solution.py:380
  51.5 3.5 %project.5 = (bf16[256,640]{1,0:T(8,128)(2,1)S(1)}, f32[256,640]{1,0:T(8,128)S(1)}, f32[256,896]{1,0:T(8,128)S(1)}) custom-call(s32[3]{0:T(128)S(1)} %pad_add_fusion.place_ref, bf16[256,1024]{1,0:T(8,128)(2,1)S(1)} %hidden.2.rest_3_.rest_0_, bf16[256,1024]{1,0:T(8,128)(2,1)S(1)} %hidden.3.rest_1_.rest_0_, ...), custom_call_target="tpu_custom_call" | custom-call | flops 2281701376 | bytes 8912896 | tf_op jit(solution)/shard_map/project/pallas_call | solution.py:587
  54.9 0.0 collective-permute-done.7.got_ref
  54.9 0.6 collective-permute-start.6
  55.5 0.1 relay.2.rest_4_
  55.6 0.0 collective-permute-done.13.rest_3_
  55.6 1.6 %collective-permute-start.8 = (bf16[256,640]{1,0:T(8,128)(2,1)S(1)}, bf16[256,640]{1,0:T(8,128)(2,1)S(1)}, u32[]{:S(2)}, u32[]{:S(2)}) collective-permute-start(bf16[256,640]{1,0:T(8,128)(2,1)S(1)} %relay.2.rest_4_), channel_id=1, source_target_pairs={{0,4},{2,6},{4,0},{6,2},{1,5},{3,7},{5,1},{7,3},{8,12},{10,14},{12... | collective-permute-start | bytes 983048 | tf_op jit(solution)/shard_map/ppermute | solution.py:380
  57.2 0.0 collective-permute-done.12.rest_2_
  57.2 0.0 copy-done
  57.2 0.0 copy-done.1
  57.2 1.7 %decode_rows.1.rows_ref = bf16[16,2048]{1,0:T(8,128)(2,1)S(1)} custom-call(s32[3]{0:T(128)S(1)} %pad_add_fusion.place_ref, s32[4]{0:T(128)S(1)} %copy-done.1, bf16[4,2,2048]{2,1,0:T(2,128)(2,1)S(1)} %get-tuple-element.71.q_ref, bf16[4,2,2048]{2,1,0:T(2,128)(2,1)S(1)} %get-tuple-element.72.k_ref, bf16[4,2,2048]{2,1,0:T(2,128)(2,1)S(1)} %get-tuple-element.73.v_ref, ...), custom_call_target="tpu_custom_call" | custom-call | flops 33554432 | bytes 262144 | tf_op jit(solution)/shard_map/decode_rows/pallas_call | solution.py:549
  59.0 3.9 %decode_project.1 = (f32[8,1536]{1,0:T(8,128)S(1)}, bf16[8,1536]{1,0:T(8,128)(2,1)S(1)}, bf16[8,1536]{1,0:T(8,128)(2,1)S(1)}, bf16[8,1536]{1,0:T(8,128)(2,1)S(1)}) custom-call(s32[3]{0:T(128)S(1)} %pad_add_fusion.place_ref, bf16[16,2048]{1,0:T(8,128)(2,1)S(1)} %decode_rows.1.rows_ref, bf16[256,6144]{1,0:T(8,128)(2,1)S(1)} %get-tuple-element.54.rest_2_.rest_1_.rest_0_, ...), custom_call_target="tpu_custom_call" | custom-call | flops 402653184 | bytes 1572864 | tf_op jit(solution)/shard_map/decode_project/pallas_call | solution.py:626
  62.9 1.6 %collective-permute-start.14 = (bf16[8,1536]{1,0:T(8,128)(2,1)S(1)}, bf16[8,1536]{1,0:T(8,128)(2,1)S(1)}, u32[]{:S(2)}, u32[]{:S(2)}) collective-permute-start(bf16[8,1536]{1,0:T(8,128)(2,1)S(1)} %get-tuple-element.75), channel_id=1, source_target_pairs={{0,2},{2,0},{4,6},{6,4},{1,3},{3,1},{5,7},{7,5},{8,10},{10,8},{12,... | collective-permute-start | bytes 73736 | tf_op jit(solution)/shard_map/ppermute | solution.py:380
  64.5 5.1 %collective-permute-done.6.ax = bf16[256,640]{1,0:T(8,128)(2,1)S(1)} collective-permute-done((bf16[256,640]{1,0:T(8,128)(2,1)S(1)}, bf16[256,640]{1,0:T(8,128)(2,1)S(1)}, u32[]{:S(2)}, u32[]{:S(2)}) %collective-permute-start.6) | collective-permute-done | bytes 327712 | tf_op jit(solution)/shard_map/ppermute | solution.py:380
  69.6 1.1 %collective-permute-start.15 = (bf16[8,1536]{1,0:T(8,128)(2,1)S(1)}, bf16[8,1536]{1,0:T(8,128)(2,1)S(1)}, u32[]{:S(2)}, u32[]{:S(2)}) collective-permute-start(bf16[8,1536]{1,0:T(8,128)(2,1)S(1)} %get-tuple-element.76), channel_id=1, source_target_pairs={{0,4},{2,6},{4,0},{6,2},{1,5},{3,7},{5,1},{7,3},{8,12},{10,14},{12... | collective-permute-start | bytes 73736 | tf_op jit(solution)/shard_map/ppermute | solution.py:380
  70.6 0.0 collective-permute-done.11.by
  70.7 1.9 %collective-permute-start.16 = (bf16[8,1536]{1,0:T(8,128)(2,1)S(1)}, bf16[8,1536]{1,0:T(8,128)(2,1)S(1)}, u32[]{:S(2)}, u32[]{:S(2)}) collective-permute-start(bf16[8,1536]{1,0:T(8,128)(2,1)S(1)} %get-tuple-element.77), channel_id=1, source_target_pairs={{0,6},{2,4},{4,2},{6,0},{1,7},{3,5},{5,3},{7,1},{8,14},{10,12},{12... | collective-permute-start | bytes 73736 | tf_op jit(solution)/shard_map/ppermute | solution.py:380
  72.6 0.0 collective-permute-done.14.d_x
  72.6 0.9 %collective-permute-done.15.d_y = bf16[8,1536]{1,0:T(8,128)(2,1)S(1)} collective-permute-done((bf16[8,1536]{1,0:T(8,128)(2,1)S(1)}, bf16[8,1536]{1,0:T(8,128)(2,1)S(1)}, u32[]{:S(2)}, u32[]{:S(2)}) %collective-permute-start.15) | collective-permute-done | bytes 24608 | tf_op jit(solution)/shard_map/ppermute | solution.py:380
  73.4 2.0 %collective-permute-done.16.d_far = bf16[8,1536]{1,0:T(8,128)(2,1)S(1)} collective-permute-done((bf16[8,1536]{1,0:T(8,128)(2,1)S(1)}, bf16[8,1536]{1,0:T(8,128)(2,1)S(1)}, u32[]{:S(2)}, u32[]{:S(2)}) %collective-permute-start.16) | collective-permute-done | bytes 24608 | tf_op jit(solution)/shard_map/ppermute | solution.py:380
  75.4 0.0 collective-permute-done.8.ay
  75.4 0.0 collective-permute-done.10.bx
  75.4 1.6 %finish.1 = (bf16[1,256,1536]{2,1,0:T(8,128)(2,1)}, bf16[4,2,1536]{2,1,0:T(2,128)(2,1)}) custom-call(f32[256,640]{1,0:T(8,128)S(1)} %get-tuple-element.62.own_a, f32[256,896]{1,0:T(8,128)S(1)} %get-tuple-element.63.own_b, bf16[256,640]{1,0:T(8,128)(2,1)S(1)} %collective-permute-done.6.ax, bf16[256,640]{1,0:T(8,128)(2,1)S(1)} %collective-permute-done.8.ay, ...), custom_call_target="tpu_custom_call" | custom-call | flops 1179648 | bytes 3932160 | tf_op jit(solution)/shard_map/finish/pallas_call | solution.py:634
Async XLA Ops:
  4.0 9.5 %collective-permute-start = (bf16[1040,128]{1,0:T(8,128)(2,1)S(1)}, bf16[1040,128]{1,0:T(8,128)(2,1)S(1)}, u32[]{:S(2)}, u32[]{:S(2)}) collective-permute-start(bf16[1040,128]{1,0:T(8,128)(2,1)S(1)} %get-tuple-element.46), channel_id=1, source_target_pairs={{0,8},{1,9},{8,0},{9,1},{16,24},{17,25},{24,16},{25,17},{2,10},{3,... | collective-permute-start | bytes 798728 | tf_op jit(solution)/shard_map/ppermute | solution.py:513
  12.4 7.9 %collective-permute-start.3 = (bf16[1040,128]{1,0:T(8,128)(2,1)S(1)}, bf16[1040,128]{1,0:T(8,128)(2,1)S(1)}, u32[]{:S(2)}, u32[]{:S(2)}) collective-permute-start(bf16[1040,128]{1,0:T(8,128)(2,1)S(1)} %get-tuple-element.50.rest_0_), channel_id=1, source_target_pairs={{0,8},{1,9},{8,0},{9,1},{16,24},{17,25},{24,16},{25,17},{2,10},{3,... | collective-permute-start | bytes 798728 | tf_op jit(solution)/shard_map/ppermute | solution.py:513
  14.2 7.0 %collective-permute-start.1 = (bf16[1040,128]{1,0:T(8,128)(2,1)S(1)}, bf16[1040,128]{1,0:T(8,128)(2,1)S(1)}, u32[]{:S(2)}, u32[]{:S(2)}) collective-permute-start(bf16[1040,128]{1,0:T(8,128)(2,1)S(1)} %chain.4.rest_0_), channel_id=1, source_target_pairs={{0,1},{1,0},{8,16},{9,17},{16,8},{17,9},{24,25},{25,24},{2,3},{3,2... | collective-permute-start | bytes 798728 | tf_op jit(solution)/shard_map/ppermute | solution.py:513
  21.1 7.8 %collective-permute-start.4 = (bf16[1040,128]{1,0:T(8,128)(2,1)S(1)}, bf16[1040,128]{1,0:T(8,128)(2,1)S(1)}, u32[]{:S(2)}, u32[]{:S(2)}) collective-permute-start(bf16[1040,128]{1,0:T(8,128)(2,1)S(1)} %chain.6), channel_id=1, source_target_pairs={{0,1},{1,0},{8,16},{9,17},{16,8},{17,9},{24,25},{25,24},{2,3},{3,2... | collective-permute-start | bytes 798728 | tf_op jit(solution)/shard_map/ppermute | solution.py:513
  21.9 9.2 %collective-permute-start.2 = (bf16[1040,128]{1,0:T(8,128)(2,1)S(1)}, bf16[1040,128]{1,0:T(8,128)(2,1)S(1)}, u32[]{:S(2)}, u32[]{:S(2)}) collective-permute-start(bf16[1040,128]{1,0:T(8,128)(2,1)S(1)} %chain.5.rest_0_), channel_id=1, source_target_pairs={{0,8},{1,9},{8,0},{9,1},{16,24},{17,25},{24,16},{25,17},{2,10},{3,... | collective-permute-start | bytes 798728 | tf_op jit(solution)/shard_map/ppermute | solution.py:513
  29.6 6.8 %collective-permute-start.5 = (bf16[1040,128]{1,0:T(8,128)(2,1)S(1)}, bf16[1040,128]{1,0:T(8,128)(2,1)S(1)}, u32[]{:S(2)}, u32[]{:S(2)}) collective-permute-start(bf16[1040,128]{1,0:T(8,128)(2,1)S(1)} %chain.7), channel_id=1, source_target_pairs={{0,8},{1,9},{8,0},{9,1},{16,24},{17,25},{24,16},{25,17},{2,10},{3,... | collective-permute-start | bytes 798728 | tf_op jit(solution)/shard_map/ppermute | solution.py:513
  39.8 10.0 %collective-permute-start.9 = (bf16[256,896]{1,0:T(8,128)(2,1)S(1)}, bf16[256,896]{1,0:T(8,128)(2,1)S(1)}, u32[]{:S(2)}, u32[]{:S(2)}) collective-permute-start(bf16[256,896]{1,0:T(8,128)(2,1)S(1)} %get-tuple-element.70.rest_3_), channel_id=1, source_target_pairs={{0,4},{2,6},{4,0},{6,2},{1,5},{3,7},{5,1},{7,3},{8,12},{10,14},{12... | collective-permute-start | bytes 1376264 | tf_op jit(solution)/shard_map/ppermute | solution.py:380
  42.3 13.4 %collective-permute-start.13 = (f32[8,128,128]{2,1,0:T(8,128)S(1)}, f32[8,128,128]{2,1,0:T(8,128)S(1)}, u32[]{:S(2)}, u32[]{:S(2)}) collective-permute-start(f32[8,128,128]{2,1,0:T(8,128)S(1)} %final_state.3.rest_1_), channel_id=1, source_target_pairs={{0,1},{1,0},{2,3},{3,2},{4,5},{5,4},{6,7},{7,6},{8,9},{9,8},{10,11... | collective-permute-start | bytes 1572872 | tf_op jit(solution)/shard_map/ppermute | solution.py:380
  42.4 12.6 %collective-permute-start.7 = (bf16[256,640]{1,0:T(8,128)(2,1)S(1)}, bf16[256,640]{1,0:T(8,128)(2,1)S(1)}, u32[]{:S(2)}, u32[]{:S(2)}) collective-permute-start(bf16[256,640]{1,0:T(8,128)(2,1)S(1)} %get-tuple-element.68), channel_id=1, source_target_pairs={{0,2},{2,0},{4,6},{6,4},{1,3},{3,1},{5,7},{7,5},{8,10},{10,8},{12,... | collective-permute-start | bytes 983048 | tf_op jit(solution)/shard_map/ppermute | solution.py:380
  46.6 10.7 %collective-permute-start.12 = (f32[8,128,128]{2,1,0:T(8,128)S(1)}, f32[8,128,128]{2,1,0:T(8,128)S(1)}, u32[]{:S(2)}, u32[]{:S(2)}) collective-permute-start(f32[8,128,128]{2,1,0:T(8,128)S(1)} %final_state.2.rest_3_.rest_0_), channel_id=1, source_target_pairs={{0,1},{1,0},{2,3},{3,2},{4,5},{5,4},{6,7},{7,6},{8,9},{9,8},{10,11... | collective-permute-start | bytes 1572872 | tf_op jit(solution)/shard_map/ppermute | solution.py:380
  48.6 22.0 %collective-permute-start.11 = (bf16[256,896]{1,0:T(8,128)(2,1)S(1)}, bf16[256,896]{1,0:T(8,128)(2,1)S(1)}, u32[]{:S(2)}, u32[]{:S(2)}) collective-permute-start(bf16[256,896]{1,0:T(8,128)(2,1)S(1)} %project.9), channel_id=1, source_target_pairs={{0,4},{2,6},{4,0},{6,2},{1,5},{3,7},{5,1},{7,3},{8,12},{10,14},{12... | collective-permute-start | bytes 1376264 | tf_op jit(solution)/shard_map/ppermute | solution.py:380
  49.9 7.3 %copy-start = (f32[4,16,2]{1,2,0:T(2,128)S(1)}, f32[4,16,2]{1,2,0:T(2,128)}, u32[]{:S(2)}) copy-start(f32[4,16,2]{1,2,0:T(2,128)} %param.18) | copy-start | bytes 1540
  49.9 7.3 %copy-start.1 = (s32[4]{0:T(128)S(1)}, s32[4]{0:T(128)}, u32[]{:S(2)}) copy-start(s32[4]{0:T(128)} %prompt_ref.1) | copy-start | bytes 52
  49.9 25.5 %collective-permute-start.10 = (bf16[256,896]{1,0:T(8,128)(2,1)S(1)}, bf16[256,896]{1,0:T(8,128)(2,1)S(1)}, u32[]{:S(2)}, u32[]{:S(2)}) collective-permute-start(bf16[256,896]{1,0:T(8,128)(2,1)S(1)} %relay.3.rest_5_), channel_id=1, source_target_pairs={{0,2},{2,0},{4,6},{6,4},{1,3},{3,1},{5,7},{7,5},{8,10},{10,8},{12,... | collective-permute-start | bytes 1376264 | tf_op jit(solution)/shard_map/ppermute | solution.py:380
  54.9 14.6 %collective-permute-start.6 = (bf16[256,640]{1,0:T(8,128)(2,1)S(1)}, bf16[256,640]{1,0:T(8,128)(2,1)S(1)}, u32[]{:S(2)}, u32[]{:S(2)}) collective-permute-start(bf16[256,640]{1,0:T(8,128)(2,1)S(1)} %get-tuple-element.64), channel_id=1, source_target_pairs={{0,2},{2,0},{4,6},{6,4},{1,3},{3,1},{5,7},{7,5},{8,10},{10,8},{12,... | collective-permute-start | bytes 983048 | tf_op jit(solution)/shard_map/ppermute | solution.py:380
  55.6 19.7 %collective-permute-start.8 = (bf16[256,640]{1,0:T(8,128)(2,1)S(1)}, bf16[256,640]{1,0:T(8,128)(2,1)S(1)}, u32[]{:S(2)}, u32[]{:S(2)}) collective-permute-start(bf16[256,640]{1,0:T(8,128)(2,1)S(1)} %relay.2.rest_4_), channel_id=1, source_target_pairs={{0,4},{2,6},{4,0},{6,2},{1,5},{3,7},{5,1},{7,3},{8,12},{10,14},{12... | collective-permute-start | bytes 983048 | tf_op jit(solution)/shard_map/ppermute | solution.py:380
  62.9 9.7 %collective-permute-start.14 = (bf16[8,1536]{1,0:T(8,128)(2,1)S(1)}, bf16[8,1536]{1,0:T(8,128)(2,1)S(1)}, u32[]{:S(2)}, u32[]{:S(2)}) collective-permute-start(bf16[8,1536]{1,0:T(8,128)(2,1)S(1)} %get-tuple-element.75), channel_id=1, source_target_pairs={{0,2},{2,0},{4,6},{6,4},{1,3},{3,1},{5,7},{7,5},{8,10},{10,8},{12,... | collective-permute-start | bytes 73736 | tf_op jit(solution)/shard_map/ppermute | solution.py:380
  69.6 3.8 %collective-permute-start.15 = (bf16[8,1536]{1,0:T(8,128)(2,1)S(1)}, bf16[8,1536]{1,0:T(8,128)(2,1)S(1)}, u32[]{:S(2)}, u32[]{:S(2)}) collective-permute-start(bf16[8,1536]{1,0:T(8,128)(2,1)S(1)} %get-tuple-element.76), channel_id=1, source_target_pairs={{0,4},{2,6},{4,0},{6,2},{1,5},{3,7},{5,1},{7,3},{8,12},{10,14},{12... | collective-permute-start | bytes 73736 | tf_op jit(solution)/shard_map/ppermute | solution.py:380
  70.7 4.7 %collective-permute-start.16 = (bf16[8,1536]{1,0:T(8,128)(2,1)S(1)}, bf16[8,1536]{1,0:T(8,128)(2,1)S(1)}, u32[]{:S(2)}, u32[]{:S(2)}) collective-permute-start(bf16[8,1536]{1,0:T(8,128)(2,1)S(1)} %get-tuple-element.77), channel_id=1, source_target_pairs={{0,6},{2,4},{4,2},{6,0},{1,7},{3,5},{5,3},{7,1},{8,14},{10,12},{12... | collective-permute-start | bytes 73736 | tf_op jit(solution)/shard_map/ppermute | solution.py:380

commit v13 on v12

--- a/solution.py
+++ b/solution.py
@@ -324,9 +324,9 @@
     return total
 
 
-def project_kernel(pieces, width, chunks, added, place_ref, *rest):
+def project_kernel(pieces, width, chunks, added, used, place_ref, *rest):
     hidden, rest = rest[:chunks], rest[chunks:]
-    addends, weights = rest[:added], rest[added : -len(pieces)]
+    addends, weights = rest[:added], rest[added : added + used]
     outs = rest[-len(pieces) :]
     rows = jnp.concatenate([ref[...] for ref in hidden], axis=1)
     for n, ((bits, first, columns), out_ref) in enumerate(zip(pieces, outs)):
@@ -578,20 +578,20 @@
     split = (width * 5 // 12) // HEAD_DIM * HEAD_DIM
     side_x, side_y = (0, split), (split, width - split)
 
-    def project(pieces, dtype, inputs=None, parts_used=None, addends=()):
+    def project(pieces, dtype, inputs=None, parts_used=None, addends=(), after=()):
         dtypes = dtype if isinstance(dtype, tuple) else (dtype,) * len(pieces)
         inputs = hidden if inputs is None else inputs
         used = weights if parts_used is None else weights[parts_used]
         moved = sum(columns for _, _, columns in pieces)
         depth = sum(array.shape[1] for array in inputs)
         return call(
-            functools.partial(project_kernel, pieces, width, len(inputs), len(addends)),
+            functools.partial(project_kernel, pieces, width, len(inputs), len(addends), len(used)),
             "project",
-            [SMEM] + [VMEM] * (len(inputs) + len(addends) + len(used)),
+            [SMEM] + [VMEM] * (len(inputs) + len(addends) + len(used)) + [ANY] * len(after),
             [sds((length, columns), kind) for (_, _, columns), kind in zip(pieces, dtypes)],
             (),
             cost(2 * length * depth * moved, depth * moved * 2),
-        )(place, *inputs, *addends, *used)
+        )(place, *inputs, *addends, *used, *after)
 
     def relay(own_term, got):
         return call(
@@ -613,24 +613,25 @@
         to_x, to_y = project(far, BF16)
     far_a = swap(to_x, "head", parts, 1)
     far_b = swap(to_y, "head", parts, 2)
-    near_x, own_a, own_b = project([(1, *side_x), (0, *side_x), (0, *side_y)], (BF16, F32, F32))
+    near_y, near_x = project([(2, *side_y), (1, *side_x)], BF16)
     x_a = swap(near_x, "head", parts, 1)
-    y_b = swap(project([(2, *side_y)], BF16)[0], "head", parts, 2)
-    pass_a, pass_b = project([(2, *side_x), (1, *side_y)], F32)
+    y_b = swap(near_y, "head", parts, 2)
+    finals.append(make_final(count - 1, to_y))
+    d_hidden = decode_rows(*zip(*finals), near_y)
+    pass_a, pass_b = project([(2, *side_x), (1, *side_y)], F32, after=(d_hidden,))
+    own_a, own_b = project([(0, *side_x), (0, *side_y)], F32)
     sent_a, sent_b = relay(pass_a, far_a), relay(pass_b, far_b)
     y_a = swap(sent_a, "head", parts, 2)
     x_b = swap(sent_b, "head", parts, 1)
 
-    finals.append(make_final(count - 1, to_y))
-    d_hidden = decode_rows(*zip(*finals), sent_a, sent_b)
     d_own, d_x, d_y, d_far = call(
         decode_project_kernel,
         "decode_project",
-        [SMEM] + [VMEM] * (1 + WEIGHT_PARTS),
+        [SMEM] + [VMEM] * (1 + WEIGHT_PARTS) + [ANY] * 2,
         [sds((d_rows, width), F32)] + [sds((d_rows, width), BF16)] * 3,
         (),
         cost(2 * d_pad * features * out_columns, features * out_columns // 8),
-    )(place, d_hidden, *weights)
+    )(place, d_hidden, *weights, sent_a, sent_b)
     prefill_out, decode_out = call(
         finish_kernel,
         "finish",

time: 77.4 us -> 73.6 us (0.951)
  waiting for transfers between devices: 14.8 us -> 12.4 us
  starting transfers between devices: 19.5 us -> 18.1 us
    ppermute x11, waiting for transfers between devices: 8.58 us -> 6.27 us  [swap(): return lax.ppermute(array, axis, [(i, i ^ bit) for i in range(size)])]
    ppermute x11, starting transfers between devices: 12.3 us -> 11 us  [swap(): return lax.ppermute(array, axis, [(i, i ^ bit) for i in range(size)])]
  transfers between devices with their start and end apart: 17 -> 17, of which waited for: 8 -> 8; matrix products, arithmetic and copies ran while one was open for 0% -> 0% of each run, Pallas kernels for 44% -> 50%
where the time goes in v13:
time: 73.6 us; the launch traced here: 73.4 us
  Pallas kernels  41.7 us (57%)
  starting transfers between devices  18.1 us (25%)
  waiting for transfers between devices  12.4 us (17%)
  between operations  1 us (1%)
    pallas_call x5, Pallas kernels, project(): call(functools.partial(project_kernel, pieces, width, len(inputs), len(ad...  11.3 us
    ppermute x11, starting transfers between devices, swap(): return lax.ppermute(array, axis, [(i, i ^ bit) for i in range(size)])  11 us
    ppermute x6, starting transfers between devices, body(): lax.ppermute(value, ('ctx', 'rep'), pairs)  7.18 us
    pallas_call x2, Pallas kernels, load_weight(): call(functools.partial(load_kernel, places), 'load_weight', [HBM] + [ANY]...  6.65 us
    ppermute x11, waiting for transfers between devices, swap(): return lax.ppermute(array, axis, [(i, i ^ bit) for i in range(size)])  6.27 us
    ppermute x6, waiting for transfers between devices, body(): lax.ppermute(value, ('ctx', 'rep'), pairs)  6.18 us
    pallas_call x1, Pallas kernels, body(): call(functools.partial(local_kernel, len(arrays)), 'local_attention', [VM...  4.17 us
    pallas_call x1, Pallas kernels, body(): call(decode_project_kernel, 'decode_project', [SMEM] + [VMEM] * (1 + WEIG...  3.88 us
  transfers between devices with their start and end apart: 17, of which 8 were waited for; matrix products, arithmetic and copies ran while one was open for 0% of the time, Pallas kernels for 50%

profile of v13, /device:TPU:0, one launch (start us, length us, event | category | flops | bytes accessed | tf_op | source)
XLA Modules:
  0.0 73.4 jit_solution(4101549571840145754)
XLA Ops:
  0.6 0.1 pad_add_fusion.place_ref
  0.7 3.2 %own_state.1 = (f32[8,128,128]{2,1,0:T(8,128)S(1)}, f32[1,128]{1,0:T(1,128)S(1)}, f32[256,16]{1,0:T(8,128)S(1)}, f32[1,16,256]{2,1,0:T(8,128)S(1)}, bf16[256,204...) custom-call(s32[3]{0:T(128)S(1)} %pad_add_fusion.place_ref, ...), custom_call_target="tpu_custom_call" | custom-call | flops 268435456 | bytes 8388608 | tf_op jit(solution)/shard_map/own_state/pallas_call | solution.py:423
  4.0 3.1 %collective-permute-start = (bf16[1040,128]{1,0:T(8,128)(2,1)S(1)}, bf16[1040,128]{1,0:T(8,128)(2,1)S(1)}, u32[]{:S(2)}, u32[]{:S(2)}) collective-permute-start(bf16[1040,128]{1,0:T(8,128)(2,1)S(1)} %get-tuple-element.47), channel_id=1, source_target_pairs={{0,8},{1,9},{8,0},{9,1},{16,24},{17,25},{24,16},{25,17},{2,10},{3,... | collective-permute-start | bytes 798728 | tf_op jit(solution)/shard_map/ppermute | solution.py:513
  7.0 4.2 %local_attention.1 = (bf16[1,256,2048]{2,1,0:T(8,128)(2,1)S(1)}, bf16[4,2,2048]{2,1,0:T(2,128)(2,1)S(1)}, bf16[4,2,2048]{2,1,0:T(2,128)(2,1)S(1)}, bf16[4,2,2048...) custom-call(bf16[256,2048]{1,0:T(8,128)(2,1)S(1)} %get-tuple-element, ...), custom_call_target="tpu_custom_call" | custom-call | flops 536870912 | bytes 6291456 | tf_op jit(solution)/shard_map/local_attention/pallas_call | solution.py:445
  11.2 1.2 %more_state.1 = (f32[8,128,128]{2,1,0:T(8,128)S(1)}, bf16[1040,128]{1,0:T(8,128)(2,1)S(1)}) custom-call(bf16[256,2048]{1,0:T(8,128)(2,1)S(1)} %get-tuple-element.41.k_ref, bf16[256,2048]{1,0:T(8,128)(2,1)S(1)} %get-tuple-element.42.v_ref, f32[256,16]{1,0:T(8,128)S(1)} %get-tuple-element.43.col_ref, f32[1,128]{1,0:T(1,128)S(1)} %get-tuple-element.49.log_ref, ...), custom_call_target="tpu_custom_call" | custom-call | flops 134217728 | bytes 4194304 | tf_op jit(solution)/shard_map/more_state/pallas_call | solution.py:459
  12.4 0.1 collective-permute-start.3
  12.5 1.0 %collective-permute-done.got_ref.rest_0_ = bf16[1040,128]{1,0:T(8,128)(2,1)S(1)} collective-permute-done((bf16[1040,128]{1,0:T(8,128)(2,1)S(1)}, bf16[1040,128]{1,0:T(8,128)(2,1)S(1)}, u32[]{:S(2)}, u32[]{:S(2)}) %collective-permute-start) | collective-permute-done | bytes 266272 | tf_op jit(solution)/shard_map/ppermute | solution.py:513
  13.4 0.7 chain.4.rest_0_
  14.2 0.1 collective-permute-start.1
  14.3 2.9 %load_weight.2 = (bf16[256,6144]{1,0:T(8,128)(2,1)S(1)}, bf16[256,6144]{1,0:T(8,128)(2,1)S(1)}, f32[8,128]{1,0:T(8,128)S(1)}) custom-call(bf16[2048,6144]{1,0:T(8,128)(2,1)} %weight_hbm.5, bf16[1040,128]{1,0:T(8,128)(2,1)S(1)} %chain.4.rest_0_), custom_call_target="tpu_custom_call" | custom-call | flops 1 | bytes 1 | tf_op jit(solution)/shard_map/load_weight/pallas_call | solution.py:476
  17.1 3.2 %collective-permute-done.3.got_ref.rest_0_ = bf16[1040,128]{1,0:T(8,128)(2,1)S(1)} collective-permute-done((bf16[1040,128]{1,0:T(8,128)(2,1)S(1)}, bf16[1040,128]{1,0:T(8,128)(2,1)S(1)}, u32[]{:S(2)}, u32[]{:S(2)}) %collective-permute-start.3) | collective-permute-done | bytes 266272 | tf_op jit(solution)/shard_map/ppermute | solution.py:513
  20.3 0.7 chain.6
  21.1 0.1 collective-permute-start.4
  21.1 0.0 collective-permute-done.1.got_ref.rest_1_
  21.1 0.7 chain.5.rest_0_
  21.9 3.2 %collective-permute-start.2 = (bf16[1040,128]{1,0:T(8,128)(2,1)S(1)}, bf16[1040,128]{1,0:T(8,128)(2,1)S(1)}, u32[]{:S(2)}, u32[]{:S(2)}) collective-permute-start(bf16[1040,128]{1,0:T(8,128)(2,1)S(1)} %chain.5.rest_0_), channel_id=1, source_target_pairs={{0,8},{1,9},{8,0},{9,1},{16,24},{17,25},{24,16},{25,17},{2,10},{3,... | collective-permute-start | bytes 798728 | tf_op jit(solution)/shard_map/ppermute | solution.py:513
  25.1 3.8 %load_weight.3 = (bf16[256,6144]{1,0:T(8,128)(2,1)S(1)}, bf16[256,6144]{1,0:T(8,128)(2,1)S(1)}, bf16[256,6144]{1,0:T(8,128)(2,1)S(1)}, f32[8,128]{1,0:T(8,128)S(1)}) custom-call(bf16[2048,6144]{1,0:T(8,128)(2,1)} %weight_hbm.5, bf16[1040,128]{1,0:T(8,128)(2,1)S(1)} %chain.5.rest_0_), custom_call_target="tpu_custom_call" | custom-call | flops 1 | bytes 1 | tf_op jit(solution)/shard_map/load_weight/pallas_call | solution.py:476
  28.9 0.0 collective-permute-done.4.got_ref.rest_1_
  28.9 0.7 chain.7
  29.6 0.7 collective-permute-start.5
  30.3 0.8 %collective-permute-done.2.rest_2_ = bf16[1040,128]{1,0:T(8,128)(2,1)S(1)} collective-permute-done((bf16[1040,128]{1,0:T(8,128)(2,1)S(1)}, bf16[1040,128]{1,0:T(8,128)(2,1)S(1)}, u32[]{:S(2)}, u32[]{:S(2)}) %collective-permute-start.2) | collective-permute-done | bytes 266272 | tf_op jit(solution)/shard_map/ppermute | solution.py:513
  31.0 1.6 %hidden.2.rest_3_.rest_0_ = bf16[256,1024]{1,0:T(8,128)(2,1)S(1)} custom-call(s32[3]{0:T(128)S(1)} %pad_add_fusion.place_ref, bf16[1,256,2048]{2,1,0:T(8,128)(2,1)S(1)} %get-tuple-element.45.q_ref, f32[256,16]{1,0:T(8,128)S(1)} %get-tuple-element.43.col_ref, f32[256,2048]{1,0:T(8,128)S(1)} %get-tuple-element.46.local_ref, ...), custom_call_target="tpu_custom_call" | custom-call | flops 67108864 | bytes 5242880 | tf_op jit(solution)/shard_map/hidden/pallas_call | solution.py:521
  32.7 0.7 %final_state.2.rest_3_.rest_0_ = f32[8,128,128]{2,1,0:T(8,128)S(1)} custom-call(s32[3]{0:T(128)S(1)} %pad_add_fusion.place_ref, f32[8,128,128]{2,1,0:T(8,128)S(1)} %get-tuple-element.48.own_ref, f32[1,128]{1,0:T(1,128)S(1)} %get-tuple-element.49.log_ref, bf16[1040,128]{1,0:T(8,128)(2,1)S(1)} %collective-permute-done.got_ref.rest_0_, ...), custom_call_target="tpu_custom_call" | custom-call | flops 524288 | bytes 1048576 | tf_op jit(solution)/shard_map/final_state/pallas_call | solution.py:532
  33.4 0.1 collective-permute-start.7
  33.5 1.7 %project.7 = (f32[256,640]{1,0:T(8,128)S(1)}, f32[256,896]{1,0:T(8,128)S(1)}) custom-call(s32[3]{0:T(128)S(1)} %pad_add_fusion.place_ref, bf16[256,1024]{1,0:T(8,128)(2,1)S(1)} %hidden.2.rest_3_.rest_0_, bf16[256,6144]{1,0:T(8,128)(2,1)S(1)} %get-tuple-element.55.rest_2_.rest_1_.rest_0_, bf16[256,6144]{1,0:T(8,128)(2,1)S(1)} %get-tuple-element.56.rest_3_.rest_2_.rest_1_, ...), custom_call_target="tpu_custom_call" | custom-call | flops 805306368 | bytes 3145728 | tf_op jit(solution)/shard_map/project/pallas_call | solution.py:587
  35.2 1.3 %collective-permute-done.5.rest_2_ = bf16[1040,128]{1,0:T(8,128)(2,1)S(1)} collective-permute-done((bf16[1040,128]{1,0:T(8,128)(2,1)S(1)}, bf16[1040,128]{1,0:T(8,128)(2,1)S(1)}, u32[]{:S(2)}, u32[]{:S(2)}) %collective-permute-start.5) | collective-permute-done | bytes 266272 | tf_op jit(solution)/shard_map/ppermute | solution.py:513
  36.4 1.6 %hidden.3.rest_1_.rest_0_ = bf16[256,1024]{1,0:T(8,128)(2,1)S(1)} custom-call(s32[3]{0:T(128)S(1)} %pad_add_fusion.place_ref, bf16[1,256,2048]{2,1,0:T(8,128)(2,1)S(1)} %get-tuple-element.45.q_ref, f32[256,16]{1,0:T(8,128)S(1)} %get-tuple-element.43.col_ref, f32[256,2048]{1,0:T(8,128)S(1)} %get-tuple-element.46.local_ref, ...), custom_call_target="tpu_custom_call" | custom-call | flops 67108864 | bytes 5242880 | tf_op jit(solution)/shard_map/hidden/pallas_call | solution.py:521
  38.1 1.7 %project.8 = (bf16[256,640]{1,0:T(8,128)(2,1)S(1)}, bf16[256,896]{1,0:T(8,128)(2,1)S(1)}) custom-call(s32[3]{0:T(128)S(1)} %pad_add_fusion.place_ref, bf16[256,1024]{1,0:T(8,128)(2,1)S(1)} %hidden.3.rest_1_.rest_0_, f32[256,640]{1,0:T(8,128)S(1)} %get-tuple-element.69.rest_1_, f32[256,896]{1,0:T(8,128)S(1)} %get-tuple-element.70.rest_2_, ...), custom_call_target="tpu_custom_call" | custom-call | flops 805306368 | bytes 3145728 | tf_op jit(solution)/shard_map/project/pallas_call | solution.py:587
  39.8 0.9 %final_state.3.rest_1_ = f32[8,128,128]{2,1,0:T(8,128)S(1)} custom-call(s32[3]{0:T(128)S(1)} %pad_add_fusion.place_ref, f32[8,128,128]{2,1,0:T(8,128)S(1)} %get-tuple-element.52.own_ref, f32[1,128]{1,0:T(1,128)S(1)} %get-tuple-element.49.log_ref, bf16[1040,128]{1,0:T(8,128)(2,1)S(1)} %collective-permute-done.3.got_ref.rest_0_, ...), custom_call_target="tpu_custom_call" | custom-call | flops 524288 | bytes 1048576 | tf_op jit(solution)/shard_map/final_state/pallas_call | solution.py:532
  40.7 0.1 collective-permute-start.8
  40.8 1.6 %collective-permute-start.11 = (bf16[256,896]{1,0:T(8,128)(2,1)S(1)}, bf16[256,896]{1,0:T(8,128)(2,1)S(1)}, u32[]{:S(2)}, u32[]{:S(2)}) collective-permute-start(bf16[256,896]{1,0:T(8,128)(2,1)S(1)} %get-tuple-element.71.rest_3_), channel_id=1, source_target_pairs={{0,4},{2,6},{4,0},{6,2},{1,5},{3,7},{5,1},{7,3},{8,12},{10,14},{12... | collective-permute-start | bytes 1376264 | tf_op jit(solution)/shard_map/ppermute | solution.py:380
  42.4 0.0 copy-start
  42.4 0.0 copy-start.1
  42.4 1.5 %collective-permute-start.9 = (bf16[256,640]{1,0:T(8,128)(2,1)S(1)}, bf16[256,640]{1,0:T(8,128)(2,1)S(1)}, u32[]{:S(2)}, u32[]{:S(2)}) collective-permute-start(bf16[256,640]{1,0:T(8,128)(2,1)S(1)} %get-tuple-element.74), channel_id=1, source_target_pairs={{0,2},{2,0},{4,6},{6,4},{1,3},{3,1},{5,7},{7,5},{8,10},{10,8},{12,... | collective-permute-start | bytes 983048 | tf_op jit(solution)/shard_map/ppermute | solution.py:380
  43.9 2.7 %project.6 = (bf16[256,896]{1,0:T(8,128)(2,1)S(1)}, bf16[256,640]{1,0:T(8,128)(2,1)S(1)}) custom-call(s32[3]{0:T(128)S(1)} %pad_add_fusion.place_ref, bf16[256,1024]{1,0:T(8,128)(2,1)S(1)} %hidden.2.rest_3_.rest_0_, bf16[256,1024]{1,0:T(8,128)(2,1)S(1)} %hidden.3.rest_1_.rest_0_, bf16[256,6144]{1,0:T(8,128)(2,1)S(1)} %get-tuple-element.55.rest_2_.rest_1_.rest_0_, ...), custom_call_target="tpu_custom_call" | custom-call | flops 1610612736 | bytes 6291456 | tf_op jit(solution)/shard_map/project/pallas_call | solution.py:587
  46.5 0.6 collective-permute-start.6
  47.1 0.0 collective-permute-done.7.rest_2_
  47.1 0.5 collective-permute-start.13
  47.6 0.0 collective-permute-done.8.rest_3_
  47.6 0.0 copy-done
  47.6 0.0 copy-done.1
  47.6 1.7 %decode_rows.1.rest_10_.rows_ref = bf16[16,2048]{1,0:T(8,128)(2,1)S(1)} custom-call(s32[3]{0:T(128)S(1)} %pad_add_fusion.place_ref, s32[4]{0:T(128)S(1)} %copy-done.1, bf16[4,2,2048]{2,1,0:T(2,128)(2,1)S(1)} %get-tuple-element.66.q_ref, bf16[4,2,2048]{2,1,0:T(2,128)(2,1)S(1)} %get-tuple-element.67.k_ref, bf16[4,2,2048]{2,1,0:T(2,128)(2,1)S(1)} %get-tuple-element.68.v_ref, ...), custom_call_target="tpu_custom_call" | custom-call | flops 33554432 | bytes 262144 | tf_op jit(solution)/shard_map/decode_rows/pallas_call | solution.py:549
  49.3 2.7 %project.9 = (f32[256,640]{1,0:T(8,128)S(1)}, f32[256,896]{1,0:T(8,128)S(1)}) custom-call(s32[3]{0:T(128)S(1)} %pad_add_fusion.place_ref, bf16[256,1024]{1,0:T(8,128)(2,1)S(1)} %hidden.2.rest_3_.rest_0_, bf16[256,1024]{1,0:T(8,128)(2,1)S(1)} %hidden.3.rest_1_.rest_0_, bf16[256,6144]{1,0:T(8,128)(2,1)S(1)} %get-tuple-element.55.rest_2_.rest_1_.rest_0_, ...), custom_call_target="tpu_custom_call" | custom-call | flops 1610612736 | bytes 6291456 | tf_op jit(solution)/shard_map/project/pallas_call | solution.py:587
  52.0 2.1 %collective-permute-done.11.got_ref = bf16[256,896]{1,0:T(8,128)(2,1)S(1)} collective-permute-done((bf16[256,896]{1,0:T(8,128)(2,1)S(1)}, bf16[256,896]{1,0:T(8,128)(2,1)S(1)}, u32[]{:S(2)}, u32[]{:S(2)}) %collective-permute-start.11) | collective-permute-done | bytes 458784 | tf_op jit(solution)/shard_map/ppermute | solution.py:380
  54.2 0.1 relay.3.rest_9_
  54.3 1.6 %collective-permute-start.12 = (bf16[256,896]{1,0:T(8,128)(2,1)S(1)}, bf16[256,896]{1,0:T(8,128)(2,1)S(1)}, u32[]{:S(2)}, u32[]{:S(2)}) collective-permute-start(bf16[256,896]{1,0:T(8,128)(2,1)S(1)} %relay.3.rest_9_), channel_id=1, source_target_pairs={{0,2},{2,0},{4,6},{6,4},{1,3},{3,1},{5,7},{7,5},{8,10},{10,8},{12,... | collective-permute-start | bytes 1376264 | tf_op jit(solution)/shard_map/ppermute | solution.py:380
  55.8 0.0 collective-permute-done.9.got_ref
  55.8 0.1 relay.2.rest_8_
  55.9 1.6 %collective-permute-start.10 = (bf16[256,640]{1,0:T(8,128)(2,1)S(1)}, bf16[256,640]{1,0:T(8,128)(2,1)S(1)}, u32[]{:S(2)}, u32[]{:S(2)}) collective-permute-start(bf16[256,640]{1,0:T(8,128)(2,1)S(1)} %relay.2.rest_8_), channel_id=1, source_target_pairs={{0,4},{2,6},{4,0},{6,2},{1,5},{3,7},{5,1},{7,3},{8,12},{10,14},{12... | collective-permute-start | bytes 983048 | tf_op jit(solution)/shard_map/ppermute | solution.py:380
  57.5 3.9 %decode_project.1 = (f32[8,1536]{1,0:T(8,128)S(1)}, bf16[8,1536]{1,0:T(8,128)(2,1)S(1)}, bf16[8,1536]{1,0:T(8,128)(2,1)S(1)}, bf16[8,1536]{1,0:T(8,128)(2,1)S(1)}) custom-call(s32[3]{0:T(128)S(1)} %pad_add_fusion.place_ref, bf16[16,2048]{1,0:T(8,128)(2,1)S(1)} %decode_rows.1.rest_10_.rows_ref, ...), custom_call_target="tpu_custom_call" | custom-call | flops 402653184 | bytes 1572864 | tf_op jit(solution)/shard_map/decode_project/pallas_call | solution.py:627
  61.4 0.5 collective-permute-start.14
  61.9 0.0 collective-permute-done.6.ax
  61.9 0.5 collective-permute-start.15
  62.4 1.6 %collective-permute-done.13.by = bf16[256,896]{1,0:T(8,128)(2,1)S(1)} collective-permute-done((bf16[256,896]{1,0:T(8,128)(2,1)S(1)}, bf16[256,896]{1,0:T(8,128)(2,1)S(1)}, u32[]{:S(2)}, u32[]{:S(2)}) %collective-permute-start.13) | collective-permute-done | bytes 458784 | tf_op jit(solution)/shard_map/ppermute | solution.py:380
  64.0 2.5 %collective-permute-start.16 = (bf16[8,1536]{1,0:T(8,128)(2,1)S(1)}, bf16[8,1536]{1,0:T(8,128)(2,1)S(1)}, u32[]{:S(2)}, u32[]{:S(2)}) collective-permute-start(bf16[8,1536]{1,0:T(8,128)(2,1)S(1)} %get-tuple-element.79), channel_id=1, source_target_pairs={{0,6},{2,4},{4,2},{6,0},{1,7},{3,5},{5,3},{7,1},{8,14},{10,12},{12... | collective-permute-start | bytes 73736 | tf_op jit(solution)/shard_map/ppermute | solution.py:380
  66.4 2.6 %project.5 = (f32[256,640]{1,0:T(8,128)S(1)}, f32[256,896]{1,0:T(8,128)S(1)}) custom-call(s32[3]{0:T(128)S(1)} %pad_add_fusion.place_ref, bf16[256,1024]{1,0:T(8,128)(2,1)S(1)} %hidden.2.rest_3_.rest_0_, bf16[256,1024]{1,0:T(8,128)(2,1)S(1)} %hidden.3.rest_1_.rest_0_, bf16[256,6144]{1,0:T(8,128)(2,1)S(1)} %get-tuple-element.55.rest_2_.rest_1_.rest_0_, ...), custom_call_target="tpu_custom_call" | custom-call | flops 1610612736 | bytes 6291456 | tf_op jit(solution)/shard_map/project/pallas_call | solution.py:587
  69.1 0.7 collective-permute-done.14.d_x
  69.8 1.8 %collective-permute-done.15.d_y = bf16[8,1536]{1,0:T(8,128)(2,1)S(1)} collective-permute-done((bf16[8,1536]{1,0:T(8,128)(2,1)S(1)}, bf16[8,1536]{1,0:T(8,128)(2,1)S(1)}, u32[]{:S(2)}, u32[]{:S(2)}) %collective-permute-start.15) | collective-permute-done | bytes 24608 | tf_op jit(solution)/shard_map/ppermute | solution.py:380
  71.6 0.0 collective-permute-done.16.d_far
  71.6 0.0 collective-permute-done.10.ay
  71.6 0.0 collective-permute-done.12.bx
  71.6 1.6 %finish.1 = (bf16[1,256,1536]{2,1,0:T(8,128)(2,1)}, bf16[4,2,1536]{2,1,0:T(2,128)(2,1)}) custom-call(f32[256,640]{1,0:T(8,128)S(1)} %get-tuple-element.63.own_a, f32[256,896]{1,0:T(8,128)S(1)} %get-tuple-element.64.own_b, bf16[256,640]{1,0:T(8,128)(2,1)S(1)} %collective-permute-done.6.ax, bf16[256,640]{1,0:T(8,128)(2,1)S(1)} %collective-permute-done.10.ay, ...), custom_call_target="tpu_custom_call" | custom-call | flops 1179648 | bytes 3932160 | tf_op jit(solution)/shard_map/finish/pallas_call | solution.py:635
Async XLA Ops:
  4.0 9.5 %collective-permute-start = (bf16[1040,128]{1,0:T(8,128)(2,1)S(1)}, bf16[1040,128]{1,0:T(8,128)(2,1)S(1)}, u32[]{:S(2)}, u32[]{:S(2)}) collective-permute-start(bf16[1040,128]{1,0:T(8,128)(2,1)S(1)} %get-tuple-element.47), channel_id=1, source_target_pairs={{0,8},{1,9},{8,0},{9,1},{16,24},{17,25},{24,16},{25,17},{2,10},{3,... | collective-permute-start | bytes 798728 | tf_op jit(solution)/shard_map/ppermute | solution.py:513
  12.4 7.9 %collective-permute-start.3 = (bf16[1040,128]{1,0:T(8,128)(2,1)S(1)}, bf16[1040,128]{1,0:T(8,128)(2,1)S(1)}, u32[]{:S(2)}, u32[]{:S(2)}) collective-permute-start(bf16[1040,128]{1,0:T(8,128)(2,1)S(1)} %get-tuple-element.51.rest_0_), channel_id=1, source_target_pairs={{0,8},{1,9},{8,0},{9,1},{16,24},{17,25},{24,16},{25,17},{2,10},{3,... | collective-permute-start | bytes 798728 | tf_op jit(solution)/shard_map/ppermute | solution.py:513
  14.2 7.0 %collective-permute-start.1 = (bf16[1040,128]{1,0:T(8,128)(2,1)S(1)}, bf16[1040,128]{1,0:T(8,128)(2,1)S(1)}, u32[]{:S(2)}, u32[]{:S(2)}) collective-permute-start(bf16[1040,128]{1,0:T(8,128)(2,1)S(1)} %chain.4.rest_0_), channel_id=1, source_target_pairs={{0,1},{1,0},{8,16},{9,17},{16,8},{17,9},{24,25},{25,24},{2,3},{3,2... | collective-permute-start | bytes 798728 | tf_op jit(solution)/shard_map/ppermute | solution.py:513
  21.1 7.8 %collective-permute-start.4 = (bf16[1040,128]{1,0:T(8,128)(2,1)S(1)}, bf16[1040,128]{1,0:T(8,128)(2,1)S(1)}, u32[]{:S(2)}, u32[]{:S(2)}) collective-permute-start(bf16[1040,128]{1,0:T(8,128)(2,1)S(1)} %chain.6), channel_id=1, source_target_pairs={{0,1},{1,0},{8,16},{9,17},{16,8},{17,9},{24,25},{25,24},{2,3},{3,2... | collective-permute-start | bytes 798728 | tf_op jit(solution)/shard_map/ppermute | solution.py:513
  21.9 9.2 %collective-permute-start.2 = (bf16[1040,128]{1,0:T(8,128)(2,1)S(1)}, bf16[1040,128]{1,0:T(8,128)(2,1)S(1)}, u32[]{:S(2)}, u32[]{:S(2)}) collective-permute-start(bf16[1040,128]{1,0:T(8,128)(2,1)S(1)} %chain.5.rest_0_), channel_id=1, source_target_pairs={{0,8},{1,9},{8,0},{9,1},{16,24},{17,25},{24,16},{25,17},{2,10},{3,... | collective-permute-start | bytes 798728 | tf_op jit(solution)/shard_map/ppermute | solution.py:513
  29.6 6.8 %collective-permute-start.5 = (bf16[1040,128]{1,0:T(8,128)(2,1)S(1)}, bf16[1040,128]{1,0:T(8,128)(2,1)S(1)}, u32[]{:S(2)}, u32[]{:S(2)}) collective-permute-start(bf16[1040,128]{1,0:T(8,128)(2,1)S(1)} %chain.7), channel_id=1, source_target_pairs={{0,8},{1,9},{8,0},{9,1},{16,24},{17,25},{24,16},{25,17},{2,10},{3,... | collective-permute-start | bytes 798728 | tf_op jit(solution)/shard_map/ppermute | solution.py:513
  33.4 13.7 %collective-permute-start.7 = (f32[8,128,128]{2,1,0:T(8,128)S(1)}, f32[8,128,128]{2,1,0:T(8,128)S(1)}, u32[]{:S(2)}, u32[]{:S(2)}) collective-permute-start(f32[8,128,128]{2,1,0:T(8,128)S(1)} %final_state.2.rest_3_.rest_0_), channel_id=1, source_target_pairs={{0,1},{1,0},{2,3},{3,2},{4,5},{5,4},{6,7},{7,6},{8,9},{9,8},{10,11... | collective-permute-start | bytes 1572872 | tf_op jit(solution)/shard_map/ppermute | solution.py:380
  40.7 6.9 %collective-permute-start.8 = (f32[8,128,128]{2,1,0:T(8,128)S(1)}, f32[8,128,128]{2,1,0:T(8,128)S(1)}, u32[]{:S(2)}, u32[]{:S(2)}) collective-permute-start(f32[8,128,128]{2,1,0:T(8,128)S(1)} %final_state.3.rest_1_), channel_id=1, source_target_pairs={{0,1},{1,0},{2,3},{3,2},{4,5},{5,4},{6,7},{7,6},{8,9},{9,8},{10,11... | collective-permute-start | bytes 1572872 | tf_op jit(solution)/shard_map/ppermute | solution.py:380
  40.8 13.4 %collective-permute-start.11 = (bf16[256,896]{1,0:T(8,128)(2,1)S(1)}, bf16[256,896]{1,0:T(8,128)(2,1)S(1)}, u32[]{:S(2)}, u32[]{:S(2)}) collective-permute-start(bf16[256,896]{1,0:T(8,128)(2,1)S(1)} %get-tuple-element.71.rest_3_), channel_id=1, source_target_pairs={{0,4},{2,6},{4,0},{6,2},{1,5},{3,7},{5,1},{7,3},{8,12},{10,14},{12... | collective-permute-start | bytes 1376264 | tf_op jit(solution)/shard_map/ppermute | solution.py:380
  42.4 5.3 %copy-start = (f32[4,16,2]{1,2,0:T(2,128)S(1)}, f32[4,16,2]{1,2,0:T(2,128)}, u32[]{:S(2)}) copy-start(f32[4,16,2]{1,2,0:T(2,128)} %param.18) | copy-start | bytes 1540
  42.4 5.3 %copy-start.1 = (s32[4]{0:T(128)S(1)}, s32[4]{0:T(128)}, u32[]{:S(2)}) copy-start(s32[4]{0:T(128)} %prompt_ref.1) | copy-start | bytes 52
  42.4 13.5 %collective-permute-start.9 = (bf16[256,640]{1,0:T(8,128)(2,1)S(1)}, bf16[256,640]{1,0:T(8,128)(2,1)S(1)}, u32[]{:S(2)}, u32[]{:S(2)}) collective-permute-start(bf16[256,640]{1,0:T(8,128)(2,1)S(1)} %get-tuple-element.74), channel_id=1, source_target_pairs={{0,2},{2,0},{4,6},{6,4},{1,3},{3,1},{5,7},{7,5},{8,10},{10,8},{12,... | collective-permute-start | bytes 983048 | tf_op jit(solution)/shard_map/ppermute | solution.py:380
  46.5 15.4 %collective-permute-start.6 = (bf16[256,640]{1,0:T(8,128)(2,1)S(1)}, bf16[256,640]{1,0:T(8,128)(2,1)S(1)}, u32[]{:S(2)}, u32[]{:S(2)}) collective-permute-start(bf16[256,640]{1,0:T(8,128)(2,1)S(1)} %get-tuple-element.65), channel_id=1, source_target_pairs={{0,2},{2,0},{4,6},{6,4},{1,3},{3,1},{5,7},{7,5},{8,10},{10,8},{12,... | collective-permute-start | bytes 983048 | tf_op jit(solution)/shard_map/ppermute | solution.py:380
  47.1 16.9 %collective-permute-start.13 = (bf16[256,896]{1,0:T(8,128)(2,1)S(1)}, bf16[256,896]{1,0:T(8,128)(2,1)S(1)}, u32[]{:S(2)}, u32[]{:S(2)}) collective-permute-start(bf16[256,896]{1,0:T(8,128)(2,1)S(1)} %get-tuple-element.72.rest_4_), channel_id=1, source_target_pairs={{0,4},{2,6},{4,0},{6,2},{1,5},{3,7},{5,1},{7,3},{8,12},{10,14},{12... | collective-permute-start | bytes 1376264 | tf_op jit(solution)/shard_map/ppermute | solution.py:380
  54.3 17.4 %collective-permute-start.12 = (bf16[256,896]{1,0:T(8,128)(2,1)S(1)}, bf16[256,896]{1,0:T(8,128)(2,1)S(1)}, u32[]{:S(2)}, u32[]{:S(2)}) collective-permute-start(bf16[256,896]{1,0:T(8,128)(2,1)S(1)} %relay.3.rest_9_), channel_id=1, source_target_pairs={{0,2},{2,0},{4,6},{6,4},{1,3},{3,1},{5,7},{7,5},{8,10},{10,8},{12,... | collective-permute-start | bytes 1376264 | tf_op jit(solution)/shard_map/ppermute | solution.py:380
  55.9 15.7 %collective-permute-start.10 = (bf16[256,640]{1,0:T(8,128)(2,1)S(1)}, bf16[256,640]{1,0:T(8,128)(2,1)S(1)}, u32[]{:S(2)}, u32[]{:S(2)}) collective-permute-start(bf16[256,640]{1,0:T(8,128)(2,1)S(1)} %relay.2.rest_8_), channel_id=1, source_target_pairs={{0,4},{2,6},{4,0},{6,2},{1,5},{3,7},{5,1},{7,3},{8,12},{10,14},{12... | collective-permute-start | bytes 983048 | tf_op jit(solution)/shard_map/ppermute | solution.py:380
  61.4 8.4 %collective-permute-start.14 = (bf16[8,1536]{1,0:T(8,128)(2,1)S(1)}, bf16[8,1536]{1,0:T(8,128)(2,1)S(1)}, u32[]{:S(2)}, u32[]{:S(2)}) collective-permute-start(bf16[8,1536]{1,0:T(8,128)(2,1)S(1)} %get-tuple-element.77), channel_id=1, source_target_pairs={{0,2},{2,0},{4,6},{6,4},{1,3},{3,1},{5,7},{7,5},{8,10},{10,8},{12,... | collective-permute-start | bytes 73736 | tf_op jit(solution)/shard_map/ppermute | solution.py:380
  61.9 9.7 %collective-permute-start.15 = (bf16[8,1536]{1,0:T(8,128)(2,1)S(1)}, bf16[8,1536]{1,0:T(8,128)(2,1)S(1)}, u32[]{:S(2)}, u32[]{:S(2)}) collective-permute-start(bf16[8,1536]{1,0:T(8,128)(2,1)S(1)} %get-tuple-element.78), channel_id=1, source_target_pairs={{0,4},{2,6},{4,0},{6,2},{1,5},{3,7},{5,1},{7,3},{8,12},{10,14},{12... | collective-permute-start | bytes 73736 | tf_op jit(solution)/shard_map/ppermute | solution.py:380
  64.0 7.6 %collective-permute-start.16 = (bf16[8,1536]{1,0:T(8,128)(2,1)S(1)}, bf16[8,1536]{1,0:T(8,128)(2,1)S(1)}, u32[]{:S(2)}, u32[]{:S(2)}) collective-permute-start(bf16[8,1536]{1,0:T(8,128)(2,1)S(1)} %get-tuple-element.79), channel_id=1, source_target_pairs={{0,6},{2,4},{4,2},{6,0},{1,7},{3,5},{5,3},{7,1},{8,14},{10,12},{12... | collective-permute-start | bytes 73736 | tf_op jit(solution)/shard_map/ppermute | solution.py:380

commit v14 on v12

--- a/solution.py
+++ b/solution.py
@@ -613,10 +613,11 @@
         to_x, to_y = project(far, BF16)
     far_a = swap(to_x, "head", parts, 1)
     far_b = swap(to_y, "head", parts, 2)
-    near_x, own_a, own_b = project([(1, *side_x), (0, *side_x), (0, *side_y)], (BF16, F32, F32))
+    near_y, near_x = project([(2, *side_y), (1, *side_x)], BF16)
     x_a = swap(near_x, "head", parts, 1)
-    y_b = swap(project([(2, *side_y)], BF16)[0], "head", parts, 2)
+    y_b = swap(near_y, "head", parts, 2)
     pass_a, pass_b = project([(2, *side_x), (1, *side_y)], F32)
+    own_a, own_b = project([(0, *side_x), (0, *side_y)], F32)
     sent_a, sent_b = relay(pass_a, far_a), relay(pass_b, far_b)
     y_a = swap(sent_a, "head", parts, 2)
     x_b = swap(sent_b, "head", parts, 1)

time: 77.4 us -> 72.3 us (0.934)
  waiting for transfers between devices: 14.8 us -> 9.52 us
    ppermute x11, waiting for transfers between devices: 8.58 us -> 3.25 us  [swap(): return lax.ppermute(array, axis, [(i, i ^ bit) for i in range(size)])]
  transfers between devices with their start and end apart: 17 -> 17, of which waited for: 8 -> 7; matrix products, arithmetic and copies ran while one was open for 0% -> 0% of each run, Pallas kernels for 44% -> 46%
where the time goes in v14:
time: 72.3 us; the launch traced here: 72.1 us
  Pallas kernels  41.7 us (58%)
  starting transfers between devices  19.8 us (27%)
  waiting for transfers between devices  9.52 us (13%)
  between operations  1.03 us (1%)
    ppermute x11, starting transfers between devices, swap(): return lax.ppermute(array, axis, [(i, i ^ bit) for i in range(size)])  12.6 us
    pallas_call x5, Pallas kernels, project(): call(functools.partial(project_kernel, pieces, width, len(inputs), len(ad...  11.3 us
    ppermute x6, starting transfers between devices, body(): lax.ppermute(value, ('ctx', 'rep'), pairs)  7.17 us
    pallas_call x2, Pallas kernels, load_weight(): call(functools.partial(load_kernel, places), 'load_weight', [HBM] + [ANY]...  6.65 us
    ppermute x6, waiting for transfers between devices, body(): lax.ppermute(value, ('ctx', 'rep'), pairs)  6.27 us
    pallas_call x1, Pallas kernels, body(): call(functools.partial(local_kernel, len(arrays)), 'local_attention', [VM...  4.17 us
    pallas_call x1, Pallas kernels, body(): call(decode_project_kernel, 'decode_project', [SMEM] + [VMEM] * (1 + WEIG...  3.91 us
    ppermute x11, waiting for transfers between devices, swap(): return lax.ppermute(array, axis, [(i, i ^ bit) for i in range(size)])  3.25 us
  transfers between devices with their start and end apart: 17, of which 7 were waited for; matrix products, arithmetic and copies ran while one was open for 0% of the time, Pallas kernels for 46%

profile of v14, /device:TPU:0, one launch (start us, length us, event | category | flops | bytes accessed | tf_op | source)
XLA Modules:
  0.0 72.1 jit_solution(7657690342084380633)
XLA Ops:
  0.6 0.1 pad_add_fusion.place_ref
  0.7 3.2 %own_state.1 = (f32[8,128,128]{2,1,0:T(8,128)S(1)}, f32[1,128]{1,0:T(1,128)S(1)}, f32[256,16]{1,0:T(8,128)S(1)}, f32[1,16,256]{2,1,0:T(8,128)S(1)}, bf16[256,204...) custom-call(s32[3]{0:T(128)S(1)} %pad_add_fusion.place_ref, ...), custom_call_target="tpu_custom_call" | custom-call | flops 268435456 | bytes 8388608 | tf_op jit(solution)/shard_map/own_state/pallas_call | solution.py:423
  4.0 3.1 %collective-permute-start = (bf16[1040,128]{1,0:T(8,128)(2,1)S(1)}, bf16[1040,128]{1,0:T(8,128)(2,1)S(1)}, u32[]{:S(2)}, u32[]{:S(2)}) collective-permute-start(bf16[1040,128]{1,0:T(8,128)(2,1)S(1)} %get-tuple-element.47), channel_id=1, source_target_pairs={{0,8},{1,9},{8,0},{9,1},{16,24},{17,25},{24,16},{25,17},{2,10},{3,... | collective-permute-start | bytes 798728 | tf_op jit(solution)/shard_map/ppermute | solution.py:513
  7.0 4.2 %local_attention.1 = (bf16[1,256,2048]{2,1,0:T(8,128)(2,1)S(1)}, bf16[4,2,2048]{2,1,0:T(2,128)(2,1)S(1)}, bf16[4,2,2048]{2,1,0:T(2,128)(2,1)S(1)}, bf16[4,2,2048...) custom-call(bf16[256,2048]{1,0:T(8,128)(2,1)S(1)} %get-tuple-element, ...), custom_call_target="tpu_custom_call" | custom-call | flops 536870912 | bytes 6291456 | tf_op jit(solution)/shard_map/local_attention/pallas_call | solution.py:445
  11.2 1.2 %more_state.1 = (f32[8,128,128]{2,1,0:T(8,128)S(1)}, bf16[1040,128]{1,0:T(8,128)(2,1)S(1)}) custom-call(bf16[256,2048]{1,0:T(8,128)(2,1)S(1)} %get-tuple-element.41.k_ref, bf16[256,2048]{1,0:T(8,128)(2,1)S(1)} %get-tuple-element.42.v_ref, f32[256,16]{1,0:T(8,128)S(1)} %get-tuple-element.43.col_ref, f32[1,128]{1,0:T(1,128)S(1)} %get-tuple-element.49.log_ref, ...), custom_call_target="tpu_custom_call" | custom-call | flops 134217728 | bytes 4194304 | tf_op jit(solution)/shard_map/more_state/pallas_call | solution.py:459
  12.4 0.1 collective-permute-start.3
  12.5 1.0 %collective-permute-done.got_ref.rest_0_ = bf16[1040,128]{1,0:T(8,128)(2,1)S(1)} collective-permute-done((bf16[1040,128]{1,0:T(8,128)(2,1)S(1)}, bf16[1040,128]{1,0:T(8,128)(2,1)S(1)}, u32[]{:S(2)}, u32[]{:S(2)}) %collective-permute-start) | collective-permute-done | bytes 266272 | tf_op jit(solution)/shard_map/ppermute | solution.py:513
  13.4 0.7 %chain.4.rest_0_ = bf16[1040,128]{1,0:T(8,128)(2,1)S(1)} custom-call(s32[3]{0:T(128)S(1)} %pad_add_fusion.place_ref, f32[8,128,128]{2,1,0:T(8,128)S(1)} %get-tuple-element.48.own_ref, f32[1,128]{1,0:T(1,128)S(1)} %get-tuple-element.49.log_ref, bf16[1040,128]{1,0:T(8,128)(2,1)S(1)} %collective-permute-done.got_ref.rest_0_, ...), custom_call_target="tpu_custom_call" | custom-call | flops 262144 | bytes 3145728 | tf_op jit(solution)/shard_map/chain/pallas_call | solution.py:503
  14.2 0.1 collective-permute-start.1
  14.2 2.9 %load_weight.2 = (bf16[256,6144]{1,0:T(8,128)(2,1)S(1)}, bf16[256,6144]{1,0:T(8,128)(2,1)S(1)}, f32[8,128]{1,0:T(8,128)S(1)}) custom-call(bf16[2048,6144]{1,0:T(8,128)(2,1)} %weight_hbm.5, bf16[1040,128]{1,0:T(8,128)(2,1)S(1)} %chain.4.rest_0_), custom_call_target="tpu_custom_call" | custom-call | flops 1 | bytes 1 | tf_op jit(solution)/shard_map/load_weight/pallas_call | solution.py:476
  17.1 3.2 %collective-permute-done.3.got_ref.rest_0_ = bf16[1040,128]{1,0:T(8,128)(2,1)S(1)} collective-permute-done((bf16[1040,128]{1,0:T(8,128)(2,1)S(1)}, bf16[1040,128]{1,0:T(8,128)(2,1)S(1)}, u32[]{:S(2)}, u32[]{:S(2)}) %collective-permute-start.3) | collective-permute-done | bytes 266272 | tf_op jit(solution)/shard_map/ppermute | solution.py:513
  20.3 0.7 %chain.6 = bf16[1040,128]{1,0:T(8,128)(2,1)S(1)} custom-call(s32[3]{0:T(128)S(1)} %pad_add_fusion.place_ref, f32[8,128,128]{2,1,0:T(8,128)S(1)} %get-tuple-element.52.own_ref, f32[1,128]{1,0:T(1,128)S(1)} %get-tuple-element.49.log_ref, bf16[1040,128]{1,0:T(8,128)(2,1)S(1)} %collective-permute-done.3.got_ref.rest_0_, f32[8,128]{1,0:T(8,128)S(1)} %get-tuple-element.53.rest_0_), custom_call_target="tpu_custom_call" | custom-call | flops 262144 | bytes 3145728 | tf_op jit(solution)/shard_map/chain/pallas_call | solution.py:503
  21.1 0.1 collective-permute-start.4
  21.1 0.0 collective-permute-done.1.got_ref.rest_1_
  21.1 0.7 %chain.5.rest_0_ = bf16[1040,128]{1,0:T(8,128)(2,1)S(1)} custom-call(s32[3]{0:T(128)S(1)} %pad_add_fusion.place_ref, f32[8,128,128]{2,1,0:T(8,128)S(1)} %get-tuple-element.48.own_ref, f32[1,128]{1,0:T(1,128)S(1)} %get-tuple-element.49.log_ref, bf16[1040,128]{1,0:T(8,128)(2,1)S(1)} %collective-permute-done.1.got_ref.rest_1_), custom_call_target="tpu_custom_call" | custom-call | flops 262144 | bytes 3145728 | tf_op jit(solution)/shard_map/chain/pallas_call | solution.py:503
  21.9 3.2 %collective-permute-start.2 = (bf16[1040,128]{1,0:T(8,128)(2,1)S(1)}, bf16[1040,128]{1,0:T(8,128)(2,1)S(1)}, u32[]{:S(2)}, u32[]{:S(2)}) collective-permute-start(bf16[1040,128]{1,0:T(8,128)(2,1)S(1)} %chain.5.rest_0_), channel_id=1, source_target_pairs={{0,8},{1,9},{8,0},{9,1},{16,24},{17,25},{24,16},{25,17},{2,10},{3,... | collective-permute-start | bytes 798728 | tf_op jit(solution)/shard_map/ppermute | solution.py:513
  25.1 3.8 %load_weight.3 = (bf16[256,6144]{1,0:T(8,128)(2,1)S(1)}, bf16[256,6144]{1,0:T(8,128)(2,1)S(1)}, bf16[256,6144]{1,0:T(8,128)(2,1)S(1)}, f32[8,128]{1,0:T(8,128)S(1)}) custom-call(bf16[2048,6144]{1,0:T(8,128)(2,1)} %weight_hbm.5, bf16[1040,128]{1,0:T(8,128)(2,1)S(1)} %chain.5.rest_0_), custom_call_target="tpu_custom_call" | custom-call | flops 1 | bytes 1 | tf_op jit(solution)/shard_map/load_weight/pallas_call | solution.py:476
  28.9 0.0 collective-permute-done.4.got_ref.rest_1_
  28.9 0.7 %chain.7 = bf16[1040,128]{1,0:T(8,128)(2,1)S(1)} custom-call(s32[3]{0:T(128)S(1)} %pad_add_fusion.place_ref, f32[8,128,128]{2,1,0:T(8,128)S(1)} %get-tuple-element.52.own_ref, f32[1,128]{1,0:T(1,128)S(1)} %get-tuple-element.49.log_ref, bf16[1040,128]{1,0:T(8,128)(2,1)S(1)} %collective-permute-done.4.got_ref.rest_1_, f32[8,128]{1,0:T(8,128)S(1)} %get-tuple-element.54.rest_0_), custom_call_target="tpu_custom_call" | custom-call | flops 262144 | bytes 3145728 | tf_op jit(solution)/shard_map/chain/pallas_call | solution.py:503
  29.6 0.7 collective-permute-start.5
  30.3 0.8 %collective-permute-done.2.rest_2_ = bf16[1040,128]{1,0:T(8,128)(2,1)S(1)} collective-permute-done((bf16[1040,128]{1,0:T(8,128)(2,1)S(1)}, bf16[1040,128]{1,0:T(8,128)(2,1)S(1)}, u32[]{:S(2)}, u32[]{:S(2)}) %collective-permute-start.2) | collective-permute-done | bytes 266272 | tf_op jit(solution)/shard_map/ppermute | solution.py:513
  31.0 1.6 %hidden.2.rest_3_.rest_0_ = bf16[256,1024]{1,0:T(8,128)(2,1)S(1)} custom-call(s32[3]{0:T(128)S(1)} %pad_add_fusion.place_ref, bf16[1,256,2048]{2,1,0:T(8,128)(2,1)S(1)} %get-tuple-element.45.q_ref, f32[256,16]{1,0:T(8,128)S(1)} %get-tuple-element.43.col_ref, f32[256,2048]{1,0:T(8,128)S(1)} %get-tuple-element.46.local_ref, ...), custom_call_target="tpu_custom_call" | custom-call | flops 67108864 | bytes 5242880 | tf_op jit(solution)/shard_map/hidden/pallas_call | solution.py:521
  32.7 0.7 %final_state.2.rest_3_.rest_0_ = f32[8,128,128]{2,1,0:T(8,128)S(1)} custom-call(s32[3]{0:T(128)S(1)} %pad_add_fusion.place_ref, f32[8,128,128]{2,1,0:T(8,128)S(1)} %get-tuple-element.48.own_ref, f32[1,128]{1,0:T(1,128)S(1)} %get-tuple-element.49.log_ref, bf16[1040,128]{1,0:T(8,128)(2,1)S(1)} %collective-permute-done.got_ref.rest_0_, ...), custom_call_target="tpu_custom_call" | custom-call | flops 524288 | bytes 1048576 | tf_op jit(solution)/shard_map/final_state/pallas_call | solution.py:532
  33.4 1.7 %project.8 = (f32[256,640]{1,0:T(8,128)S(1)}, f32[256,896]{1,0:T(8,128)S(1)}) custom-call(s32[3]{0:T(128)S(1)} %pad_add_fusion.place_ref, bf16[256,1024]{1,0:T(8,128)(2,1)S(1)} %hidden.2.rest_3_.rest_0_, bf16[256,6144]{1,0:T(8,128)(2,1)S(1)} %get-tuple-element.55.rest_2_.rest_1_.rest_0_, bf16[256,6144]{1,0:T(8,128)(2,1)S(1)} %get-tuple-element.56.rest_3_.rest_2_.rest_1_, ...), custom_call_target="tpu_custom_call" | custom-call | flops 805306368 | bytes 3145728 | tf_op jit(solution)/shard_map/project/pallas_call | solution.py:587
  35.1 1.3 %collective-permute-done.5.rest_2_ = bf16[1040,128]{1,0:T(8,128)(2,1)S(1)} collective-permute-done((bf16[1040,128]{1,0:T(8,128)(2,1)S(1)}, bf16[1040,128]{1,0:T(8,128)(2,1)S(1)}, u32[]{:S(2)}, u32[]{:S(2)}) %collective-permute-start.5) | collective-permute-done | bytes 266272 | tf_op jit(solution)/shard_map/ppermute | solution.py:513
  36.4 1.6 %hidden.3.rest_1_.rest_0_ = bf16[256,1024]{1,0:T(8,128)(2,1)S(1)} custom-call(s32[3]{0:T(128)S(1)} %pad_add_fusion.place_ref, bf16[1,256,2048]{2,1,0:T(8,128)(2,1)S(1)} %get-tuple-element.45.q_ref, f32[256,16]{1,0:T(8,128)S(1)} %get-tuple-element.43.col_ref, f32[256,2048]{1,0:T(8,128)S(1)} %get-tuple-element.46.local_ref, ...), custom_call_target="tpu_custom_call" | custom-call | flops 67108864 | bytes 5242880 | tf_op jit(solution)/shard_map/hidden/pallas_call | solution.py:521
  38.1 1.7 %project.9 = (bf16[256,640]{1,0:T(8,128)(2,1)S(1)}, bf16[256,896]{1,0:T(8,128)(2,1)S(1)}) custom-call(s32[3]{0:T(128)S(1)} %pad_add_fusion.place_ref, bf16[256,1024]{1,0:T(8,128)(2,1)S(1)} %hidden.3.rest_1_.rest_0_, f32[256,640]{1,0:T(8,128)S(1)} %get-tuple-element.67.rest_1_, f32[256,896]{1,0:T(8,128)S(1)} %get-tuple-element.68.rest_2_, ...), custom_call_target="tpu_custom_call" | custom-call | flops 805306368 | bytes 3145728 | tf_op jit(solution)/shard_map/project/pallas_call | solution.py:587
  39.8 1.6 %collective-permute-start.9 = (bf16[256,896]{1,0:T(8,128)(2,1)S(1)}, bf16[256,896]{1,0:T(8,128)(2,1)S(1)}, u32[]{:S(2)}, u32[]{:S(2)}) collective-permute-start(bf16[256,896]{1,0:T(8,128)(2,1)S(1)} %get-tuple-element.71.rest_3_), channel_id=1, source_target_pairs={{0,4},{2,6},{4,0},{6,2},{1,5},{3,7},{5,1},{7,3},{8,12},{10,14},{12... | collective-permute-start | bytes 1376264 | tf_op jit(solution)/shard_map/ppermute | solution.py:380
  41.3 0.9 %final_state.3.rest_1_ = f32[8,128,128]{2,1,0:T(8,128)S(1)} custom-call(s32[3]{0:T(128)S(1)} %pad_add_fusion.place_ref, f32[8,128,128]{2,1,0:T(8,128)S(1)} %get-tuple-element.52.own_ref, f32[1,128]{1,0:T(1,128)S(1)} %get-tuple-element.49.log_ref, bf16[1040,128]{1,0:T(8,128)(2,1)S(1)} %collective-permute-done.3.got_ref.rest_0_, ...), custom_call_target="tpu_custom_call" | custom-call | flops 524288 | bytes 1048576 | tf_op jit(solution)/shard_map/final_state/pallas_call | solution.py:532
  42.3 0.1 collective-permute-start.13
  42.4 1.6 %collective-permute-start.7 = (bf16[256,640]{1,0:T(8,128)(2,1)S(1)}, bf16[256,640]{1,0:T(8,128)(2,1)S(1)}, u32[]{:S(2)}, u32[]{:S(2)}) collective-permute-start(bf16[256,640]{1,0:T(8,128)(2,1)S(1)} %get-tuple-element.69), channel_id=1, source_target_pairs={{0,2},{2,0},{4,6},{6,4},{1,3},{3,1},{5,7},{7,5},{8,10},{10,8},{12,... | collective-permute-start | bytes 983048 | tf_op jit(solution)/shard_map/ppermute | solution.py:380
  43.9 0.2 collective-permute-start.12
  44.1 2.7 %project.6 = (bf16[256,896]{1,0:T(8,128)(2,1)S(1)}, bf16[256,640]{1,0:T(8,128)(2,1)S(1)}) custom-call(s32[3]{0:T(128)S(1)} %pad_add_fusion.place_ref, bf16[256,1024]{1,0:T(8,128)(2,1)S(1)} %hidden.2.rest_3_.rest_0_, bf16[256,1024]{1,0:T(8,128)(2,1)S(1)} %hidden.3.rest_1_.rest_0_, bf16[256,6144]{1,0:T(8,128)(2,1)S(1)} %get-tuple-element.55.rest_2_.rest_1_.rest_0_, ...), custom_call_target="tpu_custom_call" | custom-call | flops 1610612736 | bytes 6291456 | tf_op jit(solution)/shard_map/project/pallas_call | solution.py:587
  46.7 0.6 collective-permute-start.11
  47.3 2.5 %collective-permute-done.9.got_ref = bf16[256,896]{1,0:T(8,128)(2,1)S(1)} collective-permute-done((bf16[256,896]{1,0:T(8,128)(2,1)S(1)}, bf16[256,896]{1,0:T(8,128)(2,1)S(1)}, u32[]{:S(2)}, u32[]{:S(2)}) %collective-permute-start.9) | collective-permute-done | bytes 458784 | tf_op jit(solution)/shard_map/ppermute | solution.py:380
  49.8 2.5 %collective-permute-start.6 = (bf16[256,640]{1,0:T(8,128)(2,1)S(1)}, bf16[256,640]{1,0:T(8,128)(2,1)S(1)}, u32[]{:S(2)}, u32[]{:S(2)}) collective-permute-start(bf16[256,640]{1,0:T(8,128)(2,1)S(1)} %get-tuple-element.65), channel_id=1, source_target_pairs={{0,2},{2,0},{4,6},{6,4},{1,3},{3,1},{5,7},{7,5},{8,10},{10,8},{12,... | collective-permute-start | bytes 983048 | tf_op jit(solution)/shard_map/ppermute | solution.py:380
  52.3 2.6 %project.7 = (f32[256,640]{1,0:T(8,128)S(1)}, f32[256,896]{1,0:T(8,128)S(1)}) custom-call(s32[3]{0:T(128)S(1)} %pad_add_fusion.place_ref, bf16[256,1024]{1,0:T(8,128)(2,1)S(1)} %hidden.2.rest_3_.rest_0_, bf16[256,1024]{1,0:T(8,128)(2,1)S(1)} %hidden.3.rest_1_.rest_0_, bf16[256,6144]{1,0:T(8,128)(2,1)S(1)} %get-tuple-element.55.rest_2_.rest_1_.rest_0_, ...), custom_call_target="tpu_custom_call" | custom-call | flops 1610612736 | bytes 6291456 | tf_op jit(solution)/shard_map/project/pallas_call | solution.py:587
  54.9 0.0 copy-start
  54.9 0.0 copy-start.1
  55.0 0.1 relay.3.rest_5_
  55.0 0.0 collective-permute-done.7.got_ref
  55.1 0.1 collective-permute-start.10
  55.1 0.1 relay.2.rest_4_
  55.2 0.0 collective-permute-done.13.rest_3_
  55.2 2.5 %collective-permute-start.8 = (bf16[256,640]{1,0:T(8,128)(2,1)S(1)}, bf16[256,640]{1,0:T(8,128)(2,1)S(1)}, u32[]{:S(2)}, u32[]{:S(2)}) collective-permute-start(bf16[256,640]{1,0:T(8,128)(2,1)S(1)} %relay.2.rest_4_), channel_id=1, source_target_pairs={{0,4},{2,6},{4,0},{6,2},{1,5},{3,7},{5,1},{7,3},{8,12},{10,14},{12... | collective-permute-start | bytes 983048 | tf_op jit(solution)/shard_map/ppermute | solution.py:380
  57.8 0.0 collective-permute-done.12.rest_2_
  57.8 0.0 copy-done
  57.8 0.0 copy-done.1
  57.8 1.7 %decode_rows.1.rows_ref = bf16[16,2048]{1,0:T(8,128)(2,1)S(1)} custom-call(s32[3]{0:T(128)S(1)} %pad_add_fusion.place_ref, s32[4]{0:T(128)S(1)} %copy-done.1, bf16[4,2,2048]{2,1,0:T(2,128)(2,1)S(1)} %get-tuple-element.73.q_ref, bf16[4,2,2048]{2,1,0:T(2,128)(2,1)S(1)} %get-tuple-element.74.k_ref, bf16[4,2,2048]{2,1,0:T(2,128)(2,1)S(1)} %get-tuple-element.75.v_ref, ...), custom_call_target="tpu_custom_call" | custom-call | flops 33554432 | bytes 262144 | tf_op jit(solution)/shard_map/decode_rows/pallas_call | solution.py:549
  59.5 3.9 %decode_project.1 = (f32[8,1536]{1,0:T(8,128)S(1)}, bf16[8,1536]{1,0:T(8,128)(2,1)S(1)}, bf16[8,1536]{1,0:T(8,128)(2,1)S(1)}, bf16[8,1536]{1,0:T(8,128)(2,1)S(1)}) custom-call(s32[3]{0:T(128)S(1)} %pad_add_fusion.place_ref, bf16[16,2048]{1,0:T(8,128)(2,1)S(1)} %decode_rows.1.rows_ref, bf16[256,6144]{1,0:T(8,128)(2,1)S(1)} %get-tuple-element.55.rest_2_.rest_1_.rest_0_, ...), custom_call_target="tpu_custom_call" | custom-call | flops 402653184 | bytes 1572864 | tf_op jit(solution)/shard_map/decode_project/pallas_call | solution.py:627
  63.4 2.0 %collective-permute-start.14 = (bf16[8,1536]{1,0:T(8,128)(2,1)S(1)}, bf16[8,1536]{1,0:T(8,128)(2,1)S(1)}, u32[]{:S(2)}, u32[]{:S(2)}) collective-permute-start(bf16[8,1536]{1,0:T(8,128)(2,1)S(1)} %get-tuple-element.77), channel_id=1, source_target_pairs={{0,2},{2,0},{4,6},{6,4},{1,3},{3,1},{5,7},{7,5},{8,10},{10,8},{12,... | collective-permute-start | bytes 73736 | tf_op jit(solution)/shard_map/ppermute | solution.py:380
  65.4 0.0 collective-permute-done.6.ax
  65.4 0.0 collective-permute-start.15
  65.5 0.0 collective-permute-done.11.by
  65.5 1.5 %collective-permute-start.16 = (bf16[8,1536]{1,0:T(8,128)(2,1)S(1)}, bf16[8,1536]{1,0:T(8,128)(2,1)S(1)}, u32[]{:S(2)}, u32[]{:S(2)}) collective-permute-start(bf16[8,1536]{1,0:T(8,128)(2,1)S(1)} %get-tuple-element.79), channel_id=1, source_target_pairs={{0,6},{2,4},{4,2},{6,0},{1,7},{3,5},{5,3},{7,1},{8,14},{10,12},{12... | collective-permute-start | bytes 73736 | tf_op jit(solution)/shard_map/ppermute | solution.py:380
  67.0 2.6 %project.5 = (f32[256,640]{1,0:T(8,128)S(1)}, f32[256,896]{1,0:T(8,128)S(1)}) custom-call(s32[3]{0:T(128)S(1)} %pad_add_fusion.place_ref, bf16[256,1024]{1,0:T(8,128)(2,1)S(1)} %hidden.2.rest_3_.rest_0_, bf16[256,1024]{1,0:T(8,128)(2,1)S(1)} %hidden.3.rest_1_.rest_0_, bf16[256,6144]{1,0:T(8,128)(2,1)S(1)} %get-tuple-element.55.rest_2_.rest_1_.rest_0_, ...), custom_call_target="tpu_custom_call" | custom-call | flops 1610612736 | bytes 6291456 | tf_op jit(solution)/shard_map/project/pallas_call | solution.py:587
  69.6 0.5 collective-permute-done.14.d_x
  70.1 0.0 collective-permute-done.15.d_y
  70.1 0.2 collective-permute-done.16.d_far
  70.3 0.0 collective-permute-done.8.ay
  70.3 0.0 collective-permute-done.10.bx
  70.3 1.6 %finish.1 = (bf16[1,256,1536]{2,1,0:T(8,128)(2,1)}, bf16[4,2,1536]{2,1,0:T(2,128)(2,1)}) custom-call(f32[256,640]{1,0:T(8,128)S(1)} %get-tuple-element.63.own_a, f32[256,896]{1,0:T(8,128)S(1)} %get-tuple-element.64.own_b, bf16[256,640]{1,0:T(8,128)(2,1)S(1)} %collective-permute-done.6.ax, bf16[256,640]{1,0:T(8,128)(2,1)S(1)} %collective-permute-done.8.ay, ...), custom_call_target="tpu_custom_call" | custom-call | flops 1179648 | bytes 3932160 | tf_op jit(solution)/shard_map/finish/pallas_call | solution.py:635
Async XLA Ops:
  4.0 9.5 %collective-permute-start = (bf16[1040,128]{1,0:T(8,128)(2,1)S(1)}, bf16[1040,128]{1,0:T(8,128)(2,1)S(1)}, u32[]{:S(2)}, u32[]{:S(2)}) collective-permute-start(bf16[1040,128]{1,0:T(8,128)(2,1)S(1)} %get-tuple-element.47), channel_id=1, source_target_pairs={{0,8},{1,9},{8,0},{9,1},{16,24},{17,25},{24,16},{25,17},{2,10},{3,... | collective-permute-start | bytes 798728 | tf_op jit(solution)/shard_map/ppermute | solution.py:513
  12.4 7.9 %collective-permute-start.3 = (bf16[1040,128]{1,0:T(8,128)(2,1)S(1)}, bf16[1040,128]{1,0:T(8,128)(2,1)S(1)}, u32[]{:S(2)}, u32[]{:S(2)}) collective-permute-start(bf16[1040,128]{1,0:T(8,128)(2,1)S(1)} %get-tuple-element.51.rest_0_), channel_id=1, source_target_pairs={{0,8},{1,9},{8,0},{9,1},{16,24},{17,25},{24,16},{25,17},{2,10},{3,... | collective-permute-start | bytes 798728 | tf_op jit(solution)/shard_map/ppermute | solution.py:513
  14.2 7.0 %collective-permute-start.1 = (bf16[1040,128]{1,0:T(8,128)(2,1)S(1)}, bf16[1040,128]{1,0:T(8,128)(2,1)S(1)}, u32[]{:S(2)}, u32[]{:S(2)}) collective-permute-start(bf16[1040,128]{1,0:T(8,128)(2,1)S(1)} %chain.4.rest_0_), channel_id=1, source_target_pairs={{0,1},{1,0},{8,16},{9,17},{16,8},{17,9},{24,25},{25,24},{2,3},{3,2... | collective-permute-start | bytes 798728 | tf_op jit(solution)/shard_map/ppermute | solution.py:513
  21.1 7.8 %collective-permute-start.4 = (bf16[1040,128]{1,0:T(8,128)(2,1)S(1)}, bf16[1040,128]{1,0:T(8,128)(2,1)S(1)}, u32[]{:S(2)}, u32[]{:S(2)}) collective-permute-start(bf16[1040,128]{1,0:T(8,128)(2,1)S(1)} %chain.6), channel_id=1, source_target_pairs={{0,1},{1,0},{8,16},{9,17},{16,8},{17,9},{24,25},{25,24},{2,3},{3,2... | collective-permute-start | bytes 798728 | tf_op jit(solution)/shard_map/ppermute | solution.py:513
  21.9 9.2 %collective-permute-start.2 = (bf16[1040,128]{1,0:T(8,128)(2,1)S(1)}, bf16[1040,128]{1,0:T(8,128)(2,1)S(1)}, u32[]{:S(2)}, u32[]{:S(2)}) collective-permute-start(bf16[1040,128]{1,0:T(8,128)(2,1)S(1)} %chain.5.rest_0_), channel_id=1, source_target_pairs={{0,8},{1,9},{8,0},{9,1},{16,24},{17,25},{24,16},{25,17},{2,10},{3,... | collective-permute-start | bytes 798728 | tf_op jit(solution)/shard_map/ppermute | solution.py:513
  29.6 6.8 %collective-permute-start.5 = (bf16[1040,128]{1,0:T(8,128)(2,1)S(1)}, bf16[1040,128]{1,0:T(8,128)(2,1)S(1)}, u32[]{:S(2)}, u32[]{:S(2)}) collective-permute-start(bf16[1040,128]{1,0:T(8,128)(2,1)S(1)} %chain.7), channel_id=1, source_target_pairs={{0,8},{1,9},{8,0},{9,1},{16,24},{17,25},{24,16},{25,17},{2,10},{3,... | collective-permute-start | bytes 798728 | tf_op jit(solution)/shard_map/ppermute | solution.py:513
  39.8 10.1 %collective-permute-start.9 = (bf16[256,896]{1,0:T(8,128)(2,1)S(1)}, bf16[256,896]{1,0:T(8,128)(2,1)S(1)}, u32[]{:S(2)}, u32[]{:S(2)}) collective-permute-start(bf16[256,896]{1,0:T(8,128)(2,1)S(1)} %get-tuple-element.71.rest_3_), channel_id=1, source_target_pairs={{0,4},{2,6},{4,0},{6,2},{1,5},{3,7},{5,1},{7,3},{8,12},{10,14},{12... | collective-permute-start | bytes 1376264 | tf_op jit(solution)/shard_map/ppermute | solution.py:380
  42.3 12.9 %collective-permute-start.13 = (f32[8,128,128]{2,1,0:T(8,128)S(1)}, f32[8,128,128]{2,1,0:T(8,128)S(1)}, u32[]{:S(2)}, u32[]{:S(2)}) collective-permute-start(f32[8,128,128]{2,1,0:T(8,128)S(1)} %final_state.3.rest_1_), channel_id=1, source_target_pairs={{0,1},{1,0},{2,3},{3,2},{4,5},{5,4},{6,7},{7,6},{8,9},{9,8},{10,11... | collective-permute-start | bytes 1572872 | tf_op jit(solution)/shard_map/ppermute | solution.py:380
  42.4 12.7 %collective-permute-start.7 = (bf16[256,640]{1,0:T(8,128)(2,1)S(1)}, bf16[256,640]{1,0:T(8,128)(2,1)S(1)}, u32[]{:S(2)}, u32[]{:S(2)}) collective-permute-start(bf16[256,640]{1,0:T(8,128)(2,1)S(1)} %get-tuple-element.69), channel_id=1, source_target_pairs={{0,2},{2,0},{4,6},{6,4},{1,3},{3,1},{5,7},{7,5},{8,10},{10,8},{12,... | collective-permute-start | bytes 983048 | tf_op jit(solution)/shard_map/ppermute | solution.py:380
  43.9 13.8 %collective-permute-start.12 = (f32[8,128,128]{2,1,0:T(8,128)S(1)}, f32[8,128,128]{2,1,0:T(8,128)S(1)}, u32[]{:S(2)}, u32[]{:S(2)}) collective-permute-start(f32[8,128,128]{2,1,0:T(8,128)S(1)} %final_state.2.rest_3_.rest_0_), channel_id=1, source_target_pairs={{0,1},{1,0},{2,3},{3,2},{4,5},{5,4},{6,7},{7,6},{8,9},{9,8},{10,11... | collective-permute-start | bytes 1572872 | tf_op jit(solution)/shard_map/ppermute | solution.py:380
  46.7 18.7 %collective-permute-start.11 = (bf16[256,896]{1,0:T(8,128)(2,1)S(1)}, bf16[256,896]{1,0:T(8,128)(2,1)S(1)}, u32[]{:S(2)}, u32[]{:S(2)}) collective-permute-start(bf16[256,896]{1,0:T(8,128)(2,1)S(1)} %get-tuple-element.72), channel_id=1, source_target_pairs={{0,4},{2,6},{4,0},{6,2},{1,5},{3,7},{5,1},{7,3},{8,12},{10,14},{12... | collective-permute-start | bytes 1376264 | tf_op jit(solution)/shard_map/ppermute | solution.py:380
  49.8 15.6 %collective-permute-start.6 = (bf16[256,640]{1,0:T(8,128)(2,1)S(1)}, bf16[256,640]{1,0:T(8,128)(2,1)S(1)}, u32[]{:S(2)}, u32[]{:S(2)}) collective-permute-start(bf16[256,640]{1,0:T(8,128)(2,1)S(1)} %get-tuple-element.65), channel_id=1, source_target_pairs={{0,2},{2,0},{4,6},{6,4},{1,3},{3,1},{5,7},{7,5},{8,10},{10,8},{12,... | collective-permute-start | bytes 983048 | tf_op jit(solution)/shard_map/ppermute | solution.py:380
  54.9 2.8 %copy-start = (f32[4,16,2]{1,2,0:T(2,128)S(1)}, f32[4,16,2]{1,2,0:T(2,128)}, u32[]{:S(2)}) copy-start(f32[4,16,2]{1,2,0:T(2,128)} %param.18) | copy-start | bytes 1540
  54.9 2.8 %copy-start.1 = (s32[4]{0:T(128)S(1)}, s32[4]{0:T(128)}, u32[]{:S(2)}) copy-start(s32[4]{0:T(128)} %prompt_ref.1) | copy-start | bytes 52
  55.1 15.3 %collective-permute-start.10 = (bf16[256,896]{1,0:T(8,128)(2,1)S(1)}, bf16[256,896]{1,0:T(8,128)(2,1)S(1)}, u32[]{:S(2)}, u32[]{:S(2)}) collective-permute-start(bf16[256,896]{1,0:T(8,128)(2,1)S(1)} %relay.3.rest_5_), channel_id=1, source_target_pairs={{0,2},{2,0},{4,6},{6,4},{1,3},{3,1},{5,7},{7,5},{8,10},{10,8},{12,... | collective-permute-start | bytes 1376264 | tf_op jit(solution)/shard_map/ppermute | solution.py:380
  55.2 15.1 %collective-permute-start.8 = (bf16[256,640]{1,0:T(8,128)(2,1)S(1)}, bf16[256,640]{1,0:T(8,128)(2,1)S(1)}, u32[]{:S(2)}, u32[]{:S(2)}) collective-permute-start(bf16[256,640]{1,0:T(8,128)(2,1)S(1)} %relay.2.rest_4_), channel_id=1, source_target_pairs={{0,4},{2,6},{4,0},{6,2},{1,5},{3,7},{5,1},{7,3},{8,12},{10,14},{12... | collective-permute-start | bytes 983048 | tf_op jit(solution)/shard_map/ppermute | solution.py:380
  63.4 6.7 %collective-permute-start.14 = (bf16[8,1536]{1,0:T(8,128)(2,1)S(1)}, bf16[8,1536]{1,0:T(8,128)(2,1)S(1)}, u32[]{:S(2)}, u32[]{:S(2)}) collective-permute-start(bf16[8,1536]{1,0:T(8,128)(2,1)S(1)} %get-tuple-element.77), channel_id=1, source_target_pairs={{0,2},{2,0},{4,6},{6,4},{1,3},{3,1},{5,7},{7,5},{8,10},{10,8},{12,... | collective-permute-start | bytes 73736 | tf_op jit(solution)/shard_map/ppermute | solution.py:380
  65.4 4.7 %collective-permute-start.15 = (bf16[8,1536]{1,0:T(8,128)(2,1)S(1)}, bf16[8,1536]{1,0:T(8,128)(2,1)S(1)}, u32[]{:S(2)}, u32[]{:S(2)}) collective-permute-start(bf16[8,1536]{1,0:T(8,128)(2,1)S(1)} %get-tuple-element.78), channel_id=1, source_target_pairs={{0,4},{2,6},{4,0},{6,2},{1,5},{3,7},{5,1},{7,3},{8,12},{10,14},{12... | collective-permute-start | bytes 73736 | tf_op jit(solution)/shard_map/ppermute | solution.py:380
  65.5 4.9 %collective-permute-start.16 = (bf16[8,1536]{1,0:T(8,128)(2,1)S(1)}, bf16[8,1536]{1,0:T(8,128)(2,1)S(1)}, u32[]{:S(2)}, u32[]{:S(2)}) collective-permute-start(bf16[8,1536]{1,0:T(8,128)(2,1)S(1)} %get-tuple-element.79), channel_id=1, source_target_pairs={{0,6},{2,4},{4,2},{6,0},{1,7},{3,5},{5,3},{7,1},{8,14},{10,12},{12... | collective-permute-start | bytes 73736 | tf_op jit(solution)/shard_map/ppermute | solution.py:380
